TPU v7x, 32 devices: a whole 2x2x4 slice. The times are simulated.
32 devices in a mesh: pool: 4 (over x, core), dp: 8 (over z, y).
Axes of the slice: x: 2, y: 2, z: 4, core: 2. Of those that a mesh axis runs over, the one named last changes fastest.
Arguments:
- activations: bfloat16 [4096, 8192], P('dp', 'pool')
- gradient: bfloat16 [8192, 28672], P('pool', 'dp')
- owner_slot: int32 [4, 4], replicated, may hold values from 0 to 15, as said below
Outputs:
- update: bfloat16 [8192, 28672], P('pool', 'dp')
- owned_roots: bfloat16 [4, 16, 512, 512], P('pool', 'dp')
Inputs may be any that keep to these rules, and one draw needn't show every extreme that they name: `owner_slot`: in each row the 4 entries are distinct; entry e names slot e % 2 of the device e // 2 along dp within that group; in every row some device holds 2 of the row's blocks.
All inputs are finite; a program needn't handle non-finite values. Where the computation divides by a largest or mean magnitude, that divisor is 1e-20 or more.
Results may differ from a plain program's by a relative error of at most 0.0053.
Values may be sent and summed in bfloat16 or wider, within the bound.
No kernel may reach another device: no remote copies, remote signals or barrier semaphores. Data moves between devices by JAX's collectives and lax.ppermute only.
A program may use at most 192 MiB of HBM per device.

v0:
```python
import jax
import jax.numpy as jnp
from jax import lax
from jax.sharding import PartitionSpec as P

BLK = 512
ITERS = 3
SLOTS = 2


damping = 0.01


def from_root(block, axis, source):
    block = jnp.where(lax.axis_index(axis) == source, block, jnp.zeros_like(block))
    return lax.psum(block, axis)


def batch_dot(left, right):
    return jnp.einsum(
        "kab,kbc->kac",
        left,
        right,
        precision=lax.Precision.HIGHEST,
        preferred_element_type=jnp.float32,
    )


def solve_blocks(stats, identity):
    matrix = stats + damping * identity
    bound = jnp.max(jnp.sum(jnp.abs(matrix), axis=2), axis=1)
    scale = (2.0 / bound)[:, None, None]
    iterate = scale * matrix
    estimate = jnp.sqrt(jnp.sqrt(scale)) * identity
    for step in range(ITERS):
        factor = (5.0 * identity - iterate) / 4.0
        estimate = batch_dot(estimate, factor)
        if step + 1 < ITERS:
            square = batch_dot(factor, factor)
            iterate = batch_dot(batch_dot(square, square), iterate)
    return estimate


def solve_held(stat, hits, identity):

    def solve_single(matrix):
        return solve_blocks(matrix[None], identity)[0]

    def empty_slot(matrix):
        return jnp.zeros_like(matrix)

    return lax.cond(jnp.any(hits), solve_single, empty_slot, stat).astype(jnp.bfloat16)


def per_device(activations, gradient, owner_slot):
    block_count = activations.shape[1] // BLK
    peer_count = lax.axis_size("dp")
    my_index = lax.axis_index("dp")
    group_index = lax.axis_index("pool")
    owner_row = lax.dynamic_index_in_dim(owner_slot, group_index, 0, keepdims=False)
    tokens_all = activations.shape[0] * peer_count
    identity = jnp.eye(BLK, dtype=jnp.float32)
    features = activations.reshape(activations.shape[0], block_count, BLK)
    partial_value = jnp.einsum(
        "tka,tkb->kab", features, features, preferred_element_type=jnp.float32
    )
    summed = lax.psum(partial_value, "dp") / tokens_all
    held_list = []
    for slot in range(SLOTS):
        hits = owner_row == my_index * SLOTS + slot
        weights = hits.astype(jnp.float32)
        stat = jnp.einsum("k,kab->ab", weights, summed, precision=lax.Precision.HIGHEST)
        held_list.append(solve_held(stat, hits, identity))
    held = jnp.stack(held_list)
    fetched = []
    for block in range(block_count):
        entry = owner_row[block]
        piece = lax.dynamic_index_in_dim(held, entry % SLOTS, 0, keepdims=False)
        fetched.append(from_root(piece, "dp", entry // SLOTS))
    roots = jnp.stack(fetched)
    grad_blocks = gradient.reshape(block_count, BLK, gradient.shape[1])
    preconditioned = jnp.einsum(
        "kab,kbc->kac", roots, grad_blocks, preferred_element_type=jnp.float32
    )
    grad_square = jnp.sum(jnp.square(gradient.astype(jnp.float32)))
    update_square = jnp.sum(preconditioned * preconditioned)
    totals = lax.psum((grad_square, update_square), ("pool", "dp"))
    ratio = jnp.sqrt(totals[0] / (totals[1] + 1e-06))
    update = (preconditioned * ratio).astype(jnp.bfloat16).reshape(gradient.shape)
    return (update, held[None])


def solution(mesh):
    in_specs = (P("dp", "pool"), P("pool", "dp"), P())
    out_specs = (P("pool", "dp"), P("pool", "dp", None, None))
    return jax.shard_map(
        per_device, mesh=mesh, in_specs=in_specs, out_specs=out_specs, check_vma=False
    )
```

profile of v0, /device:TPU:0, one launch (start us, length us, event | category | flops | bytes accessed | tf_op | source)
XLA Modules:
  0.0 426.2 jit_solution(1933366764508905413)
XLA Ops:
  7.2 0.0 all-reduce.5.cloned.1.call-start
  7.2 5.5 %fusion.42 = f32[4,512,512]{2,1,0:T(8,128)} fusion(bf16[64,4,8,512]{3,2,1,0:T(8,128)(2,1)} %bitcast.57), kind=kOutput, calls=%fused_computation.57 | convolution fusion | flops 1073741824 | bytes 6291456 | tf_op jit(solution)/shard_map/tka,tkb->kab/dot_general | solution.py:64
  12.8 0.0 all-reduce.7.cloned.1.call-start
  12.8 1.3 compare_reduce_fusion
  14.2 0.7 fusion.70
  25.9 0.1 fusion.54
  26.0 145.9 %all-reduce.5.cloned.1.call-done = f32[4,512,512]{2,1,0:T(8,128)} async-done(((f32[4,512,512]{2,1,0:T(8,128)}), f32[4,512,512]{2,1,0:T(8,128)}) %all-reduce.5.cloned.1.call-update) | async-done | bytes 4194320 | tf_op jit(solution)/shard_map/psum | solution.py:67
  171.9 2.7 broadcast_multiply_fusion
  174.6 5.4 %fusion.38 = f32[1,512,512]{2,0,1:T(1,128)S(1)} fusion(f32[4,512,512]{2,1,0:T(8,128)S(1)} %broadcast_multiply_fusion, s32[1,4]{1,0:T(1,128)S(1)} %get-tuple-element.50, s32[]{:T(128)S(6)} %add.63), kind=kOutput, calls=%fused_computation.53 | convolution fusion | flops 12582916 | bytes 5242900 | tf_op jit(solution)/shard_map/k,kab->ab/dot_general | solution.py:72
  180.0 5.4 %fusion.40 = f32[1,512,512]{2,0,1:T(1,128)S(1)} fusion(f32[4,512,512]{2,1,0:T(8,128)S(1)} %broadcast_multiply_fusion, s32[1,4]{1,0:T(1,128)S(1)} %get-tuple-element.50, s32[]{:T(128)S(6)} %mul.73), kind=kOutput, calls=%fused_computation.55 | convolution fusion | flops 12582916 | bytes 5242900 | tf_op jit(solution)/shard_map/k,kab->ab/dot_general | solution.py:72
  185.5 1.0 copy.22
  186.5 1.0 copy.21
  187.6 25.4 %conditional.3 = (bf16[1,512,512]{2,1,0:T(8,128)(2,1)S(1)}) conditional(s32[]{:T(128)} %convert_element_type.49, () %tuple.26, (f32[512,512]{1,0:T(8,128)S(1)}, f32[512,512]{1,0:T(8,128)}, f32[512,512]{1,0:T(8,128)S(1)}, f32[512,512]{1,0:T(8,128)S(1)}, f32[512,512]{1,0:T(8,128)S(1)}, /*index=5*/f32[512,512]{1,0:T(8,128)S(1)}) %tuple.50), branch_computations={%region_7.8_spmd, %region_8.11_spmd} | conditional | flops 14501806080 | bytes 31985724 | solution.py:52
  187.8 1.5 abs_reduce_fusion.1
  189.3 0.7 reduce_max.17
  190.8 2.0 fusion.21
  192.8 2.1 fusion.29
  194.9 1.8 fusion.73
  196.7 1.9 fusion.23
  198.6 1.9 fusion.28
  200.5 2.0 fusion.27
  202.6 2.4 fusion.74
  204.9 1.9 fusion.19
  206.9 1.9 fusion.20
  213.0 10.8 %conditional.2 = (bf16[1,512,512]{2,1,0:T(8,128)(2,1)S(1)}) conditional(s32[]{:T(128)} %convert_element_type.47, () %tuple.24, (f32[512,512]{1,0:T(8,128)S(1)}, f32[512,512]{1,0:T(8,128)}, f32[512,512]{1,0:T(8,128)S(1)}, f32[512,512]{1,0:T(8,128)S(1)}, f32[512,512]{1,0:T(8,128)S(1)}, /*index=5*/f32[512,512]{1,0:T(8,128)S(1)}) %tuple.49), branch_computations={%region_2.3_spmd, %region_3.6_spmd} | conditional | flops 14501806080 | bytes 31985724 | solution.py:52
  223.8 2.0 fusion.56
  225.8 13.4 %multiply_reduce_fusion.1 = f32[]{:T(128)} fusion(bf16[2048,3584]{1,0:T(8,128)(2,1)} %param.8), kind=kLoop, calls=%fused_computation.52 | loop fusion | flops 22020096 | bytes 14680068 | tf_op jit(solution)/shard_map/reduce_sum | solution.py:85
  239.3 1.1 fusion.53
  240.3 100.5 %all-reduce.7.cloned.1.call-done = (bf16[1,512,512]{2,1,0:T(8,128)(2,1)}, bf16[1,512,512]{2,1,0:T(8,128)(2,1)}, bf16[1,512,512]{2,1,0:T(8,128)(2,1)}, bf16[1,512,512]{2,1,0:T(8,128)(2,1)}) async-done(((bf16[1,512,512]{2,1,0:T(8,128)(2,1)}, bf16[1,512,512]{2,1,0:T(8,128)(2,1)}, bf16[1,512,512]{2,1,0:T(8,128)(2,1)}, bf16[1,512,512]{2,1,0:T(8,128)(2,1)}), (bf16[1,512,512]{2,1,0:T(8,128)(2,1)}, ...) | async-done | bytes 2097168 | tf_op jit(solution)/shard_map/psum | solution.py:16
  340.8 19.9 %multiply_reduce_fusion = (f32[]{:T(128)}, f32[4,512,3584]{2,1,0:T(8,128)}) fusion(bf16[4,512,3584]{2,1,0:T(8,128)(2,1)} %bitcast.53, bf16[1,512,512]{2,1,0:T(8,128)(2,1)} %get-tuple-element.42, bf16[1,512,512]{2,1,0:T(8,128)(2,1)} %get-tuple-element.43, bf16[1,512,512]{2,1,0:T(8,128)(2,1)} %get-tuple-element.44, bf16[1,512,512]{2,1,0:T(8,128)(2,1)} %get-tuple-element.45), kind=kOutput, calls=%fused_computation.51 | convolution fusion | flops 7534018560 | bytes 46137348 | tf_op jit(solution)/shard_map/kab,kbc->kac/dot_general | solution.py:82
  360.7 39.6 %all-reduce = (f32[]{:T(128)}, f32[]{:T(128)}) all-reduce(f32[]{:T(128)} %multiply_reduce_fusion.1, f32[]{:T(128)} %get-tuple-element.59), channel_id=1, replica_groups=mesh['pool'=4,'dp'=8] {'pool','dp'}, use_global_device_ids=true, to_apply=%region_16.17 | all-reduce | flops 2 | bytes 16 | tf_op jit(solution)/shard_map/psum | solution.py:87
  401.7 17.4 %multiply_convert_fusion = bf16[4,512,3584]{2,1,0:T(8,128)(2,1)} fusion(f32[4,512,3584]{2,1,0:T(8,128)} %get-tuple-element.60, f32[]{:T(128)S(6)} %sqrt.23), kind=kLoop, calls=%fused_computation.50 | loop fusion | flops 14680064 | bytes 44040196 | tf_op jit(solution)/shard_map/convert_element_type | solution.py:89
  (3 shorter events, 0.1 us)
Async XLA Ops:
  7.2 164.7 %all-reduce.5.cloned.1.call-start = ((), (), s32[]{:S(2)}) async-start(), calls=%async_computation | async-start | bytes 8388608 | tf_op jit(solution)/shard_map/psum | solution.py:67
  12.8 328.1 %all-reduce.7.cloned.1.call-start = ((), (), s32[]{:S(2)}) async-start(), calls=%async_computation.1 | async-start | bytes 4194304 | tf_op jit(solution)/shard_map/psum | solution.py:16
Sparse Core Ops, SparseCore 0:
  12.9 158.9 all-reduce.4
  226.0 114.8 all-reduce.6
where the time goes:
time: 433 us; the launch traced here: 426 us
  waiting for transfers between devices  246 us (57%)
  matrix products  54.1 us (12%)
  other arithmetic  40.2 us (9%)
  blocking collectives  39.6 us (9%)
  between operations  26.8 us (6%)
  loops' own time  16.2 us (4%)
    psum x1, waiting for transfers between devices, per_device(): summed = lax.psum(partial_value, 'dp') / tokens_all  146 us
    psum x1, waiting for transfers between devices, from_root(): return lax.psum(block, axis)  101 us
    psum x1, blocking collectives, per_device(): totals = lax.psum((grad_square, update_square), ('pool', 'dp'))  39.6 us
    dot_general x1, matrix products, per_device(): jnp.einsum('kab,kbc->kac', roots, grad_blocks, preferred_element_type=jnp...  19.9 us
    dot_general x9, matrix products, batch_dot(): jnp.einsum('kab,kbc->kac', left, right, precision=lax.Precision.HIGHEST,...  17.8 us
    convert_element_type x1, other arithmetic, per_device(): (preconditioned * ratio).astype(jnp.bfloat16).reshape(gradient.shape)  17.4 us
    another operation x2, loops' own time, solve_held(): lax.cond(jnp.any(hits), solve_single, empty_slot, stat).astype(jnp.bfloat16)  16.2 us
    reduce_sum x1, other arithmetic, per_device(): grad_square = jnp.sum(jnp.square(gradient.astype(jnp.float32)))  13.4 us
  transfers between devices with their start and end apart: 2, of which 2 were waited for; matrix products, arithmetic and copies ran while one was open for 4% of the time, Pallas kernels for 0%

commit v1 on v0

v1 whole, which is shorter than its diff:
```python
import functools

import jax
import jax.numpy as jnp
from jax import lax
from jax.experimental import pallas as pl
from jax.experimental.pallas import tpu as pltpu
from jax.sharding import PartitionSpec as P

BLK = 512
HALF = BLK // 2
TAIL = HALF + 16
ITERS = 3
SLOTS = 2
QUAD = 4

damping = 0.01
F32 = jnp.float32
BF16 = jnp.bfloat16
SMEM = pl.BlockSpec(memory_space=pltpu.SMEM)
VMEM = pl.BlockSpec(memory_space=pltpu.VMEM)


def params(mib):
    return pltpu.CompilerParams(vmem_limit_bytes=mib * 2**20)


def dot(left, right, dims=((1,), (0,))):
    return lax.dot_general(left, right, (dims, ((), ())), preferred_element_type=F32)


def places():
    row = lax.broadcasted_iota(jnp.int32, (HALF, HALF), 0)
    col = lax.broadcasted_iota(jnp.int32, (HALF, HALF), 1)
    return row, col


def fold(first, last):
    row, col = places()
    body = jnp.where(row <= col, first, last)
    diagonal = jnp.sum(jnp.where(row == col, last, 0.0), axis=0, keepdims=True)
    return body, jnp.broadcast_to(diagonal, (TAIL - HALF, HALF))


def unfold(body, diagonal):
    row, col = places()
    turned = body.T
    first = jnp.where(row <= col, body, turned)
    last = jnp.where(row > col, body, jnp.where(row < col, turned, diagonal))
    return first, last


def stat_kernel(order, x_ref, *out):
    for place in (3, 1, 2, 0):
        start = pl.multiple_of(order[place] * BLK, BLK)
        left = x_ref[:, pl.ds(start, HALF)]
        right = x_ref[:, pl.ds(pl.multiple_of(start + HALF, HALF), HALF)]
        along = ((0,), (0,))
        out[2 * place][...] = dot(left, right, along).astype(BF16)
        body, diagonal = fold(dot(left, left, along), dot(right, right, along))
        out[2 * place + 1][:HALF] = body.astype(BF16)
        out[2 * place + 1][HALF:] = diagonal.astype(BF16)


def statistics(order, activations):
    shapes = [
        jax.ShapeDtypeStruct((rows, HALF), BF16) for _ in range(QUAD) for rows in (HALF, TAIL)
    ]
    return pl.pallas_call(
        stat_kernel,
        out_shape=shapes,
        in_specs=[SMEM, VMEM],
        out_specs=[VMEM] * len(shapes),
        compiler_params=params(32),
        name="statistics",
    )(order, activations)


def gram_kernel(order, g_ref, gram_ref):
    tile = g_ref[...]
    term = dot(tile, tile, ((1,), (1,)))

    @pl.when(pl.program_id(1) == 0)
    def _():
        gram_ref[0] = term

    @pl.when(pl.program_id(1) > 0)
    def _():
        gram_ref[0] += term


def tile_width(columns):
    for width in (1792, 896, 512, 256, 128):
        if columns % width == 0:
            return width
    return columns


def gram(order, gradient):
    rows, columns = gradient.shape
    width = tile_width(columns)
    return pl.pallas_call(
        gram_kernel,
        out_shape=jax.ShapeDtypeStruct((QUAD, BLK, BLK), F32),
        grid_spec=pltpu.PrefetchScalarGridSpec(
            num_scalar_prefetch=1,
            grid=(QUAD, columns // width),
            in_specs=[pl.BlockSpec((BLK, width), lambda s, j, order: (order[s], j))],
            out_specs=pl.BlockSpec((1, BLK, BLK), lambda s, j, order: (s, 0, 0)),
        ),
        compiler_params=params(32),
        cost_estimate=pl.CostEstimate(
            flops=2 * rows * columns * BLK,
            bytes_accessed=2 * rows * columns + 4 * QUAD * BLK * BLK,
            transcendentals=0,
        ),
        name="gram",
    )(order, gradient)


def product(left, right):
    return dot(left.astype(BF16), right.astype(BF16))


def newton_kernel(tokens, mine0, mine1, other0, other1, root0, root1, held):
    cross = (mine0[...].astype(F32) + other0[...].astype(F32)) / tokens
    rest = (mine1[...].astype(F32) + other1[...].astype(F32)) / tokens
    first, last = unfold(rest[:HALF], rest[HALF : HALF + 1])
    held[:HALF, :HALF] = first
    held[:HALF, HALF:] = cross
    held[HALF:, :HALF] = cross.T
    held[HALF:, HALF:] = last
    row = lax.broadcasted_iota(jnp.int32, (BLK, BLK), 0)
    col = lax.broadcasted_iota(jnp.int32, (BLK, BLK), 1)
    identity = jnp.where(row == col, 1.0, 0.0).astype(F32)
    matrix = held[...] + damping * identity
    bound = jnp.max(jnp.sum(jnp.abs(matrix), axis=0, keepdims=True), axis=1, keepdims=True)
    scale = 2.0 / bound
    iterate = matrix * scale
    estimate = None
    for step in range(ITERS):
        error = (identity - iterate) * 0.25
        if estimate is None:
            estimate = error
        else:
            estimate = estimate + error + product(estimate, error)
        if step + 1 < ITERS:
            square = 2.0 * error + product(error, error)
            fourth = 2.0 * square + product(square, square)
            iterate = iterate + product(fourth, iterate)
    held[...] = (estimate + identity) * jnp.sqrt(jnp.sqrt(scale))
    root0[...] = held[:HALF, HALF:].astype(BF16)
    body, diagonal = fold(held[:HALF, :HALF], held[HALF:, HALF:])
    root1[:HALF] = body.astype(BF16)
    root1[HALF:] = diagonal.astype(BF16)


def newton(tokens, *halves):
    return pl.pallas_call(
        functools.partial(newton_kernel, tokens),
        out_shape=[jax.ShapeDtypeStruct((rows, HALF), BF16) for rows in (HALF, TAIL)],
        in_specs=[VMEM] * 4,
        out_specs=[VMEM] * 2,
        scratch_shapes=[pltpu.VMEM((BLK, BLK), F32)],
        compiler_params=params(32),
        name="newton",
    )(*halves)


def norm_kernel(half0, half1, gram_ref, root_ref, total_ref):
    cross = half0[...].astype(F32)
    rest = half1[...].astype(F32)
    first, last = unfold(rest[:HALF], rest[HALF : HALF + 1])
    root_ref[:HALF, :HALF] = first.astype(BF16)
    root_ref[:HALF, HALF:] = cross.astype(BF16)
    root_ref[HALF:, :HALF] = cross.T.astype(BF16)
    root_ref[HALF:, HALF:] = last.astype(BF16)
    root = root_ref[...]
    weighted = dot(root, root) * gram_ref[0]
    total_ref[...] = jnp.sum(weighted, axis=0, keepdims=True).reshape(1, BLK)


def norm(place, half0, half1, grams):
    whole = lambda rows: pl.BlockSpec((rows, HALF), lambda i: (0, 0))
    return pl.pallas_call(
        norm_kernel,
        out_shape=[jax.ShapeDtypeStruct((BLK, BLK), BF16), jax.ShapeDtypeStruct((1, BLK), F32)],
        grid=(1,),
        in_specs=[
            whole(HALF),
            whole(TAIL),
            pl.BlockSpec((1, BLK, BLK), lambda i: (place, 0, 0)),
        ],
        out_specs=[
            pl.BlockSpec((BLK, BLK), lambda i: (0, 0)),
            pl.BlockSpec((1, BLK), lambda i: (0, 0)),
        ],
        compiler_params=params(32),
        cost_estimate=pl.CostEstimate(
            flops=2 * BLK**3, bytes_accessed=8 * BLK * BLK, transcendentals=0
        ),
        name="norm",
    )(half0, half1, grams)


def apply_kernel(order, slots, ratio, r0, r1, r2, r3, g_ref, update_ref, owned_ref, root):
    place, column = pl.program_id(0), pl.program_id(1)

    @pl.when((place == 0) & (column == 0))
    def _():
        owned_ref[...] = jnp.zeros_like(owned_ref)

    for one, packed in enumerate((r0, r1, r2, r3)):

        @pl.when((place == one) & (column == 0))
        def _():
            root[...] = packed[...]

    for slot in range(SLOTS):

        @pl.when((column == 0) & (slots[place] == slot))
        def _():
            owned_ref[slot] = root[...]

    update_ref[...] = (dot(root[...], g_ref[...]) * ratio[0]).astype(BF16)


def apply(order, slots, ratio, roots, gradient):
    rows, columns = gradient.shape
    width = tile_width(columns)
    square = pl.BlockSpec((BLK, BLK), lambda s, j, order, slots: (0, 0))
    tile = pl.BlockSpec((BLK, width), lambda s, j, order, slots: (order[s], j))
    return pl.pallas_call(
        apply_kernel,
        out_shape=[
            jax.ShapeDtypeStruct((rows, columns), BF16),
            jax.ShapeDtypeStruct((SLOTS, BLK, BLK), BF16),
        ],
        grid_spec=pltpu.PrefetchScalarGridSpec(
            num_scalar_prefetch=2,
            grid=(QUAD, columns // width),
            in_specs=[SMEM] + [square] * QUAD + [tile],
            out_specs=[
                tile,
                pl.BlockSpec((SLOTS, BLK, BLK), lambda s, j, order, slots: (0, 0, 0)),
            ],
            scratch_shapes=[pltpu.VMEM((BLK, BLK), BF16)],
        ),
        compiler_params=params(40),
        name="apply",
    )(order, slots, ratio, *roots, gradient)


def swap(value, flip, axis="dp"):
    count = lax.axis_size(axis)
    return lax.ppermute(value, axis, [(i, i ^ flip) for i in range(count)])


def total(value, *axes):
    for axis in axes:
        flip = 1
        while flip < lax.axis_size(axis):
            value = value + swap(value, flip, axis)
            flip *= 2
    return value


def add(*values):
    return sum(value.astype(F32) for value in values).astype(BF16)


def per_device(activations, gradient, owner_slot):
    peer_count = lax.axis_size("dp")
    my_index = lax.axis_index("dp")
    group_index = lax.axis_index("pool")
    tokens_all = activations.shape[0] * peer_count
    owner_row = lax.dynamic_index_in_dim(owner_slot, group_index, 0, keepdims=False)
    order = (my_index % QUAD) ^ jnp.arange(QUAD, dtype=jnp.int32)
    slots = owner_row[order] - my_index * SLOTS

    a0, a1, b0, b1, c0, c1, d0, d1 = statistics(order, activations)
    from_y = swap(d0, 1)
    from_z = swap(d1, 2)
    y0 = swap(b0, 1)
    z1 = swap(c1, 2)
    y1 = swap(add(b1, from_z), 1)
    z0 = swap(add(c0, from_y), 2)
    mine0 = add(a0, y0, z0)
    mine1 = add(a1, y1, z1)
    flip = QUAD
    other0, other1 = swap(mine0, flip), swap(mine1, flip)
    while 2 * flip < peer_count:
        mine0, mine1 = add(mine0, other0), add(mine1, other1)
        flip *= 2
        other0, other1 = swap(mine0, flip), swap(mine1, flip)

    grams = gram(order, gradient)
    a0, a1 = newton(tokens_all, mine0, mine1, other0, other1)
    c0 = swap(a0, 2)
    b1 = swap(a1, 1)
    c1 = swap(a1, 2)
    b0 = swap(a0, 1)
    d0 = swap(c0, 1)
    d1 = swap(b1, 2)
    roots, totals = zip(
        *[norm(place, *pair, grams) for place, pair in enumerate(((a0, a1), (b0, b1), (c0, c1), (d0, d1)))]
    )
    grad_square = sum(jnp.trace(grams[place]) for place in range(QUAD))
    update_square = jnp.sum(sum(totals))
    both = total(jnp.stack([grad_square, update_square]), "pool", "dp")
    ratio = jnp.sqrt(both[0] / (both[1] + 1e-06))
    update, owned = apply(order, slots, ratio[None], roots, gradient)
    return (update, owned[None])


def solution(mesh):
    in_specs = (P("dp", "pool"), P("pool", "dp"), P())
    out_specs = (P("pool", "dp"), P("pool", "dp", None, None))
    return jax.shard_map(
        per_device, mesh=mesh, in_specs=in_specs, out_specs=out_specs, check_vma=False
    )
```

time: 433 us -> 103 us (0.24); the launches traced: 426 us -> 103 us
  waiting for transfers between devices: 246 us -> 18.9 us
  matrix products: 54.1 us -> 0 us
  blocking collectives: 39.6 us -> 0 us
  Pallas kernels: 0 us -> 34.5 us
  other arithmetic: 40.2 us -> 5.94 us
  starting transfers between devices: 0.08 us -> 26.6 us
  between operations: 26.8 us -> 4.74 us
  loops' own time: 16.2 us -> 0 us
  local copies, waits for them, and re-layouts: 2.78 us -> 12.2 us
    psum x2 -> x0, waiting for transfers between devices: 246 us -> none  [the longest x1 146 us: per_device(): summed = lax.psum(partial_value, 'dp') / tokens_all]
    dot_general x13 -> x0, matrix products: 54.1 us -> none  [the longest x1 19.9 us: per_device(): jnp.einsum('kab,kbc->kac', roots, grad_blocks, preferred_element_type=jnp...]
    psum x1 -> x0, blocking collectives: 39.6 us -> none  [per_device(): totals = lax.psum((grad_square, update_square), ('pool', 'dp'))]
    pallas_call x0 -> x8, Pallas kernels: none -> 34.5 us  [the longest x1 16.1 us: apply(): pl.pallas_call(apply_kernel, out_shape=[jax.ShapeDtypeStruct((rows, colum...]
    ppermute x0 -> x19, starting transfers between devices: none -> 26.6 us  [swap(): return lax.ppermute(value, axis, [(i, i ^ flip) for i in range(count)])]
    ppermute x0 -> x19, waiting for transfers between devices: none -> 18.9 us  [swap(): return lax.ppermute(value, axis, [(i, i ^ flip) for i in range(count)])]
    convert_element_type x2 -> x4, other arithmetic: 17.5 us -> 0.18 us  [add(): return sum((value.astype(F32) for value in values)).astype(BF16)]
    another operation x2 -> x0, loops' own time: 16.2 us -> none  [solve_held(): lax.cond(jnp.any(hits), solve_single, empty_slot, stat).astype(jnp.bfloat16)]
  transfers between devices with their start and end apart: 2 -> 19, of which waited for: 2 -> 8; matrix products, arithmetic and copies ran while one was open for 4% -> 4% of each run, Pallas kernels for 0% -> 13%
where the time goes in v1:
time: 103 us
  Pallas kernels  34.5 us (33%)
  starting transfers between devices  26.6 us (26%)
  waiting for transfers between devices  18.9 us (18%)
  local copies, waits for them, and re-layouts  12.2 us (12%)
  other arithmetic  5.94 us (6%)
  between operations  4.74 us (5%)
    ppermute x19, starting transfers between devices, swap(): return lax.ppermute(value, axis, [(i, i ^ flip) for i in range(count)])  26.6 us
    ppermute x19, waiting for transfers between devices, swap(): return lax.ppermute(value, axis, [(i, i ^ flip) for i in range(count)])  18.9 us
    pallas_call x1, Pallas kernels, apply(): pl.pallas_call(apply_kernel, out_shape=[jax.ShapeDtypeStruct((rows, colum...  16.1 us
    pallas_call x1, Pallas kernels, gram(): pl.pallas_call(gram_kernel, out_shape=jax.ShapeDtypeStruct((QUAD, BLK, BL...  11.4 us
    unnamed x10, local copies, waits for them, and re-layouts  11 us
    pallas_call x1, Pallas kernels, newton(): pl.pallas_call(functools.partial(newton_kernel, tokens), out_shape=[jax.S...  3.2 us
    reduce_sum x1, other arithmetic, per_device(): grad_square = sum((jnp.trace(grams[place]) for place in range(QUAD)))  2.96 us
    pallas_call x4, Pallas kernels, norm(): pl.pallas_call(norm_kernel, out_shape=[jax.ShapeDtypeStruct((BLK, BLK), B...  2.16 us
  transfers between devices with their start and end apart: 19, of which 8 were waited for; matrix products, arithmetic and copies ran while one was open for 4% of the time, Pallas kernels for 13%

profile of v1, /device:TPU:0, one launch (start us, length us, event | category | flops | bytes accessed | tf_op | source)
XLA Modules:
  0.0 102.8 jit_solution(362821626981406809)
XLA Ops:
  0.7 1.6 %copy-done.4 = bf16[512,2048]{1,0:T(8,128)(2,1)S(1)} copy-done((bf16[512,2048]{1,0:T(8,128)(2,1)S(1)}, bf16[512,2048]{1,0:T(8,128)(2,1)}, u32[]{:S(2)}) %copy-start.4) | copy-done | bytes 2097176
  2.3 1.6 %statistics.1 = (bf16[256,256]{1,0:T(8,128)(2,1)S(1)}, bf16[272,256]{1,0:T(8,128)(2,1)S(1)}, bf16[256,256]{1,0:T(8,128)(2,1)S(1)}, bf16[272,256]{1,0:T(8,128)(2,...) custom-call(s32[4]{0:T(128)S(1)} %iota_xor_fusion.order, ...), custom_call_target="tpu_custom_call" | custom-call | tf_op jit(solution)/shard_map/statistics/pallas_call | solution.py:69
  3.9 3.0 %collective-permute-start = (bf16[256,256]{1,0:T(8,128)(2,1)S(1)}, bf16[256,256]{1,0:T(8,128)(2,1)S(1)}, u32[]{:S(2)}, u32[]{:S(2)}) collective-permute-start(bf16[256,256]{1,0:T(8,128)(2,1)S(1)} %get-tuple-element.23), channel_id=1, source_target_pairs={{0,1},{1,0},{2,3},{3,2},{4,5},{5,4},{6,7},{7,6},{8,9},{9,8},{10,11... | collective-permute-start | bytes 393224 | tf_op jit(solution)/shard_map/ppermute | solution.py:256
  7.0 2.0 %collective-permute-start.3 = (bf16[272,256]{1,0:T(8,128)(2,1)S(1)}, bf16[272,256]{1,0:T(8,128)(2,1)S(1)}, u32[]{:S(2)}, u32[]{:S(2)}) collective-permute-start(bf16[272,256]{1,0:T(8,128)(2,1)S(1)} %get-tuple-element.28), channel_id=1, source_target_pairs={{0,2},{1,3},{2,0},{3,1},{4,6},{5,7},{6,4},{7,5},{8,10},{9,11},{10,... | collective-permute-start | bytes 417800 | tf_op jit(solution)/shard_map/ppermute | solution.py:256
  9.0 5.2 %copy-done.3 = bf16[2048,3584]{1,0:T(8,128)(2,1)S(1)} copy-done((bf16[2048,3584]{1,0:T(8,128)(2,1)S(1)}, bf16[2048,3584]{1,0:T(8,128)(2,1)}, u32[]{:S(2)}) %copy-start.3) | copy-done | bytes 14680088
  14.2 11.4 %gram.1.gram_ref = f32[4,512,512]{2,1,0:T(8,128)S(1)} custom-call(s32[4]{0:T(128)S(1)} %iota_xor_fusion.order, bf16[2048,3584]{1,0:T(8,128)(2,1)S(1)} %copy-done.3), custom_call_target="tpu_custom_call" | custom-call | flops 7516192768 | bytes 18874368 | tf_op jit(solution)/shard_map/gram/pallas_call | solution.py:102
  25.6 2.0 %copy-done.1 = f32[4,512,512]{2,1,0:T(8,128)} copy-done((f32[4,512,512]{2,1,0:T(8,128)}, f32[4,512,512]{2,1,0:T(8,128)S(1)}, u32[]{:S(2)}) %copy-start.1) | copy-done | bytes 4194328
  27.7 2.1 %collective-permute-start.2 = (bf16[256,256]{1,0:T(8,128)(2,1)S(1)}, bf16[256,256]{1,0:T(8,128)(2,1)S(1)}, u32[]{:S(2)}, u32[]{:S(2)}) collective-permute-start(bf16[256,256]{1,0:T(8,128)(2,1)S(1)} %add_convert_fusion.3), channel_id=1, source_target_pairs={{0,2},{1,3},{2,0},{3,1},{4,6},{5,7},{6,4},{7,5},{8,10},{9,11},{10,... | collective-permute-start | bytes 393224 | tf_op jit(solution)/shard_map/ppermute | solution.py:256
  29.8 1.6 %collective-permute-start.4 = (bf16[272,256]{1,0:T(8,128)(2,1)S(1)}, bf16[272,256]{1,0:T(8,128)(2,1)S(1)}, u32[]{:S(2)}, u32[]{:S(2)}) collective-permute-start(bf16[272,256]{1,0:T(8,128)(2,1)S(1)} %add_convert_fusion.1), channel_id=1, source_target_pairs={{0,1},{1,0},{2,3},{3,2},{4,5},{5,4},{6,7},{7,6},{8,9},{9,8},{10,11... | collective-permute-start | bytes 417800 | tf_op jit(solution)/shard_map/ppermute | solution.py:256
  31.4 1.4 %collective-permute-done.2 = bf16[256,256]{1,0:T(8,128)(2,1)S(1)} collective-permute-done((bf16[256,256]{1,0:T(8,128)(2,1)S(1)}, bf16[256,256]{1,0:T(8,128)(2,1)S(1)}, u32[]{:S(2)}, u32[]{:S(2)}) %collective-permute-start.2) | collective-permute-done | bytes 131104 | tf_op jit(solution)/shard_map/ppermute | solution.py:256
  32.8 3.1 %collective-permute-start.6 = (bf16[256,256]{1,0:T(8,128)(2,1)S(1)}, bf16[256,256]{1,0:T(8,128)(2,1)S(1)}, u32[]{:S(2)}, u32[]{:S(2)}) collective-permute-start(bf16[256,256]{1,0:T(8,128)(2,1)S(1)} %add_convert_fusion.2.mine0), channel_id=1, source_target_pairs={{0,4},{1,5},{2,6},{3,7},{4,0},{5,1},{6,2},{7,3},{8,12},{9,13},{10,... | collective-permute-start | bytes 393224 | tf_op jit(solution)/shard_map/ppermute | solution.py:256
  35.9 1.7 %collective-permute-start.7 = (bf16[272,256]{1,0:T(8,128)(2,1)S(1)}, bf16[272,256]{1,0:T(8,128)(2,1)S(1)}, u32[]{:S(2)}, u32[]{:S(2)}) collective-permute-start(bf16[272,256]{1,0:T(8,128)(2,1)S(1)} %add_convert_fusion.mine1), channel_id=1, source_target_pairs={{0,4},{1,5},{2,6},{3,7},{4,0},{5,1},{6,2},{7,3},{8,12},{9,13},{10,... | collective-permute-start | bytes 417800 | tf_op jit(solution)/shard_map/ppermute | solution.py:256
  38.3 6.1 %collective-permute-done.6.other0 = bf16[256,256]{1,0:T(8,128)(2,1)S(1)} collective-permute-done((bf16[256,256]{1,0:T(8,128)(2,1)S(1)}, bf16[256,256]{1,0:T(8,128)(2,1)S(1)}, u32[]{:S(2)}, u32[]{:S(2)}) %collective-permute-start.6) | collective-permute-done | bytes 131104 | tf_op jit(solution)/shard_map/ppermute | solution.py:256
  44.4 1.5 %collective-permute-done.7.other1 = bf16[272,256]{1,0:T(8,128)(2,1)S(1)} collective-permute-done((bf16[272,256]{1,0:T(8,128)(2,1)S(1)}, bf16[272,256]{1,0:T(8,128)(2,1)S(1)}, u32[]{:S(2)}, u32[]{:S(2)}) %collective-permute-start.7) | collective-permute-done | bytes 139296 | tf_op jit(solution)/shard_map/ppermute | solution.py:256
  45.9 3.2 %newton.1 = (bf16[256,256]{1,0:T(8,128)(2,1)S(1)}, bf16[272,256]{1,0:T(8,128)(2,1)S(1)}) custom-call(bf16[256,256]{1,0:T(8,128)(2,1)S(1)} %add_convert_fusion.2.mine0, bf16[272,256]{1,0:T(8,128)(2,1)S(1)} %add_convert_fusion.mine1, bf16[256,256]{1,0:T(8,128)(2,1)S(1)} %collective-permute-done.6.other0, bf16[272,256]{1,0:T(8,128)(2,1)S(1)} %collective-permute-done.7.other1), custom_call_target="tpu_custom_call" | custom-call | tf_op jit(solution)/shard_map/newton/pallas_call | solution.py:159
  49.1 0.8 collective-permute-start.10
  49.9 1.5 %collective-permute-start.9 = (bf16[272,256]{1,0:T(8,128)(2,1)S(1)}, bf16[272,256]{1,0:T(8,128)(2,1)S(1)}, u32[]{:S(2)}, u32[]{:S(2)}) collective-permute-start(bf16[272,256]{1,0:T(8,128)(2,1)S(1)} %get-tuple-element.31.half1), channel_id=1, source_target_pairs={{0,1},{1,0},{2,3},{3,2},{4,5},{5,4},{6,7},{7,6},{8,9},{9,8},{10,11... | collective-permute-start | bytes 417800 | tf_op jit(solution)/shard_map/ppermute | solution.py:256
  51.4 3.0 %fusion.1 = (f32[]{:T(128)}, f32[]{:T(128)}, f32[]{:T(128)}, f32[]{:T(128)}) fusion(f32[4,512,512]{2,1,0:T(8,128)} %copy-done.1), kind=kLoop, calls=%fused_computation.3 | loop fusion | flops 2359292 | bytes 4194320 | tf_op jit(solution)/shard_map/jit(trace)/reduce_sum | solution.py:308
  54.8 1.3 %collective-permute-start.11 = (bf16[272,256]{1,0:T(8,128)(2,1)S(1)}, bf16[272,256]{1,0:T(8,128)(2,1)S(1)}, u32[]{:S(2)}, u32[]{:S(2)}) collective-permute-start(bf16[272,256]{1,0:T(8,128)(2,1)S(1)} %get-tuple-element.31.half1), channel_id=1, source_target_pairs={{0,2},{1,3},{2,0},{3,1},{4,6},{5,7},{6,4},{7,5},{8,10},{9,11},{10,... | collective-permute-start | bytes 417800 | tf_op jit(solution)/shard_map/ppermute | solution.py:256
  56.2 1.6 %collective-permute-start.12 = (bf16[256,256]{1,0:T(8,128)(2,1)S(1)}, bf16[256,256]{1,0:T(8,128)(2,1)S(1)}, u32[]{:S(2)}, u32[]{:S(2)}) collective-permute-start(bf16[256,256]{1,0:T(8,128)(2,1)S(1)} %collective-permute-done.10.half0), channel_id=1, source_target_pairs={{0,1},{1,0},{2,3},{3,2},{4,5},{5,4},{6,7},{7,6},{8,9},{9,8},{10,11... | collective-permute-start | bytes 393224 | tf_op jit(solution)/shard_map/ppermute | solution.py:256
  61.0 2.2 %copy-done.2 = f32[4,512,512]{2,1,0:T(8,128)S(1)} copy-done((f32[4,512,512]{2,1,0:T(8,128)S(1)}, f32[4,512,512]{2,1,0:T(8,128)}, u32[]{:S(2)}) %copy-start.2) | copy-done | bytes 4194328
  66.8 1.1 %collective-permute-done.14 = f32[2]{0:T(128)S(1)} collective-permute-done((f32[2]{0:T(128)S(1)}, f32[2]{0:T(128)S(1)}, u32[]{:S(2)}, u32[]{:S(2)}) %collective-permute-start.14) | collective-permute-done | bytes 40 | tf_op jit(solution)/shard_map/ppermute | solution.py:256
  67.9 0.7 fusion.10
  68.6 1.5 %collective-permute-start.15 = (f32[2]{0:T(128)S(1)}, f32[2]{0:T(128)S(1)}, u32[]{:S(2)}, u32[]{:S(2)}) collective-permute-start(f32[2]{0:T(128)S(1)} %fusion.10), channel_id=1, source_target_pairs={{0,16},{8,24},{16,0},{24,8},{1,17},{9,25},{17,1},{25,9},{2,18},{10... | collective-permute-start | bytes 32 | tf_op jit(solution)/shard_map/ppermute | solution.py:256
  70.1 2.1 %collective-permute-done.15 = f32[2]{0:T(128)S(1)} collective-permute-done((f32[2]{0:T(128)S(1)}, f32[2]{0:T(128)S(1)}, u32[]{:S(2)}, u32[]{:S(2)}) %collective-permute-start.15) | collective-permute-done | bytes 40 | tf_op jit(solution)/shard_map/ppermute | solution.py:256
  72.1 0.7 fusion.11
  73.4 3.0 %collective-permute-done.16 = f32[2]{0:T(128)S(1)} collective-permute-done((f32[2]{0:T(128)S(1)}, f32[2]{0:T(128)S(1)}, u32[]{:S(2)}, u32[]{:S(2)}) %collective-permute-start.16) | collective-permute-done | bytes 40 | tf_op jit(solution)/shard_map/ppermute | solution.py:256
  76.4 1.3 %collective-permute-start.17 = (f32[2]{0:T(128)S(1)}, f32[2]{0:T(128)S(1)}, u32[]{:S(2)}, u32[]{:S(2)}) collective-permute-start(f32[2]{0:T(128)S(1)} %add.90), channel_id=1, source_target_pairs={{0,2},{1,3},{2,0},{3,1},{4,6},{5,7},{6,4},{7,5},{8,10},{9,11},{10,... | collective-permute-start | bytes 32 | tf_op jit(solution)/shard_map/ppermute | solution.py:256
  77.7 2.2 %collective-permute-done.17 = f32[2]{0:T(128)S(1)} collective-permute-done((f32[2]{0:T(128)S(1)}, f32[2]{0:T(128)S(1)}, u32[]{:S(2)}, u32[]{:S(2)}) %collective-permute-start.17) | collective-permute-done | bytes 40 | tf_op jit(solution)/shard_map/ppermute | solution.py:256
  79.9 3.4 %collective-permute-start.18 = (f32[2]{0:T(128)S(1)}, f32[2]{0:T(128)S(1)}, u32[]{:S(2)}, u32[]{:S(2)}) collective-permute-start(f32[2]{0:T(128)S(1)} %add.91), channel_id=1, source_target_pairs={{0,4},{1,5},{2,6},{3,7},{4,0},{5,1},{6,2},{7,3},{8,12},{9,13},{10,... | collective-permute-start | bytes 32 | tf_op jit(solution)/shard_map/ppermute | solution.py:256
  83.3 1.5 %collective-permute-done.18 = f32[2]{0:T(128)S(1)} collective-permute-done((f32[2]{0:T(128)S(1)}, f32[2]{0:T(128)S(1)}, u32[]{:S(2)}, u32[]{:S(2)}) %collective-permute-start.18) | collective-permute-done | bytes 40 | tf_op jit(solution)/shard_map/ppermute | solution.py:256
  86.8 16.1 %apply.1 = (bf16[2048,3584]{1,0:T(8,128)(2,1)}, bf16[2,512,512]{2,1,0:T(8,128)(2,1)}) custom-call(s32[4]{0:T(128)S(1)} %iota_xor_fusion.order, s32[4]{0:T(128)S(1)} %broadcast_subtract_fusion.slots, f32[1]{0:T(128)S(6)} %sqrt.4.ratio, bf16[512,512]{1,0:T(8,128)(2,1)S(1)} %get-tuple-element.36.r0, bf16[512,512]{1,0:T(8,128)(2,1)S(1)} %get-tuple-element.37.r1, ...), custom_call_target="tpu_custom_call" | custom-call | tf_op jit(solution)/shard_map/apply/pallas_call | solution.py:233
  (43 shorter events, 6.8 us)
Async XLA Ops:
  0.6 37.0 %copy-start = (s32[4,4]{1,0:T(4,128)S(1)}, s32[4,4]{1,0:T(4,128)}, u32[]{:S(2)}) copy-start(s32[4,4]{1,0:T(4,128)} %param.5) | copy-start | bytes 196
  0.7 1.6 %copy-start.4 = (bf16[512,2048]{1,0:T(8,128)(2,1)S(1)}, bf16[512,2048]{1,0:T(8,128)(2,1)}, u32[]{:S(2)}) copy-start(bf16[512,2048]{1,0:T(8,128)(2,1)} %x_ref.1) | copy-start | bytes 6291460
  3.9 27.5 %collective-permute-start = (bf16[256,256]{1,0:T(8,128)(2,1)S(1)}, bf16[256,256]{1,0:T(8,128)(2,1)S(1)}, u32[]{:S(2)}, u32[]{:S(2)}) collective-permute-start(bf16[256,256]{1,0:T(8,128)(2,1)S(1)} %get-tuple-element.23), channel_id=1, source_target_pairs={{0,1},{1,0},{2,3},{3,2},{4,5},{5,4},{6,7},{7,6},{8,9},{9,8},{10,11... | collective-permute-start | bytes 393224 | tf_op jit(solution)/shard_map/ppermute | solution.py:256
  6.9 20.8 %collective-permute-start.1 = (bf16[256,256]{1,0:T(8,128)(2,1)S(1)}, bf16[256,256]{1,0:T(8,128)(2,1)S(1)}, u32[]{:S(2)}, u32[]{:S(2)}) collective-permute-start(bf16[256,256]{1,0:T(8,128)(2,1)S(1)} %get-tuple-element.25), channel_id=1, source_target_pairs={{0,1},{1,0},{2,3},{3,2},{4,5},{5,4},{6,7},{7,6},{8,9},{9,8},{10,11... | collective-permute-start | bytes 393224 | tf_op jit(solution)/shard_map/ppermute | solution.py:256
  7.0 22.8 %collective-permute-start.3 = (bf16[272,256]{1,0:T(8,128)(2,1)S(1)}, bf16[272,256]{1,0:T(8,128)(2,1)S(1)}, u32[]{:S(2)}, u32[]{:S(2)}) collective-permute-start(bf16[272,256]{1,0:T(8,128)(2,1)S(1)} %get-tuple-element.28), channel_id=1, source_target_pairs={{0,2},{1,3},{2,0},{3,1},{4,6},{5,7},{6,4},{7,5},{8,10},{9,11},{10,... | collective-permute-start | bytes 417800 | tf_op jit(solution)/shard_map/ppermute | solution.py:256
  9.0 26.9 %collective-permute-start.5 = (bf16[272,256]{1,0:T(8,128)(2,1)S(1)}, bf16[272,256]{1,0:T(8,128)(2,1)S(1)}, u32[]{:S(2)}, u32[]{:S(2)}) collective-permute-start(bf16[272,256]{1,0:T(8,128)(2,1)S(1)} %get-tuple-element.29), channel_id=1, source_target_pairs={{0,2},{1,3},{2,0},{3,1},{4,6},{5,7},{6,4},{7,5},{8,10},{9,11},{10,... | collective-permute-start | bytes 417800 | tf_op jit(solution)/shard_map/ppermute | solution.py:256
  9.0 5.2 %copy-start.3 = (bf16[2048,3584]{1,0:T(8,128)(2,1)S(1)}, bf16[2048,3584]{1,0:T(8,128)(2,1)}, u32[]{:S(2)}) copy-start(bf16[2048,3584]{1,0:T(8,128)(2,1)} %g_ref.3) | copy-start | bytes 44040196
  25.6 2.0 %copy-start.1 = (f32[4,512,512]{2,1,0:T(8,128)}, f32[4,512,512]{2,1,0:T(8,128)S(1)}, u32[]{:S(2)}) copy-start(f32[4,512,512]{2,1,0:T(8,128)S(1)} %gram.1.gram_ref) | copy-start | bytes 12582916
  27.7 5.0 %collective-permute-start.2 = (bf16[256,256]{1,0:T(8,128)(2,1)S(1)}, bf16[256,256]{1,0:T(8,128)(2,1)S(1)}, u32[]{:S(2)}, u32[]{:S(2)}) collective-permute-start(bf16[256,256]{1,0:T(8,128)(2,1)S(1)} %add_convert_fusion.3), channel_id=1, source_target_pairs={{0,2},{1,3},{2,0},{3,1},{4,6},{5,7},{6,4},{7,5},{8,10},{9,11},{10,... | collective-permute-start | bytes 393224 | tf_op jit(solution)/shard_map/ppermute | solution.py:256
  29.8 6.1 %collective-permute-start.4 = (bf16[272,256]{1,0:T(8,128)(2,1)S(1)}, bf16[272,256]{1,0:T(8,128)(2,1)S(1)}, u32[]{:S(2)}, u32[]{:S(2)}) collective-permute-start(bf16[272,256]{1,0:T(8,128)(2,1)S(1)} %add_convert_fusion.1), channel_id=1, source_target_pairs={{0,1},{1,0},{2,3},{3,2},{4,5},{5,4},{6,7},{7,6},{8,9},{9,8},{10,11... | collective-permute-start | bytes 417800 | tf_op jit(solution)/shard_map/ppermute | solution.py:256
  32.8 11.6 %collective-permute-start.6 = (bf16[256,256]{1,0:T(8,128)(2,1)S(1)}, bf16[256,256]{1,0:T(8,128)(2,1)S(1)}, u32[]{:S(2)}, u32[]{:S(2)}) collective-permute-start(bf16[256,256]{1,0:T(8,128)(2,1)S(1)} %add_convert_fusion.2.mine0), channel_id=1, source_target_pairs={{0,4},{1,5},{2,6},{3,7},{4,0},{5,1},{6,2},{7,3},{8,12},{9,13},{10,... | collective-permute-start | bytes 393224 | tf_op jit(solution)/shard_map/ppermute | solution.py:256
  35.9 9.9 %collective-permute-start.7 = (bf16[272,256]{1,0:T(8,128)(2,1)S(1)}, bf16[272,256]{1,0:T(8,128)(2,1)S(1)}, u32[]{:S(2)}, u32[]{:S(2)}) collective-permute-start(bf16[272,256]{1,0:T(8,128)(2,1)S(1)} %add_convert_fusion.mine1), channel_id=1, source_target_pairs={{0,4},{1,5},{2,6},{3,7},{4,0},{5,1},{6,2},{7,3},{8,12},{9,13},{10,... | collective-permute-start | bytes 417800 | tf_op jit(solution)/shard_map/ppermute | solution.py:256
  49.1 7.1 %collective-permute-start.10 = (bf16[256,256]{1,0:T(8,128)(2,1)S(1)}, bf16[256,256]{1,0:T(8,128)(2,1)S(1)}, u32[]{:S(2)}, u32[]{:S(2)}) collective-permute-start(bf16[256,256]{1,0:T(8,128)(2,1)S(1)} %get-tuple-element.30.half0), channel_id=1, source_target_pairs={{0,2},{1,3},{2,0},{3,1},{4,6},{5,7},{6,4},{7,5},{8,10},{9,11},{10,... | collective-permute-start | bytes 393224 | tf_op jit(solution)/shard_map/ppermute | solution.py:256
  49.9 7.9 %collective-permute-start.9 = (bf16[272,256]{1,0:T(8,128)(2,1)S(1)}, bf16[272,256]{1,0:T(8,128)(2,1)S(1)}, u32[]{:S(2)}, u32[]{:S(2)}) collective-permute-start(bf16[272,256]{1,0:T(8,128)(2,1)S(1)} %get-tuple-element.31.half1), channel_id=1, source_target_pairs={{0,1},{1,0},{2,3},{3,2},{4,5},{5,4},{6,7},{7,6},{8,9},{9,8},{10,11... | collective-permute-start | bytes 417800 | tf_op jit(solution)/shard_map/ppermute | solution.py:256
  54.3 9.9 %collective-permute-start.8 = (bf16[256,256]{1,0:T(8,128)(2,1)S(1)}, bf16[256,256]{1,0:T(8,128)(2,1)S(1)}, u32[]{:S(2)}, u32[]{:S(2)}) collective-permute-start(bf16[256,256]{1,0:T(8,128)(2,1)S(1)} %get-tuple-element.30.half0), channel_id=1, source_target_pairs={{0,1},{1,0},{2,3},{3,2},{4,5},{5,4},{6,7},{7,6},{8,9},{9,8},{10,11... | collective-permute-start | bytes 393224 | tf_op jit(solution)/shard_map/ppermute | solution.py:256
  54.8 8.9 %collective-permute-start.11 = (bf16[272,256]{1,0:T(8,128)(2,1)S(1)}, bf16[272,256]{1,0:T(8,128)(2,1)S(1)}, u32[]{:S(2)}, u32[]{:S(2)}) collective-permute-start(bf16[272,256]{1,0:T(8,128)(2,1)S(1)} %get-tuple-element.31.half1), channel_id=1, source_target_pairs={{0,2},{1,3},{2,0},{3,1},{4,6},{5,7},{6,4},{7,5},{8,10},{9,11},{10,... | collective-permute-start | bytes 417800 | tf_op jit(solution)/shard_map/ppermute | solution.py:256
  56.2 8.7 %collective-permute-start.12 = (bf16[256,256]{1,0:T(8,128)(2,1)S(1)}, bf16[256,256]{1,0:T(8,128)(2,1)S(1)}, u32[]{:S(2)}, u32[]{:S(2)}) collective-permute-start(bf16[256,256]{1,0:T(8,128)(2,1)S(1)} %collective-permute-done.10.half0), channel_id=1, source_target_pairs={{0,1},{1,0},{2,3},{3,2},{4,5},{5,4},{6,7},{7,6},{8,9},{9,8},{10,11... | collective-permute-start | bytes 393224 | tf_op jit(solution)/shard_map/ppermute | solution.py:256
  57.7 7.1 %collective-permute-start.13 = (bf16[272,256]{1,0:T(8,128)(2,1)S(1)}, bf16[272,256]{1,0:T(8,128)(2,1)S(1)}, u32[]{:S(2)}, u32[]{:S(2)}) collective-permute-start(bf16[272,256]{1,0:T(8,128)(2,1)S(1)} %collective-permute-done.9.half1), channel_id=1, source_target_pairs={{0,2},{1,3},{2,0},{3,1},{4,6},{5,7},{6,4},{7,5},{8,10},{9,11},{10,... | collective-permute-start | bytes 417800 | tf_op jit(solution)/shard_map/ppermute | solution.py:256
  61.0 2.2 %copy-start.2 = (f32[4,512,512]{2,1,0:T(8,128)S(1)}, f32[4,512,512]{2,1,0:T(8,128)}, u32[]{:S(2)}) copy-start(f32[4,512,512]{2,1,0:T(8,128)} %copy-done.1) | copy-start | bytes 12582916
  66.7 1.1 %collective-permute-start.14 = (f32[2]{0:T(128)S(1)}, f32[2]{0:T(128)S(1)}, u32[]{:S(2)}, u32[]{:S(2)}) collective-permute-start(f32[2]{0:T(128)S(1)} %pad_maximum_fusion), channel_id=1, source_target_pairs={{0,8},{8,0},{16,24},{24,16},{1,9},{9,1},{17,25},{25,17},{2,10},{10... | collective-permute-start | bytes 32 | tf_op jit(solution)/shard_map/ppermute | solution.py:256
  68.6 3.5 %collective-permute-start.15 = (f32[2]{0:T(128)S(1)}, f32[2]{0:T(128)S(1)}, u32[]{:S(2)}, u32[]{:S(2)}) collective-permute-start(f32[2]{0:T(128)S(1)} %fusion.10), channel_id=1, source_target_pairs={{0,16},{8,24},{16,0},{24,8},{1,17},{9,25},{17,1},{25,9},{2,18},{10... | collective-permute-start | bytes 32 | tf_op jit(solution)/shard_map/ppermute | solution.py:256
  72.9 3.5 %collective-permute-start.16 = (f32[2]{0:T(128)S(1)}, f32[2]{0:T(128)S(1)}, u32[]{:S(2)}, u32[]{:S(2)}) collective-permute-start(f32[2]{0:T(128)S(1)} %fusion.11), channel_id=1, source_target_pairs={{0,1},{1,0},{2,3},{3,2},{4,5},{5,4},{6,7},{7,6},{8,9},{9,8},{10,11... | collective-permute-start | bytes 32 | tf_op jit(solution)/shard_map/ppermute | solution.py:256
  76.4 3.5 %collective-permute-start.17 = (f32[2]{0:T(128)S(1)}, f32[2]{0:T(128)S(1)}, u32[]{:S(2)}, u32[]{:S(2)}) collective-permute-start(f32[2]{0:T(128)S(1)} %add.90), channel_id=1, source_target_pairs={{0,2},{1,3},{2,0},{3,1},{4,6},{5,7},{6,4},{7,5},{8,10},{9,11},{10,... | collective-permute-start | bytes 32 | tf_op jit(solution)/shard_map/ppermute | solution.py:256
  79.9 4.9 %collective-permute-start.18 = (f32[2]{0:T(128)S(1)}, f32[2]{0:T(128)S(1)}, u32[]{:S(2)}, u32[]{:S(2)}) collective-permute-start(f32[2]{0:T(128)S(1)} %add.91), channel_id=1, source_target_pairs={{0,4},{1,5},{2,6},{3,7},{4,0},{5,1},{6,2},{7,3},{8,12},{9,13},{10,... | collective-permute-start | bytes 32 | tf_op jit(solution)/shard_map/ppermute | solution.py:256

commit v2 on v1

--- a/solution.py
+++ b/solution.py
@@ -13,6 +13,8 @@
 ITERS = 3
 SLOTS = 2
 QUAD = 4
+ROWS = 8
+LANES = 128
 
 damping = 0.01
 F32 = jnp.float32
@@ -71,22 +73,9 @@
         out_shape=shapes,
         in_specs=[SMEM, VMEM],
         out_specs=[VMEM] * len(shapes),
-        compiler_params=params(32),
+        compiler_params=params(16),
         name="statistics",
     )(order, activations)
-
-
-def gram_kernel(order, g_ref, gram_ref):
-    tile = g_ref[...]
-    term = dot(tile, tile, ((1,), (1,)))
-
-    @pl.when(pl.program_id(1) == 0)
-    def _():
-        gram_ref[0] = term
-
-    @pl.when(pl.program_id(1) > 0)
-    def _():
-        gram_ref[0] += term
 
 
 def tile_width(columns):
@@ -96,33 +85,68 @@
     return columns
 
 
-def gram(order, gradient):
+def chunks(width):
+    start = 0
+    while width - start >= 2 * BLK:
+        yield pl.ds(start, BLK)
+        start += BLK
+    yield pl.ds(start, width - start)
+
+
+def gram_kernel(order, after0, after1, g_ref, gram_ref, norm_ref):
+    @pl.when(pl.program_id(1) == 0)
+    def _():
+        gram_ref[...] = jnp.zeros_like(gram_ref)
+
+    for part in chunks(g_ref.shape[1]):
+        tile = g_ref[:, part]
+        gram_ref[0] += dot(tile, tile, ((1,), (1,)))
+
+    @pl.when(pl.program_id(1) == pl.num_programs(1) - 1)
+    def _():
+        row = lax.broadcasted_iota(jnp.int32, (BLK, BLK), 0)
+        col = lax.broadcasted_iota(jnp.int32, (BLK, BLK), 1)
+        squares = jnp.where(row == col, gram_ref[0], 0.0)
+        norm_ref[0] = jnp.sum(squares, axis=0, keepdims=True)
+
+
+def gram(order, gradient, *after):
     rows, columns = gradient.shape
     width = tile_width(columns)
     return pl.pallas_call(
         gram_kernel,
-        out_shape=jax.ShapeDtypeStruct((QUAD, BLK, BLK), F32),
+        out_shape=[
+            jax.ShapeDtypeStruct((QUAD, BLK, BLK), F32),
+            jax.ShapeDtypeStruct((QUAD, 1, BLK), F32),
+        ],
         grid_spec=pltpu.PrefetchScalarGridSpec(
             num_scalar_prefetch=1,
             grid=(QUAD, columns // width),
-            in_specs=[pl.BlockSpec((BLK, width), lambda s, j, order: (order[s], j))],
-            out_specs=pl.BlockSpec((1, BLK, BLK), lambda s, j, order: (s, 0, 0)),
+            in_specs=[
+                pl.BlockSpec(memory_space=pl.ANY),
+                pl.BlockSpec(memory_space=pl.ANY),
+                pl.BlockSpec((BLK, width), lambda s, j, order: (order[s], j)),
+            ],
+            out_specs=[
+                pl.BlockSpec((1, BLK, BLK), lambda s, j, order: (s, 0, 0)),
+                pl.BlockSpec((1, 1, BLK), lambda s, j, order: (s, 0, 0)),
+            ],
         ),
-        compiler_params=params(32),
+        compiler_params=params(20),
         cost_estimate=pl.CostEstimate(
             flops=2 * rows * columns * BLK,
             bytes_accessed=2 * rows * columns + 4 * QUAD * BLK * BLK,
             transcendentals=0,
         ),
         name="gram",
-    )(order, gradient)
+    )(order, *after, gradient)
 
 
 def product(left, right):
     return dot(left.astype(BF16), right.astype(BF16))
 
 
-def newton_kernel(tokens, mine0, mine1, other0, other1, root0, root1, held):
+def newton_kernel(tokens, after, mine0, mine1, other0, other1, root0, root1, held):
     cross = (mine0[...].astype(F32) + other0[...].astype(F32)) / tokens
     rest = (mine1[...].astype(F32) + other1[...].astype(F32)) / tokens
     first, last = unfold(rest[:HALF], rest[HALF : HALF + 1])
@@ -155,19 +179,19 @@
     root1[HALF:] = diagonal.astype(BF16)
 
 
-def newton(tokens, *halves):
+def newton(tokens, after, *halves):
     return pl.pallas_call(
         functools.partial(newton_kernel, tokens),
         out_shape=[jax.ShapeDtypeStruct((rows, HALF), BF16) for rows in (HALF, TAIL)],
-        in_specs=[VMEM] * 4,
+        in_specs=[pl.BlockSpec(memory_space=pl.ANY)] + [VMEM] * 4,
         out_specs=[VMEM] * 2,
         scratch_shapes=[pltpu.VMEM((BLK, BLK), F32)],
-        compiler_params=params(32),
+        compiler_params=params(16),
         name="newton",
-    )(*halves)
-
-
-def norm_kernel(half0, half1, gram_ref, root_ref, total_ref):
+    )(after, *halves)
+
+
+def norm_kernel(half0, half1, gram_ref, square_ref, sums_ref, root_ref, total_ref):
     cross = half0[...].astype(F32)
     rest = half1[...].astype(F32)
     first, last = unfold(rest[:HALF], rest[HALF : HALF + 1])
@@ -177,38 +201,49 @@
     root_ref[HALF:, HALF:] = last.astype(BF16)
     root = root_ref[...]
     weighted = dot(root, root) * gram_ref[0]
-    total_ref[...] = jnp.sum(weighted, axis=0, keepdims=True).reshape(1, BLK)
-
-
-def norm(place, half0, half1, grams):
+    new = jnp.sum(weighted, axis=0, keepdims=True)
+    old = square_ref[0]
+    lanes = lambda value: sum(value[:, i : i + LANES] for i in range(0, BLK, LANES))
+    row = lax.broadcasted_iota(jnp.int32, sums_ref.shape, 0)
+    total_ref[...] = sums_ref[...] + jnp.where(row == 0, lanes(old), jnp.where(row == 1, lanes(new), 0.0))
+
+
+def norm(place, half0, half1, grams, squares, sums):
     whole = lambda rows: pl.BlockSpec((rows, HALF), lambda i: (0, 0))
     return pl.pallas_call(
         norm_kernel,
-        out_shape=[jax.ShapeDtypeStruct((BLK, BLK), BF16), jax.ShapeDtypeStruct((1, BLK), F32)],
+        out_shape=[
+            jax.ShapeDtypeStruct((BLK, BLK), BF16),
+            jax.ShapeDtypeStruct((ROWS, LANES), F32),
+        ],
         grid=(1,),
         in_specs=[
             whole(HALF),
             whole(TAIL),
             pl.BlockSpec((1, BLK, BLK), lambda i: (place, 0, 0)),
+            pl.BlockSpec((1, 1, BLK), lambda i: (place, 0, 0)),
+            pl.BlockSpec((ROWS, LANES), lambda i: (0, 0)),
         ],
         out_specs=[
             pl.BlockSpec((BLK, BLK), lambda i: (0, 0)),
-            pl.BlockSpec((1, BLK), lambda i: (0, 0)),
-        ],
-        compiler_params=params(32),
+            pl.BlockSpec((ROWS, LANES), lambda i: (0, 0)),
+        ],
+        compiler_params=params(16),
         cost_estimate=pl.CostEstimate(
             flops=2 * BLK**3, bytes_accessed=8 * BLK * BLK, transcendentals=0
         ),
         name="norm",
-    )(half0, half1, grams)
-
-
-def apply_kernel(order, slots, ratio, r0, r1, r2, r3, g_ref, update_ref, owned_ref, root):
+    )(half0, half1, grams, squares, sums)
+
+
+def apply_kernel(order, here, owner_slot, sums, r0, r1, r2, r3, g_ref, update_ref, owned_ref, root, ratio):
     place, column = pl.program_id(0), pl.program_id(1)
 
     @pl.when((place == 0) & (column == 0))
     def _():
         owned_ref[...] = jnp.zeros_like(owned_ref)
+        both = jnp.sum(sums[...], axis=1, keepdims=True)
+        ratio[...] = jnp.broadcast_to(jnp.sqrt(both[:1] / (both[1:2] + 1e-06)), ratio.shape)
 
     for one, packed in enumerate((r0, r1, r2, r3)):
 
@@ -218,18 +253,19 @@
 
     for slot in range(SLOTS):
 
-        @pl.when((column == 0) & (slots[place] == slot))
+        @pl.when((column == 0) & (owner_slot[here[0], order[place]] == here[1] + slot))
         def _():
             owned_ref[slot] = root[...]
 
-    update_ref[...] = (dot(root[...], g_ref[...]) * ratio[0]).astype(BF16)
-
-
-def apply(order, slots, ratio, roots, gradient):
+    for part in chunks(g_ref.shape[1]):
+        update_ref[:, part] = (dot(root[...], g_ref[:, part]) * ratio[:1, :1]).astype(BF16)
+
+
+def apply(order, here, owner_slot, sums, roots, gradient):
     rows, columns = gradient.shape
     width = tile_width(columns)
-    square = pl.BlockSpec((BLK, BLK), lambda s, j, order, slots: (0, 0))
-    tile = pl.BlockSpec((BLK, width), lambda s, j, order, slots: (order[s], j))
+    square = pl.BlockSpec((BLK, BLK), lambda s, j, order, *_: (0, 0))
+    tile = pl.BlockSpec((BLK, width), lambda s, j, order, *_: (order[s], j))
     return pl.pallas_call(
         apply_kernel,
         out_shape=[
@@ -237,18 +273,20 @@
             jax.ShapeDtypeStruct((SLOTS, BLK, BLK), BF16),
         ],
         grid_spec=pltpu.PrefetchScalarGridSpec(
-            num_scalar_prefetch=2,
+            num_scalar_prefetch=3,
             grid=(QUAD, columns // width),
-            in_specs=[SMEM] + [square] * QUAD + [tile],
+            in_specs=[pl.BlockSpec((ROWS, LANES), lambda s, j, order, *_: (0, 0))]
+            + [square] * QUAD
+            + [tile],
             out_specs=[
                 tile,
-                pl.BlockSpec((SLOTS, BLK, BLK), lambda s, j, order, slots: (0, 0, 0)),
+                pl.BlockSpec((SLOTS, BLK, BLK), lambda s, j, order, *_: (0, 0, 0)),
             ],
-            scratch_shapes=[pltpu.VMEM((BLK, BLK), BF16)],
+            scratch_shapes=[pltpu.VMEM((BLK, BLK), BF16), pltpu.VMEM((ROWS, LANES), F32)],
         ),
-        compiler_params=params(40),
+        compiler_params=params(24),
         name="apply",
-    )(order, slots, ratio, *roots, gradient)
+    )(order, here, owner_slot, sums, *roots, gradient)
 
 
 def swap(value, flip, axis="dp"):
@@ -274,9 +312,8 @@
     my_index = lax.axis_index("dp")
     group_index = lax.axis_index("pool")
     tokens_all = activations.shape[0] * peer_count
-    owner_row = lax.dynamic_index_in_dim(owner_slot, group_index, 0, keepdims=False)
     order = (my_index % QUAD) ^ jnp.arange(QUAD, dtype=jnp.int32)
-    slots = owner_row[order] - my_index * SLOTS
+    here = jnp.stack([group_index, my_index * SLOTS])
 
     a0, a1, b0, b1, c0, c1, d0, d1 = statistics(order, activations)
     from_y = swap(d0, 1)
@@ -294,22 +331,21 @@
         flip *= 2
         other0, other1 = swap(mine0, flip), swap(mine1, flip)
 
-    grams = gram(order, gradient)
-    a0, a1 = newton(tokens_all, mine0, mine1, other0, other1)
+    grams, squares = gram(order, gradient, mine0, mine1)
+    a0, a1 = newton(tokens_all, squares, mine0, mine1, other0, other1)
     c0 = swap(a0, 2)
     b1 = swap(a1, 1)
     c1 = swap(a1, 2)
     b0 = swap(a0, 1)
     d0 = swap(c0, 1)
     d1 = swap(b1, 2)
-    roots, totals = zip(
-        *[norm(place, *pair, grams) for place, pair in enumerate(((a0, a1), (b0, b1), (c0, c1), (d0, d1)))]
-    )
-    grad_square = sum(jnp.trace(grams[place]) for place in range(QUAD))
-    update_square = jnp.sum(sum(totals))
-    both = total(jnp.stack([grad_square, update_square]), "pool", "dp")
-    ratio = jnp.sqrt(both[0] / (both[1] + 1e-06))
-    update, owned = apply(order, slots, ratio[None], roots, gradient)
+    sums = jnp.zeros((ROWS, LANES), F32)
+    roots = []
+    for place, pair in enumerate(((a0, a1), (b0, b1), (c0, c1), (d0, d1))):
+        root, sums = norm(place, *pair, grams, squares, sums)
+        roots.append(root)
+    sums = total(sums, "pool", "dp")
+    update, owned = apply(order, here, owner_slot, sums, roots, gradient)
     return (update, owned[None])
 
 

time: 103 us -> 89.3 us (0.87)
  other arithmetic: 5.94 us -> 0.27 us
  between operations: 4.74 us -> 0.78 us
  Pallas kernels: 34.5 us -> 31 us
  waiting for transfers between devices: 18.9 us -> 17.1 us
  starting transfers between devices: 26.6 us -> 28 us
    reduce_sum x2 -> x0, other arithmetic: 3.57 us -> none  [the longest x1 2.96 us: per_device(): grad_square = sum((jnp.trace(grams[place]) for place in range(QUAD)))]
    pallas_call x1, Pallas kernels: 16.1 us -> 12.7 us  [apply(): pl.pallas_call(apply_kernel, out_shape=[jax.ShapeDtypeStruct((rows, colum...]
    ppermute x19, waiting for transfers between devices: 18.9 us -> 17.1 us  [swap(): return lax.ppermute(value, axis, [(i, i ^ flip) for i in range(count)])]
    add x5, other arithmetic: 1.45 us -> 0.02 us  [total(): value = value + swap(value, flip, axis)]
    ppermute x19, starting transfers between devices: 26.6 us -> 28 us  [swap(): return lax.ppermute(value, axis, [(i, i ^ flip) for i in range(count)])]
    unnamed x10 -> x8, local copies, waits for them, and re-layouts: 11 us -> 11.9 us
  transfers between devices with their start and end apart: 19 -> 19, of which waited for: 8 -> 10; matrix products, arithmetic and copies ran while one was open for 4% -> 0% of each run, Pallas kernels for 13% -> 15%
where the time goes in v2:
time: 89.3 us; the launch traced here: 89.1 us
  Pallas kernels  31 us (35%)
  starting transfers between devices  28 us (31%)
  waiting for transfers between devices  17.1 us (19%)
  local copies, waits for them, and re-layouts  11.9 us (13%)
    ppermute x19, starting transfers between devices, swap(): return lax.ppermute(value, axis, [(i, i ^ flip) for i in range(count)])  28 us
    ppermute x19, waiting for transfers between devices, swap(): return lax.ppermute(value, axis, [(i, i ^ flip) for i in range(count)])  17.1 us
    pallas_call x1, Pallas kernels, apply(): pl.pallas_call(apply_kernel, out_shape=[jax.ShapeDtypeStruct((rows, colum...  12.7 us
    unnamed x8, local copies, waits for them, and re-layouts  11.9 us
    pallas_call x1, Pallas kernels, gram(): pl.pallas_call(gram_kernel, out_shape=[jax.ShapeDtypeStruct((QUAD, BLK, B...  11.3 us
    pallas_call x1, Pallas kernels, newton(): pl.pallas_call(functools.partial(newton_kernel, tokens), out_shape=[jax.S...  3.21 us
    pallas_call x4, Pallas kernels, norm(): pl.pallas_call(norm_kernel, out_shape=[jax.ShapeDtypeStruct((BLK, BLK), B...  2.16 us
  transfers between devices with their start and end apart: 19, of which 10 were waited for; matrix products, arithmetic and copies ran while one was open for 0% of the time, Pallas kernels for 15%

profile of v2, /device:TPU:0, one launch (start us, length us, event | category | flops | bytes accessed | tf_op | source)
XLA Modules:
  0.0 89.1 jit_solution(18437133105541464813)
XLA Ops:
  0.7 1.6 %copy-done.2 = bf16[512,2048]{1,0:T(8,128)(2,1)S(1)} copy-done((bf16[512,2048]{1,0:T(8,128)(2,1)S(1)}, bf16[512,2048]{1,0:T(8,128)(2,1)}, u32[]{:S(2)}) %copy-start.2) | copy-done | bytes 2097176
  2.2 1.6 %statistics.1 = (bf16[256,256]{1,0:T(8,128)(2,1)S(1)}, bf16[272,256]{1,0:T(8,128)(2,1)S(1)}, bf16[256,256]{1,0:T(8,128)(2,1)S(1)}, bf16[272,256]{1,0:T(8,128)(2,...) custom-call(s32[4]{0:T(128)S(1)} %iota_xor_fusion.order, ...), custom_call_target="tpu_custom_call" | custom-call | tf_op jit(solution)/shard_map/statistics/pallas_call | solution.py:71
  3.8 3.0 %collective-permute-start.1 = (bf16[256,256]{1,0:T(8,128)(2,1)S(1)}, bf16[256,256]{1,0:T(8,128)(2,1)S(1)}, u32[]{:S(2)}, u32[]{:S(2)}) collective-permute-start(bf16[256,256]{1,0:T(8,128)(2,1)S(1)} %get-tuple-element.27), channel_id=1, source_target_pairs={{0,1},{1,0},{2,3},{3,2},{4,5},{5,4},{6,7},{7,6},{8,9},{9,8},{10,11... | collective-permute-start | bytes 393224 | tf_op jit(solution)/shard_map/ppermute | solution.py:294
  6.9 2.0 %collective-permute-start.3 = (bf16[272,256]{1,0:T(8,128)(2,1)S(1)}, bf16[272,256]{1,0:T(8,128)(2,1)S(1)}, u32[]{:S(2)}, u32[]{:S(2)}) collective-permute-start(bf16[272,256]{1,0:T(8,128)(2,1)S(1)} %get-tuple-element.30), channel_id=1, source_target_pairs={{0,2},{1,3},{2,0},{3,1},{4,6},{5,7},{6,4},{7,5},{8,10},{9,11},{10,... | collective-permute-start | bytes 417800 | tf_op jit(solution)/shard_map/ppermute | solution.py:294
  9.0 2.2 %collective-permute-done.1 = bf16[256,256]{1,0:T(8,128)(2,1)S(1)} collective-permute-done((bf16[256,256]{1,0:T(8,128)(2,1)S(1)}, bf16[256,256]{1,0:T(8,128)(2,1)S(1)}, u32[]{:S(2)}, u32[]{:S(2)}) %collective-permute-start.1) | collective-permute-done | bytes 131104 | tf_op jit(solution)/shard_map/ppermute | solution.py:294
  11.2 2.2 %collective-permute-start.2 = (bf16[256,256]{1,0:T(8,128)(2,1)S(1)}, bf16[256,256]{1,0:T(8,128)(2,1)S(1)}, u32[]{:S(2)}, u32[]{:S(2)}) collective-permute-start(bf16[256,256]{1,0:T(8,128)(2,1)S(1)} %add_convert_fusion.3), channel_id=1, source_target_pairs={{0,2},{1,3},{2,0},{3,1},{4,6},{5,7},{6,4},{7,5},{8,10},{9,11},{10,... | collective-permute-start | bytes 393224 | tf_op jit(solution)/shard_map/ppermute | solution.py:294
  13.6 2.0 %collective-permute-start.4 = (bf16[272,256]{1,0:T(8,128)(2,1)S(1)}, bf16[272,256]{1,0:T(8,128)(2,1)S(1)}, u32[]{:S(2)}, u32[]{:S(2)}) collective-permute-start(bf16[272,256]{1,0:T(8,128)(2,1)S(1)} %add_convert_fusion.1), channel_id=1, source_target_pairs={{0,1},{1,0},{2,3},{3,2},{4,5},{5,4},{6,7},{7,6},{8,9},{9,8},{10,11... | collective-permute-start | bytes 417800 | tf_op jit(solution)/shard_map/ppermute | solution.py:294
  15.6 2.3 %collective-permute-done.2 = bf16[256,256]{1,0:T(8,128)(2,1)S(1)} collective-permute-done((bf16[256,256]{1,0:T(8,128)(2,1)S(1)}, bf16[256,256]{1,0:T(8,128)(2,1)S(1)}, u32[]{:S(2)}, u32[]{:S(2)}) %collective-permute-start.2) | collective-permute-done | bytes 131104 | tf_op jit(solution)/shard_map/ppermute | solution.py:294
  17.9 2.8 %collective-permute-start.6 = (bf16[256,256]{1,0:T(8,128)(2,1)S(1)}, bf16[256,256]{1,0:T(8,128)(2,1)S(1)}, u32[]{:S(2)}, u32[]{:S(2)}) collective-permute-start(bf16[256,256]{1,0:T(8,128)(2,1)S(1)} %add_convert_fusion.2.after0.mine0), channel_id=1, source_target_pairs={{0,4},{1,5},{2,6},{3,7},{4,0},{5,1},{6,2},{7,3},{8,12},{9,13},{10,... | collective-permute-start | bytes 393224 | tf_op jit(solution)/shard_map/ppermute | solution.py:294
  20.8 1.1 %collective-permute-start.7 = (bf16[272,256]{1,0:T(8,128)(2,1)S(1)}, bf16[272,256]{1,0:T(8,128)(2,1)S(1)}, u32[]{:S(2)}, u32[]{:S(2)}) collective-permute-start(bf16[272,256]{1,0:T(8,128)(2,1)S(1)} %add_convert_fusion.after1.mine1), channel_id=1, source_target_pairs={{0,4},{1,5},{2,6},{3,7},{4,0},{5,1},{6,2},{7,3},{8,12},{9,13},{10,... | collective-permute-start | bytes 417800 | tf_op jit(solution)/shard_map/ppermute | solution.py:294
  21.9 5.2 %copy-done = bf16[2048,3584]{1,0:T(8,128)(2,1)S(1)} copy-done((bf16[2048,3584]{1,0:T(8,128)(2,1)S(1)}, bf16[2048,3584]{1,0:T(8,128)(2,1)}, u32[]{:S(2)}) %copy-start) | copy-done | bytes 14680088
  27.0 11.3 %gram.1 = (f32[4,512,512]{2,1,0:T(8,128)S(1)}, f32[4,1,512]{2,1,0:T(1,128)S(1)}) custom-call(s32[4]{0:T(128)S(1)} %iota_xor_fusion.order, bf16[256,256]{1,0:T(8,128)(2,1)S(1)} %add_convert_fusion.2.after0.mine0, bf16[272,256]{1,0:T(8,128)(2,1)S(1)} %add_convert_fusion.after1.mine1, bf16[2048,3584]{1,0:T(8,128)(2,1)S(1)} %copy-done), custom_call_target="tpu_custom_call" | custom-call | flops 7516192768 | bytes 18874368 | tf_op jit(solution)/shard_map/gram/pallas_call | solution.py:116
  38.4 3.2 %newton.1 = (bf16[256,256]{1,0:T(8,128)(2,1)S(1)}, bf16[272,256]{1,0:T(8,128)(2,1)S(1)}) custom-call(f32[4,1,512]{2,1,0:T(1,128)S(1)} %get-tuple-element.32.after.square_ref, bf16[256,256]{1,0:T(8,128)(2,1)S(1)} %add_convert_fusion.2.after0.mine0, bf16[272,256]{1,0:T(8,128)(2,1)S(1)} %add_convert_fusion.after1.mine1, ...), custom_call_target="tpu_custom_call" | custom-call | tf_op jit(solution)/shard_map/newton/pallas_call | solution.py:183
  41.6 1.6 %collective-permute-start.10 = (bf16[272,256]{1,0:T(8,128)(2,1)S(1)}, bf16[272,256]{1,0:T(8,128)(2,1)S(1)}, u32[]{:S(2)}, u32[]{:S(2)}) collective-permute-start(bf16[272,256]{1,0:T(8,128)(2,1)S(1)} %get-tuple-element.34.half1), channel_id=1, source_target_pairs={{0,1},{1,0},{2,3},{3,2},{4,5},{5,4},{6,7},{7,6},{8,9},{9,8},{10,11... | collective-permute-start | bytes 417800 | tf_op jit(solution)/shard_map/ppermute | solution.py:294
  43.2 1.6 %collective-permute-start.8 = (bf16[256,256]{1,0:T(8,128)(2,1)S(1)}, bf16[256,256]{1,0:T(8,128)(2,1)S(1)}, u32[]{:S(2)}, u32[]{:S(2)}) collective-permute-start(bf16[256,256]{1,0:T(8,128)(2,1)S(1)} %get-tuple-element.33.half0), channel_id=1, source_target_pairs={{0,2},{1,3},{2,0},{3,1},{4,6},{5,7},{6,4},{7,5},{8,10},{9,11},{10,... | collective-permute-start | bytes 393224 | tf_op jit(solution)/shard_map/ppermute | solution.py:294
  45.7 1.3 %collective-permute-done.10.half1 = bf16[272,256]{1,0:T(8,128)(2,1)S(1)} collective-permute-done((bf16[272,256]{1,0:T(8,128)(2,1)S(1)}, bf16[272,256]{1,0:T(8,128)(2,1)S(1)}, u32[]{:S(2)}, u32[]{:S(2)}) %collective-permute-start.10) | collective-permute-done | bytes 139296 | tf_op jit(solution)/shard_map/ppermute | solution.py:294
  47.0 1.6 %collective-permute-start.11 = (bf16[272,256]{1,0:T(8,128)(2,1)S(1)}, bf16[272,256]{1,0:T(8,128)(2,1)S(1)}, u32[]{:S(2)}, u32[]{:S(2)}) collective-permute-start(bf16[272,256]{1,0:T(8,128)(2,1)S(1)} %collective-permute-done.10.half1), channel_id=1, source_target_pairs={{0,2},{1,3},{2,0},{3,1},{4,6},{5,7},{6,4},{7,5},{8,10},{9,11},{10,... | collective-permute-start | bytes 417800 | tf_op jit(solution)/shard_map/ppermute | solution.py:294
  48.6 2.5 %collective-permute-start.9 = (bf16[256,256]{1,0:T(8,128)(2,1)S(1)}, bf16[256,256]{1,0:T(8,128)(2,1)S(1)}, u32[]{:S(2)}, u32[]{:S(2)}) collective-permute-start(bf16[256,256]{1,0:T(8,128)(2,1)S(1)} %collective-permute-done.8.half0), channel_id=1, source_target_pairs={{0,1},{1,0},{2,3},{3,2},{4,5},{5,4},{6,7},{7,6},{8,9},{9,8},{10,11... | collective-permute-start | bytes 393224 | tf_op jit(solution)/shard_map/ppermute | solution.py:294
  51.7 0.5 norm.5
  52.2 0.5 norm.6
  52.8 1.3 %collective-permute-done.9.half0 = bf16[256,256]{1,0:T(8,128)(2,1)S(1)} collective-permute-done((bf16[256,256]{1,0:T(8,128)(2,1)S(1)}, bf16[256,256]{1,0:T(8,128)(2,1)S(1)}, u32[]{:S(2)}, u32[]{:S(2)}) %collective-permute-start.9) | collective-permute-done | bytes 131104 | tf_op jit(solution)/shard_map/ppermute | solution.py:294
  54.7 1.2 %collective-permute-done.14 = f32[8,128]{1,0:T(8,128)S(1)} collective-permute-done((f32[8,128]{1,0:T(8,128)S(1)}, f32[8,128]{1,0:T(8,128)S(1)}, u32[]{:S(2)}, u32[]{:S(2)}) %collective-permute-start.14) | collective-permute-done | bytes 4128 | tf_op jit(solution)/shard_map/ppermute | solution.py:294
  55.8 1.5 %collective-permute-start.15 = (f32[8,128]{1,0:T(8,128)S(1)}, f32[8,128]{1,0:T(8,128)S(1)}, u32[]{:S(2)}, u32[]{:S(2)}) collective-permute-start(f32[8,128]{1,0:T(8,128)S(1)} %add.44), channel_id=1, source_target_pairs={{0,16},{8,24},{16,0},{24,8},{1,17},{9,25},{17,1},{25,9},{2,18},{10... | collective-permute-start | bytes 12296 | tf_op jit(solution)/shard_map/ppermute | solution.py:294
  57.3 2.1 %collective-permute-done.15 = f32[8,128]{1,0:T(8,128)S(1)} collective-permute-done((f32[8,128]{1,0:T(8,128)S(1)}, f32[8,128]{1,0:T(8,128)S(1)}, u32[]{:S(2)}, u32[]{:S(2)}) %collective-permute-start.15) | collective-permute-done | bytes 4128 | tf_op jit(solution)/shard_map/ppermute | solution.py:294
  59.4 2.0 %collective-permute-start.16 = (f32[8,128]{1,0:T(8,128)S(1)}, f32[8,128]{1,0:T(8,128)S(1)}, u32[]{:S(2)}, u32[]{:S(2)}) collective-permute-start(f32[8,128]{1,0:T(8,128)S(1)} %add.45), channel_id=1, source_target_pairs={{0,1},{1,0},{2,3},{3,2},{4,5},{5,4},{6,7},{7,6},{8,9},{9,8},{10,11... | collective-permute-start | bytes 12296 | tf_op jit(solution)/shard_map/ppermute | solution.py:294
  61.5 1.6 %collective-permute-done.16 = f32[8,128]{1,0:T(8,128)S(1)} collective-permute-done((f32[8,128]{1,0:T(8,128)S(1)}, f32[8,128]{1,0:T(8,128)S(1)}, u32[]{:S(2)}, u32[]{:S(2)}) %collective-permute-start.16) | collective-permute-done | bytes 4128 | tf_op jit(solution)/shard_map/ppermute | solution.py:294
  63.1 0.9 %collective-permute-start.17 = (f32[8,128]{1,0:T(8,128)S(1)}, f32[8,128]{1,0:T(8,128)S(1)}, u32[]{:S(2)}, u32[]{:S(2)}) collective-permute-start(f32[8,128]{1,0:T(8,128)S(1)} %add.46), channel_id=1, source_target_pairs={{0,2},{1,3},{2,0},{3,1},{4,6},{5,7},{6,4},{7,5},{8,10},{9,11},{10,... | collective-permute-start | bytes 12296 | tf_op jit(solution)/shard_map/ppermute | solution.py:294
  64.0 2.7 %collective-permute-done.17 = f32[8,128]{1,0:T(8,128)S(1)} collective-permute-done((f32[8,128]{1,0:T(8,128)S(1)}, f32[8,128]{1,0:T(8,128)S(1)}, u32[]{:S(2)}, u32[]{:S(2)}) %collective-permute-start.17) | collective-permute-done | bytes 4128 | tf_op jit(solution)/shard_map/ppermute | solution.py:294
  66.7 2.1 %collective-permute-start.18 = (f32[8,128]{1,0:T(8,128)S(1)}, f32[8,128]{1,0:T(8,128)S(1)}, u32[]{:S(2)}, u32[]{:S(2)}) collective-permute-start(f32[8,128]{1,0:T(8,128)S(1)} %add.47), channel_id=1, source_target_pairs={{0,4},{1,5},{2,6},{3,7},{4,0},{5,1},{6,2},{7,3},{8,12},{9,13},{10,... | collective-permute-start | bytes 12296 | tf_op jit(solution)/shard_map/ppermute | solution.py:294
  68.8 2.4 %collective-permute-done.18 = f32[8,128]{1,0:T(8,128)S(1)} collective-permute-done((f32[8,128]{1,0:T(8,128)S(1)}, f32[8,128]{1,0:T(8,128)S(1)}, u32[]{:S(2)}, u32[]{:S(2)}) %collective-permute-start.18) | collective-permute-done | bytes 4128 | tf_op jit(solution)/shard_map/ppermute | solution.py:294
  71.2 5.2 %copy-done.1 = bf16[2048,3584]{1,0:T(8,128)(2,1)S(1)} copy-done((bf16[2048,3584]{1,0:T(8,128)(2,1)S(1)}, bf16[2048,3584]{1,0:T(8,128)(2,1)}, u32[]{:S(2)}) %copy-start.1) | copy-done | bytes 14680088
  76.4 12.7 %apply.1 = (bf16[2048,3584]{1,0:T(8,128)(2,1)}, bf16[2,512,512]{2,1,0:T(8,128)(2,1)}) custom-call(s32[4]{0:T(128)S(1)} %iota_xor_fusion.order, s32[2]{0:T(128)S(1)} %pad_add_fusion.here, s32[4,4]{1,0:T(4,128)S(1)} %copy-done.3, f32[8,128]{1,0:T(8,128)S(1)} %add.48.sums, bf16[512,512]{1,0:T(8,128)(2,1)S(1)} %get-tuple-element.40.r0, ...), custom_call_target="tpu_custom_call" | custom-call | tf_op jit(solution)/shard_map/apply/pallas_call | solution.py:269
  (34 shorter events, 2.6 us)
Async XLA Ops:
  0.7 1.6 %copy-start.2 = (bf16[512,2048]{1,0:T(8,128)(2,1)S(1)}, bf16[512,2048]{1,0:T(8,128)(2,1)}, u32[]{:S(2)}) copy-start(bf16[512,2048]{1,0:T(8,128)(2,1)} %x_ref.1) | copy-start | bytes 6291460
  3.8 7.3 %collective-permute-start.1 = (bf16[256,256]{1,0:T(8,128)(2,1)S(1)}, bf16[256,256]{1,0:T(8,128)(2,1)S(1)}, u32[]{:S(2)}, u32[]{:S(2)}) collective-permute-start(bf16[256,256]{1,0:T(8,128)(2,1)S(1)} %get-tuple-element.27), channel_id=1, source_target_pairs={{0,1},{1,0},{2,3},{3,2},{4,5},{5,4},{6,7},{7,6},{8,9},{9,8},{10,11... | collective-permute-start | bytes 393224 | tf_op jit(solution)/shard_map/ppermute | solution.py:294
  6.9 8.7 %collective-permute-start = (bf16[256,256]{1,0:T(8,128)(2,1)S(1)}, bf16[256,256]{1,0:T(8,128)(2,1)S(1)}, u32[]{:S(2)}, u32[]{:S(2)}) collective-permute-start(bf16[256,256]{1,0:T(8,128)(2,1)S(1)} %get-tuple-element.25), channel_id=1, source_target_pairs={{0,1},{1,0},{2,3},{3,2},{4,5},{5,4},{6,7},{7,6},{8,9},{9,8},{10,11... | collective-permute-start | bytes 393224 | tf_op jit(solution)/shard_map/ppermute | solution.py:294
  6.9 6.6 %collective-permute-start.3 = (bf16[272,256]{1,0:T(8,128)(2,1)S(1)}, bf16[272,256]{1,0:T(8,128)(2,1)S(1)}, u32[]{:S(2)}, u32[]{:S(2)}) collective-permute-start(bf16[272,256]{1,0:T(8,128)(2,1)S(1)} %get-tuple-element.30), channel_id=1, source_target_pairs={{0,2},{1,3},{2,0},{3,1},{4,6},{5,7},{6,4},{7,5},{8,10},{9,11},{10,... | collective-permute-start | bytes 417800 | tf_op jit(solution)/shard_map/ppermute | solution.py:294
  9.0 11.8 %collective-permute-start.5 = (bf16[272,256]{1,0:T(8,128)(2,1)S(1)}, bf16[272,256]{1,0:T(8,128)(2,1)S(1)}, u32[]{:S(2)}, u32[]{:S(2)}) collective-permute-start(bf16[272,256]{1,0:T(8,128)(2,1)S(1)} %get-tuple-element.31), channel_id=1, source_target_pairs={{0,2},{1,3},{2,0},{3,1},{4,6},{5,7},{6,4},{7,5},{8,10},{9,11},{10,... | collective-permute-start | bytes 417800 | tf_op jit(solution)/shard_map/ppermute | solution.py:294
  11.2 6.6 %collective-permute-start.2 = (bf16[256,256]{1,0:T(8,128)(2,1)S(1)}, bf16[256,256]{1,0:T(8,128)(2,1)S(1)}, u32[]{:S(2)}, u32[]{:S(2)}) collective-permute-start(bf16[256,256]{1,0:T(8,128)(2,1)S(1)} %add_convert_fusion.3), channel_id=1, source_target_pairs={{0,2},{1,3},{2,0},{3,1},{4,6},{5,7},{6,4},{7,5},{8,10},{9,11},{10,... | collective-permute-start | bytes 393224 | tf_op jit(solution)/shard_map/ppermute | solution.py:294
  13.6 7.2 %collective-permute-start.4 = (bf16[272,256]{1,0:T(8,128)(2,1)S(1)}, bf16[272,256]{1,0:T(8,128)(2,1)S(1)}, u32[]{:S(2)}, u32[]{:S(2)}) collective-permute-start(bf16[272,256]{1,0:T(8,128)(2,1)S(1)} %add_convert_fusion.1), channel_id=1, source_target_pairs={{0,1},{1,0},{2,3},{3,2},{4,5},{5,4},{6,7},{7,6},{8,9},{9,8},{10,11... | collective-permute-start | bytes 417800 | tf_op jit(solution)/shard_map/ppermute | solution.py:294
  17.9 20.5 %collective-permute-start.6 = (bf16[256,256]{1,0:T(8,128)(2,1)S(1)}, bf16[256,256]{1,0:T(8,128)(2,1)S(1)}, u32[]{:S(2)}, u32[]{:S(2)}) collective-permute-start(bf16[256,256]{1,0:T(8,128)(2,1)S(1)} %add_convert_fusion.2.after0.mine0), channel_id=1, source_target_pairs={{0,4},{1,5},{2,6},{3,7},{4,0},{5,1},{6,2},{7,3},{8,12},{9,13},{10,... | collective-permute-start | bytes 393224 | tf_op jit(solution)/shard_map/ppermute | solution.py:294
  20.8 17.6 %collective-permute-start.7 = (bf16[272,256]{1,0:T(8,128)(2,1)S(1)}, bf16[272,256]{1,0:T(8,128)(2,1)S(1)}, u32[]{:S(2)}, u32[]{:S(2)}) collective-permute-start(bf16[272,256]{1,0:T(8,128)(2,1)S(1)} %add_convert_fusion.after1.mine1), channel_id=1, source_target_pairs={{0,4},{1,5},{2,6},{3,7},{4,0},{5,1},{6,2},{7,3},{8,12},{9,13},{10,... | collective-permute-start | bytes 417800 | tf_op jit(solution)/shard_map/ppermute | solution.py:294
  21.9 5.2 %copy-start = (bf16[2048,3584]{1,0:T(8,128)(2,1)S(1)}, bf16[2048,3584]{1,0:T(8,128)(2,1)}, u32[]{:S(2)}) copy-start(bf16[2048,3584]{1,0:T(8,128)(2,1)} %g_ref.3) | copy-start | bytes 44040196
  38.4 32.8 %copy-start.3 = (s32[4,4]{1,0:T(4,128)S(1)}, s32[4,4]{1,0:T(4,128)}, u32[]{:S(2)}) copy-start(s32[4,4]{1,0:T(4,128)} %owner_slot.1) | copy-start | bytes 196
  41.6 5.4 %collective-permute-start.10 = (bf16[272,256]{1,0:T(8,128)(2,1)S(1)}, bf16[272,256]{1,0:T(8,128)(2,1)S(1)}, u32[]{:S(2)}, u32[]{:S(2)}) collective-permute-start(bf16[272,256]{1,0:T(8,128)(2,1)S(1)} %get-tuple-element.34.half1), channel_id=1, source_target_pairs={{0,1},{1,0},{2,3},{3,2},{4,5},{5,4},{6,7},{7,6},{8,9},{9,8},{10,11... | collective-permute-start | bytes 417800 | tf_op jit(solution)/shard_map/ppermute | solution.py:294
  43.2 5.4 %collective-permute-start.8 = (bf16[256,256]{1,0:T(8,128)(2,1)S(1)}, bf16[256,256]{1,0:T(8,128)(2,1)S(1)}, u32[]{:S(2)}, u32[]{:S(2)}) collective-permute-start(bf16[256,256]{1,0:T(8,128)(2,1)S(1)} %get-tuple-element.33.half0), channel_id=1, source_target_pairs={{0,2},{1,3},{2,0},{3,1},{4,6},{5,7},{6,4},{7,5},{8,10},{9,11},{10,... | collective-permute-start | bytes 393224 | tf_op jit(solution)/shard_map/ppermute | solution.py:294
  44.8 6.9 %collective-permute-start.13 = (bf16[256,256]{1,0:T(8,128)(2,1)S(1)}, bf16[256,256]{1,0:T(8,128)(2,1)S(1)}, u32[]{:S(2)}, u32[]{:S(2)}) collective-permute-start(bf16[256,256]{1,0:T(8,128)(2,1)S(1)} %get-tuple-element.33.half0), channel_id=1, source_target_pairs={{0,1},{1,0},{2,3},{3,2},{4,5},{5,4},{6,7},{7,6},{8,9},{9,8},{10,11... | collective-permute-start | bytes 393224 | tf_op jit(solution)/shard_map/ppermute | solution.py:294
  45.3 6.9 %collective-permute-start.12 = (bf16[272,256]{1,0:T(8,128)(2,1)S(1)}, bf16[272,256]{1,0:T(8,128)(2,1)S(1)}, u32[]{:S(2)}, u32[]{:S(2)}) collective-permute-start(bf16[272,256]{1,0:T(8,128)(2,1)S(1)} %get-tuple-element.34.half1), channel_id=1, source_target_pairs={{0,2},{1,3},{2,0},{3,1},{4,6},{5,7},{6,4},{7,5},{8,10},{9,11},{10,... | collective-permute-start | bytes 417800 | tf_op jit(solution)/shard_map/ppermute | solution.py:294
  47.0 7.0 %collective-permute-start.11 = (bf16[272,256]{1,0:T(8,128)(2,1)S(1)}, bf16[272,256]{1,0:T(8,128)(2,1)S(1)}, u32[]{:S(2)}, u32[]{:S(2)}) collective-permute-start(bf16[272,256]{1,0:T(8,128)(2,1)S(1)} %collective-permute-done.10.half1), channel_id=1, source_target_pairs={{0,2},{1,3},{2,0},{3,1},{4,6},{5,7},{6,4},{7,5},{8,10},{9,11},{10,... | collective-permute-start | bytes 417800 | tf_op jit(solution)/shard_map/ppermute | solution.py:294
  48.6 5.4 %collective-permute-start.9 = (bf16[256,256]{1,0:T(8,128)(2,1)S(1)}, bf16[256,256]{1,0:T(8,128)(2,1)S(1)}, u32[]{:S(2)}, u32[]{:S(2)}) collective-permute-start(bf16[256,256]{1,0:T(8,128)(2,1)S(1)} %collective-permute-done.8.half0), channel_id=1, source_target_pairs={{0,1},{1,0},{2,3},{3,2},{4,5},{5,4},{6,7},{7,6},{8,9},{9,8},{10,11... | collective-permute-start | bytes 393224 | tf_op jit(solution)/shard_map/ppermute | solution.py:294
  54.6 1.2 %collective-permute-start.14 = (f32[8,128]{1,0:T(8,128)S(1)}, f32[8,128]{1,0:T(8,128)S(1)}, u32[]{:S(2)}, u32[]{:S(2)}) collective-permute-start(f32[8,128]{1,0:T(8,128)S(1)} %get-tuple-element.39), channel_id=1, source_target_pairs={{0,8},{8,0},{16,24},{24,16},{1,9},{9,1},{17,25},{25,17},{2,10},{10... | collective-permute-start | bytes 12296 | tf_op jit(solution)/shard_map/ppermute | solution.py:294
  55.8 3.6 %collective-permute-start.15 = (f32[8,128]{1,0:T(8,128)S(1)}, f32[8,128]{1,0:T(8,128)S(1)}, u32[]{:S(2)}, u32[]{:S(2)}) collective-permute-start(f32[8,128]{1,0:T(8,128)S(1)} %add.44), channel_id=1, source_target_pairs={{0,16},{8,24},{16,0},{24,8},{1,17},{9,25},{17,1},{25,9},{2,18},{10... | collective-permute-start | bytes 12296 | tf_op jit(solution)/shard_map/ppermute | solution.py:294
  59.4 3.6 %collective-permute-start.16 = (f32[8,128]{1,0:T(8,128)S(1)}, f32[8,128]{1,0:T(8,128)S(1)}, u32[]{:S(2)}, u32[]{:S(2)}) collective-permute-start(f32[8,128]{1,0:T(8,128)S(1)} %add.45), channel_id=1, source_target_pairs={{0,1},{1,0},{2,3},{3,2},{4,5},{5,4},{6,7},{7,6},{8,9},{9,8},{10,11... | collective-permute-start | bytes 12296 | tf_op jit(solution)/shard_map/ppermute | solution.py:294
  63.1 3.6 %collective-permute-start.17 = (f32[8,128]{1,0:T(8,128)S(1)}, f32[8,128]{1,0:T(8,128)S(1)}, u32[]{:S(2)}, u32[]{:S(2)}) collective-permute-start(f32[8,128]{1,0:T(8,128)S(1)} %add.46), channel_id=1, source_target_pairs={{0,2},{1,3},{2,0},{3,1},{4,6},{5,7},{6,4},{7,5},{8,10},{9,11},{10,... | collective-permute-start | bytes 12296 | tf_op jit(solution)/shard_map/ppermute | solution.py:294
  66.7 4.5 %collective-permute-start.18 = (f32[8,128]{1,0:T(8,128)S(1)}, f32[8,128]{1,0:T(8,128)S(1)}, u32[]{:S(2)}, u32[]{:S(2)}) collective-permute-start(f32[8,128]{1,0:T(8,128)S(1)} %add.47), channel_id=1, source_target_pairs={{0,4},{1,5},{2,6},{3,7},{4,0},{5,1},{6,2},{7,3},{8,12},{9,13},{10,... | collective-permute-start | bytes 12296 | tf_op jit(solution)/shard_map/ppermute | solution.py:294
  71.2 5.2 %copy-start.1 = (bf16[2048,3584]{1,0:T(8,128)(2,1)S(1)}, bf16[2048,3584]{1,0:T(8,128)(2,1)}, u32[]{:S(2)}) copy-start(bf16[2048,3584]{1,0:T(8,128)(2,1)} %g_ref.3) | copy-start | bytes 44040196

commit v3 on v2

v3 whole, which is shorter than its diff:
```python
import functools

import jax
import jax.numpy as jnp
from jax import lax
from jax.experimental import pallas as pl
from jax.experimental.pallas import tpu as pltpu
from jax.sharding import PartitionSpec as P

BLK = 512
HALF = BLK // 2
FOLD = BLK + 16
ITERS = 3
SLOTS = 2
QUAD = 4
ROWS = 8
LANES = 128

damping = 0.01
F32 = jnp.float32
BF16 = jnp.bfloat16
SMEM = pl.BlockSpec(memory_space=pltpu.SMEM)
VMEM = pl.BlockSpec(memory_space=pltpu.VMEM)
ANY = pl.BlockSpec(memory_space=pl.ANY)


def params(mib):
    return pltpu.CompilerParams(vmem_limit_bytes=mib * 2**20)


def dot(left, right, dims=((1,), (0,))):
    return lax.dot_general(left, right, (dims, ((), ())), preferred_element_type=F32)


def places():
    row = lax.broadcasted_iota(jnp.int32, (HALF, HALF), 0)
    col = lax.broadcasted_iota(jnp.int32, (HALF, HALF), 1)
    return row, col


def fold(first, last):
    row, col = places()
    body = jnp.where(row <= col, first, last)
    diagonal = jnp.sum(jnp.where(row == col, last, 0.0), axis=0, keepdims=True)
    return body, jnp.broadcast_to(diagonal, (FOLD - BLK, HALF))


def unfold(body, diagonal):
    row, col = places()
    turned = body.T
    first = jnp.where(row <= col, body, turned)
    last = jnp.where(row > col, body, jnp.where(row < col, turned, diagonal))
    return first, last


def stat_kernel(order, x_ref, *out):
    for place in (1, 2, 3, 0):
        start = pl.multiple_of(order[place] * BLK, BLK)
        left = x_ref[:, pl.ds(start, HALF)]
        right = x_ref[:, pl.ds(pl.multiple_of(start + HALF, HALF), HALF)]
        along = ((0,), (0,))
        out[place][:HALF] = dot(left, right, along).astype(BF16)
        body, diagonal = fold(dot(left, left, along), dot(right, right, along))
        out[place][HALF:BLK] = body.astype(BF16)
        out[place][BLK:] = diagonal.astype(BF16)


def statistics(order, activations):
    return pl.pallas_call(
        stat_kernel,
        out_shape=[jax.ShapeDtypeStruct((FOLD, HALF), BF16)] * QUAD,
        in_specs=[SMEM, VMEM],
        out_specs=[VMEM] * QUAD,
        compiler_params=params(16),
        name="statistics",
    )(order, activations)


def chunks(width, size):
    start = 0
    while width - start >= 2 * size:
        yield pl.ds(start, size)
        start += size
    yield pl.ds(start, width - start)


def gram_kernel(order, after, g_ref, held_ref, top_ref, last_ref, norm_ref, arrived):
    parts = list(chunks(g_ref.shape[1], 1792))

    def copy(place, index):
        rows = pl.ds(pl.multiple_of(order[place] * BLK, BLK), BLK)
        return pltpu.make_async_copy(
            g_ref.at[rows, parts[index]],
            held_ref.at[place, :, parts[index]],
            arrived.at[place, index],
        )

    for place in range(QUAD):
        for index in range(len(parts)):
            copy(place, index).start()

    def block(place, _):
        for index, part in enumerate(parts):
            copy(place, index).wait()
            upper = held_ref[place, :HALF, part]
            lower = held_ref[place, HALF:, part]
            across = ((1,), (1,))
            terms = dot(upper, upper, across), dot(upper, lower, across), dot(lower, lower, across)
            if index == 0:
                top_ref[place, :, :HALF] = terms[0]
                top_ref[place, :, HALF:] = terms[1]
                last_ref[place] = terms[2]
            else:
                top_ref[place, :, :HALF] += terms[0]
                top_ref[place, :, HALF:] += terms[1]
                last_ref[place] += terms[2]
        row, col = places()
        squares = jnp.where(row == col, top_ref[place, :, :HALF] + last_ref[place], 0.0)
        norm_ref[place] = jnp.sum(squares, axis=0, keepdims=True)
        return _

    lax.fori_loop(0, QUAD, block, 0)


def gram(order, gradient, after):
    rows, columns = gradient.shape
    parts = len(list(chunks(columns, 1792)))
    return pl.pallas_call(
        gram_kernel,
        out_shape=[
            pltpu.VMEM((QUAD, BLK, columns), BF16),
            pltpu.VMEM((QUAD, HALF, BLK), F32),
            pltpu.VMEM((QUAD, HALF, HALF), F32),
            pltpu.VMEM((QUAD, 1, HALF), F32),
        ],
        in_specs=[SMEM, ANY, ANY],
        out_specs=[VMEM] * 4,
        scratch_shapes=[pltpu.SemaphoreType.DMA((QUAD, parts))],
        compiler_params=params(16),
        cost_estimate=pl.CostEstimate(
            flops=2 * rows * columns * BLK, bytes_accessed=4 * rows * columns, transcendentals=0
        ),
        name="gram",
    )(order, after, pltpu.with_memory_space_constraint(gradient, pltpu.HBM))


def product(left, right):
    return dot(left.astype(BF16), right.astype(BF16))


def newton_kernel(tokens, after, mine, other, root, held):
    total = (mine[...].astype(F32) + other[...].astype(F32)) / tokens
    cross = total[:HALF]
    first, last = unfold(total[HALF:BLK], total[BLK : BLK + 1])
    held[:HALF, :HALF] = first
    held[:HALF, HALF:] = cross
    held[HALF:, :HALF] = cross.T
    held[HALF:, HALF:] = last
    row = lax.broadcasted_iota(jnp.int32, (BLK, BLK), 0)
    col = lax.broadcasted_iota(jnp.int32, (BLK, BLK), 1)
    identity = jnp.where(row == col, 1.0, 0.0).astype(F32)
    matrix = held[...] + damping * identity
    bound = jnp.max(jnp.sum(jnp.abs(matrix), axis=0, keepdims=True), axis=1, keepdims=True)
    scale = 2.0 / bound
    iterate = matrix * scale
    estimate = None
    for step in range(ITERS):
        error = (identity - iterate) * 0.25
        if estimate is None:
            estimate = error
        else:
            estimate = estimate + error + product(estimate, error)
        if step + 1 < ITERS:
            square = 2.0 * error + product(error, error)
            fourth = 2.0 * square + product(square, square)
            iterate = iterate + product(fourth, iterate)
    held[...] = (estimate + identity) * jnp.sqrt(jnp.sqrt(scale))
    root[:HALF] = held[:HALF, HALF:].astype(BF16)
    body, diagonal = fold(held[:HALF, :HALF], held[HALF:, HALF:])
    root[HALF:BLK] = body.astype(BF16)
    root[BLK:] = diagonal.astype(BF16)


def newton(tokens, after, mine, other):
    return pl.pallas_call(
        functools.partial(newton_kernel, tokens),
        out_shape=jax.ShapeDtypeStruct((FOLD, HALF), BF16),
        in_specs=[ANY, VMEM, VMEM],
        out_specs=VMEM,
        scratch_shapes=[pltpu.VMEM((BLK, BLK), F32)],
        compiler_params=params(16),
        cost_estimate=pl.CostEstimate(
            flops=16 * BLK**3, bytes_accessed=8 * BLK * BLK, transcendentals=0
        ),
        name="newton",
    )(after, mine, other)


def norm_kernel(place, folded, top_ref, last_ref, square_ref, sums_ref, root_ref, total_ref):
    cross = folded[:HALF]
    rest = folded[HALF:].astype(F32)
    first, last = unfold(rest[:HALF], rest[HALF : HALF + 1])
    root_ref[:HALF, :HALF] = first.astype(BF16)
    root_ref[:HALF, HALF:] = cross
    root_ref[HALF:, :HALF] = cross.astype(F32).T.astype(BF16)
    root_ref[HALF:, HALF:] = last.astype(BF16)
    upper = dot(root_ref[:HALF], root_ref[...]) * top_ref[place]
    lower = dot(root_ref[HALF:], root_ref[:, HALF:]) * last_ref[place]
    new = jnp.sum(upper[:, :HALF] + 2.0 * upper[:, HALF:] + lower, axis=0, keepdims=True)
    old = square_ref[place]
    lanes = lambda value: sum(value[:, i : i + LANES] for i in range(0, HALF, LANES))
    row = lax.broadcasted_iota(jnp.int32, sums_ref.shape, 0)
    total_ref[...] = sums_ref[...] + jnp.where(row == 0, lanes(old), jnp.where(row == 1, lanes(new), 0.0))


def norm(place, folded, grams, sums):
    return pl.pallas_call(
        functools.partial(norm_kernel, place),
        out_shape=[
            jax.ShapeDtypeStruct((BLK, BLK), BF16),
            jax.ShapeDtypeStruct((ROWS, LANES), F32),
        ],
        in_specs=[VMEM] * 5,
        out_specs=[VMEM] * 2,
        compiler_params=params(16),
        cost_estimate=pl.CostEstimate(
            flops=2 * BLK**3, bytes_accessed=8 * BLK * BLK, transcendentals=0
        ),
        name="norm",
    )(folded, *grams, sums)


def multiply_kernel(place, after, root_ref, g_ref, u_ref):
    for part in chunks(g_ref.shape[2], BLK):
        u_ref[place, :, part] = dot(root_ref[...], g_ref[place, :, part]).astype(BF16)


def multiply(place, root, held, after):
    return pl.pallas_call(
        functools.partial(multiply_kernel, place),
        out_shape=pltpu.VMEM(held.shape, BF16),
        in_specs=[ANY, VMEM, VMEM],
        out_specs=VMEM,
        input_output_aliases={2: 0},
        compiler_params=params(16),
        cost_estimate=pl.CostEstimate(
            flops=2 * BLK * BLK * held.shape[2],
            bytes_accessed=4 * BLK * held.shape[2],
            transcendentals=0,
        ),
        name="multiply",
    )(after, root, held)


def owned_kernel(order, here, owner_slot, r0, r1, r2, r3, owned_ref):
    owned_ref[...] = jnp.zeros_like(owned_ref)
    for place, root in enumerate((r0, r1, r2, r3)):
        for slot in range(SLOTS):

            @pl.when(owner_slot[here[0], order[place]] == here[1] + slot)
            def _():
                owned_ref[slot] = root[...]


def owned_roots(order, here, owner_slot, roots):
    return pl.pallas_call(
        owned_kernel,
        out_shape=jax.ShapeDtypeStruct((SLOTS, BLK, BLK), BF16),
        grid_spec=pltpu.PrefetchScalarGridSpec(
            num_scalar_prefetch=3,
            grid=(1,),
            in_specs=[pl.BlockSpec((BLK, BLK), lambda i, *_: (0, 0))] * QUAD,
            out_specs=pl.BlockSpec((SLOTS, BLK, BLK), lambda i, *_: (0, 0, 0)),
        ),
        compiler_params=params(16),
        cost_estimate=pl.CostEstimate(
            flops=0, bytes_accessed=4 * SLOTS * BLK * BLK, transcendentals=0
        ),
        name="owned",
    )(order, here, owner_slot, *roots)


def scale_kernel(order, sums, u_ref, update_ref, scaled, sent):
    both = jnp.sum(sums[...], axis=1, keepdims=True)
    ratio = jnp.sqrt(both[:1] / (both[1:2] + 1e-06))
    parts = list(chunks(u_ref.shape[2], 1792))

    def copy(place, index):
        rows = pl.ds(pl.multiple_of(order[place] * BLK, BLK), BLK)
        return pltpu.make_async_copy(
            scaled.at[place, :, parts[index]],
            update_ref.at[rows, parts[index]],
            sent.at[place, index],
        )

    def block(place, _):
        for index, part in enumerate(parts):
            scaled[place, :, part] = (u_ref[place, :, part].astype(F32) * ratio).astype(BF16)
            copy(place, index).start()
        return _

    lax.fori_loop(0, QUAD, block, 0)
    for place in range(QUAD):
        for index in range(len(parts)):
            copy(place, index).wait()


def scale(order, sums, unscaled):
    columns = unscaled.shape[2]
    parts = len(list(chunks(columns, 1792)))
    update, _ = pl.pallas_call(
        scale_kernel,
        out_shape=[
            jax.ShapeDtypeStruct((QUAD * BLK, columns), BF16),
            pltpu.VMEM(unscaled.shape, BF16),
        ],
        in_specs=[SMEM, VMEM, VMEM],
        out_specs=[ANY, VMEM],
        input_output_aliases={2: 1},
        scratch_shapes=[pltpu.SemaphoreType.DMA((QUAD, parts))],
        compiler_params=params(16),
        name="scale",
    )(order, sums, unscaled)
    return update


def swap(value, flip, axis="dp"):
    count = lax.axis_size(axis)
    return lax.ppermute(value, axis, [(i, i ^ flip) for i in range(count)])


def total(value, *axes):
    for axis in axes:
        flip = 1
        while flip < lax.axis_size(axis):
            value = value + swap(value, flip, axis)
            flip *= 2
    return value


def add(*values):
    return sum(value.astype(F32) for value in values).astype(BF16)


def per_device(activations, gradient, owner_slot):
    peer_count = lax.axis_size("dp")
    my_index = lax.axis_index("dp")
    group_index = lax.axis_index("pool")
    tokens_all = activations.shape[0] * peer_count
    order = (my_index % QUAD) ^ jnp.arange(QUAD, dtype=jnp.int32)
    here = jnp.stack([group_index, my_index * SLOTS])

    a, b, c, d = statistics(order, activations)
    mine = add(a, swap(b, 1), swap(c, 2), swap(d, 3))
    flip = QUAD
    other = swap(mine, flip)
    while 2 * flip < peer_count:
        mine = add(mine, other)
        flip *= 2
        other = swap(mine, flip)

    held, *grams = gram(order, gradient, mine)
    a = newton(tokens_all, grams[-1], mine, other)
    sums = jnp.zeros((ROWS, LANES), F32)
    roots = []
    for place, folded in enumerate((a, swap(a, 1), swap(a, 2), swap(a, 3))):
        root, sums = norm(place, folded, grams, sums)
        roots.append(root)
    for place, root in enumerate(roots):
        held = multiply(place, root, held, sums)
    owned = owned_roots(order, here, owner_slot, roots)
    update = scale(order, total(sums, "pool", "dp"), held)
    return (update, owned[None])


def solution(mesh):
    in_specs = (P("dp", "pool"), P("pool", "dp"), P())
    out_specs = (P("pool", "dp"), P("pool", "dp", None, None))
    return jax.shard_map(
        per_device, mesh=mesh, in_specs=in_specs, out_specs=out_specs, check_vma=False
    )
```

time: 89.3 us -> 98.7 us (1.11)
  starting transfers between devices: 28 us -> 16.1 us
  local copies, waits for them, and re-layouts: 11.9 us -> 22.9 us
  Pallas kernels: 31 us -> 38.4 us
  waiting for transfers between devices: 17.1 us -> 19.9 us
    ppermute x19 -> x12, starting transfers between devices: 28 us -> 16.1 us  [swap(): return lax.ppermute(value, axis, [(i, i ^ flip) for i in range(count)])]
    unnamed x8 -> x12, local copies, waits for them, and re-layouts: 11.9 us -> 22.9 us
    pallas_call x8 -> x13, Pallas kernels: 31 us -> 38.4 us  [the longest x1 10.8 us: gram(): pl.pallas_call(gram_kernel, out_shape=[pltpu.VMEM((QUAD, BLK, columns), B...]
    ppermute x19 -> x12, waiting for transfers between devices: 17.1 us -> 19.9 us  [swap(): return lax.ppermute(value, axis, [(i, i ^ flip) for i in range(count)])]
  transfers between devices with their start and end apart: 19 -> 12, of which waited for: 10 -> 7; matrix products, arithmetic and copies ran while one was open for 0% -> 0% of each run, Pallas kernels for 15% -> 25%
where the time goes in v3:
time: 98.7 us; the launch traced here: 98.4 us
  Pallas kernels  38.4 us (39%)
  local copies, waits for them, and re-layouts  22.9 us (23%)
  waiting for transfers between devices  19.9 us (20%)
  starting transfers between devices  16.1 us (16%)
    unnamed x12, local copies, waits for them, and re-layouts  22.9 us
    ppermute x12, waiting for transfers between devices, swap(): return lax.ppermute(value, axis, [(i, i ^ flip) for i in range(count)])  19.9 us
    ppermute x12, starting transfers between devices, swap(): return lax.ppermute(value, axis, [(i, i ^ flip) for i in range(count)])  16.1 us
    pallas_call x1, Pallas kernels, gram(): pl.pallas_call(gram_kernel, out_shape=[pltpu.VMEM((QUAD, BLK, columns), B...  10.8 us
    pallas_call x4, Pallas kernels, multiply(): pl.pallas_call(functools.partial(multiply_kernel, place), out_shape=pltpu...  8.91 us
    pallas_call x1, Pallas kernels, scale(): pl.pallas_call(scale_kernel, out_shape=[jax.ShapeDtypeStruct((QUAD * BLK,...  7.33 us
    pallas_call x4, Pallas kernels, norm(): pl.pallas_call(functools.partial(norm_kernel, place), out_shape=[jax.Shap...  4.9 us
    pallas_call x1, Pallas kernels, newton(): pl.pallas_call(functools.partial(newton_kernel, tokens), out_shape=jax.Sh...  3.18 us
  transfers between devices with their start and end apart: 12, of which 7 were waited for; matrix products, arithmetic and copies ran while one was open for 0% of the time, Pallas kernels for 25%

profile of v3, /device:TPU:0, one launch (start us, length us, event | category | flops | bytes accessed | tf_op | source)
XLA Modules:
  0.0 98.4 jit_solution(17796480640053717369)
XLA Ops:
  0.7 1.6 %copy-done.4 = bf16[512,2048]{1,0:T(8,128)(2,1)S(1)} copy-done((bf16[512,2048]{1,0:T(8,128)(2,1)S(1)}, bf16[512,2048]{1,0:T(8,128)(2,1)}, u32[]{:S(2)}) %copy-start.4) | copy-done | bytes 2097176
  2.2 1.6 %statistics.1 = (bf16[528,256]{1,0:T(8,128)(2,1)S(1)}, bf16[528,256]{1,0:T(8,128)(2,1)S(1)}, bf16[528,256]{1,0:T(8,128)(2,1)S(1)}, bf16[528,256]{1,0:T(8,128)(2,1)S(1)}) custom-call(s32[4]{0:T(128)S(1)} %iota_xor_fusion.order, bf16[512,2048]{1,0:T(8,128)(2,1)S(1)} %copy-done.4), custom_call_target="tpu_custom_call" | custom-call | tf_op jit(solution)/shard_map/statistics/pallas_call | solution.py:69
  3.8 3.0 %collective-permute-start = (bf16[528,256]{1,0:T(8,128)(2,1)S(1)}, bf16[528,256]{1,0:T(8,128)(2,1)S(1)}, u32[]{:S(2)}, u32[]{:S(2)}) collective-permute-start(bf16[528,256]{1,0:T(8,128)(2,1)S(1)} %get-tuple-element.20), channel_id=1, source_target_pairs={{0,1},{1,0},{2,3},{3,2},{4,5},{5,4},{6,7},{7,6},{8,9},{9,8},{10,11... | collective-permute-start | bytes 811016 | tf_op jit(solution)/shard_map/ppermute | solution.py:329
  6.9 1.6 %collective-permute-start.1 = (bf16[528,256]{1,0:T(8,128)(2,1)S(1)}, bf16[528,256]{1,0:T(8,128)(2,1)S(1)}, u32[]{:S(2)}, u32[]{:S(2)}) collective-permute-start(bf16[528,256]{1,0:T(8,128)(2,1)S(1)} %get-tuple-element.21), channel_id=1, source_target_pairs={{0,2},{1,3},{2,0},{3,1},{4,6},{5,7},{6,4},{7,5},{8,10},{9,11},{10,... | collective-permute-start | bytes 811016 | tf_op jit(solution)/shard_map/ppermute | solution.py:329
  8.4 4.9 %collective-permute-done = bf16[528,256]{1,0:T(8,128)(2,1)S(1)} collective-permute-done((bf16[528,256]{1,0:T(8,128)(2,1)S(1)}, bf16[528,256]{1,0:T(8,128)(2,1)S(1)}, u32[]{:S(2)}, u32[]{:S(2)}) %collective-permute-start) | collective-permute-done | bytes 270368 | tf_op jit(solution)/shard_map/ppermute | solution.py:329
  13.3 2.9 %collective-permute-done.1 = bf16[528,256]{1,0:T(8,128)(2,1)S(1)} collective-permute-done((bf16[528,256]{1,0:T(8,128)(2,1)S(1)}, bf16[528,256]{1,0:T(8,128)(2,1)S(1)}, u32[]{:S(2)}, u32[]{:S(2)}) %collective-permute-start.1) | collective-permute-done | bytes 270368 | tf_op jit(solution)/shard_map/ppermute | solution.py:329
  16.3 4.1 %collective-permute-done.2 = bf16[528,256]{1,0:T(8,128)(2,1)S(1)} collective-permute-done((bf16[528,256]{1,0:T(8,128)(2,1)S(1)}, bf16[528,256]{1,0:T(8,128)(2,1)S(1)}, u32[]{:S(2)}, u32[]{:S(2)}) %collective-permute-start.2) | collective-permute-done | bytes 270368 | tf_op jit(solution)/shard_map/ppermute | solution.py:329
  20.6 2.8 %collective-permute-start.3 = (bf16[528,256]{1,0:T(8,128)(2,1)S(1)}, bf16[528,256]{1,0:T(8,128)(2,1)S(1)}, u32[]{:S(2)}, u32[]{:S(2)}) collective-permute-start(bf16[528,256]{1,0:T(8,128)(2,1)S(1)} %add_convert_fusion.after.mine), channel_id=1, source_target_pairs={{0,4},{1,5},{2,6},{3,7},{4,0},{5,1},{6,2},{7,3},{8,12},{9,13},{10,... | collective-permute-start | bytes 811016 | tf_op jit(solution)/shard_map/ppermute | solution.py:329
  23.4 10.8 %gram.1 = (bf16[4,512,3584]{2,1,0:T(8,128)(2,1)S(1)}, f32[4,256,512]{2,1,0:T(8,128)S(1)}, f32[4,256,256]{2,1,0:T(8,128)S(1)}, f32[4,1,256]{2,1,0:T(1,128)S(1)}) custom-call(s32[4]{0:T(128)S(1)} %iota_xor_fusion.order, bf16[528,256]{1,0:T(8,128)(2,1)S(1)} %add_convert_fusion.after.mine, bf16[2048,3584]{1,0:T(8,128)(2,1)} %g_ref.1), custom_call_target="tpu_custom_call" | custom-call | flops 7516192768 | bytes 29360128 | tf_op jit(solution)/shard_map/gram/pallas_call | solution.py:128
  34.2 5.5 %copy-done = bf16[4,512,3584]{2,1,0:T(8,128)(2,1)} copy-done((bf16[4,512,3584]{2,1,0:T(8,128)(2,1)}, bf16[4,512,3584]{2,1,0:T(8,128)(2,1)S(1)}, u32[]{:S(2)}) %copy-start) | copy-done | bytes 14680088
  39.7 3.2 %newton.1.folded = bf16[528,256]{1,0:T(8,128)(2,1)S(1)} custom-call(f32[4,1,256]{2,1,0:T(1,128)S(1)} %get-tuple-element.23.after.square_ref, bf16[528,256]{1,0:T(8,128)(2,1)S(1)} %add_convert_fusion.after.mine, bf16[528,256]{1,0:T(8,128)(2,1)S(1)} %collective-permute-done.3.other), custom_call_target="tpu_custom_call" | custom-call | flops 2147483648 | bytes 2097152 | tf_op jit(solution)/shard_map/newton/pallas_call | solution.py:185
  42.8 1.6 %collective-permute-start.6 = (bf16[528,256]{1,0:T(8,128)(2,1)S(1)}, bf16[528,256]{1,0:T(8,128)(2,1)}, u32[]{:S(2)}, u32[]{:S(2)}) collective-permute-start(bf16[528,256]{1,0:T(8,128)(2,1)S(1)} %newton.1.folded), channel_id=1, source_target_pairs={{0,1},{1,0},{2,3},{3,2},{4,5},{5,4},{6,7},{7,6},{8,9},{9,8},{10,11... | collective-permute-start | bytes 811016 | tf_op jit(solution)/shard_map/ppermute | solution.py:329
  44.4 1.6 %collective-permute-start.5 = (bf16[528,256]{1,0:T(8,128)(2,1)S(1)}, bf16[528,256]{1,0:T(8,128)(2,1)}, u32[]{:S(2)}, u32[]{:S(2)}) collective-permute-start(bf16[528,256]{1,0:T(8,128)(2,1)S(1)} %newton.1.folded), channel_id=1, source_target_pairs={{0,2},{1,3},{2,0},{3,1},{4,6},{5,7},{6,4},{7,5},{8,10},{9,11},{10,... | collective-permute-start | bytes 811016 | tf_op jit(solution)/shard_map/ppermute | solution.py:329
  46.9 4.6 %collective-permute-done.6.folded = bf16[528,256]{1,0:T(8,128)(2,1)} collective-permute-done((bf16[528,256]{1,0:T(8,128)(2,1)S(1)}, bf16[528,256]{1,0:T(8,128)(2,1)}, u32[]{:S(2)}, u32[]{:S(2)}) %collective-permute-start.6) | collective-permute-done | bytes 270368 | tf_op jit(solution)/shard_map/ppermute | solution.py:329
  51.5 1.5 %norm.5 = (bf16[512,512]{1,0:T(8,128)(2,1)S(1)}, f32[8,128]{1,0:T(8,128)S(1)}) custom-call(bf16[528,256]{1,0:T(8,128)(2,1)} %collective-permute-done.6.folded, f32[4,256,512]{2,1,0:T(8,128)S(1)} %get-tuple-element.24.top_ref, f32[4,256,256]{2,1,0:T(8,128)S(1)} %get-tuple-element.25.last_ref, f32[4,1,256]{2,1,0:T(1,128)S(1)} %get-tuple-element.23.after.square_ref, ...), custom_call_target="tpu_custom_call" | custom-call | flops 268435456 | bytes 2097152 | tf_op jit(solution)/shard_map/norm/pallas_call | solution.py:217
  53.0 0.9 collective-permute-done.5.folded
  53.9 1.5 %norm.6 = (bf16[512,512]{1,0:T(8,128)(2,1)S(1)}, f32[8,128]{1,0:T(8,128)S(1)}) custom-call(bf16[528,256]{1,0:T(8,128)(2,1)} %collective-permute-done.5.folded, f32[4,256,512]{2,1,0:T(8,128)S(1)} %get-tuple-element.24.top_ref, f32[4,256,256]{2,1,0:T(8,128)S(1)} %get-tuple-element.25.last_ref, f32[4,1,256]{2,1,0:T(1,128)S(1)} %get-tuple-element.23.after.square_ref, ...), custom_call_target="tpu_custom_call" | custom-call | flops 268435456 | bytes 2097152 | tf_op jit(solution)/shard_map/norm/pallas_call | solution.py:217
  55.4 1.4 %collective-permute-done.4.folded = bf16[528,256]{1,0:T(8,128)(2,1)} collective-permute-done((bf16[528,256]{1,0:T(8,128)(2,1)S(1)}, bf16[528,256]{1,0:T(8,128)(2,1)}, u32[]{:S(2)}, u32[]{:S(2)}) %collective-permute-start.4) | collective-permute-done | bytes 270368 | tf_op jit(solution)/shard_map/ppermute | solution.py:329
  56.7 1.5 %norm.7 = (bf16[512,512]{1,0:T(8,128)(2,1)S(1)}, f32[8,128]{1,0:T(8,128)S(1)}) custom-call(bf16[528,256]{1,0:T(8,128)(2,1)} %collective-permute-done.4.folded, f32[4,256,512]{2,1,0:T(8,128)S(1)} %get-tuple-element.24.top_ref, f32[4,256,256]{2,1,0:T(8,128)S(1)} %get-tuple-element.25.last_ref, f32[4,1,256]{2,1,0:T(1,128)S(1)} %get-tuple-element.23.after.square_ref, ...), custom_call_target="tpu_custom_call" | custom-call | flops 268435456 | bytes 2097152 | tf_op jit(solution)/shard_map/norm/pallas_call | solution.py:217
  58.4 1.1 %collective-permute-done.7 = f32[8,128]{1,0:T(8,128)S(1)} collective-permute-done((f32[8,128]{1,0:T(8,128)S(1)}, f32[8,128]{1,0:T(8,128)S(1)}, u32[]{:S(2)}, u32[]{:S(2)}) %collective-permute-start.7) | collective-permute-done | bytes 4128 | tf_op jit(solution)/shard_map/ppermute | solution.py:329
  59.4 1.5 %collective-permute-start.8 = (f32[8,128]{1,0:T(8,128)S(1)}, f32[8,128]{1,0:T(8,128)S(1)}, u32[]{:S(2)}, u32[]{:S(2)}) collective-permute-start(f32[8,128]{1,0:T(8,128)S(1)} %add.32), channel_id=1, source_target_pairs={{0,16},{8,24},{16,0},{24,8},{1,17},{9,25},{17,1},{25,9},{2,18},{10... | collective-permute-start | bytes 12296 | tf_op jit(solution)/shard_map/ppermute | solution.py:329
  60.9 5.2 %copy-done.1 = bf16[4,512,3584]{2,1,0:T(8,128)(2,1)S(1)} copy-done((bf16[4,512,3584]{2,1,0:T(8,128)(2,1)S(1)}, bf16[4,512,3584]{2,1,0:T(8,128)(2,1)}, u32[]{:S(2)}) %copy-start.1) | copy-done | bytes 14680088
  66.1 2.2 %multiply.4.g_ref = bf16[4,512,3584]{2,1,0:T(8,128)(2,1)S(1)} custom-call(f32[8,128]{1,0:T(8,128)S(1)} %get-tuple-element.29.after, bf16[512,512]{1,0:T(8,128)(2,1)S(1)} %get-tuple-element.33.root_ref.r0, bf16[4,512,3584]{2,1,0:T(8,128)(2,1)S(1)} %copy-done.1), custom_call_target="tpu_custom_call", output_to_operand_aliasing={{}: (2, {})} | custom-call | flops 1879048192 | bytes 7340032 | tf_op jit(solution)/shard_map/multiply/pallas_call | solution.py:239
  68.4 1.6 %collective-permute-start.9 = (f32[8,128]{1,0:T(8,128)S(1)}, f32[8,128]{1,0:T(8,128)S(1)}, u32[]{:S(2)}, u32[]{:S(2)}) collective-permute-start(f32[8,128]{1,0:T(8,128)S(1)} %add.33), channel_id=1, source_target_pairs={{0,1},{1,0},{2,3},{3,2},{4,5},{5,4},{6,7},{7,6},{8,9},{9,8},{10,11... | collective-permute-start | bytes 12296 | tf_op jit(solution)/shard_map/ppermute | solution.py:329
  69.9 2.2 %multiply.5.g_ref = bf16[4,512,3584]{2,1,0:T(8,128)(2,1)S(1)} custom-call(f32[8,128]{1,0:T(8,128)S(1)} %get-tuple-element.29.after, bf16[512,512]{1,0:T(8,128)(2,1)S(1)} %get-tuple-element.32.root_ref.r1, bf16[4,512,3584]{2,1,0:T(8,128)(2,1)S(1)} %multiply.4.g_ref), custom_call_target="tpu_custom_call", output_to_operand_aliasing={{}: (2, {})} | custom-call | flops 1879048192 | bytes 7340032 | tf_op jit(solution)/shard_map/multiply/pallas_call | solution.py:239
  72.2 1.7 %collective-permute-start.10 = (f32[8,128]{1,0:T(8,128)S(1)}, f32[8,128]{1,0:T(8,128)S(1)}, u32[]{:S(2)}, u32[]{:S(2)}) collective-permute-start(f32[8,128]{1,0:T(8,128)S(1)} %add.34), channel_id=1, source_target_pairs={{0,2},{1,3},{2,0},{3,1},{4,6},{5,7},{6,4},{7,5},{8,10},{9,11},{10,... | collective-permute-start | bytes 12296 | tf_op jit(solution)/shard_map/ppermute | solution.py:329
  73.9 2.2 %multiply.6.g_ref = bf16[4,512,3584]{2,1,0:T(8,128)(2,1)S(1)} custom-call(f32[8,128]{1,0:T(8,128)S(1)} %get-tuple-element.29.after, bf16[512,512]{1,0:T(8,128)(2,1)S(1)} %get-tuple-element.31.root_ref.r2, bf16[4,512,3584]{2,1,0:T(8,128)(2,1)S(1)} %multiply.5.g_ref), custom_call_target="tpu_custom_call", output_to_operand_aliasing={{}: (2, {})} | custom-call | flops 1879048192 | bytes 7340032 | tf_op jit(solution)/shard_map/multiply/pallas_call | solution.py:239
  76.5 2.2 %multiply.7.u_ref = bf16[4,512,3584]{2,1,0:T(8,128)(2,1)S(1)} custom-call(f32[8,128]{1,0:T(8,128)S(1)} %get-tuple-element.29.after, bf16[512,512]{1,0:T(8,128)(2,1)S(1)} %get-tuple-element.30.root_ref.r3, bf16[4,512,3584]{2,1,0:T(8,128)(2,1)S(1)} %multiply.6.g_ref), custom_call_target="tpu_custom_call", output_to_operand_aliasing={{}: (2, {})} | custom-call | flops 1879048192 | bytes 7340032 | tf_op jit(solution)/shard_map/multiply/pallas_call | solution.py:239
  78.7 5.5 %copy-done.2 = bf16[4,512,3584]{2,1,0:T(8,128)(2,1)} copy-done((bf16[4,512,3584]{2,1,0:T(8,128)(2,1)}, bf16[4,512,3584]{2,1,0:T(8,128)(2,1)S(1)}, u32[]{:S(2)}) %copy-start.2) | copy-done | bytes 14680088
  84.2 1.7 %owned.1 = bf16[2,512,512]{2,1,0:T(8,128)(2,1)} custom-call(s32[4]{0:T(128)S(1)} %iota_xor_fusion.order, s32[2]{0:T(128)S(1)} %pad_add_fusion.here, s32[4,4]{1,0:T(4,128)S(1)} %copy-done.5, bf16[512,512]{1,0:T(8,128)(2,1)S(1)} %get-tuple-element.33.root_ref.r0, bf16[512,512]{1,0:T(8,128)(2,1)S(1)} %get-tuple-element.32.root_ref.r1, ...), custom_call_target="tpu_custom_call" | custom-call | bytes 2097152 | tf_op jit(solution)/shard_map/owned/pallas_call | solution.py:266
  85.9 5.2 %copy-done.3 = bf16[4,512,3584]{2,1,0:T(8,128)(2,1)S(1)} copy-done((bf16[4,512,3584]{2,1,0:T(8,128)(2,1)S(1)}, bf16[4,512,3584]{2,1,0:T(8,128)(2,1)}, u32[]{:S(2)}) %copy-start.3) | copy-done | bytes 14680088
  91.1 7.3 %scale.1 = (bf16[2048,3584]{1,0:T(8,128)(2,1)}, bf16[4,512,3584]{2,1,0:T(8,128)(2,1)S(1)}) custom-call(s32[4]{0:T(128)S(1)} %iota_xor_fusion.order, f32[8,128]{1,0:T(8,128)S(1)} %add.36.sums, bf16[4,512,3584]{2,1,0:T(8,128)(2,1)S(1)} %copy-done.3), custom_call_target="tpu_custom_call", output_to_operand_aliasing={{1}: (2, {})} | custom-call | tf_op jit(solution)/shard_map/scale/pallas_call | solution.py:311
  (26 shorter events, 1.6 us)
Async XLA Ops:
  0.7 1.6 %copy-start.4 = (bf16[512,2048]{1,0:T(8,128)(2,1)S(1)}, bf16[512,2048]{1,0:T(8,128)(2,1)}, u32[]{:S(2)}) copy-start(bf16[512,2048]{1,0:T(8,128)(2,1)} %x_ref.1) | copy-start | bytes 6291460
  3.8 9.5 %collective-permute-start = (bf16[528,256]{1,0:T(8,128)(2,1)S(1)}, bf16[528,256]{1,0:T(8,128)(2,1)S(1)}, u32[]{:S(2)}, u32[]{:S(2)}) collective-permute-start(bf16[528,256]{1,0:T(8,128)(2,1)S(1)} %get-tuple-element.20), channel_id=1, source_target_pairs={{0,1},{1,0},{2,3},{3,2},{4,5},{5,4},{6,7},{7,6},{8,9},{9,8},{10,11... | collective-permute-start | bytes 811016 | tf_op jit(solution)/shard_map/ppermute | solution.py:329
  6.9 9.4 %collective-permute-start.1 = (bf16[528,256]{1,0:T(8,128)(2,1)S(1)}, bf16[528,256]{1,0:T(8,128)(2,1)S(1)}, u32[]{:S(2)}, u32[]{:S(2)}) collective-permute-start(bf16[528,256]{1,0:T(8,128)(2,1)S(1)} %get-tuple-element.21), channel_id=1, source_target_pairs={{0,2},{1,3},{2,0},{3,1},{4,6},{5,7},{6,4},{7,5},{8,10},{9,11},{10,... | collective-permute-start | bytes 811016 | tf_op jit(solution)/shard_map/ppermute | solution.py:329
  8.4 12.0 %collective-permute-start.2 = (bf16[528,256]{1,0:T(8,128)(2,1)S(1)}, bf16[528,256]{1,0:T(8,128)(2,1)S(1)}, u32[]{:S(2)}, u32[]{:S(2)}) collective-permute-start(bf16[528,256]{1,0:T(8,128)(2,1)S(1)} %get-tuple-element.22), channel_id=1, source_target_pairs={{0,3},{1,2},{2,1},{3,0},{4,7},{5,6},{6,5},{7,4},{8,11},{9,10},{10,... | collective-permute-start | bytes 811016 | tf_op jit(solution)/shard_map/ppermute | solution.py:329
  20.6 19.1 %collective-permute-start.3 = (bf16[528,256]{1,0:T(8,128)(2,1)S(1)}, bf16[528,256]{1,0:T(8,128)(2,1)S(1)}, u32[]{:S(2)}, u32[]{:S(2)}) collective-permute-start(bf16[528,256]{1,0:T(8,128)(2,1)S(1)} %add_convert_fusion.after.mine), channel_id=1, source_target_pairs={{0,4},{1,5},{2,6},{3,7},{4,0},{5,1},{6,2},{7,3},{8,12},{9,13},{10,... | collective-permute-start | bytes 811016 | tf_op jit(solution)/shard_map/ppermute | solution.py:329
  34.2 5.5 %copy-start = (bf16[4,512,3584]{2,1,0:T(8,128)(2,1)}, bf16[4,512,3584]{2,1,0:T(8,128)(2,1)S(1)}, u32[]{:S(2)}) copy-start(bf16[4,512,3584]{2,1,0:T(8,128)(2,1)S(1)} %get-tuple-element.34.g_ref) | copy-start | bytes 44040196
  42.8 8.7 %collective-permute-start.6 = (bf16[528,256]{1,0:T(8,128)(2,1)S(1)}, bf16[528,256]{1,0:T(8,128)(2,1)}, u32[]{:S(2)}, u32[]{:S(2)}) collective-permute-start(bf16[528,256]{1,0:T(8,128)(2,1)S(1)} %newton.1.folded), channel_id=1, source_target_pairs={{0,1},{1,0},{2,3},{3,2},{4,5},{5,4},{6,7},{7,6},{8,9},{9,8},{10,11... | collective-permute-start | bytes 811016 | tf_op jit(solution)/shard_map/ppermute | solution.py:329
  44.4 9.5 %collective-permute-start.5 = (bf16[528,256]{1,0:T(8,128)(2,1)S(1)}, bf16[528,256]{1,0:T(8,128)(2,1)}, u32[]{:S(2)}, u32[]{:S(2)}) collective-permute-start(bf16[528,256]{1,0:T(8,128)(2,1)S(1)} %newton.1.folded), channel_id=1, source_target_pairs={{0,2},{1,3},{2,0},{3,1},{4,6},{5,7},{6,4},{7,5},{8,10},{9,11},{10,... | collective-permute-start | bytes 811016 | tf_op jit(solution)/shard_map/ppermute | solution.py:329
  46.0 10.7 %collective-permute-start.4 = (bf16[528,256]{1,0:T(8,128)(2,1)S(1)}, bf16[528,256]{1,0:T(8,128)(2,1)}, u32[]{:S(2)}, u32[]{:S(2)}) collective-permute-start(bf16[528,256]{1,0:T(8,128)(2,1)S(1)} %newton.1.folded), channel_id=1, source_target_pairs={{0,3},{1,2},{2,1},{3,0},{4,7},{5,6},{6,5},{7,4},{8,11},{9,10},{10,... | collective-permute-start | bytes 811016 | tf_op jit(solution)/shard_map/ppermute | solution.py:329
  58.2 1.2 %collective-permute-start.7 = (f32[8,128]{1,0:T(8,128)S(1)}, f32[8,128]{1,0:T(8,128)S(1)}, u32[]{:S(2)}, u32[]{:S(2)}) collective-permute-start(f32[8,128]{1,0:T(8,128)S(1)} %get-tuple-element.29.after), channel_id=1, source_target_pairs={{0,8},{8,0},{16,24},{24,16},{1,9},{9,1},{17,25},{25,17},{2,10},{10... | collective-permute-start | bytes 12296 | tf_op jit(solution)/shard_map/ppermute | solution.py:329
  59.4 8.9 %collective-permute-start.8 = (f32[8,128]{1,0:T(8,128)S(1)}, f32[8,128]{1,0:T(8,128)S(1)}, u32[]{:S(2)}, u32[]{:S(2)}) collective-permute-start(f32[8,128]{1,0:T(8,128)S(1)} %add.32), channel_id=1, source_target_pairs={{0,16},{8,24},{16,0},{24,8},{1,17},{9,25},{17,1},{25,9},{2,18},{10... | collective-permute-start | bytes 12296 | tf_op jit(solution)/shard_map/ppermute | solution.py:329
  60.9 5.2 %copy-start.1 = (bf16[4,512,3584]{2,1,0:T(8,128)(2,1)S(1)}, bf16[4,512,3584]{2,1,0:T(8,128)(2,1)}, u32[]{:S(2)}) copy-start(bf16[4,512,3584]{2,1,0:T(8,128)(2,1)} %copy-done) | copy-start | bytes 44040196
  68.4 3.8 %collective-permute-start.9 = (f32[8,128]{1,0:T(8,128)S(1)}, f32[8,128]{1,0:T(8,128)S(1)}, u32[]{:S(2)}, u32[]{:S(2)}) collective-permute-start(f32[8,128]{1,0:T(8,128)S(1)} %add.33), channel_id=1, source_target_pairs={{0,1},{1,0},{2,3},{3,2},{4,5},{5,4},{6,7},{7,6},{8,9},{9,8},{10,11... | collective-permute-start | bytes 12296 | tf_op jit(solution)/shard_map/ppermute | solution.py:329
  72.2 3.9 %collective-permute-start.10 = (f32[8,128]{1,0:T(8,128)S(1)}, f32[8,128]{1,0:T(8,128)S(1)}, u32[]{:S(2)}, u32[]{:S(2)}) collective-permute-start(f32[8,128]{1,0:T(8,128)S(1)} %add.34), channel_id=1, source_target_pairs={{0,2},{1,3},{2,0},{3,1},{4,6},{5,7},{6,4},{7,5},{8,10},{9,11},{10,... | collective-permute-start | bytes 12296 | tf_op jit(solution)/shard_map/ppermute | solution.py:329
  76.1 9.8 %collective-permute-start.11 = (f32[8,128]{1,0:T(8,128)S(1)}, f32[8,128]{1,0:T(8,128)S(1)}, u32[]{:S(2)}, u32[]{:S(2)}) collective-permute-start(f32[8,128]{1,0:T(8,128)S(1)} %add.35), channel_id=1, source_target_pairs={{0,4},{1,5},{2,6},{3,7},{4,0},{5,1},{6,2},{7,3},{8,12},{9,13},{10,... | collective-permute-start | bytes 12296 | tf_op jit(solution)/shard_map/ppermute | solution.py:329
  76.5 7.7 %copy-start.5 = (s32[4,4]{1,0:T(4,128)S(1)}, s32[4,4]{1,0:T(4,128)}, u32[]{:S(2)}) copy-start(s32[4,4]{1,0:T(4,128)} %owner_slot.1) | copy-start | bytes 196
  78.7 5.5 %copy-start.2 = (bf16[4,512,3584]{2,1,0:T(8,128)(2,1)}, bf16[4,512,3584]{2,1,0:T(8,128)(2,1)S(1)}, u32[]{:S(2)}) copy-start(bf16[4,512,3584]{2,1,0:T(8,128)(2,1)S(1)} %multiply.7.u_ref) | copy-start | bytes 44040196
  85.9 5.2 %copy-start.3 = (bf16[4,512,3584]{2,1,0:T(8,128)(2,1)S(1)}, bf16[4,512,3584]{2,1,0:T(8,128)(2,1)}, u32[]{:S(2)}) copy-start(bf16[4,512,3584]{2,1,0:T(8,128)(2,1)} %copy-done.2) | copy-start | bytes 44040196

commit v4 on v3

--- a/solution.py
+++ b/solution.py
@@ -84,26 +84,28 @@
     yield pl.ds(start, width - start)
 
 
-def gram_kernel(order, after, g_ref, held_ref, top_ref, last_ref, norm_ref, arrived):
+def gram_kernel(order, after, g_ref, top_ref, last_ref, norm_ref, held, arrived):
     parts = list(chunks(g_ref.shape[1], 1792))
+
+    slots = held.shape[0]
 
     def copy(place, index):
         rows = pl.ds(pl.multiple_of(order[place] * BLK, BLK), BLK)
         return pltpu.make_async_copy(
             g_ref.at[rows, parts[index]],
-            held_ref.at[place, :, parts[index]],
+            held.at[place % slots, :, parts[index]],
             arrived.at[place, index],
         )
 
-    for place in range(QUAD):
+    for place in range(slots):
         for index in range(len(parts)):
             copy(place, index).start()
 
-    def block(place, _):
+    for place in range(QUAD):
         for index, part in enumerate(parts):
             copy(place, index).wait()
-            upper = held_ref[place, :HALF, part]
-            lower = held_ref[place, HALF:, part]
+            upper = held[place % slots, :HALF, part]
+            lower = held[place % slots, HALF:, part]
             across = ((1,), (1,))
             terms = dot(upper, upper, across), dot(upper, lower, across), dot(lower, lower, across)
             if index == 0:
@@ -114,12 +116,11 @@
                 top_ref[place, :, :HALF] += terms[0]
                 top_ref[place, :, HALF:] += terms[1]
                 last_ref[place] += terms[2]
+            if place + slots < QUAD:
+                copy(place + slots, index).start()
         row, col = places()
         squares = jnp.where(row == col, top_ref[place, :, :HALF] + last_ref[place], 0.0)
         norm_ref[place] = jnp.sum(squares, axis=0, keepdims=True)
-        return _
-
-    lax.fori_loop(0, QUAD, block, 0)
 
 
 def gram(order, gradient, after):
@@ -128,20 +129,22 @@
     return pl.pallas_call(
         gram_kernel,
         out_shape=[
-            pltpu.VMEM((QUAD, BLK, columns), BF16),
-            pltpu.VMEM((QUAD, HALF, BLK), F32),
-            pltpu.VMEM((QUAD, HALF, HALF), F32),
-            pltpu.VMEM((QUAD, 1, HALF), F32),
+            jax.ShapeDtypeStruct((QUAD, HALF, BLK), F32),
+            jax.ShapeDtypeStruct((QUAD, HALF, HALF), F32),
+            jax.ShapeDtypeStruct((QUAD, 1, HALF), F32),
         ],
         in_specs=[SMEM, ANY, ANY],
-        out_specs=[VMEM] * 4,
-        scratch_shapes=[pltpu.SemaphoreType.DMA((QUAD, parts))],
+        out_specs=[VMEM] * 3,
+        scratch_shapes=[
+            pltpu.VMEM((2, BLK, columns), BF16),
+            pltpu.SemaphoreType.DMA((QUAD, parts)),
+        ],
         compiler_params=params(16),
         cost_estimate=pl.CostEstimate(
             flops=2 * rows * columns * BLK, bytes_accessed=4 * rows * columns, transcendentals=0
         ),
         name="gram",
-    )(order, after, pltpu.with_memory_space_constraint(gradient, pltpu.HBM))
+    )(order, after, gradient)
 
 
 def product(left, right):
@@ -223,33 +226,35 @@
         in_specs=[VMEM] * 5,
         out_specs=[VMEM] * 2,
         compiler_params=params(16),
-        cost_estimate=pl.CostEstimate(
-            flops=2 * BLK**3, bytes_accessed=8 * BLK * BLK, transcendentals=0
-        ),
         name="norm",
     )(folded, *grams, sums)
 
 
-def multiply_kernel(place, after, root_ref, g_ref, u_ref):
-    for part in chunks(g_ref.shape[2], BLK):
-        u_ref[place, :, part] = dot(root_ref[...], g_ref[place, :, part]).astype(BF16)
-
-
-def multiply(place, root, held, after):
+def multiply_kernel(place, order, after, root_ref, g_ref, u_ref, arrived):
+    parts = list(chunks(g_ref.shape[1], BLK))
+    rows = pl.ds(pl.multiple_of(order[place] * BLK, BLK), BLK)
+    copies = [
+        pltpu.make_async_copy(g_ref.at[rows, part], u_ref.at[:, part], arrived.at[index])
+        for index, part in enumerate(parts)
+    ]
+    for copy in copies:
+        copy.start()
+    for copy, part in zip(copies, parts):
+        copy.wait()
+        u_ref[:, part] = dot(root_ref[...], u_ref[:, part]).astype(BF16)
+
+
+def multiply(place, order, root, gradient, after):
+    columns = gradient.shape[1]
     return pl.pallas_call(
         functools.partial(multiply_kernel, place),
-        out_shape=pltpu.VMEM(held.shape, BF16),
-        in_specs=[ANY, VMEM, VMEM],
+        out_shape=pltpu.VMEM((BLK, columns), BF16),
+        in_specs=[SMEM, ANY, VMEM, ANY],
         out_specs=VMEM,
-        input_output_aliases={2: 0},
-        compiler_params=params(16),
-        cost_estimate=pl.CostEstimate(
-            flops=2 * BLK * BLK * held.shape[2],
-            bytes_accessed=4 * BLK * held.shape[2],
-            transcendentals=0,
-        ),
+        scratch_shapes=[pltpu.SemaphoreType.DMA((len(list(chunks(columns, BLK))),))],
+        compiler_params=params(16),
         name="multiply",
-    )(after, root, held)
+    )(order, after, root, gradient)
 
 
 def owned_kernel(order, here, owner_slot, r0, r1, r2, r3, owned_ref):
@@ -273,55 +278,47 @@
             out_specs=pl.BlockSpec((SLOTS, BLK, BLK), lambda i, *_: (0, 0, 0)),
         ),
         compiler_params=params(16),
-        cost_estimate=pl.CostEstimate(
-            flops=0, bytes_accessed=4 * SLOTS * BLK * BLK, transcendentals=0
-        ),
         name="owned",
     )(order, here, owner_slot, *roots)
 
 
-def scale_kernel(order, sums, u_ref, update_ref, scaled, sent):
+def scale_kernel(order, sums, u0, u1, u2, u3, update_ref, s0, s1, s2, s3, sent):
     both = jnp.sum(sums[...], axis=1, keepdims=True)
     ratio = jnp.sqrt(both[:1] / (both[1:2] + 1e-06))
-    parts = list(chunks(u_ref.shape[2], 1792))
+    parts = list(chunks(u0.shape[1], 1792))
+    scaled = (s0, s1, s2, s3)
 
     def copy(place, index):
         rows = pl.ds(pl.multiple_of(order[place] * BLK, BLK), BLK)
         return pltpu.make_async_copy(
-            scaled.at[place, :, parts[index]],
+            scaled[place].at[:, parts[index]],
             update_ref.at[rows, parts[index]],
             sent.at[place, index],
         )
 
-    def block(place, _):
+    for place, unscaled in enumerate((u0, u1, u2, u3)):
         for index, part in enumerate(parts):
-            scaled[place, :, part] = (u_ref[place, :, part].astype(F32) * ratio).astype(BF16)
+            scaled[place][:, part] = (unscaled[:, part].astype(F32) * ratio).astype(BF16)
             copy(place, index).start()
-        return _
-
-    lax.fori_loop(0, QUAD, block, 0)
     for place in range(QUAD):
         for index in range(len(parts)):
             copy(place, index).wait()
 
 
 def scale(order, sums, unscaled):
-    columns = unscaled.shape[2]
+    columns = unscaled[0].shape[1]
     parts = len(list(chunks(columns, 1792)))
-    update, _ = pl.pallas_call(
+    return pl.pallas_call(
         scale_kernel,
-        out_shape=[
-            jax.ShapeDtypeStruct((QUAD * BLK, columns), BF16),
-            pltpu.VMEM(unscaled.shape, BF16),
-        ],
-        in_specs=[SMEM, VMEM, VMEM],
-        out_specs=[ANY, VMEM],
-        input_output_aliases={2: 1},
+        out_shape=[jax.ShapeDtypeStruct((QUAD * BLK, columns), BF16)]
+        + [pltpu.VMEM((BLK, columns), BF16)] * QUAD,
+        in_specs=[SMEM] + [VMEM] * (1 + QUAD),
+        out_specs=[ANY] + [VMEM] * QUAD,
+        input_output_aliases={2 + place: 1 + place for place in range(QUAD)},
         scratch_shapes=[pltpu.SemaphoreType.DMA((QUAD, parts))],
         compiler_params=params(16),
         name="scale",
-    )(order, sums, unscaled)
-    return update
+    )(order, sums, *unscaled)[0]
 
 
 def swap(value, flip, axis="dp"):
@@ -359,15 +356,15 @@
         flip *= 2
         other = swap(mine, flip)
 
-    held, *grams = gram(order, gradient, mine)
+    gradient = pltpu.with_memory_space_constraint(gradient, pltpu.HBM)
+    grams = gram(order, gradient, mine)
     a = newton(tokens_all, grams[-1], mine, other)
     sums = jnp.zeros((ROWS, LANES), F32)
     roots = []
     for place, folded in enumerate((a, swap(a, 1), swap(a, 2), swap(a, 3))):
         root, sums = norm(place, folded, grams, sums)
         roots.append(root)
-    for place, root in enumerate(roots):
-        held = multiply(place, root, held, sums)
+    held = [multiply(place, order, root, gradient, sums) for place, root in enumerate(roots)]
     owned = owned_roots(order, here, owner_slot, roots)
     update = scale(order, total(sums, "pool", "dp"), held)
     return (update, owned[None])

time: 98.7 us -> 96.5 us (0.978)
  local copies, waits for them, and re-layouts: 22.9 us -> 1.59 us
  waiting for transfers between devices: 19.9 us -> 30.1 us
  Pallas kernels: 38.4 us -> 45.7 us
  starting transfers between devices: 16.1 us -> 17.9 us
    unnamed x12 -> x4, local copies, waits for them, and re-layouts: 22.9 us -> 1.59 us
    ppermute x12, waiting for transfers between devices: 19.9 us -> 30.1 us  [swap(): return lax.ppermute(value, axis, [(i, i ^ flip) for i in range(count)])]
    pallas_call x4, Pallas kernels: 8.91 us -> 19.1 us  [multiply(): pl.pallas_call(functools.partial(multiply_kernel, place), out_shape=pltpu...]
    pallas_call x4, Pallas kernels: 4.9 us -> 2.08 us  [norm(): pl.pallas_call(functools.partial(norm_kernel, place), out_shape=[jax.Shap...]
    ppermute x12, starting transfers between devices: 16.1 us -> 17.9 us  [swap(): return lax.ppermute(value, axis, [(i, i ^ flip) for i in range(count)])]
  transfers between devices with their start and end apart: 12 -> 12, of which waited for: 7 -> 11; matrix products, arithmetic and copies ran while one was open for 0% -> 0% of each run, Pallas kernels for 25% -> 34%
where the time goes in v4:
time: 96.5 us; the launch traced here: 96.4 us
  Pallas kernels  45.7 us (47%)
  waiting for transfers between devices  30.1 us (31%)
  starting transfers between devices  17.9 us (19%)
  local copies, waits for them, and re-layouts  1.59 us (2%)
    ppermute x12, waiting for transfers between devices, swap(): return lax.ppermute(value, axis, [(i, i ^ flip) for i in range(count)])  30.1 us
    pallas_call x4, Pallas kernels, multiply(): pl.pallas_call(functools.partial(multiply_kernel, place), out_shape=pltpu...  19.1 us
    ppermute x12, starting transfers between devices, swap(): return lax.ppermute(value, axis, [(i, i ^ flip) for i in range(count)])  17.9 us
    pallas_call x1, Pallas kernels, gram(): pl.pallas_call(gram_kernel, out_shape=[jax.ShapeDtypeStruct((QUAD, HALF,...  10.8 us
    pallas_call x1, Pallas kernels, scale(): pl.pallas_call(scale_kernel, out_shape=[jax.ShapeDtypeStruct((QUAD * BLK,...  7.22 us
    pallas_call x1, Pallas kernels, newton(): pl.pallas_call(functools.partial(newton_kernel, tokens), out_shape=jax.Sh...  3.2 us
    pallas_call x4, Pallas kernels, norm(): pl.pallas_call(functools.partial(norm_kernel, place), out_shape=[jax.Shap...  2.08 us
  transfers between devices with their start and end apart: 12, of which 11 were waited for; matrix products, arithmetic and copies ran while one was open for 0% of the time, Pallas kernels for 34%

profile of v4, /device:TPU:0, one launch (start us, length us, event | category | flops | bytes accessed | tf_op | source)
XLA Modules:
  0.0 96.4 jit_solution(10931448321488926318)
XLA Ops:
  0.7 1.6 %copy-done = bf16[512,2048]{1,0:T(8,128)(2,1)S(1)} copy-done((bf16[512,2048]{1,0:T(8,128)(2,1)S(1)}, bf16[512,2048]{1,0:T(8,128)(2,1)}, u32[]{:S(2)}) %copy-start) | copy-done | bytes 2097176
  2.2 1.6 %statistics.1 = (bf16[528,256]{1,0:T(8,128)(2,1)S(1)}, bf16[528,256]{1,0:T(8,128)(2,1)S(1)}, bf16[528,256]{1,0:T(8,128)(2,1)S(1)}, bf16[528,256]{1,0:T(8,128)(2,1)S(1)}) custom-call(s32[4]{0:T(128)S(1)} %iota_xor_fusion.order, bf16[512,2048]{1,0:T(8,128)(2,1)S(1)} %copy-done), custom_call_target="tpu_custom_call" | custom-call | tf_op jit(solution)/shard_map/statistics/pallas_call | solution.py:69
  3.8 3.0 %collective-permute-start = (bf16[528,256]{1,0:T(8,128)(2,1)S(1)}, bf16[528,256]{1,0:T(8,128)(2,1)S(1)}, u32[]{:S(2)}, u32[]{:S(2)}) collective-permute-start(bf16[528,256]{1,0:T(8,128)(2,1)S(1)} %get-tuple-element.19), channel_id=1, source_target_pairs={{0,1},{1,0},{2,3},{3,2},{4,5},{5,4},{6,7},{7,6},{8,9},{9,8},{10,11... | collective-permute-start | bytes 811016 | tf_op jit(solution)/shard_map/ppermute | solution.py:326
  6.9 1.6 %collective-permute-start.1 = (bf16[528,256]{1,0:T(8,128)(2,1)S(1)}, bf16[528,256]{1,0:T(8,128)(2,1)S(1)}, u32[]{:S(2)}, u32[]{:S(2)}) collective-permute-start(bf16[528,256]{1,0:T(8,128)(2,1)S(1)} %get-tuple-element.20), channel_id=1, source_target_pairs={{0,2},{1,3},{2,0},{3,1},{4,6},{5,7},{6,4},{7,5},{8,10},{9,11},{10,... | collective-permute-start | bytes 811016 | tf_op jit(solution)/shard_map/ppermute | solution.py:326
  8.5 4.9 %collective-permute-done = bf16[528,256]{1,0:T(8,128)(2,1)S(1)} collective-permute-done((bf16[528,256]{1,0:T(8,128)(2,1)S(1)}, bf16[528,256]{1,0:T(8,128)(2,1)S(1)}, u32[]{:S(2)}, u32[]{:S(2)}) %collective-permute-start) | collective-permute-done | bytes 270368 | tf_op jit(solution)/shard_map/ppermute | solution.py:326
  13.4 2.9 %collective-permute-done.1 = bf16[528,256]{1,0:T(8,128)(2,1)S(1)} collective-permute-done((bf16[528,256]{1,0:T(8,128)(2,1)S(1)}, bf16[528,256]{1,0:T(8,128)(2,1)S(1)}, u32[]{:S(2)}, u32[]{:S(2)}) %collective-permute-start.1) | collective-permute-done | bytes 270368 | tf_op jit(solution)/shard_map/ppermute | solution.py:326
  16.3 4.1 %collective-permute-done.2 = bf16[528,256]{1,0:T(8,128)(2,1)S(1)} collective-permute-done((bf16[528,256]{1,0:T(8,128)(2,1)S(1)}, bf16[528,256]{1,0:T(8,128)(2,1)S(1)}, u32[]{:S(2)}, u32[]{:S(2)}) %collective-permute-start.2) | collective-permute-done | bytes 270368 | tf_op jit(solution)/shard_map/ppermute | solution.py:326
  20.6 2.8 %collective-permute-start.3 = (bf16[528,256]{1,0:T(8,128)(2,1)S(1)}, bf16[528,256]{1,0:T(8,128)(2,1)S(1)}, u32[]{:S(2)}, u32[]{:S(2)}) collective-permute-start(bf16[528,256]{1,0:T(8,128)(2,1)S(1)} %add_convert_fusion.after.mine), channel_id=1, source_target_pairs={{0,4},{1,5},{2,6},{3,7},{4,0},{5,1},{6,2},{7,3},{8,12},{9,13},{10,... | collective-permute-start | bytes 811016 | tf_op jit(solution)/shard_map/ppermute | solution.py:326
  23.4 10.8 %gram.1 = (f32[4,256,512]{2,1,0:T(8,128)S(1)}, f32[4,256,256]{2,1,0:T(8,128)S(1)}, f32[4,1,256]{2,1,0:T(1,128)S(1)}) custom-call(s32[4]{0:T(128)S(1)} %iota_xor_fusion.order, bf16[528,256]{1,0:T(8,128)(2,1)S(1)} %add_convert_fusion.after.mine, bf16[2048,3584]{1,0:T(8,128)(2,1)} %g_ref.9), custom_call_target="tpu_custom_call" | custom-call | flops 7516192768 | bytes 29360128 | tf_op jit(solution)/shard_map/gram/pallas_call | solution.py:129
  34.1 0.5 collective-permute-done.3.other
  34.7 3.2 %newton.1.folded = bf16[528,256]{1,0:T(8,128)(2,1)S(1)} custom-call(f32[4,1,256]{2,1,0:T(1,128)S(1)} %get-tuple-element.22.after.square_ref, bf16[528,256]{1,0:T(8,128)(2,1)S(1)} %add_convert_fusion.after.mine, bf16[528,256]{1,0:T(8,128)(2,1)S(1)} %collective-permute-done.3.other), custom_call_target="tpu_custom_call" | custom-call | flops 2147483648 | bytes 2097152 | tf_op jit(solution)/shard_map/newton/pallas_call | solution.py:188
  37.9 1.4 %collective-permute-start.6 = (bf16[528,256]{1,0:T(8,128)(2,1)S(1)}, bf16[528,256]{1,0:T(8,128)(2,1)S(1)}, u32[]{:S(2)}, u32[]{:S(2)}) collective-permute-start(bf16[528,256]{1,0:T(8,128)(2,1)S(1)} %newton.1.folded), channel_id=1, source_target_pairs={{0,1},{1,0},{2,3},{3,2},{4,5},{5,4},{6,7},{7,6},{8,9},{9,8},{10,11... | collective-permute-start | bytes 811016 | tf_op jit(solution)/shard_map/ppermute | solution.py:326
  39.3 1.2 %collective-permute-start.5 = (bf16[528,256]{1,0:T(8,128)(2,1)S(1)}, bf16[528,256]{1,0:T(8,128)(2,1)S(1)}, u32[]{:S(2)}, u32[]{:S(2)}) collective-permute-start(bf16[528,256]{1,0:T(8,128)(2,1)S(1)} %newton.1.folded), channel_id=1, source_target_pairs={{0,2},{1,3},{2,0},{3,1},{4,6},{5,7},{6,4},{7,5},{8,10},{9,11},{10,... | collective-permute-start | bytes 811016 | tf_op jit(solution)/shard_map/ppermute | solution.py:326
  40.5 0.9 collective-permute-start.4
  42.0 4.5 %collective-permute-done.6.folded = bf16[528,256]{1,0:T(8,128)(2,1)S(1)} collective-permute-done((bf16[528,256]{1,0:T(8,128)(2,1)S(1)}, bf16[528,256]{1,0:T(8,128)(2,1)S(1)}, u32[]{:S(2)}, u32[]{:S(2)}) %collective-permute-start.6) | collective-permute-done | bytes 270368 | tf_op jit(solution)/shard_map/ppermute | solution.py:326
  47.0 1.7 %collective-permute-done.5.folded = bf16[528,256]{1,0:T(8,128)(2,1)S(1)} collective-permute-done((bf16[528,256]{1,0:T(8,128)(2,1)S(1)}, bf16[528,256]{1,0:T(8,128)(2,1)S(1)}, u32[]{:S(2)}, u32[]{:S(2)}) %collective-permute-start.5) | collective-permute-done | bytes 270368 | tf_op jit(solution)/shard_map/ppermute | solution.py:326
  48.7 0.5 norm.6
  49.2 3.2 %collective-permute-done.4.folded = bf16[528,256]{1,0:T(8,128)(2,1)S(1)} collective-permute-done((bf16[528,256]{1,0:T(8,128)(2,1)S(1)}, bf16[528,256]{1,0:T(8,128)(2,1)S(1)}, u32[]{:S(2)}, u32[]{:S(2)}) %collective-permute-start.4) | collective-permute-done | bytes 270368 | tf_op jit(solution)/shard_map/ppermute | solution.py:326
  53.0 1.2 %collective-permute-done.7 = f32[8,128]{1,0:T(8,128)S(1)} collective-permute-done((f32[8,128]{1,0:T(8,128)S(1)}, f32[8,128]{1,0:T(8,128)S(1)}, u32[]{:S(2)}, u32[]{:S(2)}) %collective-permute-start.7) | collective-permute-done | bytes 4128 | tf_op jit(solution)/shard_map/ppermute | solution.py:326
  54.2 1.2 %collective-permute-start.8 = (f32[8,128]{1,0:T(8,128)S(1)}, f32[8,128]{1,0:T(8,128)S(1)}, u32[]{:S(2)}, u32[]{:S(2)}) collective-permute-start(f32[8,128]{1,0:T(8,128)S(1)} %add.32), channel_id=1, source_target_pairs={{0,16},{8,24},{16,0},{24,8},{1,17},{9,25},{17,1},{25,9},{2,18},{10... | collective-permute-start | bytes 12296 | tf_op jit(solution)/shard_map/ppermute | solution.py:326
  55.3 2.5 %collective-permute-done.8 = f32[8,128]{1,0:T(8,128)S(1)} collective-permute-done((f32[8,128]{1,0:T(8,128)S(1)}, f32[8,128]{1,0:T(8,128)S(1)}, u32[]{:S(2)}, u32[]{:S(2)}) %collective-permute-start.8) | collective-permute-done | bytes 4128 | tf_op jit(solution)/shard_map/ppermute | solution.py:326
  57.8 1.2 %collective-permute-start.9 = (f32[8,128]{1,0:T(8,128)S(1)}, f32[8,128]{1,0:T(8,128)S(1)}, u32[]{:S(2)}, u32[]{:S(2)}) collective-permute-start(f32[8,128]{1,0:T(8,128)S(1)} %add.33), channel_id=1, source_target_pairs={{0,1},{1,0},{2,3},{3,2},{4,5},{5,4},{6,7},{7,6},{8,9},{9,8},{10,11... | collective-permute-start | bytes 12296 | tf_op jit(solution)/shard_map/ppermute | solution.py:326
  59.0 2.4 %collective-permute-done.9 = f32[8,128]{1,0:T(8,128)S(1)} collective-permute-done((f32[8,128]{1,0:T(8,128)S(1)}, f32[8,128]{1,0:T(8,128)S(1)}, u32[]{:S(2)}, u32[]{:S(2)}) %collective-permute-start.9) | collective-permute-done | bytes 4128 | tf_op jit(solution)/shard_map/ppermute | solution.py:326
  61.4 1.4 %collective-permute-start.10 = (f32[8,128]{1,0:T(8,128)S(1)}, f32[8,128]{1,0:T(8,128)S(1)}, u32[]{:S(2)}, u32[]{:S(2)}) collective-permute-start(f32[8,128]{1,0:T(8,128)S(1)} %add.34), channel_id=1, source_target_pairs={{0,2},{1,3},{2,0},{3,1},{4,6},{5,7},{6,4},{7,5},{8,10},{9,11},{10,... | collective-permute-start | bytes 12296 | tf_op jit(solution)/shard_map/ppermute | solution.py:326
  62.8 2.2 %collective-permute-done.10 = f32[8,128]{1,0:T(8,128)S(1)} collective-permute-done((f32[8,128]{1,0:T(8,128)S(1)}, f32[8,128]{1,0:T(8,128)S(1)}, u32[]{:S(2)}, u32[]{:S(2)}) %collective-permute-start.10) | collective-permute-done | bytes 4128 | tf_op jit(solution)/shard_map/ppermute | solution.py:326
  65.0 3.0 %collective-permute-start.11 = (f32[8,128]{1,0:T(8,128)S(1)}, f32[8,128]{1,0:T(8,128)S(1)}, u32[]{:S(2)}, u32[]{:S(2)}) collective-permute-start(f32[8,128]{1,0:T(8,128)S(1)} %add.35), channel_id=1, source_target_pairs={{0,4},{1,5},{2,6},{3,7},{4,0},{5,1},{6,2},{7,3},{8,12},{9,13},{10,... | collective-permute-start | bytes 12296 | tf_op jit(solution)/shard_map/ppermute | solution.py:326
  68.1 4.9 %multiply.7.u3 = bf16[512,3584]{1,0:T(8,128)(2,1)S(1)} custom-call(s32[4]{0:T(128)S(1)} %iota_xor_fusion.order, f32[8,128]{1,0:T(8,128)S(1)} %get-tuple-element.28.after, bf16[512,512]{1,0:T(8,128)(2,1)S(1)} %get-tuple-element.32.root_ref.r3, bf16[2048,3584]{1,0:T(8,128)(2,1)} %g_ref.9), custom_call_target="tpu_custom_call" | custom-call | tf_op jit(solution)/shard_map/multiply/pallas_call | solution.py:249
  73.0 4.7 %multiply.6.u2 = bf16[512,3584]{1,0:T(8,128)(2,1)S(1)} custom-call(s32[4]{0:T(128)S(1)} %iota_xor_fusion.order, f32[8,128]{1,0:T(8,128)S(1)} %get-tuple-element.28.after, bf16[512,512]{1,0:T(8,128)(2,1)S(1)} %get-tuple-element.31.root_ref.r2, bf16[2048,3584]{1,0:T(8,128)(2,1)} %g_ref.9), custom_call_target="tpu_custom_call" | custom-call | tf_op jit(solution)/shard_map/multiply/pallas_call | solution.py:249
  77.8 4.7 %multiply.5.u1 = bf16[512,3584]{1,0:T(8,128)(2,1)S(1)} custom-call(s32[4]{0:T(128)S(1)} %iota_xor_fusion.order, f32[8,128]{1,0:T(8,128)S(1)} %get-tuple-element.28.after, bf16[512,512]{1,0:T(8,128)(2,1)S(1)} %get-tuple-element.30.root_ref.r1, bf16[2048,3584]{1,0:T(8,128)(2,1)} %g_ref.9), custom_call_target="tpu_custom_call" | custom-call | tf_op jit(solution)/shard_map/multiply/pallas_call | solution.py:249
  82.5 4.7 %multiply.4.u0 = bf16[512,3584]{1,0:T(8,128)(2,1)S(1)} custom-call(s32[4]{0:T(128)S(1)} %iota_xor_fusion.order, f32[8,128]{1,0:T(8,128)S(1)} %get-tuple-element.28.after, bf16[512,512]{1,0:T(8,128)(2,1)S(1)} %get-tuple-element.29.root_ref.r0, bf16[2048,3584]{1,0:T(8,128)(2,1)} %g_ref.9), custom_call_target="tpu_custom_call" | custom-call | tf_op jit(solution)/shard_map/multiply/pallas_call | solution.py:249
  87.3 1.7 %owned.1 = bf16[2,512,512]{2,1,0:T(8,128)(2,1)} custom-call(s32[4]{0:T(128)S(1)} %iota_xor_fusion.order, s32[2]{0:T(128)S(1)} %pad_add_fusion.here, s32[4,4]{1,0:T(4,128)S(1)} %copy-done.1, bf16[512,512]{1,0:T(8,128)(2,1)S(1)} %get-tuple-element.29.root_ref.r0, bf16[512,512]{1,0:T(8,128)(2,1)S(1)} %get-tuple-element.30.root_ref.r1, ...), custom_call_target="tpu_custom_call" | custom-call | tf_op jit(solution)/shard_map/owned/pallas_call | solution.py:271
  89.0 7.2 %scale.1 = (bf16[2048,3584]{1,0:T(8,128)(2,1)}, bf16[512,3584]{1,0:T(8,128)(2,1)S(1)}, bf16[512,3584]{1,0:T(8,128)(2,1)S(1)}, bf16[512,3584]{1,0:T(8,128)(2,1)S(1)}, bf16[512,3584]{1,0:T(8,128)(2,1)S(1)}) custom-call(s32[4]{0:T(128)S(1)} %iota_xor_fusion.order, ...), custom_call_target="tpu_custom_call", output_to_operand_aliasing={{1}: (2, {}), {2}: (3, {}), {3}: (4, {}), {4}: (5, {})} | custom-call | tf_op jit(solution)/shard_map/scale/pallas_call | solution.py:311
  (18 shorter events, 1.9 us)
Async XLA Ops:
  0.7 1.6 %copy-start = (bf16[512,2048]{1,0:T(8,128)(2,1)S(1)}, bf16[512,2048]{1,0:T(8,128)(2,1)}, u32[]{:S(2)}) copy-start(bf16[512,2048]{1,0:T(8,128)(2,1)} %x_ref.1) | copy-start | bytes 6291460
  3.8 9.5 %collective-permute-start = (bf16[528,256]{1,0:T(8,128)(2,1)S(1)}, bf16[528,256]{1,0:T(8,128)(2,1)S(1)}, u32[]{:S(2)}, u32[]{:S(2)}) collective-permute-start(bf16[528,256]{1,0:T(8,128)(2,1)S(1)} %get-tuple-element.19), channel_id=1, source_target_pairs={{0,1},{1,0},{2,3},{3,2},{4,5},{5,4},{6,7},{7,6},{8,9},{9,8},{10,11... | collective-permute-start | bytes 811016 | tf_op jit(solution)/shard_map/ppermute | solution.py:326
  6.9 9.4 %collective-permute-start.1 = (bf16[528,256]{1,0:T(8,128)(2,1)S(1)}, bf16[528,256]{1,0:T(8,128)(2,1)S(1)}, u32[]{:S(2)}, u32[]{:S(2)}) collective-permute-start(bf16[528,256]{1,0:T(8,128)(2,1)S(1)} %get-tuple-element.20), channel_id=1, source_target_pairs={{0,2},{1,3},{2,0},{3,1},{4,6},{5,7},{6,4},{7,5},{8,10},{9,11},{10,... | collective-permute-start | bytes 811016 | tf_op jit(solution)/shard_map/ppermute | solution.py:326
  8.5 12.0 %collective-permute-start.2 = (bf16[528,256]{1,0:T(8,128)(2,1)S(1)}, bf16[528,256]{1,0:T(8,128)(2,1)S(1)}, u32[]{:S(2)}, u32[]{:S(2)}) collective-permute-start(bf16[528,256]{1,0:T(8,128)(2,1)S(1)} %get-tuple-element.21), channel_id=1, source_target_pairs={{0,3},{1,2},{2,1},{3,0},{4,7},{5,6},{6,5},{7,4},{8,11},{9,10},{10,... | collective-permute-start | bytes 811016 | tf_op jit(solution)/shard_map/ppermute | solution.py:326
  20.6 14.1 %collective-permute-start.3 = (bf16[528,256]{1,0:T(8,128)(2,1)S(1)}, bf16[528,256]{1,0:T(8,128)(2,1)S(1)}, u32[]{:S(2)}, u32[]{:S(2)}) collective-permute-start(bf16[528,256]{1,0:T(8,128)(2,1)S(1)} %add_convert_fusion.after.mine), channel_id=1, source_target_pairs={{0,4},{1,5},{2,6},{3,7},{4,0},{5,1},{6,2},{7,3},{8,12},{9,13},{10,... | collective-permute-start | bytes 811016 | tf_op jit(solution)/shard_map/ppermute | solution.py:326
  37.9 8.6 %collective-permute-start.6 = (bf16[528,256]{1,0:T(8,128)(2,1)S(1)}, bf16[528,256]{1,0:T(8,128)(2,1)S(1)}, u32[]{:S(2)}, u32[]{:S(2)}) collective-permute-start(bf16[528,256]{1,0:T(8,128)(2,1)S(1)} %newton.1.folded), channel_id=1, source_target_pairs={{0,1},{1,0},{2,3},{3,2},{4,5},{5,4},{6,7},{7,6},{8,9},{9,8},{10,11... | collective-permute-start | bytes 811016 | tf_op jit(solution)/shard_map/ppermute | solution.py:326
  39.3 9.4 %collective-permute-start.5 = (bf16[528,256]{1,0:T(8,128)(2,1)S(1)}, bf16[528,256]{1,0:T(8,128)(2,1)S(1)}, u32[]{:S(2)}, u32[]{:S(2)}) collective-permute-start(bf16[528,256]{1,0:T(8,128)(2,1)S(1)} %newton.1.folded), channel_id=1, source_target_pairs={{0,2},{1,3},{2,0},{3,1},{4,6},{5,7},{6,4},{7,5},{8,10},{9,11},{10,... | collective-permute-start | bytes 811016 | tf_op jit(solution)/shard_map/ppermute | solution.py:326
  40.5 11.9 %collective-permute-start.4 = (bf16[528,256]{1,0:T(8,128)(2,1)S(1)}, bf16[528,256]{1,0:T(8,128)(2,1)S(1)}, u32[]{:S(2)}, u32[]{:S(2)}) collective-permute-start(bf16[528,256]{1,0:T(8,128)(2,1)S(1)} %newton.1.folded), channel_id=1, source_target_pairs={{0,3},{1,2},{2,1},{3,0},{4,7},{5,6},{6,5},{7,4},{8,11},{9,10},{10,... | collective-permute-start | bytes 811016 | tf_op jit(solution)/shard_map/ppermute | solution.py:326
  52.9 1.2 %collective-permute-start.7 = (f32[8,128]{1,0:T(8,128)S(1)}, f32[8,128]{1,0:T(8,128)S(1)}, u32[]{:S(2)}, u32[]{:S(2)}) collective-permute-start(f32[8,128]{1,0:T(8,128)S(1)} %get-tuple-element.28.after), channel_id=1, source_target_pairs={{0,8},{8,0},{16,24},{24,16},{1,9},{9,1},{17,25},{25,17},{2,10},{10... | collective-permute-start | bytes 12296 | tf_op jit(solution)/shard_map/ppermute | solution.py:326
  54.2 3.6 %collective-permute-start.8 = (f32[8,128]{1,0:T(8,128)S(1)}, f32[8,128]{1,0:T(8,128)S(1)}, u32[]{:S(2)}, u32[]{:S(2)}) collective-permute-start(f32[8,128]{1,0:T(8,128)S(1)} %add.32), channel_id=1, source_target_pairs={{0,16},{8,24},{16,0},{24,8},{1,17},{9,25},{17,1},{25,9},{2,18},{10... | collective-permute-start | bytes 12296 | tf_op jit(solution)/shard_map/ppermute | solution.py:326
  57.8 3.6 %collective-permute-start.9 = (f32[8,128]{1,0:T(8,128)S(1)}, f32[8,128]{1,0:T(8,128)S(1)}, u32[]{:S(2)}, u32[]{:S(2)}) collective-permute-start(f32[8,128]{1,0:T(8,128)S(1)} %add.33), channel_id=1, source_target_pairs={{0,1},{1,0},{2,3},{3,2},{4,5},{5,4},{6,7},{7,6},{8,9},{9,8},{10,11... | collective-permute-start | bytes 12296 | tf_op jit(solution)/shard_map/ppermute | solution.py:326
  61.4 3.6 %collective-permute-start.10 = (f32[8,128]{1,0:T(8,128)S(1)}, f32[8,128]{1,0:T(8,128)S(1)}, u32[]{:S(2)}, u32[]{:S(2)}) collective-permute-start(f32[8,128]{1,0:T(8,128)S(1)} %add.34), channel_id=1, source_target_pairs={{0,2},{1,3},{2,0},{3,1},{4,6},{5,7},{6,4},{7,5},{8,10},{9,11},{10,... | collective-permute-start | bytes 12296 | tf_op jit(solution)/shard_map/ppermute | solution.py:326
  65.0 24.0 %collective-permute-start.11 = (f32[8,128]{1,0:T(8,128)S(1)}, f32[8,128]{1,0:T(8,128)S(1)}, u32[]{:S(2)}, u32[]{:S(2)}) collective-permute-start(f32[8,128]{1,0:T(8,128)S(1)} %add.35), channel_id=1, source_target_pairs={{0,4},{1,5},{2,6},{3,7},{4,0},{5,1},{6,2},{7,3},{8,12},{9,13},{10,... | collective-permute-start | bytes 12296 | tf_op jit(solution)/shard_map/ppermute | solution.py:326
  82.5 4.8 %copy-start.1 = (s32[4,4]{1,0:T(4,128)S(1)}, s32[4,4]{1,0:T(4,128)}, u32[]{:S(2)}) copy-start(s32[4,4]{1,0:T(4,128)} %owner_slot.1) | copy-start | bytes 196

commit v5 on v4

--- a/solution.py
+++ b/solution.py
@@ -1,4 +1,5 @@
 import functools
+import math
 
 import jax
 import jax.numpy as jnp
@@ -53,27 +54,26 @@
     return first, last
 
 
-def stat_kernel(order, x_ref, *out):
-    for place in (1, 2, 3, 0):
-        start = pl.multiple_of(order[place] * BLK, BLK)
-        left = x_ref[:, pl.ds(start, HALF)]
-        right = x_ref[:, pl.ds(pl.multiple_of(start + HALF, HALF), HALF)]
+def stat_kernel(x_ref, out):
+    for block in range(QUAD):
+        left = x_ref[:, block * BLK : block * BLK + HALF]
+        right = x_ref[:, block * BLK + HALF : (block + 1) * BLK]
         along = ((0,), (0,))
-        out[place][:HALF] = dot(left, right, along).astype(BF16)
+        out[block, :HALF] = dot(left, right, along).astype(BF16)
         body, diagonal = fold(dot(left, left, along), dot(right, right, along))
-        out[place][HALF:BLK] = body.astype(BF16)
-        out[place][BLK:] = diagonal.astype(BF16)
-
-
-def statistics(order, activations):
+        out[block, HALF:BLK] = body.astype(BF16)
+        out[block, BLK:] = diagonal.astype(BF16)
+
+
+def statistics(activations):
     return pl.pallas_call(
         stat_kernel,
-        out_shape=[jax.ShapeDtypeStruct((FOLD, HALF), BF16)] * QUAD,
-        in_specs=[SMEM, VMEM],
-        out_specs=[VMEM] * QUAD,
+        out_shape=jax.ShapeDtypeStruct((QUAD, FOLD, HALF), BF16),
+        in_specs=[VMEM],
+        out_specs=VMEM,
         compiler_params=params(16),
         name="statistics",
-    )(order, activations)
+    )(activations)
 
 
 def chunks(width, size):
@@ -230,95 +230,67 @@
     )(folded, *grams, sums)
 
 
-def multiply_kernel(place, order, after, root_ref, g_ref, u_ref, arrived):
-    parts = list(chunks(g_ref.shape[1], BLK))
-    rows = pl.ds(pl.multiple_of(order[place] * BLK, BLK), BLK)
-    copies = [
-        pltpu.make_async_copy(g_ref.at[rows, part], u_ref.at[:, part], arrived.at[index])
-        for index, part in enumerate(parts)
-    ]
-    for copy in copies:
-        copy.start()
-    for copy, part in zip(copies, parts):
-        copy.wait()
-        u_ref[:, part] = dot(root_ref[...], u_ref[:, part]).astype(BF16)
-
-
-def multiply(place, order, root, gradient, after):
-    columns = gradient.shape[1]
-    return pl.pallas_call(
-        functools.partial(multiply_kernel, place),
-        out_shape=pltpu.VMEM((BLK, columns), BF16),
-        in_specs=[SMEM, ANY, VMEM, ANY],
-        out_specs=VMEM,
-        scratch_shapes=[pltpu.SemaphoreType.DMA((len(list(chunks(columns, BLK))),))],
-        compiler_params=params(16),
-        name="multiply",
-    )(order, after, root, gradient)
-
-
-def owned_kernel(order, here, owner_slot, r0, r1, r2, r3, owned_ref):
-    owned_ref[...] = jnp.zeros_like(owned_ref)
-    for place, root in enumerate((r0, r1, r2, r3)):
+def finish_kernel(order, here, owner_slot, sums, *refs):
+    roots, g_ref = refs[:QUAD], refs[QUAD]
+    update_ref, owned_ref, held, owned, arrived, sent, stored = refs[QUAD + 1 :]
+    pieces = list(chunks(held.shape[2], 1792))
+
+    def copy(place, index, fetch):
+        rows = pl.ds(pl.multiple_of(order[place] * BLK, BLK), BLK)
+        here = held.at[place, :, pieces[index]]
+        if fetch:
+            return pltpu.make_async_copy(g_ref.at[rows, pieces[index]], here, arrived.at[place, index])
+        return pltpu.make_async_copy(here, update_ref.at[rows, pieces[index]], sent.at[place, index])
+
+    every = [(place, index) for place in range(QUAD) for index in range(len(pieces))]
+    for place, index in every:
+        copy(place, index, True).start()
+    whole = jnp.sum(sums[...], axis=0)
+    both = jnp.sum(whole, axis=1, keepdims=True)
+    ratio = jnp.sqrt(both[:1] / (both[1:2] + 1e-06))
+    owned[...] = jnp.zeros_like(owned)
+    for place, root in enumerate(roots):
         for slot in range(SLOTS):
 
             @pl.when(owner_slot[here[0], order[place]] == here[1] + slot)
             def _():
-                owned_ref[slot] = root[...]
-
-
-def owned_roots(order, here, owner_slot, roots):
-    return pl.pallas_call(
-        owned_kernel,
-        out_shape=jax.ShapeDtypeStruct((SLOTS, BLK, BLK), BF16),
-        grid_spec=pltpu.PrefetchScalarGridSpec(
-            num_scalar_prefetch=3,
-            grid=(1,),
-            in_specs=[pl.BlockSpec((BLK, BLK), lambda i, *_: (0, 0))] * QUAD,
-            out_specs=pl.BlockSpec((SLOTS, BLK, BLK), lambda i, *_: (0, 0, 0)),
-        ),
-        compiler_params=params(16),
-        name="owned",
-    )(order, here, owner_slot, *roots)
-
-
-def scale_kernel(order, sums, u0, u1, u2, u3, update_ref, s0, s1, s2, s3, sent):
-    both = jnp.sum(sums[...], axis=1, keepdims=True)
-    ratio = jnp.sqrt(both[:1] / (both[1:2] + 1e-06))
-    parts = list(chunks(u0.shape[1], 1792))
-    scaled = (s0, s1, s2, s3)
-
-    def copy(place, index):
-        rows = pl.ds(pl.multiple_of(order[place] * BLK, BLK), BLK)
-        return pltpu.make_async_copy(
-            scaled[place].at[:, parts[index]],
-            update_ref.at[rows, parts[index]],
-            sent.at[place, index],
-        )
-
-    for place, unscaled in enumerate((u0, u1, u2, u3)):
-        for index, part in enumerate(parts):
-            scaled[place][:, part] = (unscaled[:, part].astype(F32) * ratio).astype(BF16)
-            copy(place, index).start()
-    for place in range(QUAD):
-        for index in range(len(parts)):
-            copy(place, index).wait()
-
-
-def scale(order, sums, unscaled):
-    columns = unscaled[0].shape[1]
-    parts = len(list(chunks(columns, 1792)))
-    return pl.pallas_call(
-        scale_kernel,
-        out_shape=[jax.ShapeDtypeStruct((QUAD * BLK, columns), BF16)]
-        + [pltpu.VMEM((BLK, columns), BF16)] * QUAD,
-        in_specs=[SMEM] + [VMEM] * (1 + QUAD),
-        out_specs=[ANY] + [VMEM] * QUAD,
-        input_output_aliases={2 + place: 1 + place for place in range(QUAD)},
-        scratch_shapes=[pltpu.SemaphoreType.DMA((QUAD, parts))],
-        compiler_params=params(16),
-        name="scale",
-    )(order, sums, *unscaled)[0]
+                owned[slot] = root[...]
+
+    store = pltpu.make_async_copy(owned, owned_ref, stored)
+    store.start()
+    for place, index in every:
+        copy(place, index, True).wait()
+        for part in chunks(pieces[index].size, BLK):
+            part = pl.ds(pieces[index].start + part.start, part.size)
+            product = dot(roots[place][...], held[place, :, part])
+            held[place, :, part] = (product * ratio).astype(BF16)
+        copy(place, index, False).start()
+    for place, index in every:
+        copy(place, index, False).wait()
+    store.wait()
+
+
+def finish(order, here, owner_slot, sums, roots, gradient):
+    rows, columns = gradient.shape
+    pieces = len(list(chunks(columns, 1792)))
+    return pl.pallas_call(
+        finish_kernel,
+        out_shape=[
+            jax.ShapeDtypeStruct((rows, columns), BF16),
+            jax.ShapeDtypeStruct((SLOTS, BLK, BLK), BF16),
+        ],
+        in_specs=[SMEM] * 3 + [VMEM] * (1 + QUAD) + [ANY],
+        out_specs=[ANY] * 2,
+        scratch_shapes=[
+            pltpu.VMEM((QUAD, BLK, columns), BF16),
+            pltpu.VMEM((SLOTS, BLK, BLK), BF16),
+            pltpu.SemaphoreType.DMA((QUAD, pieces)),
+            pltpu.SemaphoreType.DMA((QUAD, pieces)),
+            pltpu.SemaphoreType.DMA,
+        ],
+        compiler_params=params(32),
+        name="finish",
+    )(order, here, owner_slot, sums, *roots, gradient)
 
 
 def swap(value, flip, axis="dp"):
@@ -326,13 +298,10 @@
     return lax.ppermute(value, axis, [(i, i ^ flip) for i in range(count)])
 
 
-def total(value, *axes):
-    for axis in axes:
-        flip = 1
-        while flip < lax.axis_size(axis):
-            value = value + swap(value, flip, axis)
-            flip *= 2
-    return value
+def everywhere(value, axes):
+    count = math.prod(lax.axis_size(axis) for axis in axes)
+    copies = jnp.broadcast_to(value[None], (count, *value.shape))
+    return lax.all_to_all(copies, axes, 0, 0, tiled=True)
 
 
 def add(*values):
@@ -347,8 +316,9 @@
     order = (my_index % QUAD) ^ jnp.arange(QUAD, dtype=jnp.int32)
     here = jnp.stack([group_index, my_index * SLOTS])
 
-    a, b, c, d = statistics(order, activations)
-    mine = add(a, swap(b, 1), swap(c, 2), swap(d, 3))
+    groups = [list(range(i, i + QUAD)) for i in range(0, peer_count, QUAD)]
+    parts = lax.all_to_all(statistics(activations), "dp", 0, 0, axis_index_groups=groups, tiled=True)
+    mine = add(*parts)
     flip = QUAD
     other = swap(mine, flip)
     while 2 * flip < peer_count:
@@ -358,15 +328,15 @@
 
     gradient = pltpu.with_memory_space_constraint(gradient, pltpu.HBM)
     grams = gram(order, gradient, mine)
-    a = newton(tokens_all, grams[-1], mine, other)
+    root = newton(tokens_all, grams[-1], mine, other)
+    folded = (root, swap(root, 1), swap(root, 2), swap(root, 3))
     sums = jnp.zeros((ROWS, LANES), F32)
     roots = []
-    for place, folded in enumerate((a, swap(a, 1), swap(a, 2), swap(a, 3))):
-        root, sums = norm(place, folded, grams, sums)
+    for place in range(QUAD):
+        root, sums = norm(place, folded[place], grams, sums)
         roots.append(root)
-    held = [multiply(place, order, root, gradient, sums) for place, root in enumerate(roots)]
-    owned = owned_roots(order, here, owner_slot, roots)
-    update = scale(order, total(sums, "pool", "dp"), held)
+    sums = everywhere(sums, ("pool", "dp"))
+    update, owned = finish(order, here, owner_slot, sums, roots, gradient)
     return (update, owned[None])
 
 

time: 96.5 us -> 85 us (0.88)
  Pallas kernels: 45.7 us -> 31.9 us
  waiting for transfers between devices: 30.1 us -> 31.6 us
    all_to_all x0 -> x2, waiting for transfers between devices: none -> 21.6 us  [the longest x1 14 us: per_device(): lax.all_to_all(statistics(activations), 'dp', 0, 0, axis_index_groups=gro...]
    ppermute x12 -> x4, waiting for transfers between devices: 30.1 us -> 9.95 us  [swap(): return lax.ppermute(value, axis, [(i, i ^ flip) for i in range(count)])]
    pallas_call x7 -> x2, Pallas kernels: 29.6 us -> 15.9 us  [the longest x1 13.8 us: finish(): pl.pallas_call(finish_kernel, out_shape=[jax.ShapeDtypeStruct((rows, colu...]
    all_to_all x0 -> x2, starting transfers between devices: none -> 11.7 us  [the longest x1 6.4 us: everywhere(): return lax.all_to_all(copies, axes, 0, 0, tiled=True)]
    ppermute x12 -> x4, starting transfers between devices: 17.9 us -> 6.21 us  [swap(): return lax.ppermute(value, axis, [(i, i ^ flip) for i in range(count)])]
  transfers between devices with their start and end apart: 12 -> 6, of which waited for: 11 -> 6; matrix products, arithmetic and copies ran while one was open for 0% -> 0% of each run, Pallas kernels for 34% -> 15%
where the time goes in v5:
time: 85 us; the launch traced here: 84.7 us
  Pallas kernels  31.9 us (38%)
  waiting for transfers between devices  31.6 us (37%)
  starting transfers between devices  17.9 us (21%)
  local copies, waits for them, and re-layouts  2.26 us (3%)
  between operations  0.87 us (1%)
    all_to_all x1, waiting for transfers between devices, per_device(): lax.all_to_all(statistics(activations), 'dp', 0, 0, axis_index_groups=gro...  14 us
    pallas_call x1, Pallas kernels, finish(): pl.pallas_call(finish_kernel, out_shape=[jax.ShapeDtypeStruct((rows, colu...  13.8 us
    pallas_call x1, Pallas kernels, gram(): pl.pallas_call(gram_kernel, out_shape=[jax.ShapeDtypeStruct((QUAD, HALF,...  10.8 us
    ppermute x4, waiting for transfers between devices, swap(): return lax.ppermute(value, axis, [(i, i ^ flip) for i in range(count)])  9.95 us
    all_to_all x1, waiting for transfers between devices, everywhere(): return lax.all_to_all(copies, axes, 0, 0, tiled=True)  7.66 us
    all_to_all x1, starting transfers between devices, everywhere(): return lax.all_to_all(copies, axes, 0, 0, tiled=True)  6.4 us
    ppermute x4, starting transfers between devices, swap(): return lax.ppermute(value, axis, [(i, i ^ flip) for i in range(count)])  6.21 us
    all_to_all x1, starting transfers between devices, per_device(): lax.all_to_all(statistics(activations), 'dp', 0, 0, axis_index_groups=gro...  5.25 us
  transfers between devices with their start and end apart: 6, of which 6 were waited for; matrix products, arithmetic and copies ran while one was open for 0% of the time, Pallas kernels for 15%

profile of v5, /device:TPU:0, one launch (start us, length us, event | category | flops | bytes accessed | tf_op | source)
XLA Modules:
  0.0 84.7 jit_solution(16924518485395158314)
XLA Ops:
  0.6 0.0 copy-start
  0.6 1.6 %copy-done = bf16[512,2048]{1,0:T(8,128)(2,1)S(1)} copy-done((bf16[512,2048]{1,0:T(8,128)(2,1)S(1)}, bf16[512,2048]{1,0:T(8,128)(2,1)}, u32[]{:S(2)}) %copy-start) | copy-done | bytes 2097176
  2.2 2.0 %statistics.1 = bf16[4,528,256]{2,1,0:T(8,128)(2,1)} custom-call(bf16[512,2048]{1,0:T(8,128)(2,1)S(1)} %copy-done), custom_call_target="tpu_custom_call" | custom-call | tf_op jit(solution)/shard_map/statistics/pallas_call | solution.py:69
  4.2 5.2 %all-to-all-start = ((bf16[4,528,256]{2,1,0:T(8,128)(2,1)}), bf16[4,528,256]{2,1,0:T(8,128)(2,1)S(1)}, u32[]{:S(2)}, u32[]{:S(2)}) async-start(bf16[4,528,256]{2,1,0:T(8,128)(2,1)} %statistics.1), calls=%async_computation | async-start | bytes 2162688 | tf_op jit(solution)/shard_map/all_to_all | solution.py:320
  9.5 14.0 %all-to-all-done = bf16[4,528,256]{2,1,0:T(8,128)(2,1)S(1)} async-done(((bf16[4,528,256]{2,1,0:T(8,128)(2,1)}), bf16[4,528,256]{2,1,0:T(8,128)(2,1)S(1)}, u32[]{:S(2)}, u32[]{:S(2)}) %all-to-all-start) | async-done | bytes 1081376 | tf_op jit(solution)/shard_map/all_to_all | solution.py:320
  23.5 0.1 fusion.after.mine
  23.6 2.7 %collective-permute-start = (bf16[528,256]{1,0:T(8,128)(2,1)S(1)}, bf16[528,256]{1,0:T(8,128)(2,1)S(1)}, u32[]{:S(2)}, u32[]{:S(2)}) collective-permute-start(bf16[528,256]{1,0:T(8,128)(2,1)S(1)} %fusion.after.mine), channel_id=1, source_target_pairs={{0,4},{1,5},{2,6},{3,7},{4,0},{5,1},{6,2},{7,3},{8,12},{9,13},{10,... | collective-permute-start | bytes 811016 | tf_op jit(solution)/shard_map/ppermute | solution.py:298
  26.3 10.8 %gram.1 = (f32[4,256,512]{2,1,0:T(8,128)S(1)}, f32[4,256,256]{2,1,0:T(8,128)S(1)}, f32[4,1,256]{2,1,0:T(1,128)S(1)}) custom-call(s32[4]{0:T(128)S(1)} %iota_xor_fusion.order, bf16[528,256]{1,0:T(8,128)(2,1)S(1)} %fusion.after.mine, bf16[2048,3584]{1,0:T(8,128)(2,1)} %refs_4_.1), custom_call_target="tpu_custom_call" | custom-call | flops 7516192768 | bytes 29360128 | tf_op jit(solution)/shard_map/gram/pallas_call | solution.py:129
  37.0 0.7 collective-permute-done.other
  37.8 3.2 %newton.1.folded = bf16[528,256]{1,0:T(8,128)(2,1)S(1)} custom-call(f32[4,1,256]{2,1,0:T(1,128)S(1)} %get-tuple-element.15.after.square_ref, bf16[528,256]{1,0:T(8,128)(2,1)S(1)} %fusion.after.mine, bf16[528,256]{1,0:T(8,128)(2,1)S(1)} %collective-permute-done.other), custom_call_target="tpu_custom_call" | custom-call | flops 2147483648 | bytes 2097152 | tf_op jit(solution)/shard_map/newton/pallas_call | solution.py:188
  41.0 1.2 %collective-permute-start.3 = (bf16[528,256]{1,0:T(8,128)(2,1)S(1)}, bf16[528,256]{1,0:T(8,128)(2,1)S(1)}, u32[]{:S(2)}, u32[]{:S(2)}) collective-permute-start(bf16[528,256]{1,0:T(8,128)(2,1)S(1)} %newton.1.folded), channel_id=1, source_target_pairs={{0,1},{1,0},{2,3},{3,2},{4,5},{5,4},{6,7},{7,6},{8,9},{9,8},{10,11... | collective-permute-start | bytes 811016 | tf_op jit(solution)/shard_map/ppermute | solution.py:298
  42.2 0.7 collective-permute-start.2
  42.8 1.7 %collective-permute-start.1 = (bf16[528,256]{1,0:T(8,128)(2,1)S(1)}, bf16[528,256]{1,0:T(8,128)(2,1)S(1)}, u32[]{:S(2)}, u32[]{:S(2)}) collective-permute-start(bf16[528,256]{1,0:T(8,128)(2,1)S(1)} %newton.1.folded), channel_id=1, source_target_pairs={{0,3},{1,2},{2,1},{3,0},{4,7},{5,6},{6,5},{7,4},{8,11},{9,10},{10,... | collective-permute-start | bytes 811016 | tf_op jit(solution)/shard_map/ppermute | solution.py:298
  44.5 0.5 norm.4
  45.1 3.2 %collective-permute-done.3.folded = bf16[528,256]{1,0:T(8,128)(2,1)S(1)} collective-permute-done((bf16[528,256]{1,0:T(8,128)(2,1)S(1)}, bf16[528,256]{1,0:T(8,128)(2,1)S(1)}, u32[]{:S(2)}, u32[]{:S(2)}) %collective-permute-start.3) | collective-permute-done | bytes 270368 | tf_op jit(solution)/shard_map/ppermute | solution.py:298
  48.3 0.5 norm.5
  48.8 2.8 %collective-permute-done.2.folded = bf16[528,256]{1,0:T(8,128)(2,1)S(1)} collective-permute-done((bf16[528,256]{1,0:T(8,128)(2,1)S(1)}, bf16[528,256]{1,0:T(8,128)(2,1)S(1)}, u32[]{:S(2)}, u32[]{:S(2)}) %collective-permute-start.2) | collective-permute-done | bytes 270368 | tf_op jit(solution)/shard_map/ppermute | solution.py:298
  51.6 0.5 norm.6
  52.1 0.0 copy-start.1
  52.1 3.2 %collective-permute-done.1.folded = bf16[528,256]{1,0:T(8,128)(2,1)S(1)} collective-permute-done((bf16[528,256]{1,0:T(8,128)(2,1)S(1)}, bf16[528,256]{1,0:T(8,128)(2,1)S(1)}, u32[]{:S(2)}, u32[]{:S(2)}) %collective-permute-start.1) | collective-permute-done | bytes 270368 | tf_op jit(solution)/shard_map/ppermute | solution.py:298
  55.4 0.5 norm.7
  55.9 0.7 broadcast_in_dim.13
  56.6 6.4 %all-to-all-start.1 = ((f32[32,8,128]{2,1,0:T(8,128)}), f32[32,8,128]{2,1,0:T(8,128)S(1)}, u32[]{:S(2)}, u32[]{:S(2)}) async-start(f32[32,8,128]{2,1,0:T(8,128)} %broadcast_in_dim.13), calls=%async_computation.1 | async-start | bytes 262144 | tf_op jit(solution)/shard_map/all_to_all | solution.py:304
  63.0 0.1 pad_add_fusion.here
  63.0 7.7 %all-to-all-done.1.sums = f32[32,8,128]{2,1,0:T(8,128)S(1)} async-done(((f32[32,8,128]{2,1,0:T(8,128)}), f32[32,8,128]{2,1,0:T(8,128)S(1)}, u32[]{:S(2)}, u32[]{:S(2)}) %all-to-all-start.1) | async-done | bytes 131104 | tf_op jit(solution)/shard_map/all_to_all | solution.py:304
  70.7 0.0 copy-done.1
  70.7 13.8 %finish.1 = (bf16[2048,3584]{1,0:T(8,128)(2,1)}, bf16[2,512,512]{2,1,0:T(8,128)(2,1)}) custom-call(s32[4]{0:T(128)S(1)} %iota_xor_fusion.order, s32[2]{0:T(128)S(1)} %pad_add_fusion.here, s32[4,4]{1,0:T(4,128)S(1)} %copy-done.1, f32[32,8,128]{2,1,0:T(8,128)S(1)} %all-to-all-done.1.sums, bf16[512,512]{1,0:T(8,128)(2,1)S(1)} %get-tuple-element.22.refs_0_, ...), custom_call_target="tpu_custom_call" | custom-call | tf_op jit(solution)/shard_map/finish/pallas_call | solution.py:276
  (2 shorter events, 0.0 us)
Async XLA Ops:
  0.6 1.6 %copy-start = (bf16[512,2048]{1,0:T(8,128)(2,1)S(1)}, bf16[512,2048]{1,0:T(8,128)(2,1)}, u32[]{:S(2)}) copy-start(bf16[512,2048]{1,0:T(8,128)(2,1)} %x_ref.1) | copy-start | bytes 6291460
  4.2 19.2 %all-to-all-start = ((bf16[4,528,256]{2,1,0:T(8,128)(2,1)}), bf16[4,528,256]{2,1,0:T(8,128)(2,1)S(1)}, u32[]{:S(2)}, u32[]{:S(2)}) async-start(bf16[4,528,256]{2,1,0:T(8,128)(2,1)} %statistics.1), calls=%async_computation | async-start | bytes 2162688 | tf_op jit(solution)/shard_map/all_to_all | solution.py:320
  23.6 14.2 %collective-permute-start = (bf16[528,256]{1,0:T(8,128)(2,1)S(1)}, bf16[528,256]{1,0:T(8,128)(2,1)S(1)}, u32[]{:S(2)}, u32[]{:S(2)}) collective-permute-start(bf16[528,256]{1,0:T(8,128)(2,1)S(1)} %fusion.after.mine), channel_id=1, source_target_pairs={{0,4},{1,5},{2,6},{3,7},{4,0},{5,1},{6,2},{7,3},{8,12},{9,13},{10,... | collective-permute-start | bytes 811016 | tf_op jit(solution)/shard_map/ppermute | solution.py:298
  41.0 7.3 %collective-permute-start.3 = (bf16[528,256]{1,0:T(8,128)(2,1)S(1)}, bf16[528,256]{1,0:T(8,128)(2,1)S(1)}, u32[]{:S(2)}, u32[]{:S(2)}) collective-permute-start(bf16[528,256]{1,0:T(8,128)(2,1)S(1)} %newton.1.folded), channel_id=1, source_target_pairs={{0,1},{1,0},{2,3},{3,2},{4,5},{5,4},{6,7},{7,6},{8,9},{9,8},{10,11... | collective-permute-start | bytes 811016 | tf_op jit(solution)/shard_map/ppermute | solution.py:298
  42.2 9.4 %collective-permute-start.2 = (bf16[528,256]{1,0:T(8,128)(2,1)S(1)}, bf16[528,256]{1,0:T(8,128)(2,1)S(1)}, u32[]{:S(2)}, u32[]{:S(2)}) collective-permute-start(bf16[528,256]{1,0:T(8,128)(2,1)S(1)} %newton.1.folded), channel_id=1, source_target_pairs={{0,2},{1,3},{2,0},{3,1},{4,6},{5,7},{6,4},{7,5},{8,10},{9,11},{10,... | collective-permute-start | bytes 811016 | tf_op jit(solution)/shard_map/ppermute | solution.py:298
  42.8 12.5 %collective-permute-start.1 = (bf16[528,256]{1,0:T(8,128)(2,1)S(1)}, bf16[528,256]{1,0:T(8,128)(2,1)S(1)}, u32[]{:S(2)}, u32[]{:S(2)}) collective-permute-start(bf16[528,256]{1,0:T(8,128)(2,1)S(1)} %newton.1.folded), channel_id=1, source_target_pairs={{0,3},{1,2},{2,1},{3,0},{4,7},{5,6},{6,5},{7,4},{8,11},{9,10},{10,... | collective-permute-start | bytes 811016 | tf_op jit(solution)/shard_map/ppermute | solution.py:298
  52.1 18.6 %copy-start.1 = (s32[4,4]{1,0:T(4,128)S(1)}, s32[4,4]{1,0:T(4,128)}, u32[]{:S(2)}) copy-start(s32[4,4]{1,0:T(4,128)} %owner_slot.1) | copy-start | bytes 196
  56.6 14.2 %all-to-all-start.1 = ((f32[32,8,128]{2,1,0:T(8,128)}), f32[32,8,128]{2,1,0:T(8,128)S(1)}, u32[]{:S(2)}, u32[]{:S(2)}) async-start(f32[32,8,128]{2,1,0:T(8,128)} %broadcast_in_dim.13), calls=%async_computation.1 | async-start | bytes 262144 | tf_op jit(solution)/shard_map/all_to_all | solution.py:304

commit v6 on v3

v6 whole, which is shorter than its diff:
```python
import functools
import math

import jax
import jax.numpy as jnp
from jax import lax
from jax.experimental import pallas as pl
from jax.experimental.pallas import tpu as pltpu
from jax.sharding import PartitionSpec as P

BLK = 512
HALF = BLK // 2
FOLD = BLK + 16
ITERS = 3
SLOTS = 2
QUAD = 4
ROWS = 8
LANES = 128

damping = 0.01
F32 = jnp.float32
BF16 = jnp.bfloat16
SMEM = pl.BlockSpec(memory_space=pltpu.SMEM)
VMEM = pl.BlockSpec(memory_space=pltpu.VMEM)
ANY = pl.BlockSpec(memory_space=pl.ANY)


def params(mib):
    return pltpu.CompilerParams(vmem_limit_bytes=mib * 2**20)


def dot(left, right, dims=((1,), (0,))):
    return lax.dot_general(left, right, (dims, ((), ())), preferred_element_type=F32)


def places():
    row = lax.broadcasted_iota(jnp.int32, (HALF, HALF), 0)
    col = lax.broadcasted_iota(jnp.int32, (HALF, HALF), 1)
    return row, col


def fold(first, last):
    row, col = places()
    body = jnp.where(row <= col, first, last)
    diagonal = jnp.sum(jnp.where(row == col, last, 0.0), axis=0, keepdims=True)
    return body, jnp.broadcast_to(diagonal, (FOLD - BLK, HALF))


def unfold(body, diagonal):
    row, col = places()
    turned = body.T
    first = jnp.where(row <= col, body, turned)
    last = jnp.where(row > col, body, jnp.where(row < col, turned, diagonal))
    return first, last


def stat_kernel(order, x_ref, *out):
    for place in (1, 2, 3, 0):
        start = pl.multiple_of(order[place] * BLK, BLK)
        left = x_ref[:, pl.ds(start, HALF)]
        right = x_ref[:, pl.ds(pl.multiple_of(start + HALF, HALF), HALF)]
        along = ((0,), (0,))
        out[place][:HALF] = dot(left, right, along).astype(BF16)
        body, diagonal = fold(dot(left, left, along), dot(right, right, along))
        out[place][HALF:BLK] = body.astype(BF16)
        out[place][BLK:] = diagonal.astype(BF16)


def statistics(order, activations):
    return pl.pallas_call(
        stat_kernel,
        out_shape=[jax.ShapeDtypeStruct((FOLD, HALF), BF16)] * QUAD,
        in_specs=[SMEM, VMEM],
        out_specs=[VMEM] * QUAD,
        compiler_params=params(12),
        name="statistics",
    )(order, activations)


def chunks(width, size):
    start = 0
    while width - start >= 2 * size:
        yield pl.ds(start, size)
        start += size
    yield pl.ds(start, width - start)


def gram_kernel(order, after, g_ref, *refs):
    held, folded = refs[:QUAD], refs[QUAD : 2 * QUAD]
    norm_ref, top, last, arrived = refs[2 * QUAD :]
    parts = list(chunks(g_ref.shape[1], 1792))

    def copy(place, index):
        rows = pl.ds(pl.multiple_of(order[place] * BLK, BLK), BLK)
        return pltpu.make_async_copy(
            g_ref.at[rows, parts[index]], held[place].at[:, parts[index]], arrived.at[place, index]
        )

    for place in range(QUAD):
        for index in range(len(parts)):
            copy(place, index).start()
    norm_ref[...] = jnp.zeros_like(norm_ref)
    row, col = places()
    for place in range(QUAD):
        for index, part in enumerate(parts):
            copy(place, index).wait()
            upper = held[place][:HALF, part]
            lower = held[place][HALF:, part]
            across = ((1,), (1,))
            terms = dot(upper, upper, across), dot(upper, lower, across), dot(lower, lower, across)
            if index == 0:
                top[:, :HALF] = terms[0]
                top[:, HALF:] = terms[1]
                last[...] = terms[2]
            else:
                top[:, :HALF] += terms[0]
                top[:, HALF:] += terms[1]
                last[...] += terms[2]
        squares = jnp.where(row == col, top[:, :HALF] + last[...], 0.0)
        norm_ref[...] += jnp.sum(squares, axis=0, keepdims=True)
        body, diagonal = fold(top[:, :HALF], last[...])
        folded[place][:HALF] = top[:, HALF:].astype(BF16)
        folded[place][HALF:BLK] = body.astype(BF16)
        folded[place][BLK:] = diagonal.astype(BF16)


def gram(order, gradient, after):
    rows, columns = gradient.shape
    parts = len(list(chunks(columns, 1792)))
    results = pl.pallas_call(
        gram_kernel,
        out_shape=[pltpu.VMEM((BLK, columns), BF16)] * QUAD
        + [jax.ShapeDtypeStruct((FOLD, HALF), BF16)] * QUAD
        + [jax.ShapeDtypeStruct((1, HALF), F32)],
        in_specs=[SMEM, ANY, ANY],
        out_specs=[VMEM] * (2 * QUAD + 1),
        scratch_shapes=[
            pltpu.VMEM((HALF, BLK), F32),
            pltpu.VMEM((HALF, HALF), F32),
            pltpu.SemaphoreType.DMA((QUAD, parts)),
        ],
        compiler_params=params(12),
        cost_estimate=pl.CostEstimate(
            flops=2 * rows * columns * BLK, bytes_accessed=2 * rows * columns, transcendentals=0
        ),
        name="gram",
    )(order, after, pltpu.with_memory_space_constraint(gradient, pltpu.HBM))
    return results[:QUAD], results[QUAD : 2 * QUAD], results[-1]


def product(left, right):
    return dot(left.astype(BF16), right.astype(BF16))


def newton_kernel(tokens, after, mine, other, root, held):
    total = (mine[...].astype(F32) + other[...].astype(F32)) / tokens
    cross = total[:HALF]
    first, last = unfold(total[HALF:BLK], total[BLK : BLK + 1])
    held[:HALF, :HALF] = first
    held[:HALF, HALF:] = cross
    held[HALF:, :HALF] = cross.T
    held[HALF:, HALF:] = last
    row = lax.broadcasted_iota(jnp.int32, (BLK, BLK), 0)
    col = lax.broadcasted_iota(jnp.int32, (BLK, BLK), 1)
    identity = jnp.where(row == col, 1.0, 0.0).astype(F32)
    matrix = held[...] + damping * identity
    bound = jnp.max(jnp.sum(jnp.abs(matrix), axis=0, keepdims=True), axis=1, keepdims=True)
    scale = 2.0 / bound
    iterate = matrix * scale
    estimate = None
    for step in range(ITERS):
        error = (identity - iterate) * 0.25
        if estimate is None:
            estimate = error
        else:
            estimate = estimate + error + product(estimate, error)
        if step + 1 < ITERS:
            square = 2.0 * error + product(error, error)
            fourth = 2.0 * square + product(square, square)
            iterate = iterate + product(fourth, iterate)
    held[...] = (estimate + identity) * jnp.sqrt(jnp.sqrt(scale))
    root[:HALF] = held[:HALF, HALF:].astype(BF16)
    body, diagonal = fold(held[:HALF, :HALF], held[HALF:, HALF:])
    root[HALF:BLK] = body.astype(BF16)
    root[BLK:] = diagonal.astype(BF16)


def newton(tokens, after, mine, other):
    return pl.pallas_call(
        functools.partial(newton_kernel, tokens),
        out_shape=jax.ShapeDtypeStruct((FOLD, HALF), BF16),
        in_specs=[ANY, VMEM, VMEM],
        out_specs=VMEM,
        scratch_shapes=[pltpu.VMEM((BLK, BLK), F32)],
        compiler_params=params(12),
        cost_estimate=pl.CostEstimate(
            flops=16 * BLK**3, bytes_accessed=8 * BLK * BLK, transcendentals=0
        ),
        name="newton",
    )(after, mine, other)


def unfold_root(folded, root_ref):
    cross = folded[:HALF]
    rest = folded[HALF:].astype(F32)
    first, last = unfold(rest[:HALF], rest[HALF : HALF + 1])
    root_ref[:HALF, :HALF] = first.astype(BF16)
    root_ref[:HALF, HALF:] = cross
    root_ref[HALF:, :HALF] = cross.astype(F32).T.astype(BF16)
    root_ref[HALF:, HALF:] = last.astype(BF16)


def norm_kernel(folded, mine, from_y, from_z, squares, total_ref, root):
    unfold_root(folded, root)
    grams = mine[...].astype(F32) + from_y[...].astype(F32) + from_z[...].astype(F32)
    upper = dot(root[:HALF], root[...])
    last = dot(root[HALF:], root[:, HALF:])
    first, cross = upper[:, :HALF], upper[:, HALF:]
    row, col = places()
    weights = jnp.where(row < col, 2.0 * first, jnp.where(row > col, 2.0 * last, first))
    terms = weights * grams[HALF:BLK] + 2.0 * cross * grams[:HALF]
    terms += jnp.where(row == col, last, 0.0) * grams[BLK : BLK + 1]
    lanes = lambda value: sum(value[:, i : i + LANES] for i in range(0, HALF, LANES))
    new = lanes(jnp.sum(terms, axis=0, keepdims=True))
    row = lax.broadcasted_iota(jnp.int32, total_ref.shape, 0)
    total_ref[...] = jnp.where(row == 0, lanes(squares[...]), jnp.where(row == 1, new, 0.0))


def norm(*operands):
    return pl.pallas_call(
        norm_kernel,
        out_shape=jax.ShapeDtypeStruct((ROWS, LANES), F32),
        in_specs=[VMEM] * 5,
        out_specs=VMEM,
        scratch_shapes=[pltpu.VMEM((BLK, BLK), BF16)],
        compiler_params=params(12),
        name="norm",
    )(*operands)


def multiply_kernel(after, folded, held_ref, u_ref, root_ref):
    unfold_root(folded, root_ref)
    for part in chunks(u_ref.shape[1], BLK):
        u_ref[:, part] = dot(root_ref[...], held_ref[:, part]).astype(BF16)


def multiply(folded, held, after):
    return pl.pallas_call(
        multiply_kernel,
        out_shape=[pltpu.VMEM(held.shape, BF16), jax.ShapeDtypeStruct((BLK, BLK), BF16)],
        in_specs=[ANY, VMEM, VMEM],
        out_specs=[VMEM] * 2,
        input_output_aliases={2: 0},
        compiler_params=params(12),
        cost_estimate=pl.CostEstimate(
            flops=2 * BLK * BLK * held.shape[1], bytes_accessed=1, transcendentals=0
        ),
        name="multiply",
    )(after, folded, held)


def finish_kernel(order, owner_slot, sums, folded, *refs):
    roots, blocks = refs[: QUAD - 1], refs[QUAD - 1 : 2 * QUAD - 1]
    update_ref, owned_ref = refs[2 * QUAD - 1 : 2 * QUAD + 1]
    scaled = refs[2 * QUAD + 1 : 3 * QUAD + 1]
    final, owned, sent, stored = refs[3 * QUAD + 1 :]
    both = jnp.sum(sums[...], axis=1, keepdims=True)
    ratio = jnp.sqrt(both[:1] / (both[1:2] + 1e-06))
    parts = list(chunks(blocks[0].shape[1], BLK))

    def copy(place, index):
        rows = pl.ds(pl.multiple_of(order[place] * BLK, BLK), BLK)
        return pltpu.make_async_copy(
            scaled[place].at[:, parts[index]],
            update_ref.at[rows, parts[index]],
            sent.at[place, index],
        )

    def rescale(place):
        for index, part in enumerate(parts):
            scaled[place][:, part] = (blocks[place][:, part].astype(F32) * ratio).astype(BF16)
            copy(place, index).start()

    rescale(0)
    unfold_root(folded, final)
    for index, part in enumerate(parts):
        product = dot(final[...], blocks[-1][:, part])
        scaled[-1][:, part] = (product * ratio).astype(BF16)
        copy(QUAD - 1, index).start()
    rescale(1)
    owned[...] = jnp.zeros_like(owned)
    for place, root in enumerate((*roots, final)):
        for slot in range(SLOTS):

            @pl.when(owner_slot[order[QUAD], order[place]] == order[QUAD + 1] + slot)
            def _():
                owned[slot] = root[...]

    store = pltpu.make_async_copy(owned, owned_ref, stored)
    store.start()
    rescale(2)
    for place in range(QUAD):
        for index in range(len(parts)):
            copy(place, index).wait()
    store.wait()


def finish(order, owner_slot, sums, folded, roots, blocks):
    columns = blocks[0].shape[1]
    parts = len(list(chunks(columns, BLK)))
    return pl.pallas_call(
        finish_kernel,
        out_shape=[
            jax.ShapeDtypeStruct((QUAD * BLK, columns), BF16),
            jax.ShapeDtypeStruct((SLOTS, BLK, BLK), BF16),
        ]
        + [pltpu.VMEM((BLK, columns), BF16)] * QUAD,
        in_specs=[SMEM] * 2 + [VMEM] * (1 + 2 * QUAD),
        out_specs=[ANY] * 2 + [VMEM] * QUAD,
        input_output_aliases={3 + QUAD + place: 2 + place for place in range(QUAD)},
        scratch_shapes=[
            pltpu.VMEM((BLK, BLK), BF16),
            pltpu.VMEM((SLOTS, BLK, BLK), BF16),
            pltpu.SemaphoreType.DMA((QUAD, parts)),
            pltpu.SemaphoreType.DMA,
        ],
        compiler_params=params(12),
        name="finish",
    )(order, owner_slot, sums, folded, *roots, *blocks)[:2]


def swap(value, flip):
    axes = ("pool", "dp")
    count = math.prod(lax.axis_size(axis) for axis in axes)
    return lax.ppermute(value, axes, [(i, i ^ flip) for i in range(count)])


def rounds():
    peer_bits = lax.axis_size("dp").bit_length() - 1
    bits = [1 << i for i in range(peer_bits + lax.axis_size("pool").bit_length() - 1)]
    bits = bits[:peer_bits] + bits[peer_bits:][::-1]
    pairs = [bits[i : i + 2] for i in range(0, len(bits), 2)]
    return [pair if len(pair) == 1 else [*pair, sum(pair)] for pair in pairs]


def add(*values):
    return sum(value.astype(F32) for value in values).astype(BF16)


def per_device(activations, gradient, owner_slot):
    peer_count = lax.axis_size("dp")
    my_index = lax.axis_index("dp")
    group_index = lax.axis_index("pool")
    tokens_all = activations.shape[0] * peer_count
    order = (my_index % QUAD) ^ jnp.arange(QUAD, dtype=jnp.int32)
    order = jnp.concatenate([order, jnp.stack([group_index, my_index * SLOTS])])

    a, b, c, d = statistics(order, activations)
    b, c, d = swap(b, 1), swap(c, 2), swap(d, 3)
    blocks, grams, squares = gram(order, gradient, a)
    mine = add(a, b, c, d)
    flip = QUAD
    other = swap(mine, flip)
    while 2 * flip < peer_count:
        mine = add(mine, other)
        flip *= 2
        other = swap(mine, flip)

    across = swap(grams[3], 1)
    from_y = swap(grams[1], 1)
    from_z = swap(add(grams[2], across), 2)
    root = newton(tokens_all, squares, mine, other)
    folded = (root, swap(root, 1), swap(root, 2), swap(root, 3))
    blocks, folded, roots = list(blocks), list(folded), []

    def precondition(place):
        blocks[place], root = multiply(folded[place], blocks[place], folded[place])
        roots.append(root)

    precondition(0)
    blocks[0], from_y = lax.optimization_barrier((blocks[0], from_y))
    sums = norm(root, grams[0], from_y, from_z, squares)
    for step, flips in enumerate(rounds()):
        if step == 1:
            sums, folded[2] = lax.optimization_barrier((sums, folded[2]))
        if step == 2:
            sums, folded[3] = lax.optimization_barrier((sums, folded[3]))
        received = [swap(sums, flip) for flip in flips]
        if step < QUAD - 2:
            precondition(step + 1)
            blocks[step + 1], *received = lax.optimization_barrier((blocks[step + 1], *received))
        sums = sums + sum(received)
    update, owned = finish(order, owner_slot, sums, folded[-1], roots, blocks)
    return (update, owned[None])


def solution(mesh):
    in_specs = (P("dp", "pool"), P("pool", "dp"), P())
    out_specs = (P("pool", "dp"), P("pool", "dp", None, None))
    return jax.shard_map(
        per_device, mesh=mesh, in_specs=in_specs, out_specs=out_specs, check_vma=False
    )
```

time: 98.7 us -> 74 us (0.75); the launches traced: 98.4 us -> 72.6 us
  local copies, waits for them, and re-layouts: 22.9 us -> 1.6 us
  starting transfers between devices: 16.1 us -> 23.1 us
  Pallas kernels: 38.4 us -> 31.9 us
  waiting for transfers between devices: 19.9 us -> 14.7 us
    unnamed x12 -> x4, local copies, waits for them, and re-layouts: 22.9 us -> 1.6 us
    ppermute x12 -> x17, starting transfers between devices: 16.1 us -> 23.1 us  [swap(): return lax.ppermute(value, axes, [(i, i ^ flip) for i in range(count)])]
    pallas_call x11 -> x6, Pallas kernels: 33.6 us -> 27.1 us  [the longest x1 10.8 us: gram(): pl.pallas_call(gram_kernel, out_shape=[pltpu.VMEM((BLK, columns), BF16)]...]
    ppermute x12 -> x17, waiting for transfers between devices: 19.9 us -> 14.7 us  [swap(): return lax.ppermute(value, axes, [(i, i ^ flip) for i in range(count)])]
  transfers between devices with their start and end apart: 12 -> 17, of which waited for: 7 -> 6; matrix products, arithmetic and copies ran while one was open for 0% -> 0% of each run, Pallas kernels for 25% -> 30%
where the time goes in v6:
time: 74 us; the launch traced here: 72.6 us
  Pallas kernels  31.9 us (43%)
  starting transfers between devices  23.1 us (31%)
  waiting for transfers between devices  14.7 us (20%)
  local copies, waits for them, and re-layouts  1.6 us (2%)
  between operations  0.95 us (1%)
    ppermute x17, starting transfers between devices, swap(): return lax.ppermute(value, axes, [(i, i ^ flip) for i in range(count)])  23.1 us
    ppermute x17, waiting for transfers between devices, swap(): return lax.ppermute(value, axes, [(i, i ^ flip) for i in range(count)])  14.7 us
    pallas_call x1, Pallas kernels, gram(): pl.pallas_call(gram_kernel, out_shape=[pltpu.VMEM((BLK, columns), BF16)]...  10.8 us
    pallas_call x1, Pallas kernels, finish(): pl.pallas_call(finish_kernel, out_shape=[jax.ShapeDtypeStruct((QUAD * BLK...  8.6 us
    pallas_call x3, Pallas kernels, multiply(): pl.pallas_call(multiply_kernel, out_shape=[pltpu.VMEM(held.shape, BF16),...  7.12 us
    pallas_call x1, Pallas kernels, newton(): pl.pallas_call(functools.partial(newton_kernel, tokens), out_shape=jax.Sh...  3.21 us
    unnamed x4, local copies, waits for them, and re-layouts  1.6 us
    pallas_call x1, Pallas kernels, statistics(): pl.pallas_call(stat_kernel, out_shape=[jax.ShapeDtypeStruct((FOLD, HALF),...  1.59 us
  transfers between devices with their start and end apart: 17, of which 6 were waited for; matrix products, arithmetic and copies ran while one was open for 0% of the time, Pallas kernels for 30%

profile of v6, /device:TPU:0, one launch (start us, length us, event | category | flops | bytes accessed | tf_op | source)
XLA Modules:
  0.0 72.6 jit_solution(9478981393610235232)
XLA Ops:
  0.7 0.1 pad_add_fusion.order
  0.7 1.6 %copy-done = bf16[512,2048]{1,0:T(8,128)(2,1)S(1)} copy-done((bf16[512,2048]{1,0:T(8,128)(2,1)S(1)}, bf16[512,2048]{1,0:T(8,128)(2,1)}, u32[]{:S(2)}) %copy-start) | copy-done | bytes 2097176
  2.3 1.6 %statistics.1 = (bf16[528,256]{1,0:T(8,128)(2,1)S(1)}, bf16[528,256]{1,0:T(8,128)(2,1)S(1)}, bf16[528,256]{1,0:T(8,128)(2,1)S(1)}, bf16[528,256]{1,0:T(8,128)(2,1)S(1)}) custom-call(s32[6]{0:T(128)S(1)} %pad_add_fusion.order, bf16[512,2048]{1,0:T(8,128)(2,1)S(1)} %copy-done), custom_call_target="tpu_custom_call" | custom-call | tf_op jit(solution)/shard_map/statistics/pallas_call | solution.py:70
  3.9 3.0 %collective-permute-start = (bf16[528,256]{1,0:T(8,128)(2,1)S(1)}, bf16[528,256]{1,0:T(8,128)(2,1)S(1)}, u32[]{:S(2)}, u32[]{:S(2)}) collective-permute-start(bf16[528,256]{1,0:T(8,128)(2,1)S(1)} %get-tuple-element.39), channel_id=1, source_target_pairs={{0,1},{1,0},{2,3},{3,2},{4,5},{5,4},{6,7},{7,6},{8,9},{9,8},{10,11... | collective-permute-start | bytes 811016 | tf_op jit(solution)/shard_map/ppermute | solution.py:335
  6.9 1.6 %collective-permute-start.1 = (bf16[528,256]{1,0:T(8,128)(2,1)S(1)}, bf16[528,256]{1,0:T(8,128)(2,1)S(1)}, u32[]{:S(2)}, u32[]{:S(2)}) collective-permute-start(bf16[528,256]{1,0:T(8,128)(2,1)S(1)} %get-tuple-element.40), channel_id=1, source_target_pairs={{0,2},{1,3},{2,0},{3,1},{4,6},{5,7},{6,4},{7,5},{8,10},{9,11},{10,... | collective-permute-start | bytes 811016 | tf_op jit(solution)/shard_map/ppermute | solution.py:335
  8.5 10.8 %gram.1 = (bf16[512,3584]{1,0:T(8,128)(2,1)S(1)}, bf16[512,3584]{1,0:T(8,128)(2,1)S(1)}, bf16[512,3584]{1,0:T(8,128)(2,1)S(1)}, bf16[512,3584]{1,0:T(8,128)(2,1)...) custom-call(s32[6]{0:T(128)S(1)} %pad_add_fusion.order, ...), custom_call_target="tpu_custom_call" | custom-call | flops 7516192768 | bytes 14680064 | tf_op jit(solution)/shard_map/gram/pallas_call | solution.py:130
  19.3 2.0 %collective-permute-start.5 = (bf16[528,256]{1,0:T(8,128)(2,1)S(1)}, bf16[528,256]{1,0:T(8,128)(2,1)S(1)}, u32[]{:S(2)}, u32[]{:S(2)}) collective-permute-start(bf16[528,256]{1,0:T(8,128)(2,1)S(1)} %get-tuple-element.48), channel_id=1, source_target_pairs={{0,1},{1,0},{2,3},{3,2},{4,5},{5,4},{6,7},{7,6},{8,9},{9,8},{10,11... | collective-permute-start | bytes 811016 | tf_op jit(solution)/shard_map/ppermute | solution.py:335
  21.3 0.2 add_convert_fusion.1.mine
  21.5 2.7 %collective-permute-start.3 = (bf16[528,256]{1,0:T(8,128)(2,1)S(1)}, bf16[528,256]{1,0:T(8,128)(2,1)S(1)}, u32[]{:S(2)}, u32[]{:S(2)}) collective-permute-start(bf16[528,256]{1,0:T(8,128)(2,1)S(1)} %add_convert_fusion.1.mine), channel_id=1, source_target_pairs={{0,4},{1,5},{2,6},{3,7},{4,0},{5,1},{6,2},{7,3},{8,12},{9,13},{10,... | collective-permute-start | bytes 811016 | tf_op jit(solution)/shard_map/ppermute | solution.py:335
  24.1 0.8 %collective-permute-start.4 = (bf16[528,256]{1,0:T(8,128)(2,1)S(1)}, bf16[528,256]{1,0:T(8,128)(2,1)S(1)}, u32[]{:S(2)}, u32[]{:S(2)}) collective-permute-start(bf16[528,256]{1,0:T(8,128)(2,1)S(1)} %get-tuple-element.45), channel_id=1, source_target_pairs={{0,1},{1,0},{2,3},{3,2},{4,5},{5,4},{6,7},{7,6},{8,9},{9,8},{10,11... | collective-permute-start | bytes 811016 | tf_op jit(solution)/shard_map/ppermute | solution.py:335
  25.0 3.9 %collective-permute-done.5 = bf16[528,256]{1,0:T(8,128)(2,1)S(1)} collective-permute-done((bf16[528,256]{1,0:T(8,128)(2,1)S(1)}, bf16[528,256]{1,0:T(8,128)(2,1)S(1)}, u32[]{:S(2)}, u32[]{:S(2)}) %collective-permute-start.5) | collective-permute-done | bytes 270368 | tf_op jit(solution)/shard_map/ppermute | solution.py:335
  28.9 1.9 %collective-permute-start.6 = (bf16[528,256]{1,0:T(8,128)(2,1)S(1)}, bf16[528,256]{1,0:T(8,128)(2,1)S(1)}, u32[]{:S(2)}, u32[]{:S(2)}) collective-permute-start(bf16[528,256]{1,0:T(8,128)(2,1)S(1)} %add_convert_fusion), channel_id=1, source_target_pairs={{0,2},{1,3},{2,0},{3,1},{4,6},{5,7},{6,4},{7,5},{8,10},{9,11},{10,... | collective-permute-start | bytes 811016 | tf_op jit(solution)/shard_map/ppermute | solution.py:335
  30.8 4.6 %collective-permute-done.3.other = bf16[528,256]{1,0:T(8,128)(2,1)S(1)} collective-permute-done((bf16[528,256]{1,0:T(8,128)(2,1)S(1)}, bf16[528,256]{1,0:T(8,128)(2,1)S(1)}, u32[]{:S(2)}, u32[]{:S(2)}) %collective-permute-start.3) | collective-permute-done | bytes 270368 | tf_op jit(solution)/shard_map/ppermute | solution.py:335
  35.4 3.2 %newton.1.after.folded = bf16[528,256]{1,0:T(8,128)(2,1)S(1)} custom-call(f32[1,256]{1,0:T(1,128)S(1)} %get-tuple-element.38.after.squares, bf16[528,256]{1,0:T(8,128)(2,1)S(1)} %add_convert_fusion.1.mine, bf16[528,256]{1,0:T(8,128)(2,1)S(1)} %collective-permute-done.3.other), custom_call_target="tpu_custom_call" | custom-call | flops 2147483648 | bytes 2097152 | tf_op jit(solution)/shard_map/newton/pallas_call | solution.py:189
  38.7 0.8 %collective-permute-start.7 = (bf16[528,256]{1,0:T(8,128)(2,1)S(1)}, bf16[528,256]{1,0:T(8,128)(2,1)S(1)}, u32[]{:S(2)}, u32[]{:S(2)}) collective-permute-start(bf16[528,256]{1,0:T(8,128)(2,1)S(1)} %newton.1.after.folded), channel_id=1, source_target_pairs={{0,1},{1,0},{2,3},{3,2},{4,5},{5,4},{6,7},{7,6},{8,9},{9,8},{10,11... | collective-permute-start | bytes 811016 | tf_op jit(solution)/shard_map/ppermute | solution.py:335
  39.5 1.3 %collective-permute-start.15 = (bf16[528,256]{1,0:T(8,128)(2,1)S(1)}, bf16[528,256]{1,0:T(8,128)(2,1)S(1)}, u32[]{:S(2)}, u32[]{:S(2)}) collective-permute-start(bf16[528,256]{1,0:T(8,128)(2,1)S(1)} %newton.1.after.folded), channel_id=1, source_target_pairs={{0,3},{1,2},{2,1},{3,0},{4,7},{5,6},{6,5},{7,4},{8,11},{9,10},{10,... | collective-permute-start | bytes 811016 | tf_op jit(solution)/shard_map/ppermute | solution.py:335
  40.8 1.4 %collective-permute-start.11 = (bf16[528,256]{1,0:T(8,128)(2,1)S(1)}, bf16[528,256]{1,0:T(8,128)(2,1)S(1)}, u32[]{:S(2)}, u32[]{:S(2)}) collective-permute-start(bf16[528,256]{1,0:T(8,128)(2,1)S(1)} %newton.1.after.folded), channel_id=1, source_target_pairs={{0,2},{1,3},{2,0},{3,1},{4,6},{5,7},{6,4},{7,5},{8,10},{9,11},{10,... | collective-permute-start | bytes 811016 | tf_op jit(solution)/shard_map/ppermute | solution.py:335
  42.2 2.3 %multiply.3 = (bf16[512,3584]{1,0:T(8,128)(2,1)S(1)}, bf16[512,512]{1,0:T(8,128)(2,1)S(1)}) custom-call(bf16[528,256]{1,0:T(8,128)(2,1)S(1)} %newton.1.after.folded, bf16[528,256]{1,0:T(8,128)(2,1)S(1)} %newton.1.after.folded, bf16[512,3584]{1,0:T(8,128)(2,1)S(1)} %get-tuple-element.43.held_ref), custom_call_target="tpu_custom_call", output_to_operand_aliasing={{0}: (2, {})} | custom-call | flops 1879048192 | bytes 1 | tf_op jit(solution)/shard_map/multiply/pallas_call | solution.py:248
  44.5 0.6 norm.1
  45.1 0.9 %collective-permute-start.10 = (f32[8,128]{1,0:T(8,128)S(1)}, f32[8,128]{1,0:T(8,128)S(1)}, u32[]{:S(2)}, u32[]{:S(2)}) collective-permute-start(f32[8,128]{1,0:T(8,128)S(1)} %norm.1), channel_id=1, source_target_pairs={{0,3},{1,2},{2,1},{3,0},{4,7},{5,6},{6,5},{7,4},{8,11},{9,10},{10,... | collective-permute-start | bytes 12296 | tf_op jit(solution)/shard_map/ppermute | solution.py:335
  46.0 1.4 %collective-permute-start.9 = (f32[8,128]{1,0:T(8,128)S(1)}, f32[8,128]{1,0:T(8,128)S(1)}, u32[]{:S(2)}, u32[]{:S(2)}) collective-permute-start(f32[8,128]{1,0:T(8,128)S(1)} %norm.1), channel_id=1, source_target_pairs={{0,2},{1,3},{2,0},{3,1},{4,6},{5,7},{6,4},{7,5},{8,10},{9,11},{10,... | collective-permute-start | bytes 12296 | tf_op jit(solution)/shard_map/ppermute | solution.py:335
  47.4 4.4 %collective-permute-done.7.after.folded = bf16[528,256]{1,0:T(8,128)(2,1)S(1)} collective-permute-done((bf16[528,256]{1,0:T(8,128)(2,1)S(1)}, bf16[528,256]{1,0:T(8,128)(2,1)S(1)}, u32[]{:S(2)}, u32[]{:S(2)}) %collective-permute-start.7) | collective-permute-done | bytes 270368 | tf_op jit(solution)/shard_map/ppermute | solution.py:335
  51.8 0.8 %collective-permute-start.8 = (f32[8,128]{1,0:T(8,128)S(1)}, f32[8,128]{1,0:T(8,128)S(1)}, u32[]{:S(2)}, u32[]{:S(2)}) collective-permute-start(f32[8,128]{1,0:T(8,128)S(1)} %norm.1), channel_id=1, source_target_pairs={{0,1},{1,0},{2,3},{3,2},{4,5},{5,4},{6,7},{7,6},{8,9},{9,8},{10,11... | collective-permute-start | bytes 12296 | tf_op jit(solution)/shard_map/ppermute | solution.py:335
  52.6 2.5 %multiply.4 = (bf16[512,3584]{1,0:T(8,128)(2,1)S(1)}, bf16[512,512]{1,0:T(8,128)(2,1)S(1)}) custom-call(bf16[528,256]{1,0:T(8,128)(2,1)S(1)} %collective-permute-done.7.after.folded, bf16[528,256]{1,0:T(8,128)(2,1)S(1)} %collective-permute-done.7.after.folded, bf16[512,3584]{1,0:T(8,128)(2,1)S(1)} %get-tuple-element.49.held_ref), custom_call_target="tpu_custom_call", output_to_operand_aliasing={{0}: (2, {})} | custom-call | flops 1879048192 | bytes 1 | tf_op jit(solution)/shard_map/multiply/pallas_call | solution.py:248
  55.1 0.3 collective-permute-done.8
  55.4 2.1 %collective-permute-start.14 = (f32[8,128]{1,0:T(8,128)S(1)}, f32[8,128]{1,0:T(8,128)S(1)}, u32[]{:S(2)}, u32[]{:S(2)}) collective-permute-start(f32[8,128]{1,0:T(8,128)S(1)} %add_add_fusion.1), channel_id=1, source_target_pairs={{0,20},{1,21},{2,22},{3,23},{4,16},{5,17},{6,18},{7,19},{8,28},{9,... | collective-permute-start | bytes 12296 | tf_op jit(solution)/shard_map/ppermute | solution.py:335
  57.5 0.5 collective-permute-start.13
  58.1 1.8 %collective-permute-start.12 = (f32[8,128]{1,0:T(8,128)S(1)}, f32[8,128]{1,0:T(8,128)S(1)}, u32[]{:S(2)}, u32[]{:S(2)}) collective-permute-start(f32[8,128]{1,0:T(8,128)S(1)} %add_add_fusion.1), channel_id=1, source_target_pairs={{0,4},{1,5},{2,6},{3,7},{4,0},{5,1},{6,2},{7,3},{8,12},{9,13},{10,... | collective-permute-start | bytes 12296 | tf_op jit(solution)/shard_map/ppermute | solution.py:335
  59.9 2.3 %multiply.5 = (bf16[512,3584]{1,0:T(8,128)(2,1)S(1)}, bf16[512,512]{1,0:T(8,128)(2,1)S(1)}) custom-call(bf16[528,256]{1,0:T(8,128)(2,1)S(1)} %collective-permute-done.11.after.folded, bf16[528,256]{1,0:T(8,128)(2,1)S(1)} %collective-permute-done.11.after.folded, bf16[512,3584]{1,0:T(8,128)(2,1)S(1)} %get-tuple-element.56.held_ref), custom_call_target="tpu_custom_call", output_to_operand_aliasing={{0}: (2, {})} | custom-call | flops 1879048192 | bytes 1 | tf_op jit(solution)/shard_map/multiply/pallas_call | solution.py:248
  62.2 0.4 collective-permute-done.12
  62.7 1.2 %collective-permute-done.16 = f32[8,128]{1,0:T(8,128)S(1)} collective-permute-done((f32[8,128]{1,0:T(8,128)S(1)}, f32[8,128]{1,0:T(8,128)S(1)}, u32[]{:S(2)}, u32[]{:S(2)}) %collective-permute-start.16) | collective-permute-done | bytes 4128 | tf_op jit(solution)/shard_map/ppermute | solution.py:335
  63.8 8.6 %finish.1 = (bf16[2048,3584]{1,0:T(8,128)(2,1)}, bf16[2,512,512]{2,1,0:T(8,128)(2,1)}, bf16[512,3584]{1,0:T(8,128)(2,1)S(1)}, bf16[512,3584]{1,0:T(8,128)(2,1)S(...) custom-call(s32[6]{0:T(128)S(1)} %pad_add_fusion.order, ...), custom_call_target="tpu_custom_call", output_to_operand_aliasing={{2}: (7, {}), {3}: (8, {}), {4}: (9, {}), {5}: (10, {})} | custom-call | tf_op jit(solution)/shard_map/finish/pallas_call | solution.py:311
  (21 shorter events, 0.2 us)
Async XLA Ops:
  0.7 1.6 %copy-start = (bf16[512,2048]{1,0:T(8,128)(2,1)S(1)}, bf16[512,2048]{1,0:T(8,128)(2,1)}, u32[]{:S(2)}) copy-start(bf16[512,2048]{1,0:T(8,128)(2,1)} %x_ref.1) | copy-start | bytes 6291460
  3.9 17.4 %collective-permute-start = (bf16[528,256]{1,0:T(8,128)(2,1)S(1)}, bf16[528,256]{1,0:T(8,128)(2,1)S(1)}, u32[]{:S(2)}, u32[]{:S(2)}) collective-permute-start(bf16[528,256]{1,0:T(8,128)(2,1)S(1)} %get-tuple-element.39), channel_id=1, source_target_pairs={{0,1},{1,0},{2,3},{3,2},{4,5},{5,4},{6,7},{7,6},{8,9},{9,8},{10,11... | collective-permute-start | bytes 811016 | tf_op jit(solution)/shard_map/ppermute | solution.py:335
  6.9 14.4 %collective-permute-start.1 = (bf16[528,256]{1,0:T(8,128)(2,1)S(1)}, bf16[528,256]{1,0:T(8,128)(2,1)S(1)}, u32[]{:S(2)}, u32[]{:S(2)}) collective-permute-start(bf16[528,256]{1,0:T(8,128)(2,1)S(1)} %get-tuple-element.40), channel_id=1, source_target_pairs={{0,2},{1,3},{2,0},{3,1},{4,6},{5,7},{6,4},{7,5},{8,10},{9,11},{10,... | collective-permute-start | bytes 811016 | tf_op jit(solution)/shard_map/ppermute | solution.py:335
  8.5 12.8 %collective-permute-start.2 = (bf16[528,256]{1,0:T(8,128)(2,1)S(1)}, bf16[528,256]{1,0:T(8,128)(2,1)S(1)}, u32[]{:S(2)}, u32[]{:S(2)}) collective-permute-start(bf16[528,256]{1,0:T(8,128)(2,1)S(1)} %get-tuple-element.41), channel_id=1, source_target_pairs={{0,3},{1,2},{2,1},{3,0},{4,7},{5,6},{6,5},{7,4},{8,11},{9,10},{10,... | collective-permute-start | bytes 811016 | tf_op jit(solution)/shard_map/ppermute | solution.py:335
  19.3 9.5 %collective-permute-start.5 = (bf16[528,256]{1,0:T(8,128)(2,1)S(1)}, bf16[528,256]{1,0:T(8,128)(2,1)S(1)}, u32[]{:S(2)}, u32[]{:S(2)}) collective-permute-start(bf16[528,256]{1,0:T(8,128)(2,1)S(1)} %get-tuple-element.48), channel_id=1, source_target_pairs={{0,1},{1,0},{2,3},{3,2},{4,5},{5,4},{6,7},{7,6},{8,9},{9,8},{10,11... | collective-permute-start | bytes 811016 | tf_op jit(solution)/shard_map/ppermute | solution.py:335
  21.5 14.0 %collective-permute-start.3 = (bf16[528,256]{1,0:T(8,128)(2,1)S(1)}, bf16[528,256]{1,0:T(8,128)(2,1)S(1)}, u32[]{:S(2)}, u32[]{:S(2)}) collective-permute-start(bf16[528,256]{1,0:T(8,128)(2,1)S(1)} %add_convert_fusion.1.mine), channel_id=1, source_target_pairs={{0,4},{1,5},{2,6},{3,7},{4,0},{5,1},{6,2},{7,3},{8,12},{9,13},{10,... | collective-permute-start | bytes 811016 | tf_op jit(solution)/shard_map/ppermute | solution.py:335
  24.1 20.4 %collective-permute-start.4 = (bf16[528,256]{1,0:T(8,128)(2,1)S(1)}, bf16[528,256]{1,0:T(8,128)(2,1)S(1)}, u32[]{:S(2)}, u32[]{:S(2)}) collective-permute-start(bf16[528,256]{1,0:T(8,128)(2,1)S(1)} %get-tuple-element.45), channel_id=1, source_target_pairs={{0,1},{1,0},{2,3},{3,2},{4,5},{5,4},{6,7},{7,6},{8,9},{9,8},{10,11... | collective-permute-start | bytes 811016 | tf_op jit(solution)/shard_map/ppermute | solution.py:335
  28.9 15.6 %collective-permute-start.6 = (bf16[528,256]{1,0:T(8,128)(2,1)S(1)}, bf16[528,256]{1,0:T(8,128)(2,1)S(1)}, u32[]{:S(2)}, u32[]{:S(2)}) collective-permute-start(bf16[528,256]{1,0:T(8,128)(2,1)S(1)} %add_convert_fusion), channel_id=1, source_target_pairs={{0,2},{1,3},{2,0},{3,1},{4,6},{5,7},{6,4},{7,5},{8,10},{9,11},{10,... | collective-permute-start | bytes 811016 | tf_op jit(solution)/shard_map/ppermute | solution.py:335
  38.7 13.2 %collective-permute-start.7 = (bf16[528,256]{1,0:T(8,128)(2,1)S(1)}, bf16[528,256]{1,0:T(8,128)(2,1)S(1)}, u32[]{:S(2)}, u32[]{:S(2)}) collective-permute-start(bf16[528,256]{1,0:T(8,128)(2,1)S(1)} %newton.1.after.folded), channel_id=1, source_target_pairs={{0,1},{1,0},{2,3},{3,2},{4,5},{5,4},{6,7},{7,6},{8,9},{9,8},{10,11... | collective-permute-start | bytes 811016 | tf_op jit(solution)/shard_map/ppermute | solution.py:335
  39.5 23.1 %collective-permute-start.15 = (bf16[528,256]{1,0:T(8,128)(2,1)S(1)}, bf16[528,256]{1,0:T(8,128)(2,1)S(1)}, u32[]{:S(2)}, u32[]{:S(2)}) collective-permute-start(bf16[528,256]{1,0:T(8,128)(2,1)S(1)} %newton.1.after.folded), channel_id=1, source_target_pairs={{0,3},{1,2},{2,1},{3,0},{4,7},{5,6},{6,5},{7,4},{8,11},{9,10},{10,... | collective-permute-start | bytes 811016 | tf_op jit(solution)/shard_map/ppermute | solution.py:335
  40.8 14.7 %collective-permute-start.11 = (bf16[528,256]{1,0:T(8,128)(2,1)S(1)}, bf16[528,256]{1,0:T(8,128)(2,1)S(1)}, u32[]{:S(2)}, u32[]{:S(2)}) collective-permute-start(bf16[528,256]{1,0:T(8,128)(2,1)S(1)} %newton.1.after.folded), channel_id=1, source_target_pairs={{0,2},{1,3},{2,0},{3,1},{4,6},{5,7},{6,4},{7,5},{8,10},{9,11},{10,... | collective-permute-start | bytes 811016 | tf_op jit(solution)/shard_map/ppermute | solution.py:335
  45.1 10.0 %collective-permute-start.10 = (f32[8,128]{1,0:T(8,128)S(1)}, f32[8,128]{1,0:T(8,128)S(1)}, u32[]{:S(2)}, u32[]{:S(2)}) collective-permute-start(f32[8,128]{1,0:T(8,128)S(1)} %norm.1), channel_id=1, source_target_pairs={{0,3},{1,2},{2,1},{3,0},{4,7},{5,6},{6,5},{7,4},{8,11},{9,10},{10,... | collective-permute-start | bytes 12296 | tf_op jit(solution)/shard_map/ppermute | solution.py:335
  46.0 9.1 %collective-permute-start.9 = (f32[8,128]{1,0:T(8,128)S(1)}, f32[8,128]{1,0:T(8,128)S(1)}, u32[]{:S(2)}, u32[]{:S(2)}) collective-permute-start(f32[8,128]{1,0:T(8,128)S(1)} %norm.1), channel_id=1, source_target_pairs={{0,2},{1,3},{2,0},{3,1},{4,6},{5,7},{6,4},{7,5},{8,10},{9,11},{10,... | collective-permute-start | bytes 12296 | tf_op jit(solution)/shard_map/ppermute | solution.py:335
  51.8 3.6 %collective-permute-start.8 = (f32[8,128]{1,0:T(8,128)S(1)}, f32[8,128]{1,0:T(8,128)S(1)}, u32[]{:S(2)}, u32[]{:S(2)}) collective-permute-start(f32[8,128]{1,0:T(8,128)S(1)} %norm.1), channel_id=1, source_target_pairs={{0,1},{1,0},{2,3},{3,2},{4,5},{5,4},{6,7},{7,6},{8,9},{9,8},{10,11... | collective-permute-start | bytes 12296 | tf_op jit(solution)/shard_map/ppermute | solution.py:335
  55.1 8.7 %copy-start.1 = (s32[4,4]{1,0:T(4,128)S(1)}, s32[4,4]{1,0:T(4,128)}, u32[]{:S(2)}) copy-start(s32[4,4]{1,0:T(4,128)} %owner_slot.1) | copy-start | bytes 196
  55.4 6.8 %collective-permute-start.14 = (f32[8,128]{1,0:T(8,128)S(1)}, f32[8,128]{1,0:T(8,128)S(1)}, u32[]{:S(2)}, u32[]{:S(2)}) collective-permute-start(f32[8,128]{1,0:T(8,128)S(1)} %add_add_fusion.1), channel_id=1, source_target_pairs={{0,20},{1,21},{2,22},{3,23},{4,16},{5,17},{6,18},{7,19},{8,28},{9,... | collective-permute-start | bytes 12296 | tf_op jit(solution)/shard_map/ppermute | solution.py:335
  57.5 4.7 %collective-permute-start.13 = (f32[8,128]{1,0:T(8,128)S(1)}, f32[8,128]{1,0:T(8,128)S(1)}, u32[]{:S(2)}, u32[]{:S(2)}) collective-permute-start(f32[8,128]{1,0:T(8,128)S(1)} %add_add_fusion.1), channel_id=1, source_target_pairs={{0,16},{1,17},{2,18},{3,19},{4,20},{5,21},{6,22},{7,23},{8,24},{9,... | collective-permute-start | bytes 12296 | tf_op jit(solution)/shard_map/ppermute | solution.py:335
  58.1 4.5 %collective-permute-start.12 = (f32[8,128]{1,0:T(8,128)S(1)}, f32[8,128]{1,0:T(8,128)S(1)}, u32[]{:S(2)}, u32[]{:S(2)}) collective-permute-start(f32[8,128]{1,0:T(8,128)S(1)} %add_add_fusion.1), channel_id=1, source_target_pairs={{0,4},{1,5},{2,6},{3,7},{4,0},{5,1},{6,2},{7,3},{8,12},{9,13},{10,... | collective-permute-start | bytes 12296 | tf_op jit(solution)/shard_map/ppermute | solution.py:335
  62.6 1.2 %collective-permute-start.16 = (f32[8,128]{1,0:T(8,128)S(1)}, f32[8,128]{1,0:T(8,128)S(1)}, u32[]{:S(2)}, u32[]{:S(2)}) collective-permute-start(f32[8,128]{1,0:T(8,128)S(1)} %add_add_fusion), channel_id=1, source_target_pairs={{0,8},{1,9},{2,10},{3,11},{4,12},{5,13},{6,14},{7,15},{8,0},{9,1},... | collective-permute-start | bytes 12296 | tf_op jit(solution)/shard_map/ppermute | solution.py:335

commit v7 on v6

--- a/solution.py
+++ b/solution.py
@@ -14,6 +14,8 @@
 ITERS = 3
 SLOTS = 2
 QUAD = 4
+EARLY = 2
+BAND = 128
 ROWS = 8
 LANES = 128
 
@@ -252,62 +254,64 @@
         out_specs=[VMEM] * 2,
         input_output_aliases={2: 0},
         compiler_params=params(12),
-        cost_estimate=pl.CostEstimate(
-            flops=2 * BLK * BLK * held.shape[1], bytes_accessed=1, transcendentals=0
-        ),
+        cost_estimate=pl.CostEstimate(flops=1880000000, bytes_accessed=1, transcendentals=0),
         name="multiply",
     )(after, folded, held)
 
 
-def finish_kernel(order, owner_slot, sums, folded, *refs):
-    roots, blocks = refs[: QUAD - 1], refs[QUAD - 1 : 2 * QUAD - 1]
-    update_ref, owned_ref = refs[2 * QUAD - 1 : 2 * QUAD + 1]
-    scaled = refs[2 * QUAD + 1 : 3 * QUAD + 1]
-    final, owned, sent, stored = refs[3 * QUAD + 1 :]
+def finish_kernel(order, owner_slot, sums, *refs):
+    roots, folded, blocks = refs[:EARLY], refs[EARLY:QUAD], refs[QUAD : 2 * QUAD]
+    update_ref, owned_ref = refs[2 * QUAD : 2 * QUAD + 2]
+    scaled = refs[2 * QUAD + 2 : 3 * QUAD + 2]
+    late, owned, sent, stored = refs[3 * QUAD + 2 :]
     both = jnp.sum(sums[...], axis=1, keepdims=True)
     ratio = jnp.sqrt(both[:1] / (both[1:2] + 1e-06))
     parts = list(chunks(blocks[0].shape[1], BLK))
-
-    def copy(place, index):
-        rows = pl.ds(pl.multiple_of(order[place] * BLK, BLK), BLK)
-        return pltpu.make_async_copy(
-            scaled[place].at[:, parts[index]],
-            update_ref.at[rows, parts[index]],
-            sent.at[place, index],
+    waits = []
+
+    def send(place, rows, columns):
+        at = pl.multiple_of(order[place] * BLK + rows.start, rows.size)
+        copy = pltpu.make_async_copy(
+            scaled[place].at[rows, columns],
+            update_ref.at[pl.ds(at, rows.size), columns],
+            sent.at[len(waits)],
         )
+        copy.start()
+        waits.append(copy)
 
     def rescale(place):
-        for index, part in enumerate(parts):
-            scaled[place][:, part] = (blocks[place][:, part].astype(F32) * ratio).astype(BF16)
-            copy(place, index).start()
-
-    rescale(0)
-    unfold_root(folded, final)
-    for index, part in enumerate(parts):
-        product = dot(final[...], blocks[-1][:, part])
-        scaled[-1][:, part] = (product * ratio).astype(BF16)
-        copy(QUAD - 1, index).start()
-    rescale(1)
+        for start in range(0, BLK, BAND):
+            rows = pl.ds(start, BAND)
+            scaled[place][rows] = (blocks[place][rows].astype(F32) * ratio).astype(BF16)
+            send(place, rows, pl.ds(0, blocks[0].shape[1]))
+
+    for place in range(EARLY):
+        rescale(place)
+    for place in range(EARLY, QUAD):
+        final = late.at[place - EARLY]
+        unfold_root(folded[place - EARLY], final)
+        for part in parts:
+            product = dot(final[...], blocks[place][:, part])
+            scaled[place][:, part] = (product * ratio).astype(BF16)
+            send(place, pl.ds(0, BLK), part)
     owned[...] = jnp.zeros_like(owned)
-    for place, root in enumerate((*roots, final)):
+    for place in range(QUAD):
         for slot in range(SLOTS):
 
             @pl.when(owner_slot[order[QUAD], order[place]] == order[QUAD + 1] + slot)
             def _():
-                owned[slot] = root[...]
+                owned[slot] = roots[place][...] if place < EARLY else late[place - EARLY]
 
     store = pltpu.make_async_copy(owned, owned_ref, stored)
     store.start()
-    rescale(2)
-    for place in range(QUAD):
-        for index in range(len(parts)):
-            copy(place, index).wait()
+    for copy in waits:
+        copy.wait()
     store.wait()
 
 
-def finish(order, owner_slot, sums, folded, roots, blocks):
+def finish(order, owner_slot, sums, roots, folded, blocks):
     columns = blocks[0].shape[1]
-    parts = len(list(chunks(columns, BLK)))
+    pieces = EARLY * (BLK // BAND) + (QUAD - EARLY) * len(list(chunks(columns, BLK)))
     return pl.pallas_call(
         finish_kernel,
         out_shape=[
@@ -319,14 +323,14 @@
         out_specs=[ANY] * 2 + [VMEM] * QUAD,
         input_output_aliases={3 + QUAD + place: 2 + place for place in range(QUAD)},
         scratch_shapes=[
-            pltpu.VMEM((BLK, BLK), BF16),
+            pltpu.VMEM((QUAD - EARLY, BLK, BLK), BF16),
             pltpu.VMEM((SLOTS, BLK, BLK), BF16),
-            pltpu.SemaphoreType.DMA((QUAD, parts)),
+            pltpu.SemaphoreType.DMA((pieces,)),
             pltpu.SemaphoreType.DMA,
         ],
         compiler_params=params(12),
         name="finish",
-    )(order, owner_slot, sums, folded, *roots, *blocks)[:2]
+    )(order, owner_slot, sums, *roots, *folded, *blocks)[:2]
 
 
 def swap(value, flip):
@@ -361,11 +365,13 @@
     mine = add(a, b, c, d)
     flip = QUAD
     other = swap(mine, flip)
+    grams = list(grams)
     while 2 * flip < peer_count:
         mine = add(mine, other)
         flip *= 2
         other = swap(mine, flip)
 
+    mine, grams[1] = lax.optimization_barrier((mine, grams[1]))
     across = swap(grams[3], 1)
     from_y = swap(grams[1], 1)
     from_z = swap(add(grams[2], across), 2)
@@ -377,20 +383,17 @@
         blocks[place], root = multiply(folded[place], blocks[place], folded[place])
         roots.append(root)
 
-    precondition(0)
-    blocks[0], from_y = lax.optimization_barrier((blocks[0], from_y))
     sums = norm(root, grams[0], from_y, from_z, squares)
+    arrivals = {0: [1], 1: [2, 3]}
     for step, flips in enumerate(rounds()):
-        if step == 1:
-            sums, folded[2] = lax.optimization_barrier((sums, folded[2]))
-        if step == 2:
-            sums, folded[3] = lax.optimization_barrier((sums, folded[3]))
         received = [swap(sums, flip) for flip in flips]
-        if step < QUAD - 2:
-            precondition(step + 1)
-            blocks[step + 1], *received = lax.optimization_barrier((blocks[step + 1], *received))
+        if step < EARLY:
+            precondition(step)
+            blocks[step], *received = lax.optimization_barrier((blocks[step], *received))
+        for place in arrivals.get(step, ()):
+            folded[place], *received = lax.optimization_barrier((folded[place], *received))
         sums = sums + sum(received)
-    update, owned = finish(order, owner_slot, sums, folded[-1], roots, blocks)
+    update, owned = finish(order, owner_slot, sums, roots, folded[EARLY:], blocks)
     return (update, owned[None])
 
 

time: 74 us -> 69.2 us (0.935); the launches traced: 72.6 us -> 69 us
  waiting for transfers between devices: 14.7 us -> 12.3 us
  Pallas kernels: 31.9 us -> 29.9 us
  starting transfers between devices: 23.1 us -> 24 us
    ppermute x17, waiting for transfers between devices: 14.7 us -> 12.3 us  [swap(): return lax.ppermute(value, axes, [(i, i ^ flip) for i in range(count)])]
    pallas_call x3 -> x2, Pallas kernels: 7.12 us -> 4.78 us  [multiply(): pl.pallas_call(multiply_kernel, out_shape=[pltpu.VMEM(held.shape, BF16),...]
    ppermute x17, starting transfers between devices: 23.1 us -> 24 us  [swap(): return lax.ppermute(value, axes, [(i, i ^ flip) for i in range(count)])]
  transfers between devices with their start and end apart: 17 -> 17, of which waited for: 6 -> 6; matrix products, arithmetic and copies ran while one was open for 0% -> 0% of each run, Pallas kernels for 30% -> 28%
where the time goes in v7:
time: 69.2 us; the launch traced here: 69 us
  Pallas kernels  29.9 us (43%)
  starting transfers between devices  24 us (35%)
  waiting for transfers between devices  12.3 us (18%)
  local copies, waits for them, and re-layouts  1.6 us (2%)
  between operations  0.91 us (1%)
    ppermute x17, starting transfers between devices, swap(): return lax.ppermute(value, axes, [(i, i ^ flip) for i in range(count)])  24 us
    ppermute x17, waiting for transfers between devices, swap(): return lax.ppermute(value, axes, [(i, i ^ flip) for i in range(count)])  12.3 us
    pallas_call x1, Pallas kernels, gram(): pl.pallas_call(gram_kernel, out_shape=[pltpu.VMEM((BLK, columns), BF16)]...  10.8 us
    pallas_call x1, Pallas kernels, finish(): pl.pallas_call(finish_kernel, out_shape=[jax.ShapeDtypeStruct((QUAD * BLK...  8.95 us
    pallas_call x2, Pallas kernels, multiply(): pl.pallas_call(multiply_kernel, out_shape=[pltpu.VMEM(held.shape, BF16),...  4.78 us
    pallas_call x1, Pallas kernels, newton(): pl.pallas_call(functools.partial(newton_kernel, tokens), out_shape=jax.Sh...  3.2 us
    unnamed x4, local copies, waits for them, and re-layouts  1.6 us
    pallas_call x1, Pallas kernels, statistics(): pl.pallas_call(stat_kernel, out_shape=[jax.ShapeDtypeStruct((FOLD, HALF),...  1.59 us
  transfers between devices with their start and end apart: 17, of which 6 were waited for; matrix products, arithmetic and copies ran while one was open for 0% of the time, Pallas kernels for 28%

profile of v7, /device:TPU:0, one launch (start us, length us, event | category | flops | bytes accessed | tf_op | source)
XLA Modules:
  0.0 69.0 jit_solution(14601035406030077457)
XLA Ops:
  0.7 0.1 pad_add_fusion.order
  0.7 1.6 %copy-done = bf16[512,2048]{1,0:T(8,128)(2,1)S(1)} copy-done((bf16[512,2048]{1,0:T(8,128)(2,1)S(1)}, bf16[512,2048]{1,0:T(8,128)(2,1)}, u32[]{:S(2)}) %copy-start) | copy-done | bytes 2097176
  2.3 1.6 %statistics.1 = (bf16[528,256]{1,0:T(8,128)(2,1)S(1)}, bf16[528,256]{1,0:T(8,128)(2,1)S(1)}, bf16[528,256]{1,0:T(8,128)(2,1)S(1)}, bf16[528,256]{1,0:T(8,128)(2,1)S(1)}) custom-call(s32[6]{0:T(128)S(1)} %pad_add_fusion.order, bf16[512,2048]{1,0:T(8,128)(2,1)S(1)} %copy-done), custom_call_target="tpu_custom_call" | custom-call | tf_op jit(solution)/shard_map/statistics/pallas_call | solution.py:72
  3.9 3.0 %collective-permute-start = (bf16[528,256]{1,0:T(8,128)(2,1)S(1)}, bf16[528,256]{1,0:T(8,128)(2,1)S(1)}, u32[]{:S(2)}, u32[]{:S(2)}) collective-permute-start(bf16[528,256]{1,0:T(8,128)(2,1)S(1)} %get-tuple-element.45), channel_id=1, source_target_pairs={{0,1},{1,0},{2,3},{3,2},{4,5},{5,4},{6,7},{7,6},{8,9},{9,8},{10,11... | collective-permute-start | bytes 811016 | tf_op jit(solution)/shard_map/ppermute | solution.py:339
  6.9 1.6 %collective-permute-start.1 = (bf16[528,256]{1,0:T(8,128)(2,1)S(1)}, bf16[528,256]{1,0:T(8,128)(2,1)S(1)}, u32[]{:S(2)}, u32[]{:S(2)}) collective-permute-start(bf16[528,256]{1,0:T(8,128)(2,1)S(1)} %get-tuple-element.46), channel_id=1, source_target_pairs={{0,2},{1,3},{2,0},{3,1},{4,6},{5,7},{6,4},{7,5},{8,10},{9,11},{10,... | collective-permute-start | bytes 811016 | tf_op jit(solution)/shard_map/ppermute | solution.py:339
  8.5 10.8 %gram.1 = (bf16[512,3584]{1,0:T(8,128)(2,1)S(1)}, bf16[512,3584]{1,0:T(8,128)(2,1)S(1)}, bf16[512,3584]{1,0:T(8,128)(2,1)S(1)}, bf16[512,3584]{1,0:T(8,128)(2,1)...) custom-call(s32[6]{0:T(128)S(1)} %pad_add_fusion.order, ...), custom_call_target="tpu_custom_call" | custom-call | flops 7516192768 | bytes 14680064 | tf_op jit(solution)/shard_map/gram/pallas_call | solution.py:132
  19.3 2.0 %collective-permute-start.5 = (bf16[528,256]{1,0:T(8,128)(2,1)S(1)}, bf16[528,256]{1,0:T(8,128)(2,1)S(1)}, u32[]{:S(2)}, u32[]{:S(2)}) collective-permute-start(bf16[528,256]{1,0:T(8,128)(2,1)S(1)} %get-tuple-element.53), channel_id=1, source_target_pairs={{0,1},{1,0},{2,3},{3,2},{4,5},{5,4},{6,7},{7,6},{8,9},{9,8},{10,11... | collective-permute-start | bytes 811016 | tf_op jit(solution)/shard_map/ppermute | solution.py:339
  21.3 0.1 add_convert_fusion.1.mine
  21.5 2.7 %collective-permute-start.3 = (bf16[528,256]{1,0:T(8,128)(2,1)S(1)}, bf16[528,256]{1,0:T(8,128)(2,1)S(1)}, u32[]{:S(2)}, u32[]{:S(2)}) collective-permute-start(bf16[528,256]{1,0:T(8,128)(2,1)S(1)} %add_convert_fusion.1.mine), channel_id=1, source_target_pairs={{0,4},{1,5},{2,6},{3,7},{4,0},{5,1},{6,2},{7,3},{8,12},{9,13},{10,... | collective-permute-start | bytes 811016 | tf_op jit(solution)/shard_map/ppermute | solution.py:339
  24.1 0.8 %collective-permute-start.4 = (bf16[528,256]{1,0:T(8,128)(2,1)S(1)}, bf16[528,256]{1,0:T(8,128)(2,1)S(1)}, u32[]{:S(2)}, u32[]{:S(2)}) collective-permute-start(bf16[528,256]{1,0:T(8,128)(2,1)S(1)} %get-tuple-element.51), channel_id=1, source_target_pairs={{0,1},{1,0},{2,3},{3,2},{4,5},{5,4},{6,7},{7,6},{8,9},{9,8},{10,11... | collective-permute-start | bytes 811016 | tf_op jit(solution)/shard_map/ppermute | solution.py:339
  25.0 3.9 %collective-permute-done.5 = bf16[528,256]{1,0:T(8,128)(2,1)S(1)} collective-permute-done((bf16[528,256]{1,0:T(8,128)(2,1)S(1)}, bf16[528,256]{1,0:T(8,128)(2,1)S(1)}, u32[]{:S(2)}, u32[]{:S(2)}) %collective-permute-start.5) | collective-permute-done | bytes 270368 | tf_op jit(solution)/shard_map/ppermute | solution.py:339
  28.9 1.9 %collective-permute-start.6 = (bf16[528,256]{1,0:T(8,128)(2,1)S(1)}, bf16[528,256]{1,0:T(8,128)(2,1)S(1)}, u32[]{:S(2)}, u32[]{:S(2)}) collective-permute-start(bf16[528,256]{1,0:T(8,128)(2,1)S(1)} %add_convert_fusion), channel_id=1, source_target_pairs={{0,2},{1,3},{2,0},{3,1},{4,6},{5,7},{6,4},{7,5},{8,10},{9,11},{10,... | collective-permute-start | bytes 811016 | tf_op jit(solution)/shard_map/ppermute | solution.py:339
  30.8 4.6 %collective-permute-done.3.other = bf16[528,256]{1,0:T(8,128)(2,1)S(1)} collective-permute-done((bf16[528,256]{1,0:T(8,128)(2,1)S(1)}, bf16[528,256]{1,0:T(8,128)(2,1)S(1)}, u32[]{:S(2)}, u32[]{:S(2)}) %collective-permute-start.3) | collective-permute-done | bytes 270368 | tf_op jit(solution)/shard_map/ppermute | solution.py:339
  35.4 3.2 %newton.1.folded.after = bf16[528,256]{1,0:T(8,128)(2,1)S(1)} custom-call(f32[1,256]{1,0:T(1,128)S(1)} %get-tuple-element.44.after.squares, bf16[528,256]{1,0:T(8,128)(2,1)S(1)} %add_convert_fusion.1.mine, bf16[528,256]{1,0:T(8,128)(2,1)S(1)} %collective-permute-done.3.other), custom_call_target="tpu_custom_call" | custom-call | flops 2147483648 | bytes 2097152 | tf_op jit(solution)/shard_map/newton/pallas_call | solution.py:191
  38.6 0.8 %collective-permute-start.7 = (bf16[528,256]{1,0:T(8,128)(2,1)S(1)}, bf16[528,256]{1,0:T(8,128)(2,1)S(1)}, u32[]{:S(2)}, u32[]{:S(2)}) collective-permute-start(bf16[528,256]{1,0:T(8,128)(2,1)S(1)} %newton.1.folded.after), channel_id=1, source_target_pairs={{0,1},{1,0},{2,3},{3,2},{4,5},{5,4},{6,7},{7,6},{8,9},{9,8},{10,11... | collective-permute-start | bytes 811016 | tf_op jit(solution)/shard_map/ppermute | solution.py:339
  39.5 0.6 collective-permute-start.12
  40.1 0.6 norm.1
  40.7 2.2 %collective-permute-start.10 = (f32[8,128]{1,0:T(8,128)S(1)}, f32[8,128]{1,0:T(8,128)S(1)}, u32[]{:S(2)}, u32[]{:S(2)}) collective-permute-start(f32[8,128]{1,0:T(8,128)S(1)} %norm.1), channel_id=1, source_target_pairs={{0,3},{1,2},{2,1},{3,0},{4,7},{5,6},{6,5},{7,4},{8,11},{9,10},{10,... | collective-permute-start | bytes 12296 | tf_op jit(solution)/shard_map/ppermute | solution.py:339
  42.8 0.6 collective-permute-start.9
  43.4 0.8 %collective-permute-start.8 = (f32[8,128]{1,0:T(8,128)S(1)}, f32[8,128]{1,0:T(8,128)S(1)}, u32[]{:S(2)}, u32[]{:S(2)}) collective-permute-start(f32[8,128]{1,0:T(8,128)S(1)} %norm.1), channel_id=1, source_target_pairs={{0,1},{1,0},{2,3},{3,2},{4,5},{5,4},{6,7},{7,6},{8,9},{9,8},{10,11... | collective-permute-start | bytes 12296 | tf_op jit(solution)/shard_map/ppermute | solution.py:339
  44.2 2.3 %multiply.2 = (bf16[512,3584]{1,0:T(8,128)(2,1)S(1)}, bf16[512,512]{1,0:T(8,128)(2,1)S(1)}) custom-call(bf16[528,256]{1,0:T(8,128)(2,1)S(1)} %newton.1.folded.after, bf16[528,256]{1,0:T(8,128)(2,1)S(1)} %newton.1.folded.after, bf16[512,3584]{1,0:T(8,128)(2,1)S(1)} %get-tuple-element.54.held_ref), custom_call_target="tpu_custom_call", output_to_operand_aliasing={{0}: (2, {})} | custom-call | flops 1880000000 | bytes 1 | tf_op jit(solution)/shard_map/multiply/pallas_call | solution.py:250
  46.5 0.8 %collective-permute-done.10 = f32[8,128]{1,0:T(8,128)S(1)} collective-permute-done((f32[8,128]{1,0:T(8,128)S(1)}, f32[8,128]{1,0:T(8,128)S(1)}, u32[]{:S(2)}, u32[]{:S(2)}) %collective-permute-start.10) | collective-permute-done | bytes 4128 | tf_op jit(solution)/shard_map/ppermute | solution.py:339
  47.3 1.9 %collective-permute-start.11 = (bf16[528,256]{1,0:T(8,128)(2,1)S(1)}, bf16[528,256]{1,0:T(8,128)(2,1)S(1)}, u32[]{:S(2)}, u32[]{:S(2)}) collective-permute-start(bf16[528,256]{1,0:T(8,128)(2,1)S(1)} %newton.1.folded.after), channel_id=1, source_target_pairs={{0,3},{1,2},{2,1},{3,0},{4,7},{5,6},{6,5},{7,4},{8,11},{9,10},{10,... | collective-permute-start | bytes 811016 | tf_op jit(solution)/shard_map/ppermute | solution.py:339
  49.3 4.4 %collective-permute-start.15 = (f32[8,128]{1,0:T(8,128)S(1)}, f32[8,128]{1,0:T(8,128)S(1)}, u32[]{:S(2)}, u32[]{:S(2)}) collective-permute-start(f32[8,128]{1,0:T(8,128)S(1)} %add_add_fusion.1), channel_id=1, source_target_pairs={{0,20},{1,21},{2,22},{3,23},{4,16},{5,17},{6,18},{7,19},{8,28},{9,... | collective-permute-start | bytes 12296 | tf_op jit(solution)/shard_map/ppermute | solution.py:339
  53.6 0.5 collective-permute-start.14
  54.1 0.1 collective-permute-start.13
  54.3 2.5 %multiply.3 = (bf16[512,3584]{1,0:T(8,128)(2,1)S(1)}, bf16[512,512]{1,0:T(8,128)(2,1)S(1)}) custom-call(bf16[528,256]{1,0:T(8,128)(2,1)S(1)} %collective-permute-done.7.after.folded, bf16[528,256]{1,0:T(8,128)(2,1)S(1)} %collective-permute-done.7.after.folded, bf16[512,3584]{1,0:T(8,128)(2,1)S(1)} %get-tuple-element.63.held_ref), custom_call_target="tpu_custom_call", output_to_operand_aliasing={{0}: (2, {})} | custom-call | flops 1880000000 | bytes 1 | tf_op jit(solution)/shard_map/multiply/pallas_call | solution.py:250
  56.8 0.4 collective-permute-done.14
  57.2 1.4 %collective-permute-done.13 = f32[8,128]{1,0:T(8,128)S(1)} collective-permute-done((f32[8,128]{1,0:T(8,128)S(1)}, f32[8,128]{1,0:T(8,128)S(1)}, u32[]{:S(2)}, u32[]{:S(2)}) %collective-permute-start.13) | collective-permute-done | bytes 4128 | tf_op jit(solution)/shard_map/ppermute | solution.py:339
  58.7 0.1 collective-permute-start.16
  58.7 1.2 %collective-permute-done.16 = f32[8,128]{1,0:T(8,128)S(1)} collective-permute-done((f32[8,128]{1,0:T(8,128)S(1)}, f32[8,128]{1,0:T(8,128)S(1)}, u32[]{:S(2)}, u32[]{:S(2)}) %collective-permute-start.16) | collective-permute-done | bytes 4128 | tf_op jit(solution)/shard_map/ppermute | solution.py:339
  59.9 9.0 %finish.1 = (bf16[2048,3584]{1,0:T(8,128)(2,1)}, bf16[2,512,512]{2,1,0:T(8,128)(2,1)}, bf16[512,3584]{1,0:T(8,128)(2,1)S(1)}, bf16[512,3584]{1,0:T(8,128)(2,1)S(...) custom-call(s32[6]{0:T(128)S(1)} %pad_add_fusion.order, ...), custom_call_target="tpu_custom_call", output_to_operand_aliasing={{2}: (7, {}), {3}: (8, {}), {4}: (9, {}), {5}: (10, {})} | custom-call | tf_op jit(solution)/shard_map/finish/pallas_call | solution.py:315
  (20 shorter events, 0.1 us)
Async XLA Ops:
  0.7 1.6 %copy-start = (bf16[512,2048]{1,0:T(8,128)(2,1)S(1)}, bf16[512,2048]{1,0:T(8,128)(2,1)}, u32[]{:S(2)}) copy-start(bf16[512,2048]{1,0:T(8,128)(2,1)} %x_ref.1) | copy-start | bytes 6291460
  3.9 17.4 %collective-permute-start = (bf16[528,256]{1,0:T(8,128)(2,1)S(1)}, bf16[528,256]{1,0:T(8,128)(2,1)S(1)}, u32[]{:S(2)}, u32[]{:S(2)}) collective-permute-start(bf16[528,256]{1,0:T(8,128)(2,1)S(1)} %get-tuple-element.45), channel_id=1, source_target_pairs={{0,1},{1,0},{2,3},{3,2},{4,5},{5,4},{6,7},{7,6},{8,9},{9,8},{10,11... | collective-permute-start | bytes 811016 | tf_op jit(solution)/shard_map/ppermute | solution.py:339
  6.9 14.4 %collective-permute-start.1 = (bf16[528,256]{1,0:T(8,128)(2,1)S(1)}, bf16[528,256]{1,0:T(8,128)(2,1)S(1)}, u32[]{:S(2)}, u32[]{:S(2)}) collective-permute-start(bf16[528,256]{1,0:T(8,128)(2,1)S(1)} %get-tuple-element.46), channel_id=1, source_target_pairs={{0,2},{1,3},{2,0},{3,1},{4,6},{5,7},{6,4},{7,5},{8,10},{9,11},{10,... | collective-permute-start | bytes 811016 | tf_op jit(solution)/shard_map/ppermute | solution.py:339
  8.5 12.8 %collective-permute-start.2 = (bf16[528,256]{1,0:T(8,128)(2,1)S(1)}, bf16[528,256]{1,0:T(8,128)(2,1)S(1)}, u32[]{:S(2)}, u32[]{:S(2)}) collective-permute-start(bf16[528,256]{1,0:T(8,128)(2,1)S(1)} %get-tuple-element.47), channel_id=1, source_target_pairs={{0,3},{1,2},{2,1},{3,0},{4,7},{5,6},{6,5},{7,4},{8,11},{9,10},{10,... | collective-permute-start | bytes 811016 | tf_op jit(solution)/shard_map/ppermute | solution.py:339
  19.3 9.5 %collective-permute-start.5 = (bf16[528,256]{1,0:T(8,128)(2,1)S(1)}, bf16[528,256]{1,0:T(8,128)(2,1)S(1)}, u32[]{:S(2)}, u32[]{:S(2)}) collective-permute-start(bf16[528,256]{1,0:T(8,128)(2,1)S(1)} %get-tuple-element.53), channel_id=1, source_target_pairs={{0,1},{1,0},{2,3},{3,2},{4,5},{5,4},{6,7},{7,6},{8,9},{9,8},{10,11... | collective-permute-start | bytes 811016 | tf_op jit(solution)/shard_map/ppermute | solution.py:339
  21.5 14.0 %collective-permute-start.3 = (bf16[528,256]{1,0:T(8,128)(2,1)S(1)}, bf16[528,256]{1,0:T(8,128)(2,1)S(1)}, u32[]{:S(2)}, u32[]{:S(2)}) collective-permute-start(bf16[528,256]{1,0:T(8,128)(2,1)S(1)} %add_convert_fusion.1.mine), channel_id=1, source_target_pairs={{0,4},{1,5},{2,6},{3,7},{4,0},{5,1},{6,2},{7,3},{8,12},{9,13},{10,... | collective-permute-start | bytes 811016 | tf_op jit(solution)/shard_map/ppermute | solution.py:339
  24.1 16.0 %collective-permute-start.4 = (bf16[528,256]{1,0:T(8,128)(2,1)S(1)}, bf16[528,256]{1,0:T(8,128)(2,1)S(1)}, u32[]{:S(2)}, u32[]{:S(2)}) collective-permute-start(bf16[528,256]{1,0:T(8,128)(2,1)S(1)} %get-tuple-element.51), channel_id=1, source_target_pairs={{0,1},{1,0},{2,3},{3,2},{4,5},{5,4},{6,7},{7,6},{8,9},{9,8},{10,11... | collective-permute-start | bytes 811016 | tf_op jit(solution)/shard_map/ppermute | solution.py:339
  28.9 11.2 %collective-permute-start.6 = (bf16[528,256]{1,0:T(8,128)(2,1)S(1)}, bf16[528,256]{1,0:T(8,128)(2,1)S(1)}, u32[]{:S(2)}, u32[]{:S(2)}) collective-permute-start(bf16[528,256]{1,0:T(8,128)(2,1)S(1)} %add_convert_fusion), channel_id=1, source_target_pairs={{0,2},{1,3},{2,0},{3,1},{4,6},{5,7},{6,4},{7,5},{8,10},{9,11},{10,... | collective-permute-start | bytes 811016 | tf_op jit(solution)/shard_map/ppermute | solution.py:339
  38.6 10.6 %collective-permute-start.7 = (bf16[528,256]{1,0:T(8,128)(2,1)S(1)}, bf16[528,256]{1,0:T(8,128)(2,1)S(1)}, u32[]{:S(2)}, u32[]{:S(2)}) collective-permute-start(bf16[528,256]{1,0:T(8,128)(2,1)S(1)} %newton.1.folded.after), channel_id=1, source_target_pairs={{0,1},{1,0},{2,3},{3,2},{4,5},{5,4},{6,7},{7,6},{8,9},{9,8},{10,11... | collective-permute-start | bytes 811016 | tf_op jit(solution)/shard_map/ppermute | solution.py:339
  39.5 19.2 %collective-permute-start.12 = (bf16[528,256]{1,0:T(8,128)(2,1)S(1)}, bf16[528,256]{1,0:T(8,128)(2,1)S(1)}, u32[]{:S(2)}, u32[]{:S(2)}) collective-permute-start(bf16[528,256]{1,0:T(8,128)(2,1)S(1)} %newton.1.folded.after), channel_id=1, source_target_pairs={{0,2},{1,3},{2,0},{3,1},{4,6},{5,7},{6,4},{7,5},{8,10},{9,11},{10,... | collective-permute-start | bytes 811016 | tf_op jit(solution)/shard_map/ppermute | solution.py:339
  40.7 6.6 %collective-permute-start.10 = (f32[8,128]{1,0:T(8,128)S(1)}, f32[8,128]{1,0:T(8,128)S(1)}, u32[]{:S(2)}, u32[]{:S(2)}) collective-permute-start(f32[8,128]{1,0:T(8,128)S(1)} %norm.1), channel_id=1, source_target_pairs={{0,3},{1,2},{2,1},{3,0},{4,7},{5,6},{6,5},{7,4},{8,11},{9,10},{10,... | collective-permute-start | bytes 12296 | tf_op jit(solution)/shard_map/ppermute | solution.py:339
  42.8 6.4 %collective-permute-start.9 = (f32[8,128]{1,0:T(8,128)S(1)}, f32[8,128]{1,0:T(8,128)S(1)}, u32[]{:S(2)}, u32[]{:S(2)}) collective-permute-start(f32[8,128]{1,0:T(8,128)S(1)} %norm.1), channel_id=1, source_target_pairs={{0,2},{1,3},{2,0},{3,1},{4,6},{5,7},{6,4},{7,5},{8,10},{9,11},{10,... | collective-permute-start | bytes 12296 | tf_op jit(solution)/shard_map/ppermute | solution.py:339
  43.4 5.8 %collective-permute-start.8 = (f32[8,128]{1,0:T(8,128)S(1)}, f32[8,128]{1,0:T(8,128)S(1)}, u32[]{:S(2)}, u32[]{:S(2)}) collective-permute-start(f32[8,128]{1,0:T(8,128)S(1)} %norm.1), channel_id=1, source_target_pairs={{0,1},{1,0},{2,3},{3,2},{4,5},{5,4},{6,7},{7,6},{8,9},{9,8},{10,11... | collective-permute-start | bytes 12296 | tf_op jit(solution)/shard_map/ppermute | solution.py:339
  46.5 13.4 %copy-start.1 = (s32[4,4]{1,0:T(4,128)S(1)}, s32[4,4]{1,0:T(4,128)}, u32[]{:S(2)}) copy-start(s32[4,4]{1,0:T(4,128)} %owner_slot.1) | copy-start | bytes 196
  47.3 11.4 %collective-permute-start.11 = (bf16[528,256]{1,0:T(8,128)(2,1)S(1)}, bf16[528,256]{1,0:T(8,128)(2,1)S(1)}, u32[]{:S(2)}, u32[]{:S(2)}) collective-permute-start(bf16[528,256]{1,0:T(8,128)(2,1)S(1)} %newton.1.folded.after), channel_id=1, source_target_pairs={{0,3},{1,2},{2,1},{3,0},{4,7},{5,6},{6,5},{7,4},{8,11},{9,10},{10,... | collective-permute-start | bytes 811016 | tf_op jit(solution)/shard_map/ppermute | solution.py:339
  49.3 7.5 %collective-permute-start.15 = (f32[8,128]{1,0:T(8,128)S(1)}, f32[8,128]{1,0:T(8,128)S(1)}, u32[]{:S(2)}, u32[]{:S(2)}) collective-permute-start(f32[8,128]{1,0:T(8,128)S(1)} %add_add_fusion.1), channel_id=1, source_target_pairs={{0,20},{1,21},{2,22},{3,23},{4,16},{5,17},{6,18},{7,19},{8,28},{9,... | collective-permute-start | bytes 12296 | tf_op jit(solution)/shard_map/ppermute | solution.py:339
  53.6 3.6 %collective-permute-start.14 = (f32[8,128]{1,0:T(8,128)S(1)}, f32[8,128]{1,0:T(8,128)S(1)}, u32[]{:S(2)}, u32[]{:S(2)}) collective-permute-start(f32[8,128]{1,0:T(8,128)S(1)} %add_add_fusion.1), channel_id=1, source_target_pairs={{0,16},{1,17},{2,18},{3,19},{4,20},{5,21},{6,22},{7,23},{8,24},{9,... | collective-permute-start | bytes 12296 | tf_op jit(solution)/shard_map/ppermute | solution.py:339
  54.1 4.5 %collective-permute-start.13 = (f32[8,128]{1,0:T(8,128)S(1)}, f32[8,128]{1,0:T(8,128)S(1)}, u32[]{:S(2)}, u32[]{:S(2)}) collective-permute-start(f32[8,128]{1,0:T(8,128)S(1)} %add_add_fusion.1), channel_id=1, source_target_pairs={{0,4},{1,5},{2,6},{3,7},{4,0},{5,1},{6,2},{7,3},{8,12},{9,13},{10,... | collective-permute-start | bytes 12296 | tf_op jit(solution)/shard_map/ppermute | solution.py:339
  58.7 1.2 %collective-permute-start.16 = (f32[8,128]{1,0:T(8,128)S(1)}, f32[8,128]{1,0:T(8,128)S(1)}, u32[]{:S(2)}, u32[]{:S(2)}) collective-permute-start(f32[8,128]{1,0:T(8,128)S(1)} %add_add_fusion), channel_id=1, source_target_pairs={{0,8},{1,9},{2,10},{3,11},{4,12},{5,13},{6,14},{7,15},{8,0},{9,1},... | collective-permute-start | bytes 12296 | tf_op jit(solution)/shard_map/ppermute | solution.py:339

commit v8 on v7

--- a/solution.py
+++ b/solution.py
@@ -56,11 +56,19 @@
     return first, last
 
 
-def stat_kernel(order, x_ref, *out):
-    for place in (1, 2, 3, 0):
-        start = pl.multiple_of(order[place] * BLK, BLK)
-        left = x_ref[:, pl.ds(start, HALF)]
-        right = x_ref[:, pl.ds(pl.multiple_of(start + HALF, HALF), HALF)]
+def stat_kernel(order, x_ref, *refs):
+    out, held, arrived = refs[:QUAD], refs[QUAD], refs[QUAD + 1]
+    places = (1, 2, 3, 0)
+
+    def copy(place):
+        columns = pl.ds(pl.multiple_of(order[place] * BLK, BLK), BLK)
+        return pltpu.make_async_copy(x_ref.at[:, columns], held.at[place], arrived.at[place])
+
+    for place in places:
+        copy(place).start()
+    for place in places:
+        copy(place).wait()
+        left, right = held[place, :, :HALF], held[place, :, HALF:]
         along = ((0,), (0,))
         out[place][:HALF] = dot(left, right, along).astype(BF16)
         body, diagonal = fold(dot(left, left, along), dot(right, right, along))
@@ -72,11 +80,15 @@
     return pl.pallas_call(
         stat_kernel,
         out_shape=[jax.ShapeDtypeStruct((FOLD, HALF), BF16)] * QUAD,
-        in_specs=[SMEM, VMEM],
+        in_specs=[SMEM, ANY],
         out_specs=[VMEM] * QUAD,
+        scratch_shapes=[
+            pltpu.VMEM((QUAD, activations.shape[0], BLK), BF16),
+            pltpu.SemaphoreType.DMA((QUAD,)),
+        ],
         compiler_params=params(12),
         name="statistics",
-    )(order, activations)
+    )(order, pltpu.with_memory_space_constraint(activations, pltpu.HBM))
 
 
 def chunks(width, size):
@@ -263,10 +275,10 @@
     roots, folded, blocks = refs[:EARLY], refs[EARLY:QUAD], refs[QUAD : 2 * QUAD]
     update_ref, owned_ref = refs[2 * QUAD : 2 * QUAD + 2]
     scaled = refs[2 * QUAD + 2 : 3 * QUAD + 2]
-    late, owned, sent, stored = refs[3 * QUAD + 2 :]
+    late, empty, sent, stored = refs[3 * QUAD + 2 :]
     both = jnp.sum(sums[...], axis=1, keepdims=True)
     ratio = jnp.sqrt(both[:1] / (both[1:2] + 1e-06))
-    parts = list(chunks(blocks[0].shape[1], BLK))
+    columns = blocks[0].shape[1]
     waits = []
 
     def send(place, rows, columns):
@@ -279,34 +291,41 @@
         copy.start()
         waits.append(copy)
 
-    def rescale(place):
-        for start in range(0, BLK, BAND):
-            rows = pl.ds(start, BAND)
-            scaled[place][rows] = (blocks[place][rows].astype(F32) * ratio).astype(BF16)
-            send(place, rows, pl.ds(0, blocks[0].shape[1]))
-
-    for place in range(EARLY):
-        rescale(place)
+    def store(source, slot):
+        return pltpu.make_async_copy(source, owned_ref.at[slot], stored.at[slot])
+
+    def rescale(place, rows):
+        scaled[place][rows] = (blocks[place][rows].astype(F32) * ratio).astype(BF16)
+
+    bands = [(place, pl.ds(i, BAND)) for place in range(EARLY) for i in range(0, BLK, BAND)]
+    products = [(place, part) for place in range(EARLY, QUAD) for part in chunks(columns, BLK)]
+    rescale(*bands[0])
+    send(*bands[0], pl.ds(0, columns))
+    bands = bands[1:]
+    empty[...] = jnp.zeros_like(empty)
     for place in range(EARLY, QUAD):
-        final = late.at[place - EARLY]
-        unfold_root(folded[place - EARLY], final)
-        for part in parts:
-            product = dot(final[...], blocks[place][:, part])
-            scaled[place][:, part] = (product * ratio).astype(BF16)
-            send(place, pl.ds(0, BLK), part)
-    owned[...] = jnp.zeros_like(owned)
-    for place in range(QUAD):
-        for slot in range(SLOTS):
-
-            @pl.when(owner_slot[order[QUAD], order[place]] == order[QUAD + 1] + slot)
-            def _():
-                owned[slot] = roots[place][...] if place < EARLY else late[place - EARLY]
-
-    store = pltpu.make_async_copy(owned, owned_ref, stored)
-    store.start()
+        unfold_root(folded[place - EARLY], late.at[place - EARLY])
+    for slot in range(SLOTS):
+        mine = [owner_slot[order[QUAD], order[place]] == order[QUAD + 1] + slot for place in range(QUAD)]
+        for place in range(QUAD):
+            source = roots[place] if place < EARLY else late.at[place - EARLY]
+            pl.when(mine[place])(store(source, slot).start)
+        pl.when(jnp.logical_not(functools.reduce(jnp.logical_or, mine)))(store(empty, slot).start)
+    for place, part in products:
+        product = dot(late[place - EARLY], blocks[place][:, part])
+        scaled[place][:, part] = (product * ratio).astype(BF16)
+        band, bands = bands[:1], bands[1:]
+        for one in band:
+            rescale(*one)
+            send(*one, pl.ds(0, columns))
+        send(place, pl.ds(0, BLK), part)
+    for one in bands:
+        rescale(*one)
+        send(*one, pl.ds(0, columns))
     for copy in waits:
         copy.wait()
-    store.wait()
+    for slot in range(SLOTS):
+        store(empty, slot).wait()
 
 
 def finish(order, owner_slot, sums, roots, folded, blocks):
@@ -324,9 +343,9 @@
         input_output_aliases={3 + QUAD + place: 2 + place for place in range(QUAD)},
         scratch_shapes=[
             pltpu.VMEM((QUAD - EARLY, BLK, BLK), BF16),
-            pltpu.VMEM((SLOTS, BLK, BLK), BF16),
+            pltpu.VMEM((BLK, BLK), BF16),
             pltpu.SemaphoreType.DMA((pieces,)),
-            pltpu.SemaphoreType.DMA,
+            pltpu.SemaphoreType.DMA((SLOTS,)),
         ],
         compiler_params=params(12),
         name="finish",
@@ -371,8 +390,8 @@
         flip *= 2
         other = swap(mine, flip)
 
-    mine, grams[1] = lax.optimization_barrier((mine, grams[1]))
     across = swap(grams[3], 1)
+    across, grams[1] = lax.optimization_barrier((across, grams[1]))
     from_y = swap(grams[1], 1)
     from_z = swap(add(grams[2], across), 2)
     root = newton(tokens_all, squares, mine, other)
@@ -384,7 +403,7 @@
         roots.append(root)
 
     sums = norm(root, grams[0], from_y, from_z, squares)
-    arrivals = {0: [1], 1: [2, 3]}
+    arrivals = {0: [1, 2], 1: [3]}
     for step, flips in enumerate(rounds()):
         received = [swap(sums, flip) for flip in flips]
         if step < EARLY:

time: 69.2 us -> 69.3 us (level)
  local copies, waits for them, and re-layouts: 1.6 us -> 0.01 us
  Pallas kernels: 29.9 us -> 31.4 us
  starting transfers between devices: 24 us -> 24.7 us
    pallas_call x1, Pallas kernels: 1.59 us -> 3.54 us  [statistics(): pl.pallas_call(stat_kernel, out_shape=[jax.ShapeDtypeStruct((FOLD, HALF),...]
    unnamed x4 -> x2, local copies, waits for them, and re-layouts: 1.6 us -> 0.01 us
where the time goes in v8:
time: 69.3 us; the launch traced here: 69.2 us
  Pallas kernels  31.4 us (45%)
  starting transfers between devices  24.7 us (36%)
  waiting for transfers between devices  11.9 us (17%)
  between operations  0.92 us (1%)
    ppermute x17, starting transfers between devices, swap(): return lax.ppermute(value, axes, [(i, i ^ flip) for i in range(count)])  24.7 us
    ppermute x17, waiting for transfers between devices, swap(): return lax.ppermute(value, axes, [(i, i ^ flip) for i in range(count)])  11.9 us
    pallas_call x1, Pallas kernels, gram(): pl.pallas_call(gram_kernel, out_shape=[pltpu.VMEM((BLK, columns), BF16)]...  10.8 us
    pallas_call x1, Pallas kernels, finish(): pl.pallas_call(finish_kernel, out_shape=[jax.ShapeDtypeStruct((QUAD * BLK...  8.7 us
    pallas_call x2, Pallas kernels, multiply(): pl.pallas_call(multiply_kernel, out_shape=[pltpu.VMEM(held.shape, BF16),...  4.59 us
    pallas_call x1, Pallas kernels, statistics(): pl.pallas_call(stat_kernel, out_shape=[jax.ShapeDtypeStruct((FOLD, HALF),...  3.54 us
    pallas_call x1, Pallas kernels, newton(): pl.pallas_call(functools.partial(newton_kernel, tokens), out_shape=jax.Sh...  3.19 us
  transfers between devices with their start and end apart: 17, of which 6 were waited for; matrix products, arithmetic and copies ran while one was open for 0% of the time, Pallas kernels for 28%

profile of v8, /device:TPU:0, one launch (start us, length us, event | category | flops | bytes accessed | tf_op | source)
XLA Modules:
  0.0 69.2 jit_solution(2907375757646206596)
XLA Ops:
  0.7 0.1 pad_add_fusion.order
  0.7 3.5 %statistics.1 = (bf16[528,256]{1,0:T(8,128)(2,1)S(1)}, bf16[528,256]{1,0:T(8,128)(2,1)S(1)}, bf16[528,256]{1,0:T(8,128)(2,1)S(1)}, bf16[528,256]{1,0:T(8,128)(2,1)S(1)}) custom-call(s32[6]{0:T(128)S(1)} %pad_add_fusion.order, bf16[512,2048]{1,0:T(8,128)(2,1)} %x_ref.1), custom_call_target="tpu_custom_call" | custom-call | tf_op jit(solution)/shard_map/statistics/pallas_call | solution.py:80
  4.3 3.0 %collective-permute-start = (bf16[528,256]{1,0:T(8,128)(2,1)S(1)}, bf16[528,256]{1,0:T(8,128)(2,1)S(1)}, u32[]{:S(2)}, u32[]{:S(2)}) collective-permute-start(bf16[528,256]{1,0:T(8,128)(2,1)S(1)} %get-tuple-element.45), channel_id=1, source_target_pairs={{0,1},{1,0},{2,3},{3,2},{4,5},{5,4},{6,7},{7,6},{8,9},{9,8},{10,11... | collective-permute-start | bytes 811016 | tf_op jit(solution)/shard_map/ppermute | solution.py:358
  7.3 1.6 %collective-permute-start.1 = (bf16[528,256]{1,0:T(8,128)(2,1)S(1)}, bf16[528,256]{1,0:T(8,128)(2,1)S(1)}, u32[]{:S(2)}, u32[]{:S(2)}) collective-permute-start(bf16[528,256]{1,0:T(8,128)(2,1)S(1)} %get-tuple-element.46), channel_id=1, source_target_pairs={{0,2},{1,3},{2,0},{3,1},{4,6},{5,7},{6,4},{7,5},{8,10},{9,11},{10,... | collective-permute-start | bytes 811016 | tf_op jit(solution)/shard_map/ppermute | solution.py:358
  8.9 10.8 %gram.1 = (bf16[512,3584]{1,0:T(8,128)(2,1)S(1)}, bf16[512,3584]{1,0:T(8,128)(2,1)S(1)}, bf16[512,3584]{1,0:T(8,128)(2,1)S(1)}, bf16[512,3584]{1,0:T(8,128)(2,1)...) custom-call(s32[6]{0:T(128)S(1)} %pad_add_fusion.order, ...), custom_call_target="tpu_custom_call" | custom-call | flops 7516192768 | bytes 14680064 | tf_op jit(solution)/shard_map/gram/pallas_call | solution.py:144
  19.7 2.0 %collective-permute-start.4 = (bf16[528,256]{1,0:T(8,128)(2,1)S(1)}, bf16[528,256]{1,0:T(8,128)(2,1)S(1)}, u32[]{:S(2)}, u32[]{:S(2)}) collective-permute-start(bf16[528,256]{1,0:T(8,128)(2,1)S(1)} %get-tuple-element.49), channel_id=1, source_target_pairs={{0,1},{1,0},{2,3},{3,2},{4,5},{5,4},{6,7},{7,6},{8,9},{9,8},{10,11... | collective-permute-start | bytes 811016 | tf_op jit(solution)/shard_map/ppermute | solution.py:358
  21.7 0.2 add_convert_fusion.1.mine
  21.8 2.6 %collective-permute-start.3 = (bf16[528,256]{1,0:T(8,128)(2,1)S(1)}, bf16[528,256]{1,0:T(8,128)(2,1)S(1)}, u32[]{:S(2)}, u32[]{:S(2)}) collective-permute-start(bf16[528,256]{1,0:T(8,128)(2,1)S(1)} %add_convert_fusion.1.mine), channel_id=1, source_target_pairs={{0,4},{1,5},{2,6},{3,7},{4,0},{5,1},{6,2},{7,3},{8,12},{9,13},{10,... | collective-permute-start | bytes 811016 | tf_op jit(solution)/shard_map/ppermute | solution.py:358
  24.5 2.9 %collective-permute-done.4 = bf16[528,256]{1,0:T(8,128)(2,1)S(1)} collective-permute-done((bf16[528,256]{1,0:T(8,128)(2,1)S(1)}, bf16[528,256]{1,0:T(8,128)(2,1)S(1)}, u32[]{:S(2)}, u32[]{:S(2)}) %collective-permute-start.4) | collective-permute-done | bytes 270368 | tf_op jit(solution)/shard_map/ppermute | solution.py:358
  27.4 0.1 add_convert_fusion
  27.5 1.8 %collective-permute-start.6 = (bf16[528,256]{1,0:T(8,128)(2,1)S(1)}, bf16[528,256]{1,0:T(8,128)(2,1)S(1)}, u32[]{:S(2)}, u32[]{:S(2)}) collective-permute-start(bf16[528,256]{1,0:T(8,128)(2,1)S(1)} %add_convert_fusion), channel_id=1, source_target_pairs={{0,2},{1,3},{2,0},{3,1},{4,6},{5,7},{6,4},{7,5},{8,10},{9,11},{10,... | collective-permute-start | bytes 811016 | tf_op jit(solution)/shard_map/ppermute | solution.py:358
  29.2 1.5 %collective-permute-start.5 = (bf16[528,256]{1,0:T(8,128)(2,1)S(1)}, bf16[528,256]{1,0:T(8,128)(2,1)S(1)}, u32[]{:S(2)}, u32[]{:S(2)}) collective-permute-start(bf16[528,256]{1,0:T(8,128)(2,1)S(1)} %get-tuple-element.51), channel_id=1, source_target_pairs={{0,1},{1,0},{2,3},{3,2},{4,5},{5,4},{6,7},{7,6},{8,9},{9,8},{10,11... | collective-permute-start | bytes 811016 | tf_op jit(solution)/shard_map/ppermute | solution.py:358
  30.8 5.0 %collective-permute-done.3.other = bf16[528,256]{1,0:T(8,128)(2,1)S(1)} collective-permute-done((bf16[528,256]{1,0:T(8,128)(2,1)S(1)}, bf16[528,256]{1,0:T(8,128)(2,1)S(1)}, u32[]{:S(2)}, u32[]{:S(2)}) %collective-permute-start.3) | collective-permute-done | bytes 270368 | tf_op jit(solution)/shard_map/ppermute | solution.py:358
  35.8 3.2 %newton.1.folded.after = bf16[528,256]{1,0:T(8,128)(2,1)S(1)} custom-call(f32[1,256]{1,0:T(1,128)S(1)} %get-tuple-element.44.after.squares, bf16[528,256]{1,0:T(8,128)(2,1)S(1)} %add_convert_fusion.1.mine, bf16[528,256]{1,0:T(8,128)(2,1)S(1)} %collective-permute-done.3.other), custom_call_target="tpu_custom_call" | custom-call | flops 2147483648 | bytes 2097152 | tf_op jit(solution)/shard_map/newton/pallas_call | solution.py:203
  39.0 0.8 %collective-permute-start.8 = (bf16[528,256]{1,0:T(8,128)(2,1)S(1)}, bf16[528,256]{1,0:T(8,128)(2,1)S(1)}, u32[]{:S(2)}, u32[]{:S(2)}) collective-permute-start(bf16[528,256]{1,0:T(8,128)(2,1)S(1)} %newton.1.folded.after), channel_id=1, source_target_pairs={{0,1},{1,0},{2,3},{3,2},{4,5},{5,4},{6,7},{7,6},{8,9},{9,8},{10,11... | collective-permute-start | bytes 811016 | tf_op jit(solution)/shard_map/ppermute | solution.py:358
  39.8 0.6 collective-permute-start.7
  40.5 0.6 norm.1
  41.0 2.2 %collective-permute-start.11 = (f32[8,128]{1,0:T(8,128)S(1)}, f32[8,128]{1,0:T(8,128)S(1)}, u32[]{:S(2)}, u32[]{:S(2)}) collective-permute-start(f32[8,128]{1,0:T(8,128)S(1)} %norm.1), channel_id=1, source_target_pairs={{0,3},{1,2},{2,1},{3,0},{4,7},{5,6},{6,5},{7,4},{8,11},{9,10},{10,... | collective-permute-start | bytes 12296 | tf_op jit(solution)/shard_map/ppermute | solution.py:358
  43.2 0.6 collective-permute-start.10
  43.8 0.8 %collective-permute-start.9 = (f32[8,128]{1,0:T(8,128)S(1)}, f32[8,128]{1,0:T(8,128)S(1)}, u32[]{:S(2)}, u32[]{:S(2)}) collective-permute-start(f32[8,128]{1,0:T(8,128)S(1)} %norm.1), channel_id=1, source_target_pairs={{0,1},{1,0},{2,3},{3,2},{4,5},{5,4},{6,7},{7,6},{8,9},{9,8},{10,11... | collective-permute-start | bytes 12296 | tf_op jit(solution)/shard_map/ppermute | solution.py:358
  44.6 2.3 %multiply.2 = (bf16[512,3584]{1,0:T(8,128)(2,1)S(1)}, bf16[512,512]{1,0:T(8,128)(2,1)S(1)}) custom-call(bf16[528,256]{1,0:T(8,128)(2,1)S(1)} %newton.1.folded.after, bf16[528,256]{1,0:T(8,128)(2,1)S(1)} %newton.1.folded.after, bf16[512,3584]{1,0:T(8,128)(2,1)S(1)} %get-tuple-element.54.held_ref), custom_call_target="tpu_custom_call", output_to_operand_aliasing={{0}: (2, {})} | custom-call | flops 1880000000 | bytes 1 | tf_op jit(solution)/shard_map/multiply/pallas_call | solution.py:262
  46.9 0.8 %collective-permute-done.11 = f32[8,128]{1,0:T(8,128)S(1)} collective-permute-done((f32[8,128]{1,0:T(8,128)S(1)}, f32[8,128]{1,0:T(8,128)S(1)}, u32[]{:S(2)}, u32[]{:S(2)}) %collective-permute-start.11) | collective-permute-done | bytes 4128 | tf_op jit(solution)/shard_map/ppermute | solution.py:358
  47.7 1.9 %collective-permute-start.12 = (bf16[528,256]{1,0:T(8,128)(2,1)S(1)}, bf16[528,256]{1,0:T(8,128)(2,1)S(1)}, u32[]{:S(2)}, u32[]{:S(2)}) collective-permute-start(bf16[528,256]{1,0:T(8,128)(2,1)S(1)} %newton.1.folded.after), channel_id=1, source_target_pairs={{0,3},{1,2},{2,1},{3,0},{4,7},{5,6},{6,5},{7,4},{8,11},{9,10},{10,... | collective-permute-start | bytes 811016 | tf_op jit(solution)/shard_map/ppermute | solution.py:358
  49.6 4.3 %collective-permute-start.15 = (f32[8,128]{1,0:T(8,128)S(1)}, f32[8,128]{1,0:T(8,128)S(1)}, u32[]{:S(2)}, u32[]{:S(2)}) collective-permute-start(f32[8,128]{1,0:T(8,128)S(1)} %add_add_fusion.1), channel_id=1, source_target_pairs={{0,20},{1,21},{2,22},{3,23},{4,16},{5,17},{6,18},{7,19},{8,28},{9,... | collective-permute-start | bytes 12296 | tf_op jit(solution)/shard_map/ppermute | solution.py:358
  54.0 0.6 collective-permute-start.14
  54.5 0.3 collective-permute-start.13
  54.8 2.3 %multiply.3 = (bf16[512,3584]{1,0:T(8,128)(2,1)S(1)}, bf16[512,512]{1,0:T(8,128)(2,1)S(1)}) custom-call(bf16[528,256]{1,0:T(8,128)(2,1)S(1)} %collective-permute-done.8.after.folded, bf16[528,256]{1,0:T(8,128)(2,1)S(1)} %collective-permute-done.8.after.folded, bf16[512,3584]{1,0:T(8,128)(2,1)S(1)} %get-tuple-element.66.held_ref), custom_call_target="tpu_custom_call", output_to_operand_aliasing={{0}: (2, {})} | custom-call | flops 1880000000 | bytes 1 | tf_op jit(solution)/shard_map/multiply/pallas_call | solution.py:262
  57.1 0.5 collective-permute-done.14
  57.6 1.5 %collective-permute-done.13 = f32[8,128]{1,0:T(8,128)S(1)} collective-permute-done((f32[8,128]{1,0:T(8,128)S(1)}, f32[8,128]{1,0:T(8,128)S(1)}, u32[]{:S(2)}, u32[]{:S(2)}) %collective-permute-start.13) | collective-permute-done | bytes 4128 | tf_op jit(solution)/shard_map/ppermute | solution.py:358
  59.1 0.1 collective-permute-start.16
  59.1 1.2 %collective-permute-done.16 = f32[8,128]{1,0:T(8,128)S(1)} collective-permute-done((f32[8,128]{1,0:T(8,128)S(1)}, f32[8,128]{1,0:T(8,128)S(1)}, u32[]{:S(2)}, u32[]{:S(2)}) %collective-permute-start.16) | collective-permute-done | bytes 4128 | tf_op jit(solution)/shard_map/ppermute | solution.py:358
  60.3 8.7 %finish.1 = (bf16[2048,3584]{1,0:T(8,128)(2,1)}, bf16[2,512,512]{2,1,0:T(8,128)(2,1)}, bf16[512,3584]{1,0:T(8,128)(2,1)S(1)}, bf16[512,3584]{1,0:T(8,128)(2,1)S(...) custom-call(s32[6]{0:T(128)S(1)} %pad_add_fusion.order, ...), custom_call_target="tpu_custom_call", output_to_operand_aliasing={{2}: (7, {}), {3}: (8, {}), {4}: (9, {}), {5}: (10, {})} | custom-call | tf_op jit(solution)/shard_map/finish/pallas_call | solution.py:334
  (18 shorter events, 0.1 us)
Async XLA Ops:
  4.3 17.4 %collective-permute-start = (bf16[528,256]{1,0:T(8,128)(2,1)S(1)}, bf16[528,256]{1,0:T(8,128)(2,1)S(1)}, u32[]{:S(2)}, u32[]{:S(2)}) collective-permute-start(bf16[528,256]{1,0:T(8,128)(2,1)S(1)} %get-tuple-element.45), channel_id=1, source_target_pairs={{0,1},{1,0},{2,3},{3,2},{4,5},{5,4},{6,7},{7,6},{8,9},{9,8},{10,11... | collective-permute-start | bytes 811016 | tf_op jit(solution)/shard_map/ppermute | solution.py:358
  7.3 14.4 %collective-permute-start.1 = (bf16[528,256]{1,0:T(8,128)(2,1)S(1)}, bf16[528,256]{1,0:T(8,128)(2,1)S(1)}, u32[]{:S(2)}, u32[]{:S(2)}) collective-permute-start(bf16[528,256]{1,0:T(8,128)(2,1)S(1)} %get-tuple-element.46), channel_id=1, source_target_pairs={{0,2},{1,3},{2,0},{3,1},{4,6},{5,7},{6,4},{7,5},{8,10},{9,11},{10,... | collective-permute-start | bytes 811016 | tf_op jit(solution)/shard_map/ppermute | solution.py:358
  8.9 12.8 %collective-permute-start.2 = (bf16[528,256]{1,0:T(8,128)(2,1)S(1)}, bf16[528,256]{1,0:T(8,128)(2,1)S(1)}, u32[]{:S(2)}, u32[]{:S(2)}) collective-permute-start(bf16[528,256]{1,0:T(8,128)(2,1)S(1)} %get-tuple-element.47), channel_id=1, source_target_pairs={{0,3},{1,2},{2,1},{3,0},{4,7},{5,6},{6,5},{7,4},{8,11},{9,10},{10,... | collective-permute-start | bytes 811016 | tf_op jit(solution)/shard_map/ppermute | solution.py:358
  19.7 7.7 %collective-permute-start.4 = (bf16[528,256]{1,0:T(8,128)(2,1)S(1)}, bf16[528,256]{1,0:T(8,128)(2,1)S(1)}, u32[]{:S(2)}, u32[]{:S(2)}) collective-permute-start(bf16[528,256]{1,0:T(8,128)(2,1)S(1)} %get-tuple-element.49), channel_id=1, source_target_pairs={{0,1},{1,0},{2,3},{3,2},{4,5},{5,4},{6,7},{7,6},{8,9},{9,8},{10,11... | collective-permute-start | bytes 811016 | tf_op jit(solution)/shard_map/ppermute | solution.py:358
  21.8 14.0 %collective-permute-start.3 = (bf16[528,256]{1,0:T(8,128)(2,1)S(1)}, bf16[528,256]{1,0:T(8,128)(2,1)S(1)}, u32[]{:S(2)}, u32[]{:S(2)}) collective-permute-start(bf16[528,256]{1,0:T(8,128)(2,1)S(1)} %add_convert_fusion.1.mine), channel_id=1, source_target_pairs={{0,4},{1,5},{2,6},{3,7},{4,0},{5,1},{6,2},{7,3},{8,12},{9,13},{10,... | collective-permute-start | bytes 811016 | tf_op jit(solution)/shard_map/ppermute | solution.py:358
  27.5 13.0 %collective-permute-start.6 = (bf16[528,256]{1,0:T(8,128)(2,1)S(1)}, bf16[528,256]{1,0:T(8,128)(2,1)S(1)}, u32[]{:S(2)}, u32[]{:S(2)}) collective-permute-start(bf16[528,256]{1,0:T(8,128)(2,1)S(1)} %add_convert_fusion), channel_id=1, source_target_pairs={{0,2},{1,3},{2,0},{3,1},{4,6},{5,7},{6,4},{7,5},{8,10},{9,11},{10,... | collective-permute-start | bytes 811016 | tf_op jit(solution)/shard_map/ppermute | solution.py:358
  29.2 11.2 %collective-permute-start.5 = (bf16[528,256]{1,0:T(8,128)(2,1)S(1)}, bf16[528,256]{1,0:T(8,128)(2,1)S(1)}, u32[]{:S(2)}, u32[]{:S(2)}) collective-permute-start(bf16[528,256]{1,0:T(8,128)(2,1)S(1)} %get-tuple-element.51), channel_id=1, source_target_pairs={{0,1},{1,0},{2,3},{3,2},{4,5},{5,4},{6,7},{7,6},{8,9},{9,8},{10,11... | collective-permute-start | bytes 811016 | tf_op jit(solution)/shard_map/ppermute | solution.py:358
  39.0 10.6 %collective-permute-start.8 = (bf16[528,256]{1,0:T(8,128)(2,1)S(1)}, bf16[528,256]{1,0:T(8,128)(2,1)S(1)}, u32[]{:S(2)}, u32[]{:S(2)}) collective-permute-start(bf16[528,256]{1,0:T(8,128)(2,1)S(1)} %newton.1.folded.after), channel_id=1, source_target_pairs={{0,1},{1,0},{2,3},{3,2},{4,5},{5,4},{6,7},{7,6},{8,9},{9,8},{10,11... | collective-permute-start | bytes 811016 | tf_op jit(solution)/shard_map/ppermute | solution.py:358
  39.8 9.8 %collective-permute-start.7 = (bf16[528,256]{1,0:T(8,128)(2,1)S(1)}, bf16[528,256]{1,0:T(8,128)(2,1)S(1)}, u32[]{:S(2)}, u32[]{:S(2)}) collective-permute-start(bf16[528,256]{1,0:T(8,128)(2,1)S(1)} %newton.1.folded.after), channel_id=1, source_target_pairs={{0,2},{1,3},{2,0},{3,1},{4,6},{5,7},{6,4},{7,5},{8,10},{9,11},{10,... | collective-permute-start | bytes 811016 | tf_op jit(solution)/shard_map/ppermute | solution.py:358
  41.0 6.6 %collective-permute-start.11 = (f32[8,128]{1,0:T(8,128)S(1)}, f32[8,128]{1,0:T(8,128)S(1)}, u32[]{:S(2)}, u32[]{:S(2)}) collective-permute-start(f32[8,128]{1,0:T(8,128)S(1)} %norm.1), channel_id=1, source_target_pairs={{0,3},{1,2},{2,1},{3,0},{4,7},{5,6},{6,5},{7,4},{8,11},{9,10},{10,... | collective-permute-start | bytes 12296 | tf_op jit(solution)/shard_map/ppermute | solution.py:358
  43.2 6.4 %collective-permute-start.10 = (f32[8,128]{1,0:T(8,128)S(1)}, f32[8,128]{1,0:T(8,128)S(1)}, u32[]{:S(2)}, u32[]{:S(2)}) collective-permute-start(f32[8,128]{1,0:T(8,128)S(1)} %norm.1), channel_id=1, source_target_pairs={{0,2},{1,3},{2,0},{3,1},{4,6},{5,7},{6,4},{7,5},{8,10},{9,11},{10,... | collective-permute-start | bytes 12296 | tf_op jit(solution)/shard_map/ppermute | solution.py:358
  43.8 5.8 %collective-permute-start.9 = (f32[8,128]{1,0:T(8,128)S(1)}, f32[8,128]{1,0:T(8,128)S(1)}, u32[]{:S(2)}, u32[]{:S(2)}) collective-permute-start(f32[8,128]{1,0:T(8,128)S(1)} %norm.1), channel_id=1, source_target_pairs={{0,1},{1,0},{2,3},{3,2},{4,5},{5,4},{6,7},{7,6},{8,9},{9,8},{10,11... | collective-permute-start | bytes 12296 | tf_op jit(solution)/shard_map/ppermute | solution.py:358
  46.9 13.4 %copy-start = (s32[4,4]{1,0:T(4,128)S(1)}, s32[4,4]{1,0:T(4,128)}, u32[]{:S(2)}) copy-start(s32[4,4]{1,0:T(4,128)} %owner_slot.1) | copy-start | bytes 196
  47.7 11.4 %collective-permute-start.12 = (bf16[528,256]{1,0:T(8,128)(2,1)S(1)}, bf16[528,256]{1,0:T(8,128)(2,1)S(1)}, u32[]{:S(2)}, u32[]{:S(2)}) collective-permute-start(bf16[528,256]{1,0:T(8,128)(2,1)S(1)} %newton.1.folded.after), channel_id=1, source_target_pairs={{0,3},{1,2},{2,1},{3,0},{4,7},{5,6},{6,5},{7,4},{8,11},{9,10},{10,... | collective-permute-start | bytes 811016 | tf_op jit(solution)/shard_map/ppermute | solution.py:358
  49.6 7.5 %collective-permute-start.15 = (f32[8,128]{1,0:T(8,128)S(1)}, f32[8,128]{1,0:T(8,128)S(1)}, u32[]{:S(2)}, u32[]{:S(2)}) collective-permute-start(f32[8,128]{1,0:T(8,128)S(1)} %add_add_fusion.1), channel_id=1, source_target_pairs={{0,20},{1,21},{2,22},{3,23},{4,16},{5,17},{6,18},{7,19},{8,28},{9,... | collective-permute-start | bytes 12296 | tf_op jit(solution)/shard_map/ppermute | solution.py:358
  54.0 3.6 %collective-permute-start.14 = (f32[8,128]{1,0:T(8,128)S(1)}, f32[8,128]{1,0:T(8,128)S(1)}, u32[]{:S(2)}, u32[]{:S(2)}) collective-permute-start(f32[8,128]{1,0:T(8,128)S(1)} %add_add_fusion.1), channel_id=1, source_target_pairs={{0,16},{1,17},{2,18},{3,19},{4,20},{5,21},{6,22},{7,23},{8,24},{9,... | collective-permute-start | bytes 12296 | tf_op jit(solution)/shard_map/ppermute | solution.py:358
  54.5 4.5 %collective-permute-start.13 = (f32[8,128]{1,0:T(8,128)S(1)}, f32[8,128]{1,0:T(8,128)S(1)}, u32[]{:S(2)}, u32[]{:S(2)}) collective-permute-start(f32[8,128]{1,0:T(8,128)S(1)} %add_add_fusion.1), channel_id=1, source_target_pairs={{0,4},{1,5},{2,6},{3,7},{4,0},{5,1},{6,2},{7,3},{8,12},{9,13},{10,... | collective-permute-start | bytes 12296 | tf_op jit(solution)/shard_map/ppermute | solution.py:358
  59.1 1.2 %collective-permute-start.16 = (f32[8,128]{1,0:T(8,128)S(1)}, f32[8,128]{1,0:T(8,128)S(1)}, u32[]{:S(2)}, u32[]{:S(2)}) collective-permute-start(f32[8,128]{1,0:T(8,128)S(1)} %add_add_fusion), channel_id=1, source_target_pairs={{0,8},{1,9},{2,10},{3,11},{4,12},{5,13},{6,14},{7,15},{8,0},{9,1},... | collective-permute-start | bytes 12296 | tf_op jit(solution)/shard_map/ppermute | solution.py:358

commit v9 on v8

--- a/solution.py
+++ b/solution.py
@@ -14,7 +14,7 @@
 ITERS = 3
 SLOTS = 2
 QUAD = 4
-EARLY = 2
+EARLY = 3
 BAND = 128
 ROWS = 8
 LANES = 128
@@ -56,19 +56,11 @@
     return first, last
 
 
-def stat_kernel(order, x_ref, *refs):
-    out, held, arrived = refs[:QUAD], refs[QUAD], refs[QUAD + 1]
-    places = (1, 2, 3, 0)
-
-    def copy(place):
-        columns = pl.ds(pl.multiple_of(order[place] * BLK, BLK), BLK)
-        return pltpu.make_async_copy(x_ref.at[:, columns], held.at[place], arrived.at[place])
-
-    for place in places:
-        copy(place).start()
-    for place in places:
-        copy(place).wait()
-        left, right = held[place, :, :HALF], held[place, :, HALF:]
+def stat_kernel(order, x_ref, *out):
+    for place in (1, 2, 3, 0):
+        start = pl.multiple_of(order[place] * BLK, BLK)
+        left = x_ref[:, pl.ds(start, HALF)]
+        right = x_ref[:, pl.ds(pl.multiple_of(start + HALF, HALF), HALF)]
         along = ((0,), (0,))
         out[place][:HALF] = dot(left, right, along).astype(BF16)
         body, diagonal = fold(dot(left, left, along), dot(right, right, along))
@@ -80,15 +72,11 @@
     return pl.pallas_call(
         stat_kernel,
         out_shape=[jax.ShapeDtypeStruct((FOLD, HALF), BF16)] * QUAD,
-        in_specs=[SMEM, ANY],
+        in_specs=[SMEM, VMEM],
         out_specs=[VMEM] * QUAD,
-        scratch_shapes=[
-            pltpu.VMEM((QUAD, activations.shape[0], BLK), BF16),
-            pltpu.SemaphoreType.DMA((QUAD,)),
-        ],
         compiler_params=params(12),
         name="statistics",
-    )(order, pltpu.with_memory_space_constraint(activations, pltpu.HBM))
+    )(order, activations)
 
 
 def chunks(width, size):
@@ -101,7 +89,7 @@
 
 def gram_kernel(order, after, g_ref, *refs):
     held, folded = refs[:QUAD], refs[QUAD : 2 * QUAD]
-    norm_ref, top, last, arrived = refs[2 * QUAD :]
+    norm_ref, left, last, arrived = refs[2 * QUAD :]
     parts = list(chunks(g_ref.shape[1], 1792))
 
     def copy(place, index):
@@ -118,22 +106,19 @@
     for place in range(QUAD):
         for index, part in enumerate(parts):
             copy(place, index).wait()
-            upper = held[place][:HALF, part]
-            lower = held[place][HALF:, part]
+            whole = held[place][:, part]
             across = ((1,), (1,))
-            terms = dot(upper, upper, across), dot(upper, lower, across), dot(lower, lower, across)
+            terms = dot(whole, whole[:HALF], across), dot(whole[HALF:], whole[HALF:], across)
             if index == 0:
-                top[:, :HALF] = terms[0]
-                top[:, HALF:] = terms[1]
-                last[...] = terms[2]
+                left[...] = terms[0]
+                last[...] = terms[1]
             else:
-                top[:, :HALF] += terms[0]
-                top[:, HALF:] += terms[1]
-                last[...] += terms[2]
-        squares = jnp.where(row == col, top[:, :HALF] + last[...], 0.0)
+                left[...] += terms[0]
+                last[...] += terms[1]
+        squares = jnp.where(row == col, left[:HALF] + last[...], 0.0)
         norm_ref[...] += jnp.sum(squares, axis=0, keepdims=True)
-        body, diagonal = fold(top[:, :HALF], last[...])
-        folded[place][:HALF] = top[:, HALF:].astype(BF16)
+        body, diagonal = fold(left[:HALF], last[...])
+        folded[place][:HALF] = left[HALF:].astype(BF16)
         folded[place][HALF:BLK] = body.astype(BF16)
         folded[place][BLK:] = diagonal.astype(BF16)
 
@@ -149,7 +134,7 @@
         in_specs=[SMEM, ANY, ANY],
         out_specs=[VMEM] * (2 * QUAD + 1),
         scratch_shapes=[
-            pltpu.VMEM((HALF, BLK), F32),
+            pltpu.VMEM((BLK, HALF), F32),
             pltpu.VMEM((HALF, HALF), F32),
             pltpu.SemaphoreType.DMA((QUAD, parts)),
         ],
@@ -227,9 +212,9 @@
 def norm_kernel(folded, mine, from_y, from_z, squares, total_ref, root):
     unfold_root(folded, root)
     grams = mine[...].astype(F32) + from_y[...].astype(F32) + from_z[...].astype(F32)
-    upper = dot(root[:HALF], root[...])
-    last = dot(root[HALF:], root[:, HALF:])
-    first, cross = upper[:, :HALF], upper[:, HALF:]
+    first = dot(root[:HALF], root[:, :HALF])
+    lower = dot(root[HALF:], root[...])
+    cross, last = lower[:, :HALF], lower[:, HALF:]
     row, col = places()
     weights = jnp.where(row < col, 2.0 * first, jnp.where(row > col, 2.0 * last, first))
     terms = weights * grams[HALF:BLK] + 2.0 * cross * grams[:HALF]
@@ -361,7 +346,7 @@
 def rounds():
     peer_bits = lax.axis_size("dp").bit_length() - 1
     bits = [1 << i for i in range(peer_bits + lax.axis_size("pool").bit_length() - 1)]
-    bits = bits[:peer_bits] + bits[peer_bits:][::-1]
+    bits = bits[peer_bits:] + bits[:peer_bits]
     pairs = [bits[i : i + 2] for i in range(0, len(bits), 2)]
     return [pair if len(pair) == 1 else [*pair, sum(pair)] for pair in pairs]
 
@@ -403,7 +388,7 @@
         roots.append(root)
 
     sums = norm(root, grams[0], from_y, from_z, squares)
-    arrivals = {0: [1, 2], 1: [3]}
+    arrivals = {0:[1,2],1:[3]}
     for step, flips in enumerate(rounds()):
         received = [swap(sums, flip) for flip in flips]
         if step < EARLY:

time: 69.3 us -> 68.6 us (0.990)
  waiting for transfers between devices: 11.9 us -> 9.43 us
  local copies, waits for them, and re-layouts: 0.01 us -> 1.6 us
    pallas_call x2 -> x3, Pallas kernels: 4.59 us -> 7.16 us  [multiply(): pl.pallas_call(multiply_kernel, out_shape=[pltpu.VMEM(held.shape, BF16),...]
    ppermute x17, waiting for transfers between devices: 11.9 us -> 9.43 us  [swap(): return lax.ppermute(value, axes, [(i, i ^ flip) for i in range(count)])]
    pallas_call x1, Pallas kernels: 3.54 us -> 1.59 us  [statistics(): pl.pallas_call(stat_kernel, out_shape=[jax.ShapeDtypeStruct((FOLD, HALF),...]
    unnamed x2 -> x4, local copies, waits for them, and re-layouts: 0.01 us -> 1.6 us
    pallas_call x1, Pallas kernels: 8.7 us -> 7.72 us  [finish(): pl.pallas_call(finish_kernel, out_shape=[jax.ShapeDtypeStruct((QUAD * BLK...]
  transfers between devices with their start and end apart: 17 -> 17, of which waited for: 6 -> 3; matrix products, arithmetic and copies ran while one was open for 0% -> 0% of each run, Pallas kernels for 28% -> 32%
where the time goes in v9:
time: 68.6 us; the launch traced here: 68.4 us
  Pallas kernels  31 us (45%)
  starting transfers between devices  25.1 us (37%)
  waiting for transfers between devices  9.43 us (14%)
  local copies, waits for them, and re-layouts  1.6 us (2%)
  between operations  0.94 us (1%)
    ppermute x17, starting transfers between devices, swap(): return lax.ppermute(value, axes, [(i, i ^ flip) for i in range(count)])  25.1 us
    pallas_call x1, Pallas kernels, gram(): pl.pallas_call(gram_kernel, out_shape=[pltpu.VMEM((BLK, columns), BF16)]...  10.8 us
    ppermute x17, waiting for transfers between devices, swap(): return lax.ppermute(value, axes, [(i, i ^ flip) for i in range(count)])  9.43 us
    pallas_call x1, Pallas kernels, finish(): pl.pallas_call(finish_kernel, out_shape=[jax.ShapeDtypeStruct((QUAD * BLK...  7.72 us
    pallas_call x3, Pallas kernels, multiply(): pl.pallas_call(multiply_kernel, out_shape=[pltpu.VMEM(held.shape, BF16),...  7.16 us
    pallas_call x1, Pallas kernels, newton(): pl.pallas_call(functools.partial(newton_kernel, tokens), out_shape=jax.Sh...  3.19 us
    unnamed x4, local copies, waits for them, and re-layouts  1.6 us
    pallas_call x1, Pallas kernels, statistics(): pl.pallas_call(stat_kernel, out_shape=[jax.ShapeDtypeStruct((FOLD, HALF),...  1.59 us
  transfers between devices with their start and end apart: 17, of which 3 were waited for; matrix products, arithmetic and copies ran while one was open for 0% of the time, Pallas kernels for 32%

profile of v9, /device:TPU:0, one launch (start us, length us, event | category | flops | bytes accessed | tf_op | source)
XLA Modules:
  0.0 68.4 jit_solution(438008900026499925)
XLA Ops:
  0.7 0.1 pad_add_fusion.order
  0.7 1.6 %copy-done = bf16[512,2048]{1,0:T(8,128)(2,1)S(1)} copy-done((bf16[512,2048]{1,0:T(8,128)(2,1)S(1)}, bf16[512,2048]{1,0:T(8,128)(2,1)}, u32[]{:S(2)}) %copy-start) | copy-done | bytes 2097176
  2.3 1.6 %statistics.1 = (bf16[528,256]{1,0:T(8,128)(2,1)S(1)}, bf16[528,256]{1,0:T(8,128)(2,1)S(1)}, bf16[528,256]{1,0:T(8,128)(2,1)S(1)}, bf16[528,256]{1,0:T(8,128)(2,1)S(1)}) custom-call(s32[6]{0:T(128)S(1)} %pad_add_fusion.order, bf16[512,2048]{1,0:T(8,128)(2,1)S(1)} %copy-done), custom_call_target="tpu_custom_call" | custom-call | tf_op jit(solution)/shard_map/statistics/pallas_call | solution.py:72
  3.9 3.0 %collective-permute-start = (bf16[528,256]{1,0:T(8,128)(2,1)S(1)}, bf16[528,256]{1,0:T(8,128)(2,1)S(1)}, u32[]{:S(2)}, u32[]{:S(2)}) collective-permute-start(bf16[528,256]{1,0:T(8,128)(2,1)S(1)} %get-tuple-element.49), channel_id=1, source_target_pairs={{0,1},{1,0},{2,3},{3,2},{4,5},{5,4},{6,7},{7,6},{8,9},{9,8},{10,11... | collective-permute-start | bytes 811016 | tf_op jit(solution)/shard_map/ppermute | solution.py:343
  6.9 1.6 %collective-permute-start.1 = (bf16[528,256]{1,0:T(8,128)(2,1)S(1)}, bf16[528,256]{1,0:T(8,128)(2,1)S(1)}, u32[]{:S(2)}, u32[]{:S(2)}) collective-permute-start(bf16[528,256]{1,0:T(8,128)(2,1)S(1)} %get-tuple-element.50), channel_id=1, source_target_pairs={{0,2},{1,3},{2,0},{3,1},{4,6},{5,7},{6,4},{7,5},{8,10},{9,11},{10,... | collective-permute-start | bytes 811016 | tf_op jit(solution)/shard_map/ppermute | solution.py:343
  8.5 10.8 %gram.1 = (bf16[512,3584]{1,0:T(8,128)(2,1)S(1)}, bf16[512,3584]{1,0:T(8,128)(2,1)S(1)}, bf16[512,3584]{1,0:T(8,128)(2,1)S(1)}, bf16[512,3584]{1,0:T(8,128)(2,1)...) custom-call(s32[6]{0:T(128)S(1)} %pad_add_fusion.order, ...), custom_call_target="tpu_custom_call" | custom-call | flops 7516192768 | bytes 14680064 | tf_op jit(solution)/shard_map/gram/pallas_call | solution.py:129
  19.3 2.0 %collective-permute-start.4 = (bf16[528,256]{1,0:T(8,128)(2,1)S(1)}, bf16[528,256]{1,0:T(8,128)(2,1)S(1)}, u32[]{:S(2)}, u32[]{:S(2)}) collective-permute-start(bf16[528,256]{1,0:T(8,128)(2,1)S(1)} %get-tuple-element.53), channel_id=1, source_target_pairs={{0,1},{1,0},{2,3},{3,2},{4,5},{5,4},{6,7},{7,6},{8,9},{9,8},{10,11... | collective-permute-start | bytes 811016 | tf_op jit(solution)/shard_map/ppermute | solution.py:343
  21.3 0.2 add_convert_fusion.1.mine
  21.5 2.7 %collective-permute-start.3 = (bf16[528,256]{1,0:T(8,128)(2,1)S(1)}, bf16[528,256]{1,0:T(8,128)(2,1)S(1)}, u32[]{:S(2)}, u32[]{:S(2)}) collective-permute-start(bf16[528,256]{1,0:T(8,128)(2,1)S(1)} %add_convert_fusion.1.mine), channel_id=1, source_target_pairs={{0,4},{1,5},{2,6},{3,7},{4,0},{5,1},{6,2},{7,3},{8,12},{9,13},{10,... | collective-permute-start | bytes 811016 | tf_op jit(solution)/shard_map/ppermute | solution.py:343
  24.1 2.9 %collective-permute-done.4 = bf16[528,256]{1,0:T(8,128)(2,1)S(1)} collective-permute-done((bf16[528,256]{1,0:T(8,128)(2,1)S(1)}, bf16[528,256]{1,0:T(8,128)(2,1)S(1)}, u32[]{:S(2)}, u32[]{:S(2)}) %collective-permute-start.4) | collective-permute-done | bytes 270368 | tf_op jit(solution)/shard_map/ppermute | solution.py:343
  27.1 0.1 add_convert_fusion
  27.1 1.8 %collective-permute-start.6 = (bf16[528,256]{1,0:T(8,128)(2,1)S(1)}, bf16[528,256]{1,0:T(8,128)(2,1)S(1)}, u32[]{:S(2)}, u32[]{:S(2)}) collective-permute-start(bf16[528,256]{1,0:T(8,128)(2,1)S(1)} %add_convert_fusion), channel_id=1, source_target_pairs={{0,2},{1,3},{2,0},{3,1},{4,6},{5,7},{6,4},{7,5},{8,10},{9,11},{10,... | collective-permute-start | bytes 811016 | tf_op jit(solution)/shard_map/ppermute | solution.py:343
  28.9 1.5 %collective-permute-start.5 = (bf16[528,256]{1,0:T(8,128)(2,1)S(1)}, bf16[528,256]{1,0:T(8,128)(2,1)S(1)}, u32[]{:S(2)}, u32[]{:S(2)}) collective-permute-start(bf16[528,256]{1,0:T(8,128)(2,1)S(1)} %get-tuple-element.55), channel_id=1, source_target_pairs={{0,1},{1,0},{2,3},{3,2},{4,5},{5,4},{6,7},{7,6},{8,9},{9,8},{10,11... | collective-permute-start | bytes 811016 | tf_op jit(solution)/shard_map/ppermute | solution.py:343
  30.4 5.0 %collective-permute-done.3.other = bf16[528,256]{1,0:T(8,128)(2,1)S(1)} collective-permute-done((bf16[528,256]{1,0:T(8,128)(2,1)S(1)}, bf16[528,256]{1,0:T(8,128)(2,1)S(1)}, u32[]{:S(2)}, u32[]{:S(2)}) %collective-permute-start.3) | collective-permute-done | bytes 270368 | tf_op jit(solution)/shard_map/ppermute | solution.py:343
  35.5 3.2 %newton.1.folded.after = bf16[528,256]{1,0:T(8,128)(2,1)S(1)} custom-call(f32[1,256]{1,0:T(1,128)S(1)} %get-tuple-element.48.after.squares, bf16[528,256]{1,0:T(8,128)(2,1)S(1)} %add_convert_fusion.1.mine, bf16[528,256]{1,0:T(8,128)(2,1)S(1)} %collective-permute-done.3.other), custom_call_target="tpu_custom_call" | custom-call | flops 2147483648 | bytes 2097152 | tf_op jit(solution)/shard_map/newton/pallas_call | solution.py:188
  38.7 0.8 %collective-permute-start.8 = (bf16[528,256]{1,0:T(8,128)(2,1)S(1)}, bf16[528,256]{1,0:T(8,128)(2,1)S(1)}, u32[]{:S(2)}, u32[]{:S(2)}) collective-permute-start(bf16[528,256]{1,0:T(8,128)(2,1)S(1)} %newton.1.folded.after), channel_id=1, source_target_pairs={{0,1},{1,0},{2,3},{3,2},{4,5},{5,4},{6,7},{7,6},{8,9},{9,8},{10,11... | collective-permute-start | bytes 811016 | tf_op jit(solution)/shard_map/ppermute | solution.py:343
  39.5 0.6 collective-permute-start.7
  40.1 0.6 norm.1
  40.7 0.6 collective-permute-start.11
  41.3 1.0 %collective-permute-start.10 = (f32[8,128]{1,0:T(8,128)S(1)}, f32[8,128]{1,0:T(8,128)S(1)}, u32[]{:S(2)}, u32[]{:S(2)}) collective-permute-start(f32[8,128]{1,0:T(8,128)S(1)} %norm.1), channel_id=1, source_target_pairs={{0,16},{1,17},{2,18},{3,19},{4,20},{5,21},{6,22},{7,23},{8,24},{9,... | collective-permute-start | bytes 12296 | tf_op jit(solution)/shard_map/ppermute | solution.py:343
  42.3 0.3 collective-permute-start.9
  42.6 2.3 %multiply.3 = (bf16[512,3584]{1,0:T(8,128)(2,1)S(1)}, bf16[512,512]{1,0:T(8,128)(2,1)S(1)}) custom-call(bf16[528,256]{1,0:T(8,128)(2,1)S(1)} %newton.1.folded.after, bf16[528,256]{1,0:T(8,128)(2,1)S(1)} %newton.1.folded.after, bf16[512,3584]{1,0:T(8,128)(2,1)S(1)} %get-tuple-element.58.held_ref), custom_call_target="tpu_custom_call", output_to_operand_aliasing={{0}: (2, {})} | custom-call | flops 1880000000 | bytes 1 | tf_op jit(solution)/shard_map/multiply/pallas_call | solution.py:247
  44.9 2.2 %collective-permute-start.12 = (bf16[528,256]{1,0:T(8,128)(2,1)S(1)}, bf16[528,256]{1,0:T(8,128)(2,1)S(1)}, u32[]{:S(2)}, u32[]{:S(2)}) collective-permute-start(bf16[528,256]{1,0:T(8,128)(2,1)S(1)} %newton.1.folded.after), channel_id=1, source_target_pairs={{0,3},{1,2},{2,1},{3,0},{4,7},{5,6},{6,5},{7,4},{8,11},{9,10},{10,... | collective-permute-start | bytes 811016 | tf_op jit(solution)/shard_map/ppermute | solution.py:343
  47.1 1.8 %collective-permute-start.15 = (f32[8,128]{1,0:T(8,128)S(1)}, f32[8,128]{1,0:T(8,128)S(1)}, u32[]{:S(2)}, u32[]{:S(2)}) collective-permute-start(f32[8,128]{1,0:T(8,128)S(1)} %add_add_fusion.1), channel_id=1, source_target_pairs={{0,3},{1,2},{2,1},{3,0},{4,7},{5,6},{6,5},{7,4},{8,11},{9,10},{10,... | collective-permute-start | bytes 12296 | tf_op jit(solution)/shard_map/ppermute | solution.py:343
  48.9 0.5 collective-permute-start.14
  49.4 1.3 %collective-permute-start.13 = (f32[8,128]{1,0:T(8,128)S(1)}, f32[8,128]{1,0:T(8,128)S(1)}, u32[]{:S(2)}, u32[]{:S(2)}) collective-permute-start(f32[8,128]{1,0:T(8,128)S(1)} %add_add_fusion.1), channel_id=1, source_target_pairs={{0,1},{1,0},{2,3},{3,2},{4,5},{5,4},{6,7},{7,6},{8,9},{9,8},{10,11... | collective-permute-start | bytes 12296 | tf_op jit(solution)/shard_map/ppermute | solution.py:343
  50.7 2.5 %multiply.4 = (bf16[512,3584]{1,0:T(8,128)(2,1)S(1)}, bf16[512,512]{1,0:T(8,128)(2,1)S(1)}) custom-call(bf16[528,256]{1,0:T(8,128)(2,1)S(1)} %collective-permute-done.8.after.folded, bf16[528,256]{1,0:T(8,128)(2,1)S(1)} %collective-permute-done.8.after.folded, bf16[512,3584]{1,0:T(8,128)(2,1)S(1)} %get-tuple-element.70.held_ref), custom_call_target="tpu_custom_call", output_to_operand_aliasing={{0}: (2, {})} | custom-call | flops 1880000000 | bytes 1 | tf_op jit(solution)/shard_map/multiply/pallas_call | solution.py:247
  53.2 0.0 copy-start.1
  53.2 1.4 %collective-permute-done.15 = f32[8,128]{1,0:T(8,128)S(1)} collective-permute-done((f32[8,128]{1,0:T(8,128)S(1)}, f32[8,128]{1,0:T(8,128)S(1)}, u32[]{:S(2)}, u32[]{:S(2)}) %collective-permute-start.15) | collective-permute-done | bytes 4128 | tf_op jit(solution)/shard_map/ppermute | solution.py:343
  54.7 3.5 %collective-permute-start.16 = (f32[8,128]{1,0:T(8,128)S(1)}, f32[8,128]{1,0:T(8,128)S(1)}, u32[]{:S(2)}, u32[]{:S(2)}) collective-permute-start(f32[8,128]{1,0:T(8,128)S(1)} %add_add_fusion), channel_id=1, source_target_pairs={{0,4},{1,5},{2,6},{3,7},{4,0},{5,1},{6,2},{7,3},{8,12},{9,13},{10,... | collective-permute-start | bytes 12296 | tf_op jit(solution)/shard_map/ppermute | solution.py:343
  58.2 2.3 %multiply.5 = (bf16[512,3584]{1,0:T(8,128)(2,1)S(1)}, bf16[512,512]{1,0:T(8,128)(2,1)S(1)}) custom-call(bf16[528,256]{1,0:T(8,128)(2,1)S(1)} %collective-permute-done.7.after.folded, bf16[528,256]{1,0:T(8,128)(2,1)S(1)} %collective-permute-done.7.after.folded, bf16[512,3584]{1,0:T(8,128)(2,1)S(1)} %get-tuple-element.79.held_ref), custom_call_target="tpu_custom_call", output_to_operand_aliasing={{0}: (2, {})} | custom-call | flops 1880000000 | bytes 1 | tf_op jit(solution)/shard_map/multiply/pallas_call | solution.py:247
  60.6 7.7 %finish.1 = (bf16[2048,3584]{1,0:T(8,128)(2,1)}, bf16[2,512,512]{2,1,0:T(8,128)(2,1)}, bf16[512,3584]{1,0:T(8,128)(2,1)S(1)}, bf16[512,3584]{1,0:T(8,128)(2,1)S(...) custom-call(s32[6]{0:T(128)S(1)} %pad_add_fusion.order, ...), custom_call_target="tpu_custom_call", output_to_operand_aliasing={{2}: (7, {}), {3}: (8, {}), {4}: (9, {}), {5}: (10, {})} | custom-call | tf_op jit(solution)/shard_map/finish/pallas_call | solution.py:319
  (21 shorter events, 0.1 us)
Async XLA Ops:
  0.7 1.6 %copy-start = (bf16[512,2048]{1,0:T(8,128)(2,1)S(1)}, bf16[512,2048]{1,0:T(8,128)(2,1)}, u32[]{:S(2)}) copy-start(bf16[512,2048]{1,0:T(8,128)(2,1)} %x_ref.1) | copy-start | bytes 6291460
  3.9 17.4 %collective-permute-start = (bf16[528,256]{1,0:T(8,128)(2,1)S(1)}, bf16[528,256]{1,0:T(8,128)(2,1)S(1)}, u32[]{:S(2)}, u32[]{:S(2)}) collective-permute-start(bf16[528,256]{1,0:T(8,128)(2,1)S(1)} %get-tuple-element.49), channel_id=1, source_target_pairs={{0,1},{1,0},{2,3},{3,2},{4,5},{5,4},{6,7},{7,6},{8,9},{9,8},{10,11... | collective-permute-start | bytes 811016 | tf_op jit(solution)/shard_map/ppermute | solution.py:343
  6.9 14.4 %collective-permute-start.1 = (bf16[528,256]{1,0:T(8,128)(2,1)S(1)}, bf16[528,256]{1,0:T(8,128)(2,1)S(1)}, u32[]{:S(2)}, u32[]{:S(2)}) collective-permute-start(bf16[528,256]{1,0:T(8,128)(2,1)S(1)} %get-tuple-element.50), channel_id=1, source_target_pairs={{0,2},{1,3},{2,0},{3,1},{4,6},{5,7},{6,4},{7,5},{8,10},{9,11},{10,... | collective-permute-start | bytes 811016 | tf_op jit(solution)/shard_map/ppermute | solution.py:343
  8.5 12.8 %collective-permute-start.2 = (bf16[528,256]{1,0:T(8,128)(2,1)S(1)}, bf16[528,256]{1,0:T(8,128)(2,1)S(1)}, u32[]{:S(2)}, u32[]{:S(2)}) collective-permute-start(bf16[528,256]{1,0:T(8,128)(2,1)S(1)} %get-tuple-element.51), channel_id=1, source_target_pairs={{0,3},{1,2},{2,1},{3,0},{4,7},{5,6},{6,5},{7,4},{8,11},{9,10},{10,... | collective-permute-start | bytes 811016 | tf_op jit(solution)/shard_map/ppermute | solution.py:343
  19.3 7.7 %collective-permute-start.4 = (bf16[528,256]{1,0:T(8,128)(2,1)S(1)}, bf16[528,256]{1,0:T(8,128)(2,1)S(1)}, u32[]{:S(2)}, u32[]{:S(2)}) collective-permute-start(bf16[528,256]{1,0:T(8,128)(2,1)S(1)} %get-tuple-element.53), channel_id=1, source_target_pairs={{0,1},{1,0},{2,3},{3,2},{4,5},{5,4},{6,7},{7,6},{8,9},{9,8},{10,11... | collective-permute-start | bytes 811016 | tf_op jit(solution)/shard_map/ppermute | solution.py:343
  21.5 14.0 %collective-permute-start.3 = (bf16[528,256]{1,0:T(8,128)(2,1)S(1)}, bf16[528,256]{1,0:T(8,128)(2,1)S(1)}, u32[]{:S(2)}, u32[]{:S(2)}) collective-permute-start(bf16[528,256]{1,0:T(8,128)(2,1)S(1)} %add_convert_fusion.1.mine), channel_id=1, source_target_pairs={{0,4},{1,5},{2,6},{3,7},{4,0},{5,1},{6,2},{7,3},{8,12},{9,13},{10,... | collective-permute-start | bytes 811016 | tf_op jit(solution)/shard_map/ppermute | solution.py:343
  27.1 12.9 %collective-permute-start.6 = (bf16[528,256]{1,0:T(8,128)(2,1)S(1)}, bf16[528,256]{1,0:T(8,128)(2,1)S(1)}, u32[]{:S(2)}, u32[]{:S(2)}) collective-permute-start(bf16[528,256]{1,0:T(8,128)(2,1)S(1)} %add_convert_fusion), channel_id=1, source_target_pairs={{0,2},{1,3},{2,0},{3,1},{4,6},{5,7},{6,4},{7,5},{8,10},{9,11},{10,... | collective-permute-start | bytes 811016 | tf_op jit(solution)/shard_map/ppermute | solution.py:343
  28.9 11.2 %collective-permute-start.5 = (bf16[528,256]{1,0:T(8,128)(2,1)S(1)}, bf16[528,256]{1,0:T(8,128)(2,1)S(1)}, u32[]{:S(2)}, u32[]{:S(2)}) collective-permute-start(bf16[528,256]{1,0:T(8,128)(2,1)S(1)} %get-tuple-element.55), channel_id=1, source_target_pairs={{0,1},{1,0},{2,3},{3,2},{4,5},{5,4},{6,7},{7,6},{8,9},{9,8},{10,11... | collective-permute-start | bytes 811016 | tf_op jit(solution)/shard_map/ppermute | solution.py:343
  38.7 8.5 %collective-permute-start.8 = (bf16[528,256]{1,0:T(8,128)(2,1)S(1)}, bf16[528,256]{1,0:T(8,128)(2,1)S(1)}, u32[]{:S(2)}, u32[]{:S(2)}) collective-permute-start(bf16[528,256]{1,0:T(8,128)(2,1)S(1)} %newton.1.folded.after), channel_id=1, source_target_pairs={{0,1},{1,0},{2,3},{3,2},{4,5},{5,4},{6,7},{7,6},{8,9},{9,8},{10,11... | collective-permute-start | bytes 811016 | tf_op jit(solution)/shard_map/ppermute | solution.py:343
  39.5 7.6 %collective-permute-start.7 = (bf16[528,256]{1,0:T(8,128)(2,1)S(1)}, bf16[528,256]{1,0:T(8,128)(2,1)S(1)}, u32[]{:S(2)}, u32[]{:S(2)}) collective-permute-start(bf16[528,256]{1,0:T(8,128)(2,1)S(1)} %newton.1.folded.after), channel_id=1, source_target_pairs={{0,2},{1,3},{2,0},{3,1},{4,6},{5,7},{6,4},{7,5},{8,10},{9,11},{10,... | collective-permute-start | bytes 811016 | tf_op jit(solution)/shard_map/ppermute | solution.py:343
  40.7 4.3 %collective-permute-start.11 = (f32[8,128]{1,0:T(8,128)S(1)}, f32[8,128]{1,0:T(8,128)S(1)}, u32[]{:S(2)}, u32[]{:S(2)}) collective-permute-start(f32[8,128]{1,0:T(8,128)S(1)} %norm.1), channel_id=1, source_target_pairs={{0,24},{1,25},{2,26},{3,27},{4,28},{5,29},{6,30},{7,31},{8,16},{9,... | collective-permute-start | bytes 12296 | tf_op jit(solution)/shard_map/ppermute | solution.py:343
  41.3 5.8 %collective-permute-start.10 = (f32[8,128]{1,0:T(8,128)S(1)}, f32[8,128]{1,0:T(8,128)S(1)}, u32[]{:S(2)}, u32[]{:S(2)}) collective-permute-start(f32[8,128]{1,0:T(8,128)S(1)} %norm.1), channel_id=1, source_target_pairs={{0,16},{1,17},{2,18},{3,19},{4,20},{5,21},{6,22},{7,23},{8,24},{9,... | collective-permute-start | bytes 12296 | tf_op jit(solution)/shard_map/ppermute | solution.py:343
  42.3 4.8 %collective-permute-start.9 = (f32[8,128]{1,0:T(8,128)S(1)}, f32[8,128]{1,0:T(8,128)S(1)}, u32[]{:S(2)}, u32[]{:S(2)}) collective-permute-start(f32[8,128]{1,0:T(8,128)S(1)} %norm.1), channel_id=1, source_target_pairs={{0,8},{1,9},{2,10},{3,11},{4,12},{5,13},{6,14},{7,15},{8,0},{9,1},... | collective-permute-start | bytes 12296 | tf_op jit(solution)/shard_map/ppermute | solution.py:343
  44.9 9.8 %collective-permute-start.12 = (bf16[528,256]{1,0:T(8,128)(2,1)S(1)}, bf16[528,256]{1,0:T(8,128)(2,1)S(1)}, u32[]{:S(2)}, u32[]{:S(2)}) collective-permute-start(bf16[528,256]{1,0:T(8,128)(2,1)S(1)} %newton.1.folded.after), channel_id=1, source_target_pairs={{0,3},{1,2},{2,1},{3,0},{4,7},{5,6},{6,5},{7,4},{8,11},{9,10},{10,... | collective-permute-start | bytes 811016 | tf_op jit(solution)/shard_map/ppermute | solution.py:343
  47.1 7.5 %collective-permute-start.15 = (f32[8,128]{1,0:T(8,128)S(1)}, f32[8,128]{1,0:T(8,128)S(1)}, u32[]{:S(2)}, u32[]{:S(2)}) collective-permute-start(f32[8,128]{1,0:T(8,128)S(1)} %add_add_fusion.1), channel_id=1, source_target_pairs={{0,3},{1,2},{2,1},{3,0},{4,7},{5,6},{6,5},{7,4},{8,11},{9,10},{10,... | collective-permute-start | bytes 12296 | tf_op jit(solution)/shard_map/ppermute | solution.py:343
  48.9 5.7 %collective-permute-start.14 = (f32[8,128]{1,0:T(8,128)S(1)}, f32[8,128]{1,0:T(8,128)S(1)}, u32[]{:S(2)}, u32[]{:S(2)}) collective-permute-start(f32[8,128]{1,0:T(8,128)S(1)} %add_add_fusion.1), channel_id=1, source_target_pairs={{0,2},{1,3},{2,0},{3,1},{4,6},{5,7},{6,4},{7,5},{8,10},{9,11},{10,... | collective-permute-start | bytes 12296 | tf_op jit(solution)/shard_map/ppermute | solution.py:343
  49.4 5.2 %collective-permute-start.13 = (f32[8,128]{1,0:T(8,128)S(1)}, f32[8,128]{1,0:T(8,128)S(1)}, u32[]{:S(2)}, u32[]{:S(2)}) collective-permute-start(f32[8,128]{1,0:T(8,128)S(1)} %add_add_fusion.1), channel_id=1, source_target_pairs={{0,1},{1,0},{2,3},{3,2},{4,5},{5,4},{6,7},{7,6},{8,9},{9,8},{10,11... | collective-permute-start | bytes 12296 | tf_op jit(solution)/shard_map/ppermute | solution.py:343
  53.2 7.3 %copy-start.1 = (s32[4,4]{1,0:T(4,128)S(1)}, s32[4,4]{1,0:T(4,128)}, u32[]{:S(2)}) copy-start(s32[4,4]{1,0:T(4,128)} %owner_slot.1) | copy-start | bytes 196
  54.7 5.8 %collective-permute-start.16 = (f32[8,128]{1,0:T(8,128)S(1)}, f32[8,128]{1,0:T(8,128)S(1)}, u32[]{:S(2)}, u32[]{:S(2)}) collective-permute-start(f32[8,128]{1,0:T(8,128)S(1)} %add_add_fusion), channel_id=1, source_target_pairs={{0,4},{1,5},{2,6},{3,7},{4,0},{5,1},{6,2},{7,3},{8,12},{9,13},{10,... | collective-permute-start | bytes 12296 | tf_op jit(solution)/shard_map/ppermute | solution.py:343

commit v10 on v9

--- a/solution.py
+++ b/solution.py
@@ -104,17 +104,12 @@
     norm_ref[...] = jnp.zeros_like(norm_ref)
     row, col = places()
     for place in range(QUAD):
-        for index, part in enumerate(parts):
+        for index in range(len(parts)):
             copy(place, index).wait()
-            whole = held[place][:, part]
-            across = ((1,), (1,))
-            terms = dot(whole, whole[:HALF], across), dot(whole[HALF:], whole[HALF:], across)
-            if index == 0:
-                left[...] = terms[0]
-                last[...] = terms[1]
-            else:
-                left[...] += terms[0]
-                last[...] += terms[1]
+        whole = held[place][...]
+        across = ((1,), (1,))
+        left[...] = dot(whole, whole[:HALF], across)
+        last[...] = dot(whole[HALF:], whole[HALF:], across)
         squares = jnp.where(row == col, left[:HALF] + last[...], 0.0)
         norm_ref[...] += jnp.sum(squares, axis=0, keepdims=True)
         body, diagonal = fold(left[:HALF], last[...])
@@ -380,20 +375,21 @@
     from_y = swap(grams[1], 1)
     from_z = swap(add(grams[2], across), 2)
     root = newton(tokens_all, squares, mine, other)
-    folded = (root, swap(root, 1), swap(root, 2), swap(root, 3))
-    blocks, folded, roots = list(blocks), list(folded), []
+    folded = [root, swap(root, 1), swap(root, 2)]
+    folded.append(swap(folded[2], 1))
+    blocks, roots = list(blocks), []
 
     def precondition(place):
         blocks[place], root = multiply(folded[place], blocks[place], folded[place])
         roots.append(root)
 
     sums = norm(root, grams[0], from_y, from_z, squares)
-    arrivals = {0:[1,2],1:[3]}
+    early, arrivals = {0:[0],1:[1],2:[2]}, {0:[1,2],1:[3]}
     for step, flips in enumerate(rounds()):
         received = [swap(sums, flip) for flip in flips]
-        if step < EARLY:
-            precondition(step)
-            blocks[step], *received = lax.optimization_barrier((blocks[step], *received))
+        for place in early.get(step, ()):
+            precondition(place)
+            blocks[place], *received = lax.optimization_barrier((blocks[place], *received))
         for place in arrivals.get(step, ()):
             folded[place], *received = lax.optimization_barrier((folded[place], *received))
         sums = sums + sum(received)

time: 68.6 us -> 68 us (level)
  starting transfers between devices: 25.1 us -> 24.2 us
    ppermute x17, starting transfers between devices: 25.1 us -> 24.2 us  [swap(): return lax.ppermute(value, axes, [(i, i ^ flip) for i in range(count)])]
  transfers between devices with their start and end apart: 17 -> 17, of which waited for: 3 -> 4; matrix products, arithmetic and copies ran while one was open for 0% -> 0% of each run, Pallas kernels for 32% -> 32%
where the time goes in v10:
time: 68 us; the launch traced here: 67.8 us
  Pallas kernels  31.2 us (46%)
  starting transfers between devices  24.2 us (36%)
  waiting for transfers between devices  9.53 us (14%)
  local copies, waits for them, and re-layouts  1.6 us (2%)
  between operations  0.97 us (1%)
    ppermute x17, starting transfers between devices, swap(): return lax.ppermute(value, axes, [(i, i ^ flip) for i in range(count)])  24.2 us
    pallas_call x1, Pallas kernels, gram(): pl.pallas_call(gram_kernel, out_shape=[pltpu.VMEM((BLK, columns), BF16)]...  11 us
    ppermute x17, waiting for transfers between devices, swap(): return lax.ppermute(value, axes, [(i, i ^ flip) for i in range(count)])  9.53 us
    pallas_call x1, Pallas kernels, finish(): pl.pallas_call(finish_kernel, out_shape=[jax.ShapeDtypeStruct((QUAD * BLK...  7.72 us
    pallas_call x3, Pallas kernels, multiply(): pl.pallas_call(multiply_kernel, out_shape=[pltpu.VMEM(held.shape, BF16),...  7.13 us
    pallas_call x1, Pallas kernels, newton(): pl.pallas_call(functools.partial(newton_kernel, tokens), out_shape=jax.Sh...  3.2 us
    unnamed x4, local copies, waits for them, and re-layouts  1.6 us
    pallas_call x1, Pallas kernels, statistics(): pl.pallas_call(stat_kernel, out_shape=[jax.ShapeDtypeStruct((FOLD, HALF),...  1.59 us
  transfers between devices with their start and end apart: 17, of which 4 were waited for; matrix products, arithmetic and copies ran while one was open for 0% of the time, Pallas kernels for 32%

profile of v10, /device:TPU:0, one launch (start us, length us, event | category | flops | bytes accessed | tf_op | source)
XLA Modules:
  0.0 67.8 jit_solution(12999837405364868854)
XLA Ops:
  0.7 0.1 pad_add_fusion.order
  0.7 1.6 %copy-done = bf16[512,2048]{1,0:T(8,128)(2,1)S(1)} copy-done((bf16[512,2048]{1,0:T(8,128)(2,1)S(1)}, bf16[512,2048]{1,0:T(8,128)(2,1)}, u32[]{:S(2)}) %copy-start) | copy-done | bytes 2097176
  2.3 1.6 %statistics.1 = (bf16[528,256]{1,0:T(8,128)(2,1)S(1)}, bf16[528,256]{1,0:T(8,128)(2,1)S(1)}, bf16[528,256]{1,0:T(8,128)(2,1)S(1)}, bf16[528,256]{1,0:T(8,128)(2,1)S(1)}) custom-call(s32[6]{0:T(128)S(1)} %pad_add_fusion.order, bf16[512,2048]{1,0:T(8,128)(2,1)S(1)} %copy-done), custom_call_target="tpu_custom_call" | custom-call | tf_op jit(solution)/shard_map/statistics/pallas_call | solution.py:72
  3.9 3.0 %collective-permute-start = (bf16[528,256]{1,0:T(8,128)(2,1)S(1)}, bf16[528,256]{1,0:T(8,128)(2,1)S(1)}, u32[]{:S(2)}, u32[]{:S(2)}) collective-permute-start(bf16[528,256]{1,0:T(8,128)(2,1)S(1)} %get-tuple-element.49), channel_id=1, source_target_pairs={{0,1},{1,0},{2,3},{3,2},{4,5},{5,4},{6,7},{7,6},{8,9},{9,8},{10,11... | collective-permute-start | bytes 811016 | tf_op jit(solution)/shard_map/ppermute | solution.py:338
  6.9 1.6 %collective-permute-start.1 = (bf16[528,256]{1,0:T(8,128)(2,1)S(1)}, bf16[528,256]{1,0:T(8,128)(2,1)S(1)}, u32[]{:S(2)}, u32[]{:S(2)}) collective-permute-start(bf16[528,256]{1,0:T(8,128)(2,1)S(1)} %get-tuple-element.50), channel_id=1, source_target_pairs={{0,2},{1,3},{2,0},{3,1},{4,6},{5,7},{6,4},{7,5},{8,10},{9,11},{10,... | collective-permute-start | bytes 811016 | tf_op jit(solution)/shard_map/ppermute | solution.py:338
  8.5 11.0 %gram.1 = (bf16[512,3584]{1,0:T(8,128)(2,1)S(1)}, bf16[512,3584]{1,0:T(8,128)(2,1)S(1)}, bf16[512,3584]{1,0:T(8,128)(2,1)S(1)}, bf16[512,3584]{1,0:T(8,128)(2,1)...) custom-call(s32[6]{0:T(128)S(1)} %pad_add_fusion.order, ...), custom_call_target="tpu_custom_call" | custom-call | flops 7516192768 | bytes 14680064 | tf_op jit(solution)/shard_map/gram/pallas_call | solution.py:124
  19.6 2.0 %collective-permute-start.4 = (bf16[528,256]{1,0:T(8,128)(2,1)S(1)}, bf16[528,256]{1,0:T(8,128)(2,1)S(1)}, u32[]{:S(2)}, u32[]{:S(2)}) collective-permute-start(bf16[528,256]{1,0:T(8,128)(2,1)S(1)} %get-tuple-element.53), channel_id=1, source_target_pairs={{0,1},{1,0},{2,3},{3,2},{4,5},{5,4},{6,7},{7,6},{8,9},{9,8},{10,11... | collective-permute-start | bytes 811016 | tf_op jit(solution)/shard_map/ppermute | solution.py:338
  21.6 0.1 add_convert_fusion.1.mine
  21.7 2.7 %collective-permute-start.3 = (bf16[528,256]{1,0:T(8,128)(2,1)S(1)}, bf16[528,256]{1,0:T(8,128)(2,1)S(1)}, u32[]{:S(2)}, u32[]{:S(2)}) collective-permute-start(bf16[528,256]{1,0:T(8,128)(2,1)S(1)} %add_convert_fusion.1.mine), channel_id=1, source_target_pairs={{0,4},{1,5},{2,6},{3,7},{4,0},{5,1},{6,2},{7,3},{8,12},{9,13},{10,... | collective-permute-start | bytes 811016 | tf_op jit(solution)/shard_map/ppermute | solution.py:338
  24.4 2.9 %collective-permute-done.4 = bf16[528,256]{1,0:T(8,128)(2,1)S(1)} collective-permute-done((bf16[528,256]{1,0:T(8,128)(2,1)S(1)}, bf16[528,256]{1,0:T(8,128)(2,1)S(1)}, u32[]{:S(2)}, u32[]{:S(2)}) %collective-permute-start.4) | collective-permute-done | bytes 270368 | tf_op jit(solution)/shard_map/ppermute | solution.py:338
  27.3 0.1 add_convert_fusion
  27.4 1.7 %collective-permute-start.6 = (bf16[528,256]{1,0:T(8,128)(2,1)S(1)}, bf16[528,256]{1,0:T(8,128)(2,1)S(1)}, u32[]{:S(2)}, u32[]{:S(2)}) collective-permute-start(bf16[528,256]{1,0:T(8,128)(2,1)S(1)} %add_convert_fusion), channel_id=1, source_target_pairs={{0,2},{1,3},{2,0},{3,1},{4,6},{5,7},{6,4},{7,5},{8,10},{9,11},{10,... | collective-permute-start | bytes 811016 | tf_op jit(solution)/shard_map/ppermute | solution.py:338
  29.1 1.5 %collective-permute-start.5 = (bf16[528,256]{1,0:T(8,128)(2,1)S(1)}, bf16[528,256]{1,0:T(8,128)(2,1)S(1)}, u32[]{:S(2)}, u32[]{:S(2)}) collective-permute-start(bf16[528,256]{1,0:T(8,128)(2,1)S(1)} %get-tuple-element.55), channel_id=1, source_target_pairs={{0,1},{1,0},{2,3},{3,2},{4,5},{5,4},{6,7},{7,6},{8,9},{9,8},{10,11... | collective-permute-start | bytes 811016 | tf_op jit(solution)/shard_map/ppermute | solution.py:338
  30.6 5.0 %collective-permute-done.3.other = bf16[528,256]{1,0:T(8,128)(2,1)S(1)} collective-permute-done((bf16[528,256]{1,0:T(8,128)(2,1)S(1)}, bf16[528,256]{1,0:T(8,128)(2,1)S(1)}, u32[]{:S(2)}, u32[]{:S(2)}) %collective-permute-start.3) | collective-permute-done | bytes 270368 | tf_op jit(solution)/shard_map/ppermute | solution.py:338
  35.7 3.2 %newton.1.folded.after = bf16[528,256]{1,0:T(8,128)(2,1)S(1)} custom-call(f32[1,256]{1,0:T(1,128)S(1)} %get-tuple-element.48.after.squares, bf16[528,256]{1,0:T(8,128)(2,1)S(1)} %add_convert_fusion.1.mine, bf16[528,256]{1,0:T(8,128)(2,1)S(1)} %collective-permute-done.3.other), custom_call_target="tpu_custom_call" | custom-call | flops 2147483648 | bytes 2097152 | tf_op jit(solution)/shard_map/newton/pallas_call | solution.py:183
  38.9 0.6 collective-permute-start.8
  39.5 0.6 collective-permute-start.7
  40.1 0.6 norm.1
  40.7 0.6 collective-permute-start.11
  41.3 1.0 %collective-permute-start.10 = (f32[8,128]{1,0:T(8,128)S(1)}, f32[8,128]{1,0:T(8,128)S(1)}, u32[]{:S(2)}, u32[]{:S(2)}) collective-permute-start(f32[8,128]{1,0:T(8,128)S(1)} %norm.1), channel_id=1, source_target_pairs={{0,16},{1,17},{2,18},{3,19},{4,20},{5,21},{6,22},{7,23},{8,24},{9,... | collective-permute-start | bytes 12296 | tf_op jit(solution)/shard_map/ppermute | solution.py:338
  42.3 0.3 collective-permute-start.9
  42.6 2.3 %multiply.3 = (bf16[512,3584]{1,0:T(8,128)(2,1)S(1)}, bf16[512,512]{1,0:T(8,128)(2,1)S(1)}) custom-call(bf16[528,256]{1,0:T(8,128)(2,1)S(1)} %newton.1.folded.after, bf16[528,256]{1,0:T(8,128)(2,1)S(1)} %newton.1.folded.after, bf16[512,3584]{1,0:T(8,128)(2,1)S(1)} %get-tuple-element.58.held_ref), custom_call_target="tpu_custom_call", output_to_operand_aliasing={{0}: (2, {})} | custom-call | flops 1880000000 | bytes 1 | tf_op jit(solution)/shard_map/multiply/pallas_call | solution.py:242
  44.9 1.3 %collective-permute-done.8.after.folded = bf16[528,256]{1,0:T(8,128)(2,1)S(1)} collective-permute-done((bf16[528,256]{1,0:T(8,128)(2,1)S(1)}, bf16[528,256]{1,0:T(8,128)(2,1)S(1)}, u32[]{:S(2)}, u32[]{:S(2)}) %collective-permute-start.8) | collective-permute-done | bytes 270368 | tf_op jit(solution)/shard_map/ppermute | solution.py:338
  46.2 0.3 collective-permute-done.7.after.folded
  46.5 1.5 %collective-permute-start.12 = (bf16[528,256]{1,0:T(8,128)(2,1)S(1)}, bf16[528,256]{1,0:T(8,128)(2,1)S(1)}, u32[]{:S(2)}, u32[]{:S(2)}) collective-permute-start(bf16[528,256]{1,0:T(8,128)(2,1)S(1)} %collective-permute-done.7.after.folded), channel_id=1, source_target_pairs={{0,1},{1,0},{2,3},{3,2},{4,5},{5,4},{6,7},{7,6},{8,9},{9,8},{10,11... | collective-permute-start | bytes 811016 | tf_op jit(solution)/shard_map/ppermute | solution.py:338
  48.0 1.7 %collective-permute-start.15 = (f32[8,128]{1,0:T(8,128)S(1)}, f32[8,128]{1,0:T(8,128)S(1)}, u32[]{:S(2)}, u32[]{:S(2)}) collective-permute-start(f32[8,128]{1,0:T(8,128)S(1)} %add_add_fusion.1), channel_id=1, source_target_pairs={{0,3},{1,2},{2,1},{3,0},{4,7},{5,6},{6,5},{7,4},{8,11},{9,10},{10,... | collective-permute-start | bytes 12296 | tf_op jit(solution)/shard_map/ppermute | solution.py:338
  49.7 0.3 collective-permute-start.14
  50.0 1.5 %collective-permute-start.13 = (f32[8,128]{1,0:T(8,128)S(1)}, f32[8,128]{1,0:T(8,128)S(1)}, u32[]{:S(2)}, u32[]{:S(2)}) collective-permute-start(f32[8,128]{1,0:T(8,128)S(1)} %add_add_fusion.1), channel_id=1, source_target_pairs={{0,1},{1,0},{2,3},{3,2},{4,5},{5,4},{6,7},{7,6},{8,9},{9,8},{10,11... | collective-permute-start | bytes 12296 | tf_op jit(solution)/shard_map/ppermute | solution.py:338
  51.4 2.5 %multiply.4 = (bf16[512,3584]{1,0:T(8,128)(2,1)S(1)}, bf16[512,512]{1,0:T(8,128)(2,1)S(1)}) custom-call(bf16[528,256]{1,0:T(8,128)(2,1)S(1)} %collective-permute-done.8.after.folded, bf16[528,256]{1,0:T(8,128)(2,1)S(1)} %collective-permute-done.8.after.folded, bf16[512,3584]{1,0:T(8,128)(2,1)S(1)} %get-tuple-element.70.held_ref), custom_call_target="tpu_custom_call", output_to_operand_aliasing={{0}: (2, {})} | custom-call | flops 1880000000 | bytes 1 | tf_op jit(solution)/shard_map/multiply/pallas_call | solution.py:242
  54.0 3.5 %collective-permute-start.16 = (f32[8,128]{1,0:T(8,128)S(1)}, f32[8,128]{1,0:T(8,128)S(1)}, u32[]{:S(2)}, u32[]{:S(2)}) collective-permute-start(f32[8,128]{1,0:T(8,128)S(1)} %add_add_fusion), channel_id=1, source_target_pairs={{0,4},{1,5},{2,6},{3,7},{4,0},{5,1},{6,2},{7,3},{8,12},{9,13},{10,... | collective-permute-start | bytes 12296 | tf_op jit(solution)/shard_map/ppermute | solution.py:338
  57.6 2.3 %multiply.5 = (bf16[512,3584]{1,0:T(8,128)(2,1)S(1)}, bf16[512,512]{1,0:T(8,128)(2,1)S(1)}) custom-call(bf16[528,256]{1,0:T(8,128)(2,1)S(1)} %collective-permute-done.7.after.folded, bf16[528,256]{1,0:T(8,128)(2,1)S(1)} %collective-permute-done.7.after.folded, bf16[512,3584]{1,0:T(8,128)(2,1)S(1)} %get-tuple-element.79.held_ref), custom_call_target="tpu_custom_call", output_to_operand_aliasing={{0}: (2, {})} | custom-call | flops 1880000000 | bytes 1 | tf_op jit(solution)/shard_map/multiply/pallas_call | solution.py:242
  59.9 7.7 %finish.1 = (bf16[2048,3584]{1,0:T(8,128)(2,1)}, bf16[2,512,512]{2,1,0:T(8,128)(2,1)}, bf16[512,3584]{1,0:T(8,128)(2,1)S(1)}, bf16[512,3584]{1,0:T(8,128)(2,1)S(...) custom-call(s32[6]{0:T(128)S(1)} %pad_add_fusion.order, ...), custom_call_target="tpu_custom_call", output_to_operand_aliasing={{2}: (7, {}), {3}: (8, {}), {4}: (9, {}), {5}: (10, {})} | custom-call | tf_op jit(solution)/shard_map/finish/pallas_call | solution.py:314
  (21 shorter events, 0.1 us)
Async XLA Ops:
  0.7 1.6 %copy-start = (bf16[512,2048]{1,0:T(8,128)(2,1)S(1)}, bf16[512,2048]{1,0:T(8,128)(2,1)}, u32[]{:S(2)}) copy-start(bf16[512,2048]{1,0:T(8,128)(2,1)} %x_ref.1) | copy-start | bytes 6291460
  3.9 17.6 %collective-permute-start = (bf16[528,256]{1,0:T(8,128)(2,1)S(1)}, bf16[528,256]{1,0:T(8,128)(2,1)S(1)}, u32[]{:S(2)}, u32[]{:S(2)}) collective-permute-start(bf16[528,256]{1,0:T(8,128)(2,1)S(1)} %get-tuple-element.49), channel_id=1, source_target_pairs={{0,1},{1,0},{2,3},{3,2},{4,5},{5,4},{6,7},{7,6},{8,9},{9,8},{10,11... | collective-permute-start | bytes 811016 | tf_op jit(solution)/shard_map/ppermute | solution.py:338
  6.9 14.6 %collective-permute-start.1 = (bf16[528,256]{1,0:T(8,128)(2,1)S(1)}, bf16[528,256]{1,0:T(8,128)(2,1)S(1)}, u32[]{:S(2)}, u32[]{:S(2)}) collective-permute-start(bf16[528,256]{1,0:T(8,128)(2,1)S(1)} %get-tuple-element.50), channel_id=1, source_target_pairs={{0,2},{1,3},{2,0},{3,1},{4,6},{5,7},{6,4},{7,5},{8,10},{9,11},{10,... | collective-permute-start | bytes 811016 | tf_op jit(solution)/shard_map/ppermute | solution.py:338
  8.5 13.0 %collective-permute-start.2 = (bf16[528,256]{1,0:T(8,128)(2,1)S(1)}, bf16[528,256]{1,0:T(8,128)(2,1)S(1)}, u32[]{:S(2)}, u32[]{:S(2)}) collective-permute-start(bf16[528,256]{1,0:T(8,128)(2,1)S(1)} %get-tuple-element.51), channel_id=1, source_target_pairs={{0,3},{1,2},{2,1},{3,0},{4,7},{5,6},{6,5},{7,4},{8,11},{9,10},{10,... | collective-permute-start | bytes 811016 | tf_op jit(solution)/shard_map/ppermute | solution.py:338
  19.6 7.7 %collective-permute-start.4 = (bf16[528,256]{1,0:T(8,128)(2,1)S(1)}, bf16[528,256]{1,0:T(8,128)(2,1)S(1)}, u32[]{:S(2)}, u32[]{:S(2)}) collective-permute-start(bf16[528,256]{1,0:T(8,128)(2,1)S(1)} %get-tuple-element.53), channel_id=1, source_target_pairs={{0,1},{1,0},{2,3},{3,2},{4,5},{5,4},{6,7},{7,6},{8,9},{9,8},{10,11... | collective-permute-start | bytes 811016 | tf_op jit(solution)/shard_map/ppermute | solution.py:338
  21.7 14.0 %collective-permute-start.3 = (bf16[528,256]{1,0:T(8,128)(2,1)S(1)}, bf16[528,256]{1,0:T(8,128)(2,1)S(1)}, u32[]{:S(2)}, u32[]{:S(2)}) collective-permute-start(bf16[528,256]{1,0:T(8,128)(2,1)S(1)} %add_convert_fusion.1.mine), channel_id=1, source_target_pairs={{0,4},{1,5},{2,6},{3,7},{4,0},{5,1},{6,2},{7,3},{8,12},{9,13},{10,... | collective-permute-start | bytes 811016 | tf_op jit(solution)/shard_map/ppermute | solution.py:338
  27.4 12.7 %collective-permute-start.6 = (bf16[528,256]{1,0:T(8,128)(2,1)S(1)}, bf16[528,256]{1,0:T(8,128)(2,1)S(1)}, u32[]{:S(2)}, u32[]{:S(2)}) collective-permute-start(bf16[528,256]{1,0:T(8,128)(2,1)S(1)} %add_convert_fusion), channel_id=1, source_target_pairs={{0,2},{1,3},{2,0},{3,1},{4,6},{5,7},{6,4},{7,5},{8,10},{9,11},{10,... | collective-permute-start | bytes 811016 | tf_op jit(solution)/shard_map/ppermute | solution.py:338
  29.1 11.0 %collective-permute-start.5 = (bf16[528,256]{1,0:T(8,128)(2,1)S(1)}, bf16[528,256]{1,0:T(8,128)(2,1)S(1)}, u32[]{:S(2)}, u32[]{:S(2)}) collective-permute-start(bf16[528,256]{1,0:T(8,128)(2,1)S(1)} %get-tuple-element.55), channel_id=1, source_target_pairs={{0,1},{1,0},{2,3},{3,2},{4,5},{5,4},{6,7},{7,6},{8,9},{9,8},{10,11... | collective-permute-start | bytes 811016 | tf_op jit(solution)/shard_map/ppermute | solution.py:338
  38.9 7.3 %collective-permute-start.8 = (bf16[528,256]{1,0:T(8,128)(2,1)S(1)}, bf16[528,256]{1,0:T(8,128)(2,1)S(1)}, u32[]{:S(2)}, u32[]{:S(2)}) collective-permute-start(bf16[528,256]{1,0:T(8,128)(2,1)S(1)} %newton.1.folded.after), channel_id=1, source_target_pairs={{0,1},{1,0},{2,3},{3,2},{4,5},{5,4},{6,7},{7,6},{8,9},{9,8},{10,11... | collective-permute-start | bytes 811016 | tf_op jit(solution)/shard_map/ppermute | solution.py:338
  39.5 7.0 %collective-permute-start.7 = (bf16[528,256]{1,0:T(8,128)(2,1)S(1)}, bf16[528,256]{1,0:T(8,128)(2,1)S(1)}, u32[]{:S(2)}, u32[]{:S(2)}) collective-permute-start(bf16[528,256]{1,0:T(8,128)(2,1)S(1)} %newton.1.folded.after), channel_id=1, source_target_pairs={{0,2},{1,3},{2,0},{3,1},{4,6},{5,7},{6,4},{7,5},{8,10},{9,11},{10,... | collective-permute-start | bytes 811016 | tf_op jit(solution)/shard_map/ppermute | solution.py:338
  40.7 4.3 %collective-permute-start.11 = (f32[8,128]{1,0:T(8,128)S(1)}, f32[8,128]{1,0:T(8,128)S(1)}, u32[]{:S(2)}, u32[]{:S(2)}) collective-permute-start(f32[8,128]{1,0:T(8,128)S(1)} %norm.1), channel_id=1, source_target_pairs={{0,24},{1,25},{2,26},{3,27},{4,28},{5,29},{6,30},{7,31},{8,16},{9,... | collective-permute-start | bytes 12296 | tf_op jit(solution)/shard_map/ppermute | solution.py:338
  41.3 3.6 %collective-permute-start.10 = (f32[8,128]{1,0:T(8,128)S(1)}, f32[8,128]{1,0:T(8,128)S(1)}, u32[]{:S(2)}, u32[]{:S(2)}) collective-permute-start(f32[8,128]{1,0:T(8,128)S(1)} %norm.1), channel_id=1, source_target_pairs={{0,16},{1,17},{2,18},{3,19},{4,20},{5,21},{6,22},{7,23},{8,24},{9,... | collective-permute-start | bytes 12296 | tf_op jit(solution)/shard_map/ppermute | solution.py:338
  42.3 2.6 %collective-permute-start.9 = (f32[8,128]{1,0:T(8,128)S(1)}, f32[8,128]{1,0:T(8,128)S(1)}, u32[]{:S(2)}, u32[]{:S(2)}) collective-permute-start(f32[8,128]{1,0:T(8,128)S(1)} %norm.1), channel_id=1, source_target_pairs={{0,8},{1,9},{2,10},{3,11},{4,12},{5,13},{6,14},{7,15},{8,0},{9,1},... | collective-permute-start | bytes 12296 | tf_op jit(solution)/shard_map/ppermute | solution.py:338
  46.5 7.5 %collective-permute-start.12 = (bf16[528,256]{1,0:T(8,128)(2,1)S(1)}, bf16[528,256]{1,0:T(8,128)(2,1)S(1)}, u32[]{:S(2)}, u32[]{:S(2)}) collective-permute-start(bf16[528,256]{1,0:T(8,128)(2,1)S(1)} %collective-permute-done.7.after.folded), channel_id=1, source_target_pairs={{0,1},{1,0},{2,3},{3,2},{4,5},{5,4},{6,7},{7,6},{8,9},{9,8},{10,11... | collective-permute-start | bytes 811016 | tf_op jit(solution)/shard_map/ppermute | solution.py:338
  48.0 6.0 %collective-permute-start.15 = (f32[8,128]{1,0:T(8,128)S(1)}, f32[8,128]{1,0:T(8,128)S(1)}, u32[]{:S(2)}, u32[]{:S(2)}) collective-permute-start(f32[8,128]{1,0:T(8,128)S(1)} %add_add_fusion.1), channel_id=1, source_target_pairs={{0,3},{1,2},{2,1},{3,0},{4,7},{5,6},{6,5},{7,4},{8,11},{9,10},{10,... | collective-permute-start | bytes 12296 | tf_op jit(solution)/shard_map/ppermute | solution.py:338
  49.7 4.3 %collective-permute-start.14 = (f32[8,128]{1,0:T(8,128)S(1)}, f32[8,128]{1,0:T(8,128)S(1)}, u32[]{:S(2)}, u32[]{:S(2)}) collective-permute-start(f32[8,128]{1,0:T(8,128)S(1)} %add_add_fusion.1), channel_id=1, source_target_pairs={{0,2},{1,3},{2,0},{3,1},{4,6},{5,7},{6,4},{7,5},{8,10},{9,11},{10,... | collective-permute-start | bytes 12296 | tf_op jit(solution)/shard_map/ppermute | solution.py:338
  50.0 4.0 %collective-permute-start.13 = (f32[8,128]{1,0:T(8,128)S(1)}, f32[8,128]{1,0:T(8,128)S(1)}, u32[]{:S(2)}, u32[]{:S(2)}) collective-permute-start(f32[8,128]{1,0:T(8,128)S(1)} %add_add_fusion.1), channel_id=1, source_target_pairs={{0,1},{1,0},{2,3},{3,2},{4,5},{5,4},{6,7},{7,6},{8,9},{9,8},{10,11... | collective-permute-start | bytes 12296 | tf_op jit(solution)/shard_map/ppermute | solution.py:338
  54.0 6.0 %copy-start.1 = (s32[4,4]{1,0:T(4,128)S(1)}, s32[4,4]{1,0:T(4,128)}, u32[]{:S(2)}) copy-start(s32[4,4]{1,0:T(4,128)} %owner_slot.1) | copy-start | bytes 196
  54.0 5.9 %collective-permute-start.16 = (f32[8,128]{1,0:T(8,128)S(1)}, f32[8,128]{1,0:T(8,128)S(1)}, u32[]{:S(2)}, u32[]{:S(2)}) collective-permute-start(f32[8,128]{1,0:T(8,128)S(1)} %add_add_fusion), channel_id=1, source_target_pairs={{0,4},{1,5},{2,6},{3,7},{4,0},{5,1},{6,2},{7,3},{8,12},{9,13},{10,... | collective-permute-start | bytes 12296 | tf_op jit(solution)/shard_map/ppermute | solution.py:338

commit v11 on v10

--- a/solution.py
+++ b/solution.py
@@ -246,7 +246,7 @@
         out_specs=[VMEM] * 2,
         input_output_aliases={2: 0},
         compiler_params=params(12),
-        cost_estimate=pl.CostEstimate(flops=1880000000, bytes_accessed=1, transcendentals=0),
+        cost_estimate=pl.CostEstimate(flops=1, bytes_accessed=1, transcendentals=0),
         name="multiply",
     )(after, folded, held)
 
@@ -384,7 +384,7 @@
         roots.append(root)
 
     sums = norm(root, grams[0], from_y, from_z, squares)
-    early, arrivals = {0:[0],1:[1],2:[2]}, {0:[1,2],1:[3]}
+    early, arrivals = {0:[0],1:[1],2:[2]}, {1:[1,2],2:[3]}
     for step, flips in enumerate(rounds()):
         received = [swap(sums, flip) for flip in flips]
         for place in early.get(step, ()):

time: 68 us -> 68 us (level)
  starting transfers between devices: 24.2 us -> 23.4 us
  waiting for transfers between devices: 9.53 us -> 10.3 us
    ppermute x17, waiting for transfers between devices: 9.53 us -> 10.3 us  [swap(): return lax.ppermute(value, axes, [(i, i ^ flip) for i in range(count)])]
    ppermute x17, starting transfers between devices: 24.2 us -> 23.4 us  [swap(): return lax.ppermute(value, axes, [(i, i ^ flip) for i in range(count)])]
  transfers between devices with their start and end apart: 17 -> 17, of which waited for: 4 -> 5; matrix products, arithmetic and copies ran while one was open for 0% -> 0% of each run, Pallas kernels for 32% -> 32%
where the time goes in v11:
time: 68 us; the launch traced here: 67.8 us
  Pallas kernels  31.2 us (46%)
  starting transfers between devices  23.4 us (34%)
  waiting for transfers between devices  10.3 us (15%)
  local copies, waits for them, and re-layouts  1.6 us (2%)
  between operations  0.94 us (1%)
    ppermute x17, starting transfers between devices, swap(): return lax.ppermute(value, axes, [(i, i ^ flip) for i in range(count)])  23.4 us
    pallas_call x1, Pallas kernels, gram(): pl.pallas_call(gram_kernel, out_shape=[pltpu.VMEM((BLK, columns), BF16)]...  11 us
    ppermute x17, waiting for transfers between devices, swap(): return lax.ppermute(value, axes, [(i, i ^ flip) for i in range(count)])  10.3 us
    pallas_call x1, Pallas kernels, finish(): pl.pallas_call(finish_kernel, out_shape=[jax.ShapeDtypeStruct((QUAD * BLK...  7.71 us
    pallas_call x3, Pallas kernels, multiply(): pl.pallas_call(multiply_kernel, out_shape=[pltpu.VMEM(held.shape, BF16),...  7.1 us
    pallas_call x1, Pallas kernels, newton(): pl.pallas_call(functools.partial(newton_kernel, tokens), out_shape=jax.Sh...  3.2 us
    unnamed x4, local copies, waits for them, and re-layouts  1.6 us
    pallas_call x1, Pallas kernels, statistics(): pl.pallas_call(stat_kernel, out_shape=[jax.ShapeDtypeStruct((FOLD, HALF),...  1.59 us
  transfers between devices with their start and end apart: 17, of which 5 were waited for; matrix products, arithmetic and copies ran while one was open for 0% of the time, Pallas kernels for 32%

profile of v11, /device:TPU:0, one launch (start us, length us, event | category | flops | bytes accessed | tf_op | source)
XLA Modules:
  0.0 67.8 jit_solution(7831768009365324587)
XLA Ops:
  0.7 0.1 pad_add_fusion.order
  0.7 1.6 %copy-done = bf16[512,2048]{1,0:T(8,128)(2,1)S(1)} copy-done((bf16[512,2048]{1,0:T(8,128)(2,1)S(1)}, bf16[512,2048]{1,0:T(8,128)(2,1)}, u32[]{:S(2)}) %copy-start) | copy-done | bytes 2097176
  2.3 1.6 %statistics.1 = (bf16[528,256]{1,0:T(8,128)(2,1)S(1)}, bf16[528,256]{1,0:T(8,128)(2,1)S(1)}, bf16[528,256]{1,0:T(8,128)(2,1)S(1)}, bf16[528,256]{1,0:T(8,128)(2,1)S(1)}) custom-call(s32[6]{0:T(128)S(1)} %pad_add_fusion.order, bf16[512,2048]{1,0:T(8,128)(2,1)S(1)} %copy-done), custom_call_target="tpu_custom_call" | custom-call | tf_op jit(solution)/shard_map/statistics/pallas_call | solution.py:72
  3.9 3.0 %collective-permute-start = (bf16[528,256]{1,0:T(8,128)(2,1)S(1)}, bf16[528,256]{1,0:T(8,128)(2,1)S(1)}, u32[]{:S(2)}, u32[]{:S(2)}) collective-permute-start(bf16[528,256]{1,0:T(8,128)(2,1)S(1)} %get-tuple-element.46), channel_id=1, source_target_pairs={{0,1},{1,0},{2,3},{3,2},{4,5},{5,4},{6,7},{7,6},{8,9},{9,8},{10,11... | collective-permute-start | bytes 811016 | tf_op jit(solution)/shard_map/ppermute | solution.py:338
  6.9 1.6 %collective-permute-start.1 = (bf16[528,256]{1,0:T(8,128)(2,1)S(1)}, bf16[528,256]{1,0:T(8,128)(2,1)S(1)}, u32[]{:S(2)}, u32[]{:S(2)}) collective-permute-start(bf16[528,256]{1,0:T(8,128)(2,1)S(1)} %get-tuple-element.47), channel_id=1, source_target_pairs={{0,2},{1,3},{2,0},{3,1},{4,6},{5,7},{6,4},{7,5},{8,10},{9,11},{10,... | collective-permute-start | bytes 811016 | tf_op jit(solution)/shard_map/ppermute | solution.py:338
  8.5 11.0 %gram.1 = (bf16[512,3584]{1,0:T(8,128)(2,1)S(1)}, bf16[512,3584]{1,0:T(8,128)(2,1)S(1)}, bf16[512,3584]{1,0:T(8,128)(2,1)S(1)}, bf16[512,3584]{1,0:T(8,128)(2,1)...) custom-call(s32[6]{0:T(128)S(1)} %pad_add_fusion.order, ...), custom_call_target="tpu_custom_call" | custom-call | flops 7516192768 | bytes 14680064 | tf_op jit(solution)/shard_map/gram/pallas_call | solution.py:124
  19.6 2.0 %collective-permute-start.4 = (bf16[528,256]{1,0:T(8,128)(2,1)S(1)}, bf16[528,256]{1,0:T(8,128)(2,1)S(1)}, u32[]{:S(2)}, u32[]{:S(2)}) collective-permute-start(bf16[528,256]{1,0:T(8,128)(2,1)S(1)} %get-tuple-element.50), channel_id=1, source_target_pairs={{0,1},{1,0},{2,3},{3,2},{4,5},{5,4},{6,7},{7,6},{8,9},{9,8},{10,11... | collective-permute-start | bytes 811016 | tf_op jit(solution)/shard_map/ppermute | solution.py:338
  21.6 0.1 add_convert_fusion.1.mine
  21.7 2.7 %collective-permute-start.3 = (bf16[528,256]{1,0:T(8,128)(2,1)S(1)}, bf16[528,256]{1,0:T(8,128)(2,1)S(1)}, u32[]{:S(2)}, u32[]{:S(2)}) collective-permute-start(bf16[528,256]{1,0:T(8,128)(2,1)S(1)} %add_convert_fusion.1.mine), channel_id=1, source_target_pairs={{0,4},{1,5},{2,6},{3,7},{4,0},{5,1},{6,2},{7,3},{8,12},{9,13},{10,... | collective-permute-start | bytes 811016 | tf_op jit(solution)/shard_map/ppermute | solution.py:338
  24.4 2.9 %collective-permute-done.4 = bf16[528,256]{1,0:T(8,128)(2,1)S(1)} collective-permute-done((bf16[528,256]{1,0:T(8,128)(2,1)S(1)}, bf16[528,256]{1,0:T(8,128)(2,1)S(1)}, u32[]{:S(2)}, u32[]{:S(2)}) %collective-permute-start.4) | collective-permute-done | bytes 270368 | tf_op jit(solution)/shard_map/ppermute | solution.py:338
  27.4 1.7 %collective-permute-start.6 = (bf16[528,256]{1,0:T(8,128)(2,1)S(1)}, bf16[528,256]{1,0:T(8,128)(2,1)S(1)}, u32[]{:S(2)}, u32[]{:S(2)}) collective-permute-start(bf16[528,256]{1,0:T(8,128)(2,1)S(1)} %add_convert_fusion), channel_id=1, source_target_pairs={{0,2},{1,3},{2,0},{3,1},{4,6},{5,7},{6,4},{7,5},{8,10},{9,11},{10,... | collective-permute-start | bytes 811016 | tf_op jit(solution)/shard_map/ppermute | solution.py:338
  29.1 1.5 %collective-permute-start.5 = (bf16[528,256]{1,0:T(8,128)(2,1)S(1)}, bf16[528,256]{1,0:T(8,128)(2,1)S(1)}, u32[]{:S(2)}, u32[]{:S(2)}) collective-permute-start(bf16[528,256]{1,0:T(8,128)(2,1)S(1)} %get-tuple-element.52), channel_id=1, source_target_pairs={{0,1},{1,0},{2,3},{3,2},{4,5},{5,4},{6,7},{7,6},{8,9},{9,8},{10,11... | collective-permute-start | bytes 811016 | tf_op jit(solution)/shard_map/ppermute | solution.py:338
  30.6 5.0 %collective-permute-done.3.other = bf16[528,256]{1,0:T(8,128)(2,1)S(1)} collective-permute-done((bf16[528,256]{1,0:T(8,128)(2,1)S(1)}, bf16[528,256]{1,0:T(8,128)(2,1)S(1)}, u32[]{:S(2)}, u32[]{:S(2)}) %collective-permute-start.3) | collective-permute-done | bytes 270368 | tf_op jit(solution)/shard_map/ppermute | solution.py:338
  35.7 3.2 %newton.1.folded.after = bf16[528,256]{1,0:T(8,128)(2,1)S(1)} custom-call(f32[1,256]{1,0:T(1,128)S(1)} %get-tuple-element.45.after.squares, bf16[528,256]{1,0:T(8,128)(2,1)S(1)} %add_convert_fusion.1.mine, bf16[528,256]{1,0:T(8,128)(2,1)S(1)} %collective-permute-done.3.other), custom_call_target="tpu_custom_call" | custom-call | flops 2147483648 | bytes 2097152 | tf_op jit(solution)/shard_map/newton/pallas_call | solution.py:183
  38.9 0.7 collective-permute-start.10
  39.6 0.5 collective-permute-start.11
  40.1 0.6 norm.1
  40.6 0.6 collective-permute-start.9
  41.3 1.0 %collective-permute-start.8 = (f32[8,128]{1,0:T(8,128)S(1)}, f32[8,128]{1,0:T(8,128)S(1)}, u32[]{:S(2)}, u32[]{:S(2)}) collective-permute-start(f32[8,128]{1,0:T(8,128)S(1)} %norm.1), channel_id=1, source_target_pairs={{0,16},{1,17},{2,18},{3,19},{4,20},{5,21},{6,22},{7,23},{8,24},{9,... | collective-permute-start | bytes 12296 | tf_op jit(solution)/shard_map/ppermute | solution.py:338
  42.3 0.3 collective-permute-start.7
  42.6 2.3 %multiply.3 = (bf16[512,3584]{1,0:T(8,128)(2,1)S(1)}, bf16[512,512]{1,0:T(8,128)(2,1)S(1)}) custom-call(bf16[528,256]{1,0:T(8,128)(2,1)S(1)} %newton.1.folded.after, bf16[528,256]{1,0:T(8,128)(2,1)S(1)} %newton.1.folded.after, bf16[512,3584]{1,0:T(8,128)(2,1)S(1)} %get-tuple-element.55.held_ref), custom_call_target="tpu_custom_call", output_to_operand_aliasing={{0}: (2, {})} | custom-call | flops 1 | bytes 1 | tf_op jit(solution)/shard_map/multiply/pallas_call | solution.py:242
  44.9 1.3 %collective-permute-done.10.after.folded = bf16[528,256]{1,0:T(8,128)(2,1)S(1)} collective-permute-done((bf16[528,256]{1,0:T(8,128)(2,1)S(1)}, bf16[528,256]{1,0:T(8,128)(2,1)S(1)}, u32[]{:S(2)}, u32[]{:S(2)}) %collective-permute-start.10) | collective-permute-done | bytes 270368 | tf_op jit(solution)/shard_map/ppermute | solution.py:338
  46.2 0.5 collective-permute-start.15
  46.8 2.7 %collective-permute-start.14 = (f32[8,128]{1,0:T(8,128)S(1)}, f32[8,128]{1,0:T(8,128)S(1)}, u32[]{:S(2)}, u32[]{:S(2)}) collective-permute-start(f32[8,128]{1,0:T(8,128)S(1)} %add_add_fusion.1), channel_id=1, source_target_pairs={{0,3},{1,2},{2,1},{3,0},{4,7},{5,6},{6,5},{7,4},{8,11},{9,10},{10,... | collective-permute-start | bytes 12296 | tf_op jit(solution)/shard_map/ppermute | solution.py:338
  49.4 0.3 collective-permute-start.13
  49.7 0.5 collective-permute-start.12
  50.2 2.5 %multiply.4 = (bf16[512,3584]{1,0:T(8,128)(2,1)S(1)}, bf16[512,512]{1,0:T(8,128)(2,1)S(1)}) custom-call(bf16[528,256]{1,0:T(8,128)(2,1)S(1)} %collective-permute-done.11.after.folded, bf16[528,256]{1,0:T(8,128)(2,1)S(1)} %collective-permute-done.11.after.folded, bf16[512,3584]{1,0:T(8,128)(2,1)S(1)} %get-tuple-element.60.held_ref), custom_call_target="tpu_custom_call", output_to_operand_aliasing={{0}: (2, {})} | custom-call | flops 1 | bytes 1 | tf_op jit(solution)/shard_map/multiply/pallas_call | solution.py:242
  52.7 0.3 collective-permute-done.13
  53.0 0.8 %collective-permute-done.12 = f32[8,128]{1,0:T(8,128)S(1)} collective-permute-done((f32[8,128]{1,0:T(8,128)S(1)}, f32[8,128]{1,0:T(8,128)S(1)}, u32[]{:S(2)}, u32[]{:S(2)}) %collective-permute-start.12) | collective-permute-done | bytes 4128 | tf_op jit(solution)/shard_map/ppermute | solution.py:338
  53.8 3.8 %collective-permute-start.16 = (f32[8,128]{1,0:T(8,128)S(1)}, f32[8,128]{1,0:T(8,128)S(1)}, u32[]{:S(2)}, u32[]{:S(2)}) collective-permute-start(f32[8,128]{1,0:T(8,128)S(1)} %add_add_fusion), channel_id=1, source_target_pairs={{0,4},{1,5},{2,6},{3,7},{4,0},{5,1},{6,2},{7,3},{8,12},{9,13},{10,... | collective-permute-start | bytes 12296 | tf_op jit(solution)/shard_map/ppermute | solution.py:338
  57.6 2.3 %multiply.5 = (bf16[512,3584]{1,0:T(8,128)(2,1)S(1)}, bf16[512,512]{1,0:T(8,128)(2,1)S(1)}) custom-call(bf16[528,256]{1,0:T(8,128)(2,1)S(1)} %collective-permute-done.10.after.folded, bf16[528,256]{1,0:T(8,128)(2,1)S(1)} %collective-permute-done.10.after.folded, bf16[512,3584]{1,0:T(8,128)(2,1)S(1)} %get-tuple-element.72.held_ref), custom_call_target="tpu_custom_call", output_to_operand_aliasing={{0}: (2, {})} | custom-call | flops 1 | bytes 1 | tf_op jit(solution)/shard_map/multiply/pallas_call | solution.py:242
  59.9 7.7 %finish.1 = (bf16[2048,3584]{1,0:T(8,128)(2,1)}, bf16[2,512,512]{2,1,0:T(8,128)(2,1)}, bf16[512,3584]{1,0:T(8,128)(2,1)S(1)}, bf16[512,3584]{1,0:T(8,128)(2,1)S(...) custom-call(s32[6]{0:T(128)S(1)} %pad_add_fusion.order, ...), custom_call_target="tpu_custom_call", output_to_operand_aliasing={{2}: (7, {}), {3}: (8, {}), {4}: (9, {}), {5}: (10, {})} | custom-call | tf_op jit(solution)/shard_map/finish/pallas_call | solution.py:314
  (21 shorter events, 0.1 us)
Async XLA Ops:
  0.7 1.6 %copy-start = (bf16[512,2048]{1,0:T(8,128)(2,1)S(1)}, bf16[512,2048]{1,0:T(8,128)(2,1)}, u32[]{:S(2)}) copy-start(bf16[512,2048]{1,0:T(8,128)(2,1)} %x_ref.1) | copy-start | bytes 6291460
  3.9 17.6 %collective-permute-start = (bf16[528,256]{1,0:T(8,128)(2,1)S(1)}, bf16[528,256]{1,0:T(8,128)(2,1)S(1)}, u32[]{:S(2)}, u32[]{:S(2)}) collective-permute-start(bf16[528,256]{1,0:T(8,128)(2,1)S(1)} %get-tuple-element.46), channel_id=1, source_target_pairs={{0,1},{1,0},{2,3},{3,2},{4,5},{5,4},{6,7},{7,6},{8,9},{9,8},{10,11... | collective-permute-start | bytes 811016 | tf_op jit(solution)/shard_map/ppermute | solution.py:338
  6.9 14.6 %collective-permute-start.1 = (bf16[528,256]{1,0:T(8,128)(2,1)S(1)}, bf16[528,256]{1,0:T(8,128)(2,1)S(1)}, u32[]{:S(2)}, u32[]{:S(2)}) collective-permute-start(bf16[528,256]{1,0:T(8,128)(2,1)S(1)} %get-tuple-element.47), channel_id=1, source_target_pairs={{0,2},{1,3},{2,0},{3,1},{4,6},{5,7},{6,4},{7,5},{8,10},{9,11},{10,... | collective-permute-start | bytes 811016 | tf_op jit(solution)/shard_map/ppermute | solution.py:338
  8.5 13.0 %collective-permute-start.2 = (bf16[528,256]{1,0:T(8,128)(2,1)S(1)}, bf16[528,256]{1,0:T(8,128)(2,1)S(1)}, u32[]{:S(2)}, u32[]{:S(2)}) collective-permute-start(bf16[528,256]{1,0:T(8,128)(2,1)S(1)} %get-tuple-element.48), channel_id=1, source_target_pairs={{0,3},{1,2},{2,1},{3,0},{4,7},{5,6},{6,5},{7,4},{8,11},{9,10},{10,... | collective-permute-start | bytes 811016 | tf_op jit(solution)/shard_map/ppermute | solution.py:338
  19.6 7.7 %collective-permute-start.4 = (bf16[528,256]{1,0:T(8,128)(2,1)S(1)}, bf16[528,256]{1,0:T(8,128)(2,1)S(1)}, u32[]{:S(2)}, u32[]{:S(2)}) collective-permute-start(bf16[528,256]{1,0:T(8,128)(2,1)S(1)} %get-tuple-element.50), channel_id=1, source_target_pairs={{0,1},{1,0},{2,3},{3,2},{4,5},{5,4},{6,7},{7,6},{8,9},{9,8},{10,11... | collective-permute-start | bytes 811016 | tf_op jit(solution)/shard_map/ppermute | solution.py:338
  21.7 14.0 %collective-permute-start.3 = (bf16[528,256]{1,0:T(8,128)(2,1)S(1)}, bf16[528,256]{1,0:T(8,128)(2,1)S(1)}, u32[]{:S(2)}, u32[]{:S(2)}) collective-permute-start(bf16[528,256]{1,0:T(8,128)(2,1)S(1)} %add_convert_fusion.1.mine), channel_id=1, source_target_pairs={{0,4},{1,5},{2,6},{3,7},{4,0},{5,1},{6,2},{7,3},{8,12},{9,13},{10,... | collective-permute-start | bytes 811016 | tf_op jit(solution)/shard_map/ppermute | solution.py:338
  27.4 12.7 %collective-permute-start.6 = (bf16[528,256]{1,0:T(8,128)(2,1)S(1)}, bf16[528,256]{1,0:T(8,128)(2,1)S(1)}, u32[]{:S(2)}, u32[]{:S(2)}) collective-permute-start(bf16[528,256]{1,0:T(8,128)(2,1)S(1)} %add_convert_fusion), channel_id=1, source_target_pairs={{0,2},{1,3},{2,0},{3,1},{4,6},{5,7},{6,4},{7,5},{8,10},{9,11},{10,... | collective-permute-start | bytes 811016 | tf_op jit(solution)/shard_map/ppermute | solution.py:338
  29.1 11.0 %collective-permute-start.5 = (bf16[528,256]{1,0:T(8,128)(2,1)S(1)}, bf16[528,256]{1,0:T(8,128)(2,1)S(1)}, u32[]{:S(2)}, u32[]{:S(2)}) collective-permute-start(bf16[528,256]{1,0:T(8,128)(2,1)S(1)} %get-tuple-element.52), channel_id=1, source_target_pairs={{0,1},{1,0},{2,3},{3,2},{4,5},{5,4},{6,7},{7,6},{8,9},{9,8},{10,11... | collective-permute-start | bytes 811016 | tf_op jit(solution)/shard_map/ppermute | solution.py:338
  38.9 7.3 %collective-permute-start.10 = (bf16[528,256]{1,0:T(8,128)(2,1)S(1)}, bf16[528,256]{1,0:T(8,128)(2,1)S(1)}, u32[]{:S(2)}, u32[]{:S(2)}) collective-permute-start(bf16[528,256]{1,0:T(8,128)(2,1)S(1)} %newton.1.folded.after), channel_id=1, source_target_pairs={{0,2},{1,3},{2,0},{3,1},{4,6},{5,7},{6,4},{7,5},{8,10},{9,11},{10,... | collective-permute-start | bytes 811016 | tf_op jit(solution)/shard_map/ppermute | solution.py:338
  39.6 10.7 %collective-permute-start.11 = (bf16[528,256]{1,0:T(8,128)(2,1)S(1)}, bf16[528,256]{1,0:T(8,128)(2,1)S(1)}, u32[]{:S(2)}, u32[]{:S(2)}) collective-permute-start(bf16[528,256]{1,0:T(8,128)(2,1)S(1)} %newton.1.folded.after), channel_id=1, source_target_pairs={{0,1},{1,0},{2,3},{3,2},{4,5},{5,4},{6,7},{7,6},{8,9},{9,8},{10,11... | collective-permute-start | bytes 811016 | tf_op jit(solution)/shard_map/ppermute | solution.py:338
  40.6 4.3 %collective-permute-start.9 = (f32[8,128]{1,0:T(8,128)S(1)}, f32[8,128]{1,0:T(8,128)S(1)}, u32[]{:S(2)}, u32[]{:S(2)}) collective-permute-start(f32[8,128]{1,0:T(8,128)S(1)} %norm.1), channel_id=1, source_target_pairs={{0,24},{1,25},{2,26},{3,27},{4,28},{5,29},{6,30},{7,31},{8,16},{9,... | collective-permute-start | bytes 12296 | tf_op jit(solution)/shard_map/ppermute | solution.py:338
  41.3 3.6 %collective-permute-start.8 = (f32[8,128]{1,0:T(8,128)S(1)}, f32[8,128]{1,0:T(8,128)S(1)}, u32[]{:S(2)}, u32[]{:S(2)}) collective-permute-start(f32[8,128]{1,0:T(8,128)S(1)} %norm.1), channel_id=1, source_target_pairs={{0,16},{1,17},{2,18},{3,19},{4,20},{5,21},{6,22},{7,23},{8,24},{9,... | collective-permute-start | bytes 12296 | tf_op jit(solution)/shard_map/ppermute | solution.py:338
  42.3 2.6 %collective-permute-start.7 = (f32[8,128]{1,0:T(8,128)S(1)}, f32[8,128]{1,0:T(8,128)S(1)}, u32[]{:S(2)}, u32[]{:S(2)}) collective-permute-start(f32[8,128]{1,0:T(8,128)S(1)} %norm.1), channel_id=1, source_target_pairs={{0,8},{1,9},{2,10},{3,11},{4,12},{5,13},{6,14},{7,15},{8,0},{9,1},... | collective-permute-start | bytes 12296 | tf_op jit(solution)/shard_map/ppermute | solution.py:338
  46.2 13.7 %collective-permute-start.15 = (bf16[528,256]{1,0:T(8,128)(2,1)S(1)}, bf16[528,256]{1,0:T(8,128)(2,1)S(1)}, u32[]{:S(2)}, u32[]{:S(2)}) collective-permute-start(bf16[528,256]{1,0:T(8,128)(2,1)S(1)} %collective-permute-done.10.after.folded), channel_id=1, source_target_pairs={{0,1},{1,0},{2,3},{3,2},{4,5},{5,4},{6,7},{7,6},{8,9},{9,8},{10,11... | collective-permute-start | bytes 811016 | tf_op jit(solution)/shard_map/ppermute | solution.py:338
  46.8 6.0 %collective-permute-start.14 = (f32[8,128]{1,0:T(8,128)S(1)}, f32[8,128]{1,0:T(8,128)S(1)}, u32[]{:S(2)}, u32[]{:S(2)}) collective-permute-start(f32[8,128]{1,0:T(8,128)S(1)} %add_add_fusion.1), channel_id=1, source_target_pairs={{0,3},{1,2},{2,1},{3,0},{4,7},{5,6},{6,5},{7,4},{8,11},{9,10},{10,... | collective-permute-start | bytes 12296 | tf_op jit(solution)/shard_map/ppermute | solution.py:338
  49.4 3.6 %collective-permute-start.13 = (f32[8,128]{1,0:T(8,128)S(1)}, f32[8,128]{1,0:T(8,128)S(1)}, u32[]{:S(2)}, u32[]{:S(2)}) collective-permute-start(f32[8,128]{1,0:T(8,128)S(1)} %add_add_fusion.1), channel_id=1, source_target_pairs={{0,2},{1,3},{2,0},{3,1},{4,6},{5,7},{6,4},{7,5},{8,10},{9,11},{10,... | collective-permute-start | bytes 12296 | tf_op jit(solution)/shard_map/ppermute | solution.py:338
  49.7 4.1 %collective-permute-start.12 = (f32[8,128]{1,0:T(8,128)S(1)}, f32[8,128]{1,0:T(8,128)S(1)}, u32[]{:S(2)}, u32[]{:S(2)}) collective-permute-start(f32[8,128]{1,0:T(8,128)S(1)} %add_add_fusion.1), channel_id=1, source_target_pairs={{0,1},{1,0},{2,3},{3,2},{4,5},{5,4},{6,7},{7,6},{8,9},{9,8},{10,11... | collective-permute-start | bytes 12296 | tf_op jit(solution)/shard_map/ppermute | solution.py:338
  50.2 9.7 %copy-start.1 = (s32[4,4]{1,0:T(4,128)S(1)}, s32[4,4]{1,0:T(4,128)}, u32[]{:S(2)}) copy-start(s32[4,4]{1,0:T(4,128)} %owner_slot.1) | copy-start | bytes 196
  53.8 6.1 %collective-permute-start.16 = (f32[8,128]{1,0:T(8,128)S(1)}, f32[8,128]{1,0:T(8,128)S(1)}, u32[]{:S(2)}, u32[]{:S(2)}) collective-permute-start(f32[8,128]{1,0:T(8,128)S(1)} %add_add_fusion), channel_id=1, source_target_pairs={{0,4},{1,5},{2,6},{3,7},{4,0},{5,1},{6,2},{7,3},{8,12},{9,13},{10,... | collective-permute-start | bytes 12296 | tf_op jit(solution)/shard_map/ppermute | solution.py:338

commit v12 on v11

--- a/solution.py
+++ b/solution.py
@@ -10,7 +10,8 @@
 
 BLK = 512
 HALF = BLK // 2
-FOLD = BLK + 16
+TAIL = HALF + 16
+FOLD = HALF + TAIL
 ITERS = 3
 SLOTS = 2
 QUAD = 4
@@ -56,27 +57,43 @@
     return first, last
 
 
+def folded_shapes(*splits):
+    rows = [part for split in splits for part in ((HALF, TAIL) if split else (FOLD,))]
+    return [jax.ShapeDtypeStruct((part, HALF), BF16) for part in rows]
+
+
+def store_folded(refs, cross, first, last):
+    body, diagonal = fold(first, last)
+    refs = list(refs) if len(refs) > 1 else [refs[0].at[:HALF], refs[0].at[HALF:]]
+    refs[0][...] = cross.astype(BF16)
+    refs[1][:HALF] = body.astype(BF16)
+    refs[1][HALF:] = diagonal.astype(BF16)
+
+
+def load_folded(refs):
+    return (refs[0][:HALF], refs[0][HALF:]) if len(refs) == 1 else (refs[0][...], refs[1][...])
+
+
 def stat_kernel(order, x_ref, *out):
-    for place in (1, 2, 3, 0):
+    for place, refs in enumerate((out[:1], out[1:2], out[2:3], out[3:])):
         start = pl.multiple_of(order[place] * BLK, BLK)
         left = x_ref[:, pl.ds(start, HALF)]
         right = x_ref[:, pl.ds(pl.multiple_of(start + HALF, HALF), HALF)]
         along = ((0,), (0,))
-        out[place][:HALF] = dot(left, right, along).astype(BF16)
-        body, diagonal = fold(dot(left, left, along), dot(right, right, along))
-        out[place][HALF:BLK] = body.astype(BF16)
-        out[place][BLK:] = diagonal.astype(BF16)
+        store_folded(refs, dot(left, right, along), dot(left, left, along), dot(right, right, along))
 
 
 def statistics(order, activations):
-    return pl.pallas_call(
+    shapes = folded_shapes(False, False, False, True)
+    a, b, c, *d = pl.pallas_call(
         stat_kernel,
-        out_shape=[jax.ShapeDtypeStruct((FOLD, HALF), BF16)] * QUAD,
+        out_shape=shapes,
         in_specs=[SMEM, VMEM],
-        out_specs=[VMEM] * QUAD,
+        out_specs=[VMEM] * len(shapes),
         compiler_params=params(12),
         name="statistics",
     )(order, activations)
+    return a, b, c, d
 
 
 def chunks(width, size):
@@ -112,10 +129,7 @@
         last[...] = dot(whole[HALF:], whole[HALF:], across)
         squares = jnp.where(row == col, left[:HALF] + last[...], 0.0)
         norm_ref[...] += jnp.sum(squares, axis=0, keepdims=True)
-        body, diagonal = fold(left[:HALF], last[...])
-        folded[place][:HALF] = left[HALF:].astype(BF16)
-        folded[place][HALF:BLK] = body.astype(BF16)
-        folded[place][BLK:] = diagonal.astype(BF16)
+        store_folded(folded[place : place + 1], left[HALF:], left[:HALF], last[...])
 
 
 def gram(order, gradient, after):
@@ -146,10 +160,10 @@
     return dot(left.astype(BF16), right.astype(BF16))
 
 
-def newton_kernel(tokens, after, mine, other, root, held):
-    total = (mine[...].astype(F32) + other[...].astype(F32)) / tokens
-    cross = total[:HALF]
-    first, last = unfold(total[HALF:BLK], total[BLK : BLK + 1])
+def newton_kernel(tokens, after, mine0, mine1, other0, other1, root, root0, root1, held):
+    cross = (mine0[...].astype(F32) + other0[...].astype(F32)) / tokens
+    rest = (mine1[...].astype(F32) + other1[...].astype(F32)) / tokens
+    first, last = unfold(rest[:HALF], rest[HALF : HALF + 1])
     held[:HALF, :HALF] = first
     held[:HALF, HALF:] = cross
     held[HALF:, :HALF] = cross.T
@@ -173,30 +187,29 @@
             fourth = 2.0 * square + product(square, square)
             iterate = iterate + product(fourth, iterate)
     held[...] = (estimate + identity) * jnp.sqrt(jnp.sqrt(scale))
-    root[:HALF] = held[:HALF, HALF:].astype(BF16)
-    body, diagonal = fold(held[:HALF, :HALF], held[HALF:, HALF:])
-    root[HALF:BLK] = body.astype(BF16)
-    root[BLK:] = diagonal.astype(BF16)
+    store_folded((root0, root1), held[:HALF, HALF:], held[:HALF, :HALF], held[HALF:, HALF:])
+    root[:HALF] = root0[...]
+    root[HALF:] = root1[...]
 
 
 def newton(tokens, after, mine, other):
     return pl.pallas_call(
         functools.partial(newton_kernel, tokens),
-        out_shape=jax.ShapeDtypeStruct((FOLD, HALF), BF16),
-        in_specs=[ANY, VMEM, VMEM],
-        out_specs=VMEM,
+        out_shape=folded_shapes(False, True),
+        in_specs=[ANY] + [VMEM] * 4,
+        out_specs=[VMEM] * 3,
         scratch_shapes=[pltpu.VMEM((BLK, BLK), F32)],
         compiler_params=params(12),
         cost_estimate=pl.CostEstimate(
             flops=16 * BLK**3, bytes_accessed=8 * BLK * BLK, transcendentals=0
         ),
         name="newton",
-    )(after, mine, other)
-
-
-def unfold_root(folded, root_ref):
-    cross = folded[:HALF]
-    rest = folded[HALF:].astype(F32)
+    )(after, *mine, *other)
+
+
+def unfold_root(refs, root_ref):
+    cross, rest = load_folded(refs)
+    rest = rest.astype(F32)
     first, last = unfold(rest[:HALF], rest[HALF : HALF + 1])
     root_ref[:HALF, :HALF] = first.astype(BF16)
     root_ref[:HALF, HALF:] = cross
@@ -205,7 +218,7 @@
 
 
 def norm_kernel(folded, mine, from_y, from_z, squares, total_ref, root):
-    unfold_root(folded, root)
+    unfold_root((folded,), root)
     grams = mine[...].astype(F32) + from_y[...].astype(F32) + from_z[...].astype(F32)
     first = dot(root[:HALF], root[:, :HALF])
     lower = dot(root[HALF:], root[...])
@@ -232,30 +245,31 @@
     )(*operands)
 
 
-def multiply_kernel(after, folded, held_ref, u_ref, root_ref):
+def multiply_kernel(*refs):
+    *folded, held_ref, u_ref, root_ref = refs
     unfold_root(folded, root_ref)
     for part in chunks(u_ref.shape[1], BLK):
         u_ref[:, part] = dot(root_ref[...], held_ref[:, part]).astype(BF16)
 
 
-def multiply(folded, held, after):
+def multiply(folded, held):
     return pl.pallas_call(
         multiply_kernel,
         out_shape=[pltpu.VMEM(held.shape, BF16), jax.ShapeDtypeStruct((BLK, BLK), BF16)],
-        in_specs=[ANY, VMEM, VMEM],
+        in_specs=[VMEM] * (len(folded) + 1),
         out_specs=[VMEM] * 2,
-        input_output_aliases={2: 0},
+        input_output_aliases={len(folded): 0},
         compiler_params=params(12),
         cost_estimate=pl.CostEstimate(flops=1, bytes_accessed=1, transcendentals=0),
         name="multiply",
-    )(after, folded, held)
+    )(*folded, held)
 
 
 def finish_kernel(order, owner_slot, sums, *refs):
-    roots, folded, blocks = refs[:EARLY], refs[EARLY:QUAD], refs[QUAD : 2 * QUAD]
-    update_ref, owned_ref = refs[2 * QUAD : 2 * QUAD + 2]
-    scaled = refs[2 * QUAD + 2 : 3 * QUAD + 2]
-    late, empty, sent, stored = refs[3 * QUAD + 2 :]
+    refs = list(refs)
+    take = lambda count: [refs.pop(0) for _ in range(count)]
+    roots, folded, blocks = take(EARLY), take(2), take(QUAD)
+    (update_ref, owned_ref), scaled, (late, empty, sent, stored) = take(2), take(QUAD), refs
     both = jnp.sum(sums[...], axis=1, keepdims=True)
     ratio = jnp.sqrt(both[:1] / (both[1:2] + 1e-06))
     columns = blocks[0].shape[1]
@@ -284,7 +298,7 @@
     bands = bands[1:]
     empty[...] = jnp.zeros_like(empty)
     for place in range(EARLY, QUAD):
-        unfold_root(folded[place - EARLY], late.at[place - EARLY])
+        unfold_root(folded, late.at[place - EARLY])
     for slot in range(SLOTS):
         mine = [owner_slot[order[QUAD], order[place]] == order[QUAD + 1] + slot for place in range(QUAD)]
         for place in range(QUAD):
@@ -318,9 +332,9 @@
             jax.ShapeDtypeStruct((SLOTS, BLK, BLK), BF16),
         ]
         + [pltpu.VMEM((BLK, columns), BF16)] * QUAD,
-        in_specs=[SMEM] * 2 + [VMEM] * (1 + 2 * QUAD),
+        in_specs=[SMEM] * 2 + [VMEM] * (3 + EARLY + QUAD),
         out_specs=[ANY] * 2 + [VMEM] * QUAD,
-        input_output_aliases={3 + QUAD + place: 2 + place for place in range(QUAD)},
+        input_output_aliases={5 + EARLY + place: 2 + place for place in range(QUAD)},
         scratch_shapes=[
             pltpu.VMEM((QUAD - EARLY, BLK, BLK), BF16),
             pltpu.VMEM((BLK, BLK), BF16),
@@ -335,15 +349,15 @@
 def swap(value, flip):
     axes = ("pool", "dp")
     count = math.prod(lax.axis_size(axis) for axis in axes)
-    return lax.ppermute(value, axes, [(i, i ^ flip) for i in range(count)])
+    pairs = [(i, i ^ flip) for i in range(count)]
+    return jax.tree.map(lambda part: lax.ppermute(part, axes, pairs), value)
 
 
 def rounds():
     peer_bits = lax.axis_size("dp").bit_length() - 1
     bits = [1 << i for i in range(peer_bits + lax.axis_size("pool").bit_length() - 1)]
-    bits = bits[peer_bits:] + bits[:peer_bits]
-    pairs = [bits[i : i + 2] for i in range(0, len(bits), 2)]
-    return [pair if len(pair) == 1 else [*pair, sum(pair)] for pair in pairs]
+    pairs = [bits[i : min(i + 2, peer_bits)] for i in range(0, peer_bits, 2)]
+    return [[bit] for bit in bits[peer_bits:][::-1]] + [pair + [sum(pair)] * (len(pair) - 1) for pair in pairs]
 
 
 def add(*values):
@@ -361,12 +375,12 @@
     a, b, c, d = statistics(order, activations)
     b, c, d = swap(b, 1), swap(c, 2), swap(d, 3)
     blocks, grams, squares = gram(order, gradient, a)
-    mine = add(a, b, c, d)
+    grams = list(grams)
+    mine = [add(a[rows], b[rows], c[rows], part) for rows, part in zip((slice(HALF), slice(HALF, None)), d)]
     flip = QUAD
     other = swap(mine, flip)
-    grams = list(grams)
     while 2 * flip < peer_count:
-        mine = add(mine, other)
+        mine = [add(*parts) for parts in zip(mine, other)]
         flip *= 2
         other = swap(mine, flip)
 
@@ -374,17 +388,17 @@
     across, grams[1] = lax.optimization_barrier((across, grams[1]))
     from_y = swap(grams[1], 1)
     from_z = swap(add(grams[2], across), 2)
-    root = newton(tokens_all, squares, mine, other)
-    folded = [root, swap(root, 1), swap(root, 2)]
-    folded.append(swap(folded[2], 1))
+    root, *halves = newton(tokens_all, squares, mine, other)
+    from_c = swap(halves, 2)
+    folded = [[root], [swap(root, 1)], from_c, swap(from_c, 1)]
     blocks, roots = list(blocks), []
 
     def precondition(place):
-        blocks[place], root = multiply(folded[place], blocks[place], folded[place])
+        blocks[place], root = multiply(folded[place], blocks[place])
         roots.append(root)
 
     sums = norm(root, grams[0], from_y, from_z, squares)
-    early, arrivals = {0:[0],1:[1],2:[2]}, {1:[1,2],2:[3]}
+    early, arrivals = {0:[0],2:[1],3:[2]}, {2:[1,2],3:[3]}
     for step, flips in enumerate(rounds()):
         received = [swap(sums, flip) for flip in flips]
         for place in early.get(step, ()):
@@ -393,7 +407,7 @@
         for place in arrivals.get(step, ()):
             folded[place], *received = lax.optimization_barrier((folded[place], *received))
         sums = sums + sum(received)
-    update, owned = finish(order, owner_slot, sums, roots, folded[EARLY:], blocks)
+    update, owned = finish(order, owner_slot, sums, roots, folded[-1], blocks)
     return (update, owned[None])
 
 

time: 68 us -> 69.9 us (1.028)
  waiting for transfers between devices: 10.3 us -> 11.6 us
  starting transfers between devices: 23.4 us -> 24.2 us
    ppermute x17 -> x20, waiting for transfers between devices: 10.3 us -> 11.6 us  [swap(): return jax.tree.map(lambda part: lax.ppermute(part, axes, pairs), value)]
    ppermute x17 -> x20, starting transfers between devices: 23.4 us -> 24.2 us  [swap(): return jax.tree.map(lambda part: lax.ppermute(part, axes, pairs), value)]
  transfers between devices with their start and end apart: 17 -> 20, of which waited for: 5 -> 5; matrix products, arithmetic and copies ran while one was open for 0% -> 0% of each run, Pallas kernels for 32% -> 31%
where the time goes in v12:
time: 69.9 us; the launch traced here: 69.8 us
  Pallas kernels  31.2 us (45%)
  starting transfers between devices  24.2 us (35%)
  waiting for transfers between devices  11.6 us (17%)
  local copies, waits for them, and re-layouts  1.6 us (2%)
  between operations  0.95 us (1%)
    ppermute x20, starting transfers between devices, swap(): return jax.tree.map(lambda part: lax.ppermute(part, axes, pairs), value)  24.2 us
    ppermute x20, waiting for transfers between devices, swap(): return jax.tree.map(lambda part: lax.ppermute(part, axes, pairs), value)  11.6 us
    pallas_call x1, Pallas kernels, gram(): pl.pallas_call(gram_kernel, out_shape=[pltpu.VMEM((BLK, columns), BF16)]...  11 us
    pallas_call x1, Pallas kernels, finish(): pl.pallas_call(finish_kernel, out_shape=[jax.ShapeDtypeStruct((QUAD * BLK...  7.71 us
    pallas_call x3, Pallas kernels, multiply(): pl.pallas_call(multiply_kernel, out_shape=[pltpu.VMEM(held.shape, BF16),...  7.07 us
    pallas_call x1, Pallas kernels, newton(): pl.pallas_call(functools.partial(newton_kernel, tokens), out_shape=folded...  3.19 us
    unnamed x4, local copies, waits for them, and re-layouts  1.6 us
    pallas_call x1, Pallas kernels, statistics(): pl.pallas_call(stat_kernel, out_shape=shapes, in_specs=[SMEM, VMEM], out_...  1.59 us
  transfers between devices with their start and end apart: 20, of which 5 were waited for; matrix products, arithmetic and copies ran while one was open for 0% of the time, Pallas kernels for 31%

profile of v12, /device:TPU:0, one launch (start us, length us, event | category | flops | bytes accessed | tf_op | source)
XLA Modules:
  0.0 69.8 jit_solution(14241518356129757420)
XLA Ops:
  0.7 0.1 pad_add_fusion.order
  0.7 1.6 %copy-done = bf16[512,2048]{1,0:T(8,128)(2,1)S(1)} copy-done((bf16[512,2048]{1,0:T(8,128)(2,1)S(1)}, bf16[512,2048]{1,0:T(8,128)(2,1)}, u32[]{:S(2)}) %copy-start) | copy-done | bytes 2097176
  2.3 1.6 %statistics.1 = (bf16[528,256]{1,0:T(8,128)(2,1)S(1)}, bf16[528,256]{1,0:T(8,128)(2,1)S(1)}, bf16[528,256]{1,0:T(8,128)(2,1)S(1)}, bf16[256,256]{1,0:T(8,128)(2,1)S(1)}, bf16[272,256]{1,0:T(8,128)(2,1)S(1)}) custom-call(s32[6]{0:T(128)S(1)} %pad_add_fusion.order, bf16[512,2048]{1,0:T(8,128)(2,1)S(1)} %copy-done), custom_call_target="tpu_custom_call" | custom-call | tf_op jit(solution)/shard_map/statistics/pallas_call | solution.py:88
  3.9 4.0 %collective-permute-start.2 = (bf16[256,256]{1,0:T(8,128)(2,1)S(1)}, bf16[256,256]{1,0:T(8,128)(2,1)S(1)}, u32[]{:S(2)}, u32[]{:S(2)}) collective-permute-start(bf16[256,256]{1,0:T(8,128)(2,1)S(1)} %get-tuple-element.52), channel_id=1, source_target_pairs={{0,3},{1,2},{2,1},{3,0},{4,7},{5,6},{6,5},{7,4},{8,11},{9,10},{10,... | collective-permute-start | bytes 393224 | tf_op jit(solution)/shard_map/ppermute | solution.py:353
  8.0 1.8 %collective-permute-start = (bf16[528,256]{1,0:T(8,128)(2,1)S(1)}, bf16[528,256]{1,0:T(8,128)(2,1)S(1)}, u32[]{:S(2)}, u32[]{:S(2)}) collective-permute-start(bf16[528,256]{1,0:T(8,128)(2,1)S(1)} %get-tuple-element.50), channel_id=1, source_target_pairs={{0,1},{1,0},{2,3},{3,2},{4,5},{5,4},{6,7},{7,6},{8,9},{9,8},{10,11... | collective-permute-start | bytes 811016 | tf_op jit(solution)/shard_map/ppermute | solution.py:353
  9.9 1.6 %collective-permute-start.1 = (bf16[528,256]{1,0:T(8,128)(2,1)S(1)}, bf16[528,256]{1,0:T(8,128)(2,1)S(1)}, u32[]{:S(2)}, u32[]{:S(2)}) collective-permute-start(bf16[528,256]{1,0:T(8,128)(2,1)S(1)} %get-tuple-element.51), channel_id=1, source_target_pairs={{0,2},{1,3},{2,0},{3,1},{4,6},{5,7},{6,4},{7,5},{8,10},{9,11},{10,... | collective-permute-start | bytes 811016 | tf_op jit(solution)/shard_map/ppermute | solution.py:353
  11.5 11.0 %gram.1 = (bf16[512,3584]{1,0:T(8,128)(2,1)S(1)}, bf16[512,3584]{1,0:T(8,128)(2,1)S(1)}, bf16[512,3584]{1,0:T(8,128)(2,1)S(1)}, bf16[512,3584]{1,0:T(8,128)(2,1)...) custom-call(s32[6]{0:T(128)S(1)} %pad_add_fusion.order, ...), custom_call_target="tpu_custom_call" | custom-call | flops 7516192768 | bytes 14680064 | tf_op jit(solution)/shard_map/gram/pallas_call | solution.py:138
  22.5 0.6 collective-permute-start.6
  23.2 2.7 %collective-permute-start.4 = (bf16[256,256]{1,0:T(8,128)(2,1)S(1)}, bf16[256,256]{1,0:T(8,128)(2,1)S(1)}, u32[]{:S(2)}, u32[]{:S(2)}) collective-permute-start(bf16[256,256]{1,0:T(8,128)(2,1)S(1)} %add_convert_fusion.2.mine0), channel_id=1, source_target_pairs={{0,4},{1,5},{2,6},{3,7},{4,0},{5,1},{6,2},{7,3},{8,12},{9,13},{10,... | collective-permute-start | bytes 393224 | tf_op jit(solution)/shard_map/ppermute | solution.py:353
  25.8 0.1 add_convert_fusion.1.mine1
  25.9 0.4 collective-permute-start.5
  26.3 3.4 %collective-permute-done.6 = bf16[528,256]{1,0:T(8,128)(2,1)S(1)} collective-permute-done((bf16[528,256]{1,0:T(8,128)(2,1)S(1)}, bf16[528,256]{1,0:T(8,128)(2,1)S(1)}, u32[]{:S(2)}, u32[]{:S(2)}) %collective-permute-start.6) | collective-permute-done | bytes 270368 | tf_op jit(solution)/shard_map/ppermute | solution.py:353
  29.7 0.5 collective-permute-start.8
  30.3 0.5 collective-permute-start.7
  30.7 4.0 %collective-permute-done.4.other0 = bf16[256,256]{1,0:T(8,128)(2,1)S(1)} collective-permute-done((bf16[256,256]{1,0:T(8,128)(2,1)S(1)}, bf16[256,256]{1,0:T(8,128)(2,1)S(1)}, u32[]{:S(2)}, u32[]{:S(2)}) %collective-permute-start.4) | collective-permute-done | bytes 131104 | tf_op jit(solution)/shard_map/ppermute | solution.py:353
  34.7 2.0 %collective-permute-done.5.other1 = bf16[272,256]{1,0:T(8,128)(2,1)S(1)} collective-permute-done((bf16[272,256]{1,0:T(8,128)(2,1)S(1)}, bf16[272,256]{1,0:T(8,128)(2,1)S(1)}, u32[]{:S(2)}, u32[]{:S(2)}) %collective-permute-start.5) | collective-permute-done | bytes 139296 | tf_op jit(solution)/shard_map/ppermute | solution.py:353
  36.7 3.2 %newton.1 = (bf16[528,256]{1,0:T(8,128)(2,1)S(1)}, bf16[256,256]{1,0:T(8,128)(2,1)S(1)}, bf16[272,256]{1,0:T(8,128)(2,1)S(1)}) custom-call(f32[1,256]{1,0:T(1,128)S(1)} %get-tuple-element.49.after.squares, bf16[256,256]{1,0:T(8,128)(2,1)S(1)} %add_convert_fusion.2.mine0, bf16[272,256]{1,0:T(8,128)(2,1)S(1)} %add_convert_fusion.1.mine1, ...), custom_call_target="tpu_custom_call" | custom-call | flops 2147483648 | bytes 2097152 | tf_op jit(solution)/shard_map/newton/pallas_call | solution.py:196
  39.9 1.6 %collective-permute-start.13 = (bf16[528,256]{1,0:T(8,128)(2,1)S(1)}, bf16[528,256]{1,0:T(8,128)(2,1)S(1)}, u32[]{:S(2)}, u32[]{:S(2)}) collective-permute-start(bf16[528,256]{1,0:T(8,128)(2,1)S(1)} %get-tuple-element.54.folded.refs_0_), channel_id=1, source_target_pairs={{0,1},{1,0},{2,3},{3,2},{4,5},{5,4},{6,7},{7,6},{8,9},{9,8},{10,11... | collective-permute-start | bytes 811016 | tf_op jit(solution)/shard_map/ppermute | solution.py:353
  41.5 2.0 %collective-permute-start.11 = (bf16[256,256]{1,0:T(8,128)(2,1)S(1)}, bf16[256,256]{1,0:T(8,128)(2,1)S(1)}, u32[]{:S(2)}, u32[]{:S(2)}) collective-permute-start(bf16[256,256]{1,0:T(8,128)(2,1)S(1)} %get-tuple-element.64), channel_id=1, source_target_pairs={{0,2},{1,3},{2,0},{3,1},{4,6},{5,7},{6,4},{7,5},{8,10},{9,11},{10,... | collective-permute-start | bytes 393224 | tf_op jit(solution)/shard_map/ppermute | solution.py:353
  43.5 0.6 norm.1
  44.1 1.6 %collective-permute-start.9 = (f32[8,128]{1,0:T(8,128)S(1)}, f32[8,128]{1,0:T(8,128)S(1)}, u32[]{:S(2)}, u32[]{:S(2)}) collective-permute-start(f32[8,128]{1,0:T(8,128)S(1)} %norm.1), channel_id=1, source_target_pairs={{0,16},{1,17},{2,18},{3,19},{4,20},{5,21},{6,22},{7,23},{8,24},{9,... | collective-permute-start | bytes 12296 | tf_op jit(solution)/shard_map/ppermute | solution.py:353
  45.7 2.3 %multiply.3 = (bf16[512,3584]{1,0:T(8,128)(2,1)S(1)}, bf16[512,512]{1,0:T(8,128)(2,1)S(1)}) custom-call(bf16[528,256]{1,0:T(8,128)(2,1)S(1)} %get-tuple-element.54.folded.refs_0_, bf16[512,3584]{1,0:T(8,128)(2,1)S(1)} %get-tuple-element.61.refs_1_), custom_call_target="tpu_custom_call", output_to_operand_aliasing={{0}: (1, {})} | custom-call | flops 1 | bytes 1 | tf_op jit(solution)/shard_map/multiply/pallas_call | solution.py:256
  48.1 1.2 %collective-permute-done.10 = f32[8,128]{1,0:T(8,128)S(1)} collective-permute-done((f32[8,128]{1,0:T(8,128)S(1)}, f32[8,128]{1,0:T(8,128)S(1)}, u32[]{:S(2)}, u32[]{:S(2)}) %collective-permute-start.10) | collective-permute-done | bytes 4128 | tf_op jit(solution)/shard_map/ppermute | solution.py:353
  49.2 2.0 %collective-permute-start.15 = (f32[8,128]{1,0:T(8,128)S(1)}, f32[8,128]{1,0:T(8,128)S(1)}, u32[]{:S(2)}, u32[]{:S(2)}) collective-permute-start(f32[8,128]{1,0:T(8,128)S(1)} %add.52), channel_id=1, source_target_pairs={{0,2},{1,3},{2,0},{3,1},{4,6},{5,7},{6,4},{7,5},{8,10},{9,11},{10,... | collective-permute-start | bytes 12296 | tf_op jit(solution)/shard_map/ppermute | solution.py:353
  51.2 1.5 %collective-permute-start.14 = (f32[8,128]{1,0:T(8,128)S(1)}, f32[8,128]{1,0:T(8,128)S(1)}, u32[]{:S(2)}, u32[]{:S(2)}) collective-permute-start(f32[8,128]{1,0:T(8,128)S(1)} %add.52), channel_id=1, source_target_pairs={{0,1},{1,0},{2,3},{3,2},{4,5},{5,4},{6,7},{7,6},{8,9},{9,8},{10,11... | collective-permute-start | bytes 12296 | tf_op jit(solution)/shard_map/ppermute | solution.py:353
  52.7 0.5 collective-permute-start.17
  53.2 1.5 %collective-permute-start.18 = (bf16[272,256]{1,0:T(8,128)(2,1)S(1)}, bf16[272,256]{1,0:T(8,128)(2,1)S(1)}, u32[]{:S(2)}, u32[]{:S(2)}) collective-permute-start(bf16[272,256]{1,0:T(8,128)(2,1)S(1)} %collective-permute-done.12.refs_1_), channel_id=1, source_target_pairs={{0,1},{1,0},{2,3},{3,2},{4,5},{5,4},{6,7},{7,6},{8,9},{9,8},{10,11... | collective-permute-start | bytes 417800 | tf_op jit(solution)/shard_map/ppermute | solution.py:353
  54.8 2.5 %multiply.4 = (bf16[512,3584]{1,0:T(8,128)(2,1)S(1)}, bf16[512,512]{1,0:T(8,128)(2,1)S(1)}) custom-call(bf16[528,256]{1,0:T(8,128)(2,1)S(1)} %collective-permute-done.13.refs_0_, bf16[512,3584]{1,0:T(8,128)(2,1)S(1)} %get-tuple-element.66.refs_1_), custom_call_target="tpu_custom_call", output_to_operand_aliasing={{0}: (1, {})} | custom-call | flops 1 | bytes 1 | tf_op jit(solution)/shard_map/multiply/pallas_call | solution.py:256
  57.3 1.2 %collective-permute-start.19 = (f32[8,128]{1,0:T(8,128)S(1)}, f32[8,128]{1,0:T(8,128)S(1)}, u32[]{:S(2)}, u32[]{:S(2)}) collective-permute-start(f32[8,128]{1,0:T(8,128)S(1)} %add_add_fusion), channel_id=1, source_target_pairs={{0,4},{1,5},{2,6},{3,7},{4,0},{5,1},{6,2},{7,3},{8,12},{9,13},{10,... | collective-permute-start | bytes 12296 | tf_op jit(solution)/shard_map/ppermute | solution.py:353
  58.6 2.3 %multiply.5 = (bf16[512,3584]{1,0:T(8,128)(2,1)S(1)}, bf16[512,512]{1,0:T(8,128)(2,1)S(1)}) custom-call(bf16[256,256]{1,0:T(8,128)(2,1)S(1)} %collective-permute-done.11.refs_0_, bf16[272,256]{1,0:T(8,128)(2,1)S(1)} %collective-permute-done.12.refs_1_, bf16[512,3584]{1,0:T(8,128)(2,1)S(1)} %get-tuple-element.79.refs_2_), custom_call_target="tpu_custom_call", output_to_operand_aliasing={{0}: (2, {})} | custom-call | flops 1 | bytes 1 | tf_op jit(solution)/shard_map/multiply/pallas_call | solution.py:256
  60.8 1.0 %collective-permute-done.19 = f32[8,128]{1,0:T(8,128)S(1)} collective-permute-done((f32[8,128]{1,0:T(8,128)S(1)}, f32[8,128]{1,0:T(8,128)S(1)}, u32[]{:S(2)}, u32[]{:S(2)}) %collective-permute-start.19) | collective-permute-done | bytes 4128 | tf_op jit(solution)/shard_map/ppermute | solution.py:353
  61.9 7.7 %finish.1 = (bf16[2048,3584]{1,0:T(8,128)(2,1)}, bf16[2,512,512]{2,1,0:T(8,128)(2,1)}, bf16[512,3584]{1,0:T(8,128)(2,1)S(1)}, bf16[512,3584]{1,0:T(8,128)(2,1)S(...) custom-call(s32[6]{0:T(128)S(1)} %pad_add_fusion.order, ...), custom_call_target="tpu_custom_call", output_to_operand_aliasing={{2}: (8, {}), {3}: (9, {}), {4}: (10, {}), {5}: (11, {})} | custom-call | tf_op jit(solution)/shard_map/finish/pallas_call | solution.py:328
  (29 shorter events, 0.4 us)
Async XLA Ops:
  0.7 1.6 %copy-start = (bf16[512,2048]{1,0:T(8,128)(2,1)S(1)}, bf16[512,2048]{1,0:T(8,128)(2,1)}, u32[]{:S(2)}) copy-start(bf16[512,2048]{1,0:T(8,128)(2,1)} %x_ref.1) | copy-start | bytes 6291460
  3.9 19.1 %collective-permute-start.2 = (bf16[256,256]{1,0:T(8,128)(2,1)S(1)}, bf16[256,256]{1,0:T(8,128)(2,1)S(1)}, u32[]{:S(2)}, u32[]{:S(2)}) collective-permute-start(bf16[256,256]{1,0:T(8,128)(2,1)S(1)} %get-tuple-element.52), channel_id=1, source_target_pairs={{0,3},{1,2},{2,1},{3,0},{4,7},{5,6},{6,5},{7,4},{8,11},{9,10},{10,... | collective-permute-start | bytes 393224 | tf_op jit(solution)/shard_map/ppermute | solution.py:353
  8.0 17.9 %collective-permute-start.3 = (bf16[272,256]{1,0:T(8,128)(2,1)S(1)}, bf16[272,256]{1,0:T(8,128)(2,1)S(1)}, u32[]{:S(2)}, u32[]{:S(2)}) collective-permute-start(bf16[272,256]{1,0:T(8,128)(2,1)S(1)} %get-tuple-element.53), channel_id=1, source_target_pairs={{0,3},{1,2},{2,1},{3,0},{4,7},{5,6},{6,5},{7,4},{8,11},{9,10},{10,... | collective-permute-start | bytes 417800 | tf_op jit(solution)/shard_map/ppermute | solution.py:353
  8.0 15.0 %collective-permute-start = (bf16[528,256]{1,0:T(8,128)(2,1)S(1)}, bf16[528,256]{1,0:T(8,128)(2,1)S(1)}, u32[]{:S(2)}, u32[]{:S(2)}) collective-permute-start(bf16[528,256]{1,0:T(8,128)(2,1)S(1)} %get-tuple-element.50), channel_id=1, source_target_pairs={{0,1},{1,0},{2,3},{3,2},{4,5},{5,4},{6,7},{7,6},{8,9},{9,8},{10,11... | collective-permute-start | bytes 811016 | tf_op jit(solution)/shard_map/ppermute | solution.py:353
  9.9 13.2 %collective-permute-start.1 = (bf16[528,256]{1,0:T(8,128)(2,1)S(1)}, bf16[528,256]{1,0:T(8,128)(2,1)S(1)}, u32[]{:S(2)}, u32[]{:S(2)}) collective-permute-start(bf16[528,256]{1,0:T(8,128)(2,1)S(1)} %get-tuple-element.51), channel_id=1, source_target_pairs={{0,2},{1,3},{2,0},{3,1},{4,6},{5,7},{6,4},{7,5},{8,10},{9,11},{10,... | collective-permute-start | bytes 811016 | tf_op jit(solution)/shard_map/ppermute | solution.py:353
  22.5 7.2 %collective-permute-start.6 = (bf16[528,256]{1,0:T(8,128)(2,1)S(1)}, bf16[528,256]{1,0:T(8,128)(2,1)S(1)}, u32[]{:S(2)}, u32[]{:S(2)}) collective-permute-start(bf16[528,256]{1,0:T(8,128)(2,1)S(1)} %get-tuple-element.56), channel_id=1, source_target_pairs={{0,1},{1,0},{2,3},{3,2},{4,5},{5,4},{6,7},{7,6},{8,9},{9,8},{10,11... | collective-permute-start | bytes 811016 | tf_op jit(solution)/shard_map/ppermute | solution.py:353
  23.2 11.6 %collective-permute-start.4 = (bf16[256,256]{1,0:T(8,128)(2,1)S(1)}, bf16[256,256]{1,0:T(8,128)(2,1)S(1)}, u32[]{:S(2)}, u32[]{:S(2)}) collective-permute-start(bf16[256,256]{1,0:T(8,128)(2,1)S(1)} %add_convert_fusion.2.mine0), channel_id=1, source_target_pairs={{0,4},{1,5},{2,6},{3,7},{4,0},{5,1},{6,2},{7,3},{8,12},{9,13},{10,... | collective-permute-start | bytes 393224 | tf_op jit(solution)/shard_map/ppermute | solution.py:353
  25.9 10.8 %collective-permute-start.5 = (bf16[272,256]{1,0:T(8,128)(2,1)S(1)}, bf16[272,256]{1,0:T(8,128)(2,1)S(1)}, u32[]{:S(2)}, u32[]{:S(2)}) collective-permute-start(bf16[272,256]{1,0:T(8,128)(2,1)S(1)} %add_convert_fusion.1.mine1), channel_id=1, source_target_pairs={{0,4},{1,5},{2,6},{3,7},{4,0},{5,1},{6,2},{7,3},{8,12},{9,13},{10,... | collective-permute-start | bytes 417800 | tf_op jit(solution)/shard_map/ppermute | solution.py:353
  29.7 13.8 %collective-permute-start.8 = (bf16[528,256]{1,0:T(8,128)(2,1)S(1)}, bf16[528,256]{1,0:T(8,128)(2,1)S(1)}, u32[]{:S(2)}, u32[]{:S(2)}) collective-permute-start(bf16[528,256]{1,0:T(8,128)(2,1)S(1)} %add_convert_fusion), channel_id=1, source_target_pairs={{0,2},{1,3},{2,0},{3,1},{4,6},{5,7},{6,4},{7,5},{8,10},{9,11},{10,... | collective-permute-start | bytes 811016 | tf_op jit(solution)/shard_map/ppermute | solution.py:353
  30.3 13.3 %collective-permute-start.7 = (bf16[528,256]{1,0:T(8,128)(2,1)S(1)}, bf16[528,256]{1,0:T(8,128)(2,1)S(1)}, u32[]{:S(2)}, u32[]{:S(2)}) collective-permute-start(bf16[528,256]{1,0:T(8,128)(2,1)S(1)} %get-tuple-element.58), channel_id=1, source_target_pairs={{0,1},{1,0},{2,3},{3,2},{4,5},{5,4},{6,7},{7,6},{8,9},{9,8},{10,11... | collective-permute-start | bytes 811016 | tf_op jit(solution)/shard_map/ppermute | solution.py:353
  39.9 13.3 %collective-permute-start.13 = (bf16[528,256]{1,0:T(8,128)(2,1)S(1)}, bf16[528,256]{1,0:T(8,128)(2,1)S(1)}, u32[]{:S(2)}, u32[]{:S(2)}) collective-permute-start(bf16[528,256]{1,0:T(8,128)(2,1)S(1)} %get-tuple-element.54.folded.refs_0_), channel_id=1, source_target_pairs={{0,1},{1,0},{2,3},{3,2},{4,5},{5,4},{6,7},{7,6},{8,9},{9,8},{10,11... | collective-permute-start | bytes 811016 | tf_op jit(solution)/shard_map/ppermute | solution.py:353
  41.5 11.2 %collective-permute-start.12 = (bf16[272,256]{1,0:T(8,128)(2,1)S(1)}, bf16[272,256]{1,0:T(8,128)(2,1)S(1)}, u32[]{:S(2)}, u32[]{:S(2)}) collective-permute-start(bf16[272,256]{1,0:T(8,128)(2,1)S(1)} %get-tuple-element.65), channel_id=1, source_target_pairs={{0,2},{1,3},{2,0},{3,1},{4,6},{5,7},{6,4},{7,5},{8,10},{9,11},{10,... | collective-permute-start | bytes 417800 | tf_op jit(solution)/shard_map/ppermute | solution.py:353
  41.5 9.7 %collective-permute-start.11 = (bf16[256,256]{1,0:T(8,128)(2,1)S(1)}, bf16[256,256]{1,0:T(8,128)(2,1)S(1)}, u32[]{:S(2)}, u32[]{:S(2)}) collective-permute-start(bf16[256,256]{1,0:T(8,128)(2,1)S(1)} %get-tuple-element.64), channel_id=1, source_target_pairs={{0,2},{1,3},{2,0},{3,1},{4,6},{5,7},{6,4},{7,5},{8,10},{9,11},{10,... | collective-permute-start | bytes 393224 | tf_op jit(solution)/shard_map/ppermute | solution.py:353
  44.1 3.8 %collective-permute-start.9 = (f32[8,128]{1,0:T(8,128)S(1)}, f32[8,128]{1,0:T(8,128)S(1)}, u32[]{:S(2)}, u32[]{:S(2)}) collective-permute-start(f32[8,128]{1,0:T(8,128)S(1)} %norm.1), channel_id=1, source_target_pairs={{0,16},{1,17},{2,18},{3,19},{4,20},{5,21},{6,22},{7,23},{8,24},{9,... | collective-permute-start | bytes 12296 | tf_op jit(solution)/shard_map/ppermute | solution.py:353
  48.0 1.2 %collective-permute-start.10 = (f32[8,128]{1,0:T(8,128)S(1)}, f32[8,128]{1,0:T(8,128)S(1)}, u32[]{:S(2)}, u32[]{:S(2)}) collective-permute-start(f32[8,128]{1,0:T(8,128)S(1)} %add.51), channel_id=1, source_target_pairs={{0,8},{1,9},{2,10},{3,11},{4,12},{5,13},{6,14},{7,15},{8,0},{9,1},... | collective-permute-start | bytes 12296 | tf_op jit(solution)/shard_map/ppermute | solution.py:353
  49.2 8.0 %collective-permute-start.16 = (f32[8,128]{1,0:T(8,128)S(1)}, f32[8,128]{1,0:T(8,128)S(1)}, u32[]{:S(2)}, u32[]{:S(2)}) collective-permute-start(f32[8,128]{1,0:T(8,128)S(1)} %add.52), channel_id=1, source_target_pairs={{0,3},{1,2},{2,1},{3,0},{4,7},{5,6},{6,5},{7,4},{8,11},{9,10},{10,... | collective-permute-start | bytes 12296 | tf_op jit(solution)/shard_map/ppermute | solution.py:353
  49.2 8.0 %collective-permute-start.15 = (f32[8,128]{1,0:T(8,128)S(1)}, f32[8,128]{1,0:T(8,128)S(1)}, u32[]{:S(2)}, u32[]{:S(2)}) collective-permute-start(f32[8,128]{1,0:T(8,128)S(1)} %add.52), channel_id=1, source_target_pairs={{0,2},{1,3},{2,0},{3,1},{4,6},{5,7},{6,4},{7,5},{8,10},{9,11},{10,... | collective-permute-start | bytes 12296 | tf_op jit(solution)/shard_map/ppermute | solution.py:353
  51.2 6.1 %collective-permute-start.14 = (f32[8,128]{1,0:T(8,128)S(1)}, f32[8,128]{1,0:T(8,128)S(1)}, u32[]{:S(2)}, u32[]{:S(2)}) collective-permute-start(f32[8,128]{1,0:T(8,128)S(1)} %add.52), channel_id=1, source_target_pairs={{0,1},{1,0},{2,3},{3,2},{4,5},{5,4},{6,7},{7,6},{8,9},{9,8},{10,11... | collective-permute-start | bytes 12296 | tf_op jit(solution)/shard_map/ppermute | solution.py:353
  52.7 9.2 %collective-permute-start.17 = (bf16[256,256]{1,0:T(8,128)(2,1)S(1)}, bf16[256,256]{1,0:T(8,128)(2,1)S(1)}, u32[]{:S(2)}, u32[]{:S(2)}) collective-permute-start(bf16[256,256]{1,0:T(8,128)(2,1)S(1)} %collective-permute-done.11.refs_0_), channel_id=1, source_target_pairs={{0,1},{1,0},{2,3},{3,2},{4,5},{5,4},{6,7},{7,6},{8,9},{9,8},{10,11... | collective-permute-start | bytes 393224 | tf_op jit(solution)/shard_map/ppermute | solution.py:353
  53.2 8.6 %collective-permute-start.18 = (bf16[272,256]{1,0:T(8,128)(2,1)S(1)}, bf16[272,256]{1,0:T(8,128)(2,1)S(1)}, u32[]{:S(2)}, u32[]{:S(2)}) collective-permute-start(bf16[272,256]{1,0:T(8,128)(2,1)S(1)} %collective-permute-done.12.refs_1_), channel_id=1, source_target_pairs={{0,1},{1,0},{2,3},{3,2},{4,5},{5,4},{6,7},{7,6},{8,9},{9,8},{10,11... | collective-permute-start | bytes 417800 | tf_op jit(solution)/shard_map/ppermute | solution.py:353
  54.8 7.1 %copy-start.1 = (s32[4,4]{1,0:T(4,128)S(1)}, s32[4,4]{1,0:T(4,128)}, u32[]{:S(2)}) copy-start(s32[4,4]{1,0:T(4,128)} %owner_slot.1) | copy-start | bytes 196
  57.3 4.6 %collective-permute-start.19 = (f32[8,128]{1,0:T(8,128)S(1)}, f32[8,128]{1,0:T(8,128)S(1)}, u32[]{:S(2)}, u32[]{:S(2)}) collective-permute-start(f32[8,128]{1,0:T(8,128)S(1)} %add_add_fusion), channel_id=1, source_target_pairs={{0,4},{1,5},{2,6},{3,7},{4,0},{5,1},{6,2},{7,3},{8,12},{9,13},{10,... | collective-permute-start | bytes 12296 | tf_op jit(solution)/shard_map/ppermute | solution.py:353

commit v13 on v11

--- a/solution.py
+++ b/solution.py
@@ -279,9 +279,11 @@
 
     bands = [(place, pl.ds(i, BAND)) for place in range(EARLY) for i in range(0, BLK, BAND)]
     products = [(place, part) for place in range(EARLY, QUAD) for part in chunks(columns, BLK)]
-    rescale(*bands[0])
-    send(*bands[0], pl.ds(0, columns))
-    bands = bands[1:]
+    ahead = len(bands) - len(products) // 2
+    for one in bands[:ahead]:
+        rescale(*one)
+        send(*one, pl.ds(0, columns))
+    bands = bands[ahead:]
     empty[...] = jnp.zeros_like(empty)
     for place in range(EARLY, QUAD):
         unfold_root(folded[place - EARLY], late.at[place - EARLY])
@@ -341,9 +343,7 @@
 def rounds():
     peer_bits = lax.axis_size("dp").bit_length() - 1
     bits = [1 << i for i in range(peer_bits + lax.axis_size("pool").bit_length() - 1)]
-    bits = bits[peer_bits:] + bits[:peer_bits]
-    pairs = [bits[i : i + 2] for i in range(0, len(bits), 2)]
-    return [pair if len(pair) == 1 else [*pair, sum(pair)] for pair in pairs]
+    return bits[peer_bits:][::-1] + bits[:peer_bits]
 
 
 def add(*values):
@@ -375,8 +375,7 @@
     from_y = swap(grams[1], 1)
     from_z = swap(add(grams[2], across), 2)
     root = newton(tokens_all, squares, mine, other)
-    folded = [root, swap(root, 1), swap(root, 2)]
-    folded.append(swap(folded[2], 1))
+    folded = [root, swap(root, 1), swap(root, 2), swap(root, 3)]
     blocks, roots = list(blocks), []
 
     def precondition(place):
@@ -384,15 +383,15 @@
         roots.append(root)
 
     sums = norm(root, grams[0], from_y, from_z, squares)
-    early, arrivals = {0:[0],1:[1],2:[2]}, {1:[1,2],2:[3]}
-    for step, flips in enumerate(rounds()):
-        received = [swap(sums, flip) for flip in flips]
+    early, arrivals = {0:[0],3:[1],4:[2]}, {3:[1,2],4:[3]}
+    for step, flip in enumerate(rounds()):
+        received = swap(sums, flip)
         for place in early.get(step, ()):
             precondition(place)
-            blocks[place], *received = lax.optimization_barrier((blocks[place], *received))
+            blocks[place], received = lax.optimization_barrier((blocks[place], received))
         for place in arrivals.get(step, ()):
-            folded[place], *received = lax.optimization_barrier((folded[place], *received))
-        sums = sums + sum(received)
+            folded[place], received = lax.optimization_barrier((folded[place], received))
+        sums = sums + received
     update, owned = finish(order, owner_slot, sums, roots, folded[EARLY:], blocks)
     return (update, owned[None])
 

time: 68 us -> 69.4 us (1.021)
  waiting for transfers between devices: 10.3 us -> 13.1 us
  starting transfers between devices: 23.4 us -> 21.8 us
    ppermute x17 -> x15, waiting for transfers between devices: 10.3 us -> 13.1 us  [swap(): return lax.ppermute(value, axes, [(i, i ^ flip) for i in range(count)])]
    ppermute x17 -> x15, starting transfers between devices: 23.4 us -> 21.8 us  [swap(): return lax.ppermute(value, axes, [(i, i ^ flip) for i in range(count)])]
  transfers between devices with their start and end apart: 17 -> 15, of which waited for: 5 -> 5; matrix products, arithmetic and copies ran while one was open for 0% -> 0% of each run, Pallas kernels for 32% -> 32%
where the time goes in v13:
time: 69.4 us; the launch traced here: 69.3 us
  Pallas kernels  31.6 us (46%)
  starting transfers between devices  21.8 us (31%)
  waiting for transfers between devices  13.1 us (19%)
  local copies, waits for them, and re-layouts  1.6 us (2%)
  between operations  0.93 us (1%)
    ppermute x15, starting transfers between devices, swap(): return lax.ppermute(value, axes, [(i, i ^ flip) for i in range(count)])  21.8 us
    ppermute x15, waiting for transfers between devices, swap(): return lax.ppermute(value, axes, [(i, i ^ flip) for i in range(count)])  13.1 us
    pallas_call x1, Pallas kernels, gram(): pl.pallas_call(gram_kernel, out_shape=[pltpu.VMEM((BLK, columns), BF16)]...  11 us
    pallas_call x1, Pallas kernels, finish(): pl.pallas_call(finish_kernel, out_shape=[jax.ShapeDtypeStruct((QUAD * BLK...  8.04 us
    pallas_call x3, Pallas kernels, multiply(): pl.pallas_call(multiply_kernel, out_shape=[pltpu.VMEM(held.shape, BF16),...  7.13 us
    pallas_call x1, Pallas kernels, newton(): pl.pallas_call(functools.partial(newton_kernel, tokens), out_shape=jax.Sh...  3.2 us
    unnamed x4, local copies, waits for them, and re-layouts  1.6 us
    pallas_call x1, Pallas kernels, statistics(): pl.pallas_call(stat_kernel, out_shape=[jax.ShapeDtypeStruct((FOLD, HALF),...  1.59 us
  transfers between devices with their start and end apart: 15, of which 5 were waited for; matrix products, arithmetic and copies ran while one was open for 0% of the time, Pallas kernels for 32%

profile of v13, /device:TPU:0, one launch (start us, length us, event | category | flops | bytes accessed | tf_op | source)
XLA Modules:
  0.0 69.3 jit_solution(1166004082423534889)
XLA Ops:
  0.7 0.1 pad_add_fusion.order
  0.7 1.6 %copy-done = bf16[512,2048]{1,0:T(8,128)(2,1)S(1)} copy-done((bf16[512,2048]{1,0:T(8,128)(2,1)S(1)}, bf16[512,2048]{1,0:T(8,128)(2,1)}, u32[]{:S(2)}) %copy-start) | copy-done | bytes 2097176
  2.3 1.6 %statistics.1 = (bf16[528,256]{1,0:T(8,128)(2,1)S(1)}, bf16[528,256]{1,0:T(8,128)(2,1)S(1)}, bf16[528,256]{1,0:T(8,128)(2,1)S(1)}, bf16[528,256]{1,0:T(8,128)(2,1)S(1)}) custom-call(s32[6]{0:T(128)S(1)} %pad_add_fusion.order, bf16[512,2048]{1,0:T(8,128)(2,1)S(1)} %copy-done), custom_call_target="tpu_custom_call" | custom-call | tf_op jit(solution)/shard_map/statistics/pallas_call | solution.py:72
  3.9 3.0 %collective-permute-start = (bf16[528,256]{1,0:T(8,128)(2,1)S(1)}, bf16[528,256]{1,0:T(8,128)(2,1)S(1)}, u32[]{:S(2)}, u32[]{:S(2)}) collective-permute-start(bf16[528,256]{1,0:T(8,128)(2,1)S(1)} %get-tuple-element.38), channel_id=1, source_target_pairs={{0,1},{1,0},{2,3},{3,2},{4,5},{5,4},{6,7},{7,6},{8,9},{9,8},{10,11... | collective-permute-start | bytes 811016 | tf_op jit(solution)/shard_map/ppermute | solution.py:340
  6.9 1.6 %collective-permute-start.1 = (bf16[528,256]{1,0:T(8,128)(2,1)S(1)}, bf16[528,256]{1,0:T(8,128)(2,1)S(1)}, u32[]{:S(2)}, u32[]{:S(2)}) collective-permute-start(bf16[528,256]{1,0:T(8,128)(2,1)S(1)} %get-tuple-element.39), channel_id=1, source_target_pairs={{0,2},{1,3},{2,0},{3,1},{4,6},{5,7},{6,4},{7,5},{8,10},{9,11},{10,... | collective-permute-start | bytes 811016 | tf_op jit(solution)/shard_map/ppermute | solution.py:340
  8.5 11.0 %gram.1 = (bf16[512,3584]{1,0:T(8,128)(2,1)S(1)}, bf16[512,3584]{1,0:T(8,128)(2,1)S(1)}, bf16[512,3584]{1,0:T(8,128)(2,1)S(1)}, bf16[512,3584]{1,0:T(8,128)(2,1)...) custom-call(s32[6]{0:T(128)S(1)} %pad_add_fusion.order, ...), custom_call_target="tpu_custom_call" | custom-call | flops 7516192768 | bytes 14680064 | tf_op jit(solution)/shard_map/gram/pallas_call | solution.py:124
  19.6 2.0 %collective-permute-start.4 = (bf16[528,256]{1,0:T(8,128)(2,1)S(1)}, bf16[528,256]{1,0:T(8,128)(2,1)S(1)}, u32[]{:S(2)}, u32[]{:S(2)}) collective-permute-start(bf16[528,256]{1,0:T(8,128)(2,1)S(1)} %get-tuple-element.42), channel_id=1, source_target_pairs={{0,1},{1,0},{2,3},{3,2},{4,5},{5,4},{6,7},{7,6},{8,9},{9,8},{10,11... | collective-permute-start | bytes 811016 | tf_op jit(solution)/shard_map/ppermute | solution.py:340
  21.6 0.1 add_convert_fusion.1.mine
  21.7 2.7 %collective-permute-start.3 = (bf16[528,256]{1,0:T(8,128)(2,1)S(1)}, bf16[528,256]{1,0:T(8,128)(2,1)S(1)}, u32[]{:S(2)}, u32[]{:S(2)}) collective-permute-start(bf16[528,256]{1,0:T(8,128)(2,1)S(1)} %add_convert_fusion.1.mine), channel_id=1, source_target_pairs={{0,4},{1,5},{2,6},{3,7},{4,0},{5,1},{6,2},{7,3},{8,12},{9,13},{10,... | collective-permute-start | bytes 811016 | tf_op jit(solution)/shard_map/ppermute | solution.py:340
  24.4 2.9 %collective-permute-done.4 = bf16[528,256]{1,0:T(8,128)(2,1)S(1)} collective-permute-done((bf16[528,256]{1,0:T(8,128)(2,1)S(1)}, bf16[528,256]{1,0:T(8,128)(2,1)S(1)}, u32[]{:S(2)}, u32[]{:S(2)}) %collective-permute-start.4) | collective-permute-done | bytes 270368 | tf_op jit(solution)/shard_map/ppermute | solution.py:340
  27.3 0.1 add_convert_fusion
  27.4 1.7 %collective-permute-start.6 = (bf16[528,256]{1,0:T(8,128)(2,1)S(1)}, bf16[528,256]{1,0:T(8,128)(2,1)S(1)}, u32[]{:S(2)}, u32[]{:S(2)}) collective-permute-start(bf16[528,256]{1,0:T(8,128)(2,1)S(1)} %add_convert_fusion), channel_id=1, source_target_pairs={{0,2},{1,3},{2,0},{3,1},{4,6},{5,7},{6,4},{7,5},{8,10},{9,11},{10,... | collective-permute-start | bytes 811016 | tf_op jit(solution)/shard_map/ppermute | solution.py:340
  29.1 1.5 %collective-permute-start.5 = (bf16[528,256]{1,0:T(8,128)(2,1)S(1)}, bf16[528,256]{1,0:T(8,128)(2,1)S(1)}, u32[]{:S(2)}, u32[]{:S(2)}) collective-permute-start(bf16[528,256]{1,0:T(8,128)(2,1)S(1)} %get-tuple-element.44), channel_id=1, source_target_pairs={{0,1},{1,0},{2,3},{3,2},{4,5},{5,4},{6,7},{7,6},{8,9},{9,8},{10,11... | collective-permute-start | bytes 811016 | tf_op jit(solution)/shard_map/ppermute | solution.py:340
  30.6 5.0 %collective-permute-done.3.other = bf16[528,256]{1,0:T(8,128)(2,1)S(1)} collective-permute-done((bf16[528,256]{1,0:T(8,128)(2,1)S(1)}, bf16[528,256]{1,0:T(8,128)(2,1)S(1)}, u32[]{:S(2)}, u32[]{:S(2)}) %collective-permute-start.3) | collective-permute-done | bytes 270368 | tf_op jit(solution)/shard_map/ppermute | solution.py:340
  35.7 3.2 %newton.1.folded.after = bf16[528,256]{1,0:T(8,128)(2,1)S(1)} custom-call(f32[1,256]{1,0:T(1,128)S(1)} %get-tuple-element.37.after.squares, bf16[528,256]{1,0:T(8,128)(2,1)S(1)} %add_convert_fusion.1.mine, bf16[528,256]{1,0:T(8,128)(2,1)S(1)} %collective-permute-done.3.other), custom_call_target="tpu_custom_call" | custom-call | flops 2147483648 | bytes 2097152 | tf_op jit(solution)/shard_map/newton/pallas_call | solution.py:183
  38.9 0.6 collective-permute-start.11
  39.5 0.6 collective-permute-start.10
  40.1 2.4 %collective-permute-start.13 = (bf16[528,256]{1,0:T(8,128)(2,1)S(1)}, bf16[528,256]{1,0:T(8,128)(2,1)S(1)}, u32[]{:S(2)}, u32[]{:S(2)}) collective-permute-start(bf16[528,256]{1,0:T(8,128)(2,1)S(1)} %newton.1.folded.after), channel_id=1, source_target_pairs={{0,3},{1,2},{2,1},{3,0},{4,7},{5,6},{6,5},{7,4},{8,11},{9,10},{10,... | collective-permute-start | bytes 811016 | tf_op jit(solution)/shard_map/ppermute | solution.py:340
  42.4 0.0 collective-permute-done.6.from_z
  42.4 0.6 norm.1
  43.0 1.5 %collective-permute-start.7 = (f32[8,128]{1,0:T(8,128)S(1)}, f32[8,128]{1,0:T(8,128)S(1)}, u32[]{:S(2)}, u32[]{:S(2)}) collective-permute-start(f32[8,128]{1,0:T(8,128)S(1)} %norm.1), channel_id=1, source_target_pairs={{0,16},{1,17},{2,18},{3,19},{4,20},{5,21},{6,22},{7,23},{8,24},{9,... | collective-permute-start | bytes 12296 | tf_op jit(solution)/shard_map/ppermute | solution.py:340
  44.5 2.3 %multiply.3 = (bf16[512,3584]{1,0:T(8,128)(2,1)S(1)}, bf16[512,512]{1,0:T(8,128)(2,1)S(1)}) custom-call(bf16[528,256]{1,0:T(8,128)(2,1)S(1)} %newton.1.folded.after, bf16[528,256]{1,0:T(8,128)(2,1)S(1)} %newton.1.folded.after, bf16[512,3584]{1,0:T(8,128)(2,1)S(1)} %get-tuple-element.47.held_ref), custom_call_target="tpu_custom_call", output_to_operand_aliasing={{0}: (2, {})} | custom-call | flops 1 | bytes 1 | tf_op jit(solution)/shard_map/multiply/pallas_call | solution.py:242
  46.9 0.1 collective-permute-start.8
  47.0 1.2 %collective-permute-done.8 = f32[8,128]{1,0:T(8,128)S(1)} collective-permute-done((f32[8,128]{1,0:T(8,128)S(1)}, f32[8,128]{1,0:T(8,128)S(1)}, u32[]{:S(2)}, u32[]{:S(2)}) %collective-permute-start.8) | collective-permute-done | bytes 4128 | tf_op jit(solution)/shard_map/ppermute | solution.py:340
  48.1 0.5 collective-permute-start.9
  48.7 3.4 %collective-permute-done.9 = f32[8,128]{1,0:T(8,128)S(1)} collective-permute-done((f32[8,128]{1,0:T(8,128)S(1)}, f32[8,128]{1,0:T(8,128)S(1)}, u32[]{:S(2)}, u32[]{:S(2)}) %collective-permute-start.9) | collective-permute-done | bytes 4128 | tf_op jit(solution)/shard_map/ppermute | solution.py:340
  52.1 0.6 collective-permute-start.12
  52.7 2.5 %multiply.4 = (bf16[512,3584]{1,0:T(8,128)(2,1)S(1)}, bf16[512,512]{1,0:T(8,128)(2,1)S(1)}) custom-call(bf16[528,256]{1,0:T(8,128)(2,1)S(1)} %collective-permute-done.11.after.folded, bf16[528,256]{1,0:T(8,128)(2,1)S(1)} %collective-permute-done.11.after.folded, bf16[512,3584]{1,0:T(8,128)(2,1)S(1)} %get-tuple-element.50.held_ref), custom_call_target="tpu_custom_call", output_to_operand_aliasing={{0}: (2, {})} | custom-call | flops 1 | bytes 1 | tf_op jit(solution)/shard_map/multiply/pallas_call | solution.py:242
  55.2 0.5 collective-permute-done.12
  55.7 3.0 %collective-permute-start.14 = (f32[8,128]{1,0:T(8,128)S(1)}, f32[8,128]{1,0:T(8,128)S(1)}, u32[]{:S(2)}, u32[]{:S(2)}) collective-permute-start(f32[8,128]{1,0:T(8,128)S(1)} %add.39), channel_id=1, source_target_pairs={{0,4},{1,5},{2,6},{3,7},{4,0},{5,1},{6,2},{7,3},{8,12},{9,13},{10,... | collective-permute-start | bytes 12296 | tf_op jit(solution)/shard_map/ppermute | solution.py:340
  58.7 2.3 %multiply.5 = (bf16[512,3584]{1,0:T(8,128)(2,1)S(1)}, bf16[512,512]{1,0:T(8,128)(2,1)S(1)}) custom-call(bf16[528,256]{1,0:T(8,128)(2,1)S(1)} %collective-permute-done.10.after.folded, bf16[528,256]{1,0:T(8,128)(2,1)S(1)} %collective-permute-done.10.after.folded, bf16[512,3584]{1,0:T(8,128)(2,1)S(1)} %get-tuple-element.56.held_ref), custom_call_target="tpu_custom_call", output_to_operand_aliasing={{0}: (2, {})} | custom-call | flops 1 | bytes 1 | tf_op jit(solution)/shard_map/multiply/pallas_call | solution.py:242
  61.1 8.0 %finish.1 = (bf16[2048,3584]{1,0:T(8,128)(2,1)}, bf16[2,512,512]{2,1,0:T(8,128)(2,1)}, bf16[512,3584]{1,0:T(8,128)(2,1)S(1)}, bf16[512,3584]{1,0:T(8,128)(2,1)S(...) custom-call(s32[6]{0:T(128)S(1)} %pad_add_fusion.order, ...), custom_call_target="tpu_custom_call", output_to_operand_aliasing={{2}: (7, {}), {3}: (8, {}), {4}: (9, {}), {5}: (10, {})} | custom-call | tf_op jit(solution)/shard_map/finish/pallas_call | solution.py:316
  (19 shorter events, 0.1 us)
Async XLA Ops:
  0.7 1.6 %copy-start = (bf16[512,2048]{1,0:T(8,128)(2,1)S(1)}, bf16[512,2048]{1,0:T(8,128)(2,1)}, u32[]{:S(2)}) copy-start(bf16[512,2048]{1,0:T(8,128)(2,1)} %x_ref.1) | copy-start | bytes 6291460
  3.9 17.6 %collective-permute-start = (bf16[528,256]{1,0:T(8,128)(2,1)S(1)}, bf16[528,256]{1,0:T(8,128)(2,1)S(1)}, u32[]{:S(2)}, u32[]{:S(2)}) collective-permute-start(bf16[528,256]{1,0:T(8,128)(2,1)S(1)} %get-tuple-element.38), channel_id=1, source_target_pairs={{0,1},{1,0},{2,3},{3,2},{4,5},{5,4},{6,7},{7,6},{8,9},{9,8},{10,11... | collective-permute-start | bytes 811016 | tf_op jit(solution)/shard_map/ppermute | solution.py:340
  6.9 14.6 %collective-permute-start.1 = (bf16[528,256]{1,0:T(8,128)(2,1)S(1)}, bf16[528,256]{1,0:T(8,128)(2,1)S(1)}, u32[]{:S(2)}, u32[]{:S(2)}) collective-permute-start(bf16[528,256]{1,0:T(8,128)(2,1)S(1)} %get-tuple-element.39), channel_id=1, source_target_pairs={{0,2},{1,3},{2,0},{3,1},{4,6},{5,7},{6,4},{7,5},{8,10},{9,11},{10,... | collective-permute-start | bytes 811016 | tf_op jit(solution)/shard_map/ppermute | solution.py:340
  8.5 13.0 %collective-permute-start.2 = (bf16[528,256]{1,0:T(8,128)(2,1)S(1)}, bf16[528,256]{1,0:T(8,128)(2,1)S(1)}, u32[]{:S(2)}, u32[]{:S(2)}) collective-permute-start(bf16[528,256]{1,0:T(8,128)(2,1)S(1)} %get-tuple-element.40), channel_id=1, source_target_pairs={{0,3},{1,2},{2,1},{3,0},{4,7},{5,6},{6,5},{7,4},{8,11},{9,10},{10,... | collective-permute-start | bytes 811016 | tf_op jit(solution)/shard_map/ppermute | solution.py:340
  19.6 7.7 %collective-permute-start.4 = (bf16[528,256]{1,0:T(8,128)(2,1)S(1)}, bf16[528,256]{1,0:T(8,128)(2,1)S(1)}, u32[]{:S(2)}, u32[]{:S(2)}) collective-permute-start(bf16[528,256]{1,0:T(8,128)(2,1)S(1)} %get-tuple-element.42), channel_id=1, source_target_pairs={{0,1},{1,0},{2,3},{3,2},{4,5},{5,4},{6,7},{7,6},{8,9},{9,8},{10,11... | collective-permute-start | bytes 811016 | tf_op jit(solution)/shard_map/ppermute | solution.py:340
  21.7 14.0 %collective-permute-start.3 = (bf16[528,256]{1,0:T(8,128)(2,1)S(1)}, bf16[528,256]{1,0:T(8,128)(2,1)S(1)}, u32[]{:S(2)}, u32[]{:S(2)}) collective-permute-start(bf16[528,256]{1,0:T(8,128)(2,1)S(1)} %add_convert_fusion.1.mine), channel_id=1, source_target_pairs={{0,4},{1,5},{2,6},{3,7},{4,0},{5,1},{6,2},{7,3},{8,12},{9,13},{10,... | collective-permute-start | bytes 811016 | tf_op jit(solution)/shard_map/ppermute | solution.py:340
  27.4 15.1 %collective-permute-start.6 = (bf16[528,256]{1,0:T(8,128)(2,1)S(1)}, bf16[528,256]{1,0:T(8,128)(2,1)S(1)}, u32[]{:S(2)}, u32[]{:S(2)}) collective-permute-start(bf16[528,256]{1,0:T(8,128)(2,1)S(1)} %add_convert_fusion), channel_id=1, source_target_pairs={{0,2},{1,3},{2,0},{3,1},{4,6},{5,7},{6,4},{7,5},{8,10},{9,11},{10,... | collective-permute-start | bytes 811016 | tf_op jit(solution)/shard_map/ppermute | solution.py:340
  29.1 13.3 %collective-permute-start.5 = (bf16[528,256]{1,0:T(8,128)(2,1)S(1)}, bf16[528,256]{1,0:T(8,128)(2,1)S(1)}, u32[]{:S(2)}, u32[]{:S(2)}) collective-permute-start(bf16[528,256]{1,0:T(8,128)(2,1)S(1)} %get-tuple-element.44), channel_id=1, source_target_pairs={{0,1},{1,0},{2,3},{3,2},{4,5},{5,4},{6,7},{7,6},{8,9},{9,8},{10,11... | collective-permute-start | bytes 811016 | tf_op jit(solution)/shard_map/ppermute | solution.py:340
  38.9 13.8 %collective-permute-start.11 = (bf16[528,256]{1,0:T(8,128)(2,1)S(1)}, bf16[528,256]{1,0:T(8,128)(2,1)S(1)}, u32[]{:S(2)}, u32[]{:S(2)}) collective-permute-start(bf16[528,256]{1,0:T(8,128)(2,1)S(1)} %newton.1.folded.after), channel_id=1, source_target_pairs={{0,1},{1,0},{2,3},{3,2},{4,5},{5,4},{6,7},{7,6},{8,9},{9,8},{10,11... | collective-permute-start | bytes 811016 | tf_op jit(solution)/shard_map/ppermute | solution.py:340
  39.5 16.2 %collective-permute-start.10 = (bf16[528,256]{1,0:T(8,128)(2,1)S(1)}, bf16[528,256]{1,0:T(8,128)(2,1)S(1)}, u32[]{:S(2)}, u32[]{:S(2)}) collective-permute-start(bf16[528,256]{1,0:T(8,128)(2,1)S(1)} %newton.1.folded.after), channel_id=1, source_target_pairs={{0,2},{1,3},{2,0},{3,1},{4,6},{5,7},{6,4},{7,5},{8,10},{9,11},{10,... | collective-permute-start | bytes 811016 | tf_op jit(solution)/shard_map/ppermute | solution.py:340
  40.1 21.0 %collective-permute-start.13 = (bf16[528,256]{1,0:T(8,128)(2,1)S(1)}, bf16[528,256]{1,0:T(8,128)(2,1)S(1)}, u32[]{:S(2)}, u32[]{:S(2)}) collective-permute-start(bf16[528,256]{1,0:T(8,128)(2,1)S(1)} %newton.1.folded.after), channel_id=1, source_target_pairs={{0,3},{1,2},{2,1},{3,0},{4,7},{5,6},{6,5},{7,4},{8,11},{9,10},{10,... | collective-permute-start | bytes 811016 | tf_op jit(solution)/shard_map/ppermute | solution.py:340
  43.0 3.9 %collective-permute-start.7 = (f32[8,128]{1,0:T(8,128)S(1)}, f32[8,128]{1,0:T(8,128)S(1)}, u32[]{:S(2)}, u32[]{:S(2)}) collective-permute-start(f32[8,128]{1,0:T(8,128)S(1)} %norm.1), channel_id=1, source_target_pairs={{0,16},{1,17},{2,18},{3,19},{4,20},{5,21},{6,22},{7,23},{8,24},{9,... | collective-permute-start | bytes 12296 | tf_op jit(solution)/shard_map/ppermute | solution.py:340
  46.9 1.2 %collective-permute-start.8 = (f32[8,128]{1,0:T(8,128)S(1)}, f32[8,128]{1,0:T(8,128)S(1)}, u32[]{:S(2)}, u32[]{:S(2)}) collective-permute-start(f32[8,128]{1,0:T(8,128)S(1)} %add.36), channel_id=1, source_target_pairs={{0,8},{1,9},{2,10},{3,11},{4,12},{5,13},{6,14},{7,15},{8,0},{9,1},... | collective-permute-start | bytes 12296 | tf_op jit(solution)/shard_map/ppermute | solution.py:340
  48.1 3.9 %collective-permute-start.9 = (f32[8,128]{1,0:T(8,128)S(1)}, f32[8,128]{1,0:T(8,128)S(1)}, u32[]{:S(2)}, u32[]{:S(2)}) collective-permute-start(f32[8,128]{1,0:T(8,128)S(1)} %add.37), channel_id=1, source_target_pairs={{0,1},{1,0},{2,3},{3,2},{4,5},{5,4},{6,7},{7,6},{8,9},{9,8},{10,11... | collective-permute-start | bytes 12296 | tf_op jit(solution)/shard_map/ppermute | solution.py:340
  52.1 3.6 %collective-permute-start.12 = (f32[8,128]{1,0:T(8,128)S(1)}, f32[8,128]{1,0:T(8,128)S(1)}, u32[]{:S(2)}, u32[]{:S(2)}) collective-permute-start(f32[8,128]{1,0:T(8,128)S(1)} %add.38), channel_id=1, source_target_pairs={{0,2},{1,3},{2,0},{3,1},{4,6},{5,7},{6,4},{7,5},{8,10},{9,11},{10,... | collective-permute-start | bytes 12296 | tf_op jit(solution)/shard_map/ppermute | solution.py:340
  52.7 8.4 %copy-start.1 = (s32[4,4]{1,0:T(4,128)S(1)}, s32[4,4]{1,0:T(4,128)}, u32[]{:S(2)}) copy-start(s32[4,4]{1,0:T(4,128)} %owner_slot.1) | copy-start | bytes 196
  55.7 5.3 %collective-permute-start.14 = (f32[8,128]{1,0:T(8,128)S(1)}, f32[8,128]{1,0:T(8,128)S(1)}, u32[]{:S(2)}, u32[]{:S(2)}) collective-permute-start(f32[8,128]{1,0:T(8,128)S(1)} %add.39), channel_id=1, source_target_pairs={{0,4},{1,5},{2,6},{3,7},{4,0},{5,1},{6,2},{7,3},{8,12},{9,13},{10,... | collective-permute-start | bytes 12296 | tf_op jit(solution)/shard_map/ppermute | solution.py:340

commit v14 on v13

--- a/solution.py
+++ b/solution.py
@@ -279,7 +279,7 @@
 
     bands = [(place, pl.ds(i, BAND)) for place in range(EARLY) for i in range(0, BLK, BAND)]
     products = [(place, part) for place in range(EARLY, QUAD) for part in chunks(columns, BLK)]
-    ahead = len(bands) - len(products) // 2
+    ahead = 1
     for one in bands[:ahead]:
         rescale(*one)
         send(*one, pl.ds(0, columns))
@@ -375,7 +375,7 @@
     from_y = swap(grams[1], 1)
     from_z = swap(add(grams[2], across), 2)
     root = newton(tokens_all, squares, mine, other)
-    folded = [root, swap(root, 1), swap(root, 2), swap(root, 3)]
+    folded = [root, swap(root, 1), swap(root, 2)]
     blocks, roots = list(blocks), []
 
     def precondition(place):
@@ -383,9 +383,12 @@
         roots.append(root)
 
     sums = norm(root, grams[0], from_y, from_z, squares)
-    early, arrivals = {0:[0],3:[1],4:[2]}, {3:[1,2],4:[3]}
+    early, arrivals = {0:[0],3:[1],4:[2]}, {2:[1,2],4:[3]}
     for step, flip in enumerate(rounds()):
         received = swap(sums, flip)
+        if step == 3:
+            folded[2], _ = lax.optimization_barrier((folded[2], sums))
+            folded.append(swap(folded[2], 1))
         for place in early.get(step, ()):
             precondition(place)
             blocks[place], received = lax.optimization_barrier((blocks[place], received))

time: 69.4 us -> 68.4 us (0.986)
  waiting for transfers between devices: 13.1 us -> 11.2 us
  starting transfers between devices: 21.8 us -> 23 us
    ppermute x15, waiting for transfers between devices: 13.1 us -> 11.2 us  [swap(): return lax.ppermute(value, axes, [(i, i ^ flip) for i in range(count)])]
    ppermute x15, starting transfers between devices: 21.8 us -> 23 us  [swap(): return lax.ppermute(value, axes, [(i, i ^ flip) for i in range(count)])]
  transfers between devices with their start and end apart: 15 -> 15, of which waited for: 5 -> 4; matrix products, arithmetic and copies ran while one was open for 0% -> 0% of each run, Pallas kernels for 32% -> 32%
where the time goes in v14:
time: 68.4 us; the launch traced here: 68.2 us
  Pallas kernels  31.2 us (46%)
  starting transfers between devices  23 us (34%)
  waiting for transfers between devices  11.2 us (16%)
  local copies, waits for them, and re-layouts  1.6 us (2%)
  between operations  0.95 us (1%)
    ppermute x15, starting transfers between devices, swap(): return lax.ppermute(value, axes, [(i, i ^ flip) for i in range(count)])  23 us
    ppermute x15, waiting for transfers between devices, swap(): return lax.ppermute(value, axes, [(i, i ^ flip) for i in range(count)])  11.2 us
    pallas_call x1, Pallas kernels, gram(): pl.pallas_call(gram_kernel, out_shape=[pltpu.VMEM((BLK, columns), BF16)]...  11 us
    pallas_call x1, Pallas kernels, finish(): pl.pallas_call(finish_kernel, out_shape=[jax.ShapeDtypeStruct((QUAD * BLK...  7.7 us
    pallas_call x3, Pallas kernels, multiply(): pl.pallas_call(multiply_kernel, out_shape=[pltpu.VMEM(held.shape, BF16),...  7.08 us
    pallas_call x1, Pallas kernels, newton(): pl.pallas_call(functools.partial(newton_kernel, tokens), out_shape=jax.Sh...  3.2 us
    unnamed x4, local copies, waits for them, and re-layouts  1.6 us
    pallas_call x1, Pallas kernels, statistics(): pl.pallas_call(stat_kernel, out_shape=[jax.ShapeDtypeStruct((FOLD, HALF),...  1.59 us
  transfers between devices with their start and end apart: 15, of which 4 were waited for; matrix products, arithmetic and copies ran while one was open for 0% of the time, Pallas kernels for 32%

profile of v14, /device:TPU:0, one launch (start us, length us, event | category | flops | bytes accessed | tf_op | source)
XLA Modules:
  0.0 68.2 jit_solution(8174360403543454383)
XLA Ops:
  0.7 0.1 pad_add_fusion.order
  0.7 1.6 %copy-done = bf16[512,2048]{1,0:T(8,128)(2,1)S(1)} copy-done((bf16[512,2048]{1,0:T(8,128)(2,1)S(1)}, bf16[512,2048]{1,0:T(8,128)(2,1)}, u32[]{:S(2)}) %copy-start) | copy-done | bytes 2097176
  2.3 1.6 %statistics.1 = (bf16[528,256]{1,0:T(8,128)(2,1)S(1)}, bf16[528,256]{1,0:T(8,128)(2,1)S(1)}, bf16[528,256]{1,0:T(8,128)(2,1)S(1)}, bf16[528,256]{1,0:T(8,128)(2,1)S(1)}) custom-call(s32[6]{0:T(128)S(1)} %pad_add_fusion.order, bf16[512,2048]{1,0:T(8,128)(2,1)S(1)} %copy-done), custom_call_target="tpu_custom_call" | custom-call | tf_op jit(solution)/shard_map/statistics/pallas_call | solution.py:72
  3.9 3.0 %collective-permute-start = (bf16[528,256]{1,0:T(8,128)(2,1)S(1)}, bf16[528,256]{1,0:T(8,128)(2,1)S(1)}, u32[]{:S(2)}, u32[]{:S(2)}) collective-permute-start(bf16[528,256]{1,0:T(8,128)(2,1)S(1)} %get-tuple-element.40), channel_id=1, source_target_pairs={{0,1},{1,0},{2,3},{3,2},{4,5},{5,4},{6,7},{7,6},{8,9},{9,8},{10,11... | collective-permute-start | bytes 811016 | tf_op jit(solution)/shard_map/ppermute | solution.py:340
  6.9 1.6 %collective-permute-start.1 = (bf16[528,256]{1,0:T(8,128)(2,1)S(1)}, bf16[528,256]{1,0:T(8,128)(2,1)S(1)}, u32[]{:S(2)}, u32[]{:S(2)}) collective-permute-start(bf16[528,256]{1,0:T(8,128)(2,1)S(1)} %get-tuple-element.41), channel_id=1, source_target_pairs={{0,2},{1,3},{2,0},{3,1},{4,6},{5,7},{6,4},{7,5},{8,10},{9,11},{10,... | collective-permute-start | bytes 811016 | tf_op jit(solution)/shard_map/ppermute | solution.py:340
  8.5 11.0 %gram.1 = (bf16[512,3584]{1,0:T(8,128)(2,1)S(1)}, bf16[512,3584]{1,0:T(8,128)(2,1)S(1)}, bf16[512,3584]{1,0:T(8,128)(2,1)S(1)}, bf16[512,3584]{1,0:T(8,128)(2,1)...) custom-call(s32[6]{0:T(128)S(1)} %pad_add_fusion.order, ...), custom_call_target="tpu_custom_call" | custom-call | flops 7516192768 | bytes 14680064 | tf_op jit(solution)/shard_map/gram/pallas_call | solution.py:124
  19.6 2.0 %collective-permute-start.4 = (bf16[528,256]{1,0:T(8,128)(2,1)S(1)}, bf16[528,256]{1,0:T(8,128)(2,1)S(1)}, u32[]{:S(2)}, u32[]{:S(2)}) collective-permute-start(bf16[528,256]{1,0:T(8,128)(2,1)S(1)} %get-tuple-element.44), channel_id=1, source_target_pairs={{0,1},{1,0},{2,3},{3,2},{4,5},{5,4},{6,7},{7,6},{8,9},{9,8},{10,11... | collective-permute-start | bytes 811016 | tf_op jit(solution)/shard_map/ppermute | solution.py:340
  21.5 0.0 collective-permute-done.1
  21.5 0.0 collective-permute-done.2
  21.6 0.1 add_convert_fusion.1.mine
  21.7 2.7 %collective-permute-start.3 = (bf16[528,256]{1,0:T(8,128)(2,1)S(1)}, bf16[528,256]{1,0:T(8,128)(2,1)S(1)}, u32[]{:S(2)}, u32[]{:S(2)}) collective-permute-start(bf16[528,256]{1,0:T(8,128)(2,1)S(1)} %add_convert_fusion.1.mine), channel_id=1, source_target_pairs={{0,4},{1,5},{2,6},{3,7},{4,0},{5,1},{6,2},{7,3},{8,12},{9,13},{10,... | collective-permute-start | bytes 811016 | tf_op jit(solution)/shard_map/ppermute | solution.py:340
  24.4 2.9 %collective-permute-done.4 = bf16[528,256]{1,0:T(8,128)(2,1)S(1)} collective-permute-done((bf16[528,256]{1,0:T(8,128)(2,1)S(1)}, bf16[528,256]{1,0:T(8,128)(2,1)S(1)}, u32[]{:S(2)}, u32[]{:S(2)}) %collective-permute-start.4) | collective-permute-done | bytes 270368 | tf_op jit(solution)/shard_map/ppermute | solution.py:340
  27.3 0.1 add_convert_fusion
  27.4 1.7 %collective-permute-start.6 = (bf16[528,256]{1,0:T(8,128)(2,1)S(1)}, bf16[528,256]{1,0:T(8,128)(2,1)S(1)}, u32[]{:S(2)}, u32[]{:S(2)}) collective-permute-start(bf16[528,256]{1,0:T(8,128)(2,1)S(1)} %add_convert_fusion), channel_id=1, source_target_pairs={{0,2},{1,3},{2,0},{3,1},{4,6},{5,7},{6,4},{7,5},{8,10},{9,11},{10,... | collective-permute-start | bytes 811016 | tf_op jit(solution)/shard_map/ppermute | solution.py:340
  29.1 1.5 %collective-permute-start.5 = (bf16[528,256]{1,0:T(8,128)(2,1)S(1)}, bf16[528,256]{1,0:T(8,128)(2,1)S(1)}, u32[]{:S(2)}, u32[]{:S(2)}) collective-permute-start(bf16[528,256]{1,0:T(8,128)(2,1)S(1)} %get-tuple-element.46), channel_id=1, source_target_pairs={{0,1},{1,0},{2,3},{3,2},{4,5},{5,4},{6,7},{7,6},{8,9},{9,8},{10,11... | collective-permute-start | bytes 811016 | tf_op jit(solution)/shard_map/ppermute | solution.py:340
  30.6 5.0 %collective-permute-done.3.other = bf16[528,256]{1,0:T(8,128)(2,1)S(1)} collective-permute-done((bf16[528,256]{1,0:T(8,128)(2,1)S(1)}, bf16[528,256]{1,0:T(8,128)(2,1)S(1)}, u32[]{:S(2)}, u32[]{:S(2)}) %collective-permute-start.3) | collective-permute-done | bytes 270368 | tf_op jit(solution)/shard_map/ppermute | solution.py:340
  35.7 3.2 %newton.1.folded.after = bf16[528,256]{1,0:T(8,128)(2,1)S(1)} custom-call(f32[1,256]{1,0:T(1,128)S(1)} %get-tuple-element.39.after.squares, bf16[528,256]{1,0:T(8,128)(2,1)S(1)} %add_convert_fusion.1.mine, bf16[528,256]{1,0:T(8,128)(2,1)S(1)} %collective-permute-done.3.other), custom_call_target="tpu_custom_call" | custom-call | flops 2147483648 | bytes 2097152 | tf_op jit(solution)/shard_map/newton/pallas_call | solution.py:183
  38.9 0.6 collective-permute-start.10
  39.5 0.6 collective-permute-start.9
  40.1 0.6 norm.1
  40.6 1.6 %collective-permute-start.7 = (f32[8,128]{1,0:T(8,128)S(1)}, f32[8,128]{1,0:T(8,128)S(1)}, u32[]{:S(2)}, u32[]{:S(2)}) collective-permute-start(f32[8,128]{1,0:T(8,128)S(1)} %norm.1), channel_id=1, source_target_pairs={{0,16},{1,17},{2,18},{3,19},{4,20},{5,21},{6,22},{7,23},{8,24},{9,... | collective-permute-start | bytes 12296 | tf_op jit(solution)/shard_map/ppermute | solution.py:340
  42.2 2.3 %multiply.3 = (bf16[512,3584]{1,0:T(8,128)(2,1)S(1)}, bf16[512,512]{1,0:T(8,128)(2,1)S(1)}) custom-call(bf16[528,256]{1,0:T(8,128)(2,1)S(1)} %newton.1.folded.after, bf16[528,256]{1,0:T(8,128)(2,1)S(1)} %newton.1.folded.after, bf16[512,3584]{1,0:T(8,128)(2,1)S(1)} %get-tuple-element.49.held_ref), custom_call_target="tpu_custom_call", output_to_operand_aliasing={{0}: (2, {})} | custom-call | flops 1 | bytes 1 | tf_op jit(solution)/shard_map/multiply/pallas_call | solution.py:242
  44.5 0.1 collective-permute-start.8
  44.6 1.2 %collective-permute-done.8 = f32[8,128]{1,0:T(8,128)S(1)} collective-permute-done((f32[8,128]{1,0:T(8,128)S(1)}, f32[8,128]{1,0:T(8,128)S(1)}, u32[]{:S(2)}, u32[]{:S(2)}) %collective-permute-start.8) | collective-permute-done | bytes 4128 | tf_op jit(solution)/shard_map/ppermute | solution.py:340
  45.8 1.5 %collective-permute-start.11 = (f32[8,128]{1,0:T(8,128)S(1)}, f32[8,128]{1,0:T(8,128)S(1)}, u32[]{:S(2)}, u32[]{:S(2)}) collective-permute-start(f32[8,128]{1,0:T(8,128)S(1)} %add.37), channel_id=1, source_target_pairs={{0,1},{1,0},{2,3},{3,2},{4,5},{5,4},{6,7},{7,6},{8,9},{9,8},{10,11... | collective-permute-start | bytes 12296 | tf_op jit(solution)/shard_map/ppermute | solution.py:340
  47.3 2.1 %collective-permute-done.11 = f32[8,128]{1,0:T(8,128)S(1)} collective-permute-done((f32[8,128]{1,0:T(8,128)S(1)}, f32[8,128]{1,0:T(8,128)S(1)}, u32[]{:S(2)}, u32[]{:S(2)}) %collective-permute-start.11) | collective-permute-done | bytes 4128 | tf_op jit(solution)/shard_map/ppermute | solution.py:340
  49.4 1.6 %collective-permute-start.13 = (bf16[528,256]{1,0:T(8,128)(2,1)S(1)}, bf16[528,256]{1,0:T(8,128)(2,1)S(1)}, u32[]{:S(2)}, u32[]{:S(2)}) collective-permute-start(bf16[528,256]{1,0:T(8,128)(2,1)S(1)} %collective-permute-done.9.after.folded), channel_id=1, source_target_pairs={{0,1},{1,0},{2,3},{3,2},{4,5},{5,4},{6,7},{7,6},{8,9},{9,8},{10,11... | collective-permute-start | bytes 811016 | tf_op jit(solution)/shard_map/ppermute | solution.py:340
  51.0 1.4 %collective-permute-start.12 = (f32[8,128]{1,0:T(8,128)S(1)}, f32[8,128]{1,0:T(8,128)S(1)}, u32[]{:S(2)}, u32[]{:S(2)}) collective-permute-start(f32[8,128]{1,0:T(8,128)S(1)} %add.38), channel_id=1, source_target_pairs={{0,2},{1,3},{2,0},{3,1},{4,6},{5,7},{6,4},{7,5},{8,10},{9,11},{10,... | collective-permute-start | bytes 12296 | tf_op jit(solution)/shard_map/ppermute | solution.py:340
  52.4 2.5 %multiply.4 = (bf16[512,3584]{1,0:T(8,128)(2,1)S(1)}, bf16[512,512]{1,0:T(8,128)(2,1)S(1)}) custom-call(bf16[528,256]{1,0:T(8,128)(2,1)S(1)} %collective-permute-done.10.after.folded, bf16[528,256]{1,0:T(8,128)(2,1)S(1)} %collective-permute-done.10.after.folded, bf16[512,3584]{1,0:T(8,128)(2,1)S(1)} %get-tuple-element.55.held_ref), custom_call_target="tpu_custom_call", output_to_operand_aliasing={{0}: (2, {})} | custom-call | flops 1 | bytes 1 | tf_op jit(solution)/shard_map/multiply/pallas_call | solution.py:242
  54.9 3.1 %collective-permute-start.14 = (f32[8,128]{1,0:T(8,128)S(1)}, f32[8,128]{1,0:T(8,128)S(1)}, u32[]{:S(2)}, u32[]{:S(2)}) collective-permute-start(f32[8,128]{1,0:T(8,128)S(1)} %add.39), channel_id=1, source_target_pairs={{0,4},{1,5},{2,6},{3,7},{4,0},{5,1},{6,2},{7,3},{8,12},{9,13},{10,... | collective-permute-start | bytes 12296 | tf_op jit(solution)/shard_map/ppermute | solution.py:340
  58.0 2.3 %multiply.5 = (bf16[512,3584]{1,0:T(8,128)(2,1)S(1)}, bf16[512,512]{1,0:T(8,128)(2,1)S(1)}) custom-call(bf16[528,256]{1,0:T(8,128)(2,1)S(1)} %collective-permute-done.9.after.folded, bf16[528,256]{1,0:T(8,128)(2,1)S(1)} %collective-permute-done.9.after.folded, bf16[512,3584]{1,0:T(8,128)(2,1)S(1)} %get-tuple-element.60.held_ref), custom_call_target="tpu_custom_call", output_to_operand_aliasing={{0}: (2, {})} | custom-call | flops 1 | bytes 1 | tf_op jit(solution)/shard_map/multiply/pallas_call | solution.py:242
  60.4 7.7 %finish.1 = (bf16[2048,3584]{1,0:T(8,128)(2,1)}, bf16[2,512,512]{2,1,0:T(8,128)(2,1)}, bf16[512,3584]{1,0:T(8,128)(2,1)S(1)}, bf16[512,3584]{1,0:T(8,128)(2,1)S(...) custom-call(s32[6]{0:T(128)S(1)} %pad_add_fusion.order, ...), custom_call_target="tpu_custom_call", output_to_operand_aliasing={{2}: (7, {}), {3}: (8, {}), {4}: (9, {}), {5}: (10, {})} | custom-call | tf_op jit(solution)/shard_map/finish/pallas_call | solution.py:316
  (19 shorter events, 0.1 us)
Async XLA Ops:
  0.7 1.6 %copy-start = (bf16[512,2048]{1,0:T(8,128)(2,1)S(1)}, bf16[512,2048]{1,0:T(8,128)(2,1)}, u32[]{:S(2)}) copy-start(bf16[512,2048]{1,0:T(8,128)(2,1)} %x_ref.1) | copy-start | bytes 6291460
  3.9 17.6 %collective-permute-start = (bf16[528,256]{1,0:T(8,128)(2,1)S(1)}, bf16[528,256]{1,0:T(8,128)(2,1)S(1)}, u32[]{:S(2)}, u32[]{:S(2)}) collective-permute-start(bf16[528,256]{1,0:T(8,128)(2,1)S(1)} %get-tuple-element.40), channel_id=1, source_target_pairs={{0,1},{1,0},{2,3},{3,2},{4,5},{5,4},{6,7},{7,6},{8,9},{9,8},{10,11... | collective-permute-start | bytes 811016 | tf_op jit(solution)/shard_map/ppermute | solution.py:340
  6.9 14.6 %collective-permute-start.1 = (bf16[528,256]{1,0:T(8,128)(2,1)S(1)}, bf16[528,256]{1,0:T(8,128)(2,1)S(1)}, u32[]{:S(2)}, u32[]{:S(2)}) collective-permute-start(bf16[528,256]{1,0:T(8,128)(2,1)S(1)} %get-tuple-element.41), channel_id=1, source_target_pairs={{0,2},{1,3},{2,0},{3,1},{4,6},{5,7},{6,4},{7,5},{8,10},{9,11},{10,... | collective-permute-start | bytes 811016 | tf_op jit(solution)/shard_map/ppermute | solution.py:340
  8.5 13.0 %collective-permute-start.2 = (bf16[528,256]{1,0:T(8,128)(2,1)S(1)}, bf16[528,256]{1,0:T(8,128)(2,1)S(1)}, u32[]{:S(2)}, u32[]{:S(2)}) collective-permute-start(bf16[528,256]{1,0:T(8,128)(2,1)S(1)} %get-tuple-element.42), channel_id=1, source_target_pairs={{0,3},{1,2},{2,1},{3,0},{4,7},{5,6},{6,5},{7,4},{8,11},{9,10},{10,... | collective-permute-start | bytes 811016 | tf_op jit(solution)/shard_map/ppermute | solution.py:340
  19.6 7.7 %collective-permute-start.4 = (bf16[528,256]{1,0:T(8,128)(2,1)S(1)}, bf16[528,256]{1,0:T(8,128)(2,1)S(1)}, u32[]{:S(2)}, u32[]{:S(2)}) collective-permute-start(bf16[528,256]{1,0:T(8,128)(2,1)S(1)} %get-tuple-element.44), channel_id=1, source_target_pairs={{0,1},{1,0},{2,3},{3,2},{4,5},{5,4},{6,7},{7,6},{8,9},{9,8},{10,11... | collective-permute-start | bytes 811016 | tf_op jit(solution)/shard_map/ppermute | solution.py:340
  21.7 14.0 %collective-permute-start.3 = (bf16[528,256]{1,0:T(8,128)(2,1)S(1)}, bf16[528,256]{1,0:T(8,128)(2,1)S(1)}, u32[]{:S(2)}, u32[]{:S(2)}) collective-permute-start(bf16[528,256]{1,0:T(8,128)(2,1)S(1)} %add_convert_fusion.1.mine), channel_id=1, source_target_pairs={{0,4},{1,5},{2,6},{3,7},{4,0},{5,1},{6,2},{7,3},{8,12},{9,13},{10,... | collective-permute-start | bytes 811016 | tf_op jit(solution)/shard_map/ppermute | solution.py:340
  27.4 12.7 %collective-permute-start.6 = (bf16[528,256]{1,0:T(8,128)(2,1)S(1)}, bf16[528,256]{1,0:T(8,128)(2,1)S(1)}, u32[]{:S(2)}, u32[]{:S(2)}) collective-permute-start(bf16[528,256]{1,0:T(8,128)(2,1)S(1)} %add_convert_fusion), channel_id=1, source_target_pairs={{0,2},{1,3},{2,0},{3,1},{4,6},{5,7},{6,4},{7,5},{8,10},{9,11},{10,... | collective-permute-start | bytes 811016 | tf_op jit(solution)/shard_map/ppermute | solution.py:340
  29.1 11.0 %collective-permute-start.5 = (bf16[528,256]{1,0:T(8,128)(2,1)S(1)}, bf16[528,256]{1,0:T(8,128)(2,1)S(1)}, u32[]{:S(2)}, u32[]{:S(2)}) collective-permute-start(bf16[528,256]{1,0:T(8,128)(2,1)S(1)} %get-tuple-element.46), channel_id=1, source_target_pairs={{0,1},{1,0},{2,3},{3,2},{4,5},{5,4},{6,7},{7,6},{8,9},{9,8},{10,11... | collective-permute-start | bytes 811016 | tf_op jit(solution)/shard_map/ppermute | solution.py:340
  38.9 10.5 %collective-permute-start.10 = (bf16[528,256]{1,0:T(8,128)(2,1)S(1)}, bf16[528,256]{1,0:T(8,128)(2,1)S(1)}, u32[]{:S(2)}, u32[]{:S(2)}) collective-permute-start(bf16[528,256]{1,0:T(8,128)(2,1)S(1)} %newton.1.folded.after), channel_id=1, source_target_pairs={{0,1},{1,0},{2,3},{3,2},{4,5},{5,4},{6,7},{7,6},{8,9},{9,8},{10,11... | collective-permute-start | bytes 811016 | tf_op jit(solution)/shard_map/ppermute | solution.py:340
  39.5 9.9 %collective-permute-start.9 = (bf16[528,256]{1,0:T(8,128)(2,1)S(1)}, bf16[528,256]{1,0:T(8,128)(2,1)S(1)}, u32[]{:S(2)}, u32[]{:S(2)}) collective-permute-start(bf16[528,256]{1,0:T(8,128)(2,1)S(1)} %newton.1.folded.after), channel_id=1, source_target_pairs={{0,2},{1,3},{2,0},{3,1},{4,6},{5,7},{6,4},{7,5},{8,10},{9,11},{10,... | collective-permute-start | bytes 811016 | tf_op jit(solution)/shard_map/ppermute | solution.py:340
  40.6 3.9 %collective-permute-start.7 = (f32[8,128]{1,0:T(8,128)S(1)}, f32[8,128]{1,0:T(8,128)S(1)}, u32[]{:S(2)}, u32[]{:S(2)}) collective-permute-start(f32[8,128]{1,0:T(8,128)S(1)} %norm.1), channel_id=1, source_target_pairs={{0,16},{1,17},{2,18},{3,19},{4,20},{5,21},{6,22},{7,23},{8,24},{9,... | collective-permute-start | bytes 12296 | tf_op jit(solution)/shard_map/ppermute | solution.py:340
  44.5 1.2 %collective-permute-start.8 = (f32[8,128]{1,0:T(8,128)S(1)}, f32[8,128]{1,0:T(8,128)S(1)}, u32[]{:S(2)}, u32[]{:S(2)}) collective-permute-start(f32[8,128]{1,0:T(8,128)S(1)} %add.36), channel_id=1, source_target_pairs={{0,8},{1,9},{2,10},{3,11},{4,12},{5,13},{6,14},{7,15},{8,0},{9,1},... | collective-permute-start | bytes 12296 | tf_op jit(solution)/shard_map/ppermute | solution.py:340
  45.8 3.6 %collective-permute-start.11 = (f32[8,128]{1,0:T(8,128)S(1)}, f32[8,128]{1,0:T(8,128)S(1)}, u32[]{:S(2)}, u32[]{:S(2)}) collective-permute-start(f32[8,128]{1,0:T(8,128)S(1)} %add.37), channel_id=1, source_target_pairs={{0,1},{1,0},{2,3},{3,2},{4,5},{5,4},{6,7},{7,6},{8,9},{9,8},{10,11... | collective-permute-start | bytes 12296 | tf_op jit(solution)/shard_map/ppermute | solution.py:340
  49.4 11.0 %collective-permute-start.13 = (bf16[528,256]{1,0:T(8,128)(2,1)S(1)}, bf16[528,256]{1,0:T(8,128)(2,1)S(1)}, u32[]{:S(2)}, u32[]{:S(2)}) collective-permute-start(bf16[528,256]{1,0:T(8,128)(2,1)S(1)} %collective-permute-done.9.after.folded), channel_id=1, source_target_pairs={{0,1},{1,0},{2,3},{3,2},{4,5},{5,4},{6,7},{7,6},{8,9},{9,8},{10,11... | collective-permute-start | bytes 811016 | tf_op jit(solution)/shard_map/ppermute | solution.py:340
  51.0 3.9 %collective-permute-start.12 = (f32[8,128]{1,0:T(8,128)S(1)}, f32[8,128]{1,0:T(8,128)S(1)}, u32[]{:S(2)}, u32[]{:S(2)}) collective-permute-start(f32[8,128]{1,0:T(8,128)S(1)} %add.38), channel_id=1, source_target_pairs={{0,2},{1,3},{2,0},{3,1},{4,6},{5,7},{6,4},{7,5},{8,10},{9,11},{10,... | collective-permute-start | bytes 12296 | tf_op jit(solution)/shard_map/ppermute | solution.py:340
  52.4 8.0 %copy-start.1 = (s32[4,4]{1,0:T(4,128)S(1)}, s32[4,4]{1,0:T(4,128)}, u32[]{:S(2)}) copy-start(s32[4,4]{1,0:T(4,128)} %owner_slot.1) | copy-start | bytes 196
  54.9 5.4 %collective-permute-start.14 = (f32[8,128]{1,0:T(8,128)S(1)}, f32[8,128]{1,0:T(8,128)S(1)}, u32[]{:S(2)}, u32[]{:S(2)}) collective-permute-start(f32[8,128]{1,0:T(8,128)S(1)} %add.39), channel_id=1, source_target_pairs={{0,4},{1,5},{2,6},{3,7},{4,0},{5,1},{6,2},{7,3},{8,12},{9,13},{10,... | collective-permute-start | bytes 12296 | tf_op jit(solution)/shard_map/ppermute | solution.py:340

commit v15 on v14

--- a/solution.py
+++ b/solution.py
@@ -246,7 +246,7 @@
         out_specs=[VMEM] * 2,
         input_output_aliases={2: 0},
         compiler_params=params(12),
-        cost_estimate=pl.CostEstimate(flops=1, bytes_accessed=1, transcendentals=0),
+        cost_estimate=pl.CostEstimate(flops=1880000000, bytes_accessed=1, transcendentals=0),
         name="multiply",
     )(after, folded, held)
 
@@ -343,7 +343,7 @@
 def rounds():
     peer_bits = lax.axis_size("dp").bit_length() - 1
     bits = [1 << i for i in range(peer_bits + lax.axis_size("pool").bit_length() - 1)]
-    return bits[peer_bits:][::-1] + bits[:peer_bits]
+    return bits[peer_bits:][::-1] + [bits[1], bits[0]] + bits[2:peer_bits]
 
 
 def add(*values):
@@ -383,7 +383,7 @@
         roots.append(root)
 
     sums = norm(root, grams[0], from_y, from_z, squares)
-    early, arrivals = {0:[0],3:[1],4:[2]}, {2:[1,2],4:[3]}
+    early, arrivals = {2:[0],3:[1],4:[2]}, {2:[1,2],4:[3]}
     for step, flip in enumerate(rounds()):
         received = swap(sums, flip)
         if step == 3:

time: 68.4 us -> 67.7 us (0.990)
  starting transfers between devices: 23 us -> 22.1 us
    ppermute x15, starting transfers between devices: 23 us -> 22.1 us  [swap(): return lax.ppermute(value, axes, [(i, i ^ flip) for i in range(count)])]
where the time goes in v15:
time: 67.7 us; the launch traced here: 67.5 us
  Pallas kernels  31.2 us (46%)
  starting transfers between devices  22.1 us (33%)
  waiting for transfers between devices  11.3 us (17%)
  local copies, waits for them, and re-layouts  1.6 us (2%)
  between operations  0.96 us (1%)
    ppermute x15, starting transfers between devices, swap(): return lax.ppermute(value, axes, [(i, i ^ flip) for i in range(count)])  22.1 us
    ppermute x15, waiting for transfers between devices, swap(): return lax.ppermute(value, axes, [(i, i ^ flip) for i in range(count)])  11.3 us
    pallas_call x1, Pallas kernels, gram(): pl.pallas_call(gram_kernel, out_shape=[pltpu.VMEM((BLK, columns), BF16)]...  11 us
    pallas_call x1, Pallas kernels, finish(): pl.pallas_call(finish_kernel, out_shape=[jax.ShapeDtypeStruct((QUAD * BLK...  7.72 us
    pallas_call x3, Pallas kernels, multiply(): pl.pallas_call(multiply_kernel, out_shape=[pltpu.VMEM(held.shape, BF16),...  7.13 us
    pallas_call x1, Pallas kernels, newton(): pl.pallas_call(functools.partial(newton_kernel, tokens), out_shape=jax.Sh...  3.2 us
    unnamed x4, local copies, waits for them, and re-layouts  1.6 us
    pallas_call x1, Pallas kernels, statistics(): pl.pallas_call(stat_kernel, out_shape=[jax.ShapeDtypeStruct((FOLD, HALF),...  1.59 us
  transfers between devices with their start and end apart: 15, of which 4 were waited for; matrix products, arithmetic and copies ran while one was open for 0% of the time, Pallas kernels for 32%

profile of v15, /device:TPU:0, one launch (start us, length us, event | category | flops | bytes accessed | tf_op | source)
XLA Modules:
  0.0 67.5 jit_solution(4095902435983907715)
XLA Ops:
  0.7 0.1 pad_add_fusion.order
  0.7 1.6 %copy-done = bf16[512,2048]{1,0:T(8,128)(2,1)S(1)} copy-done((bf16[512,2048]{1,0:T(8,128)(2,1)S(1)}, bf16[512,2048]{1,0:T(8,128)(2,1)}, u32[]{:S(2)}) %copy-start) | copy-done | bytes 2097176
  2.3 1.6 %statistics.1 = (bf16[528,256]{1,0:T(8,128)(2,1)S(1)}, bf16[528,256]{1,0:T(8,128)(2,1)S(1)}, bf16[528,256]{1,0:T(8,128)(2,1)S(1)}, bf16[528,256]{1,0:T(8,128)(2,1)S(1)}) custom-call(s32[6]{0:T(128)S(1)} %pad_add_fusion.order, bf16[512,2048]{1,0:T(8,128)(2,1)S(1)} %copy-done), custom_call_target="tpu_custom_call" | custom-call | tf_op jit(solution)/shard_map/statistics/pallas_call | solution.py:72
  3.9 3.0 %collective-permute-start = (bf16[528,256]{1,0:T(8,128)(2,1)S(1)}, bf16[528,256]{1,0:T(8,128)(2,1)S(1)}, u32[]{:S(2)}, u32[]{:S(2)}) collective-permute-start(bf16[528,256]{1,0:T(8,128)(2,1)S(1)} %get-tuple-element.40), channel_id=1, source_target_pairs={{0,1},{1,0},{2,3},{3,2},{4,5},{5,4},{6,7},{7,6},{8,9},{9,8},{10,11... | collective-permute-start | bytes 811016 | tf_op jit(solution)/shard_map/ppermute | solution.py:340
  6.9 1.6 %collective-permute-start.1 = (bf16[528,256]{1,0:T(8,128)(2,1)S(1)}, bf16[528,256]{1,0:T(8,128)(2,1)S(1)}, u32[]{:S(2)}, u32[]{:S(2)}) collective-permute-start(bf16[528,256]{1,0:T(8,128)(2,1)S(1)} %get-tuple-element.41), channel_id=1, source_target_pairs={{0,2},{1,3},{2,0},{3,1},{4,6},{5,7},{6,4},{7,5},{8,10},{9,11},{10,... | collective-permute-start | bytes 811016 | tf_op jit(solution)/shard_map/ppermute | solution.py:340
  8.5 11.0 %gram.1 = (bf16[512,3584]{1,0:T(8,128)(2,1)S(1)}, bf16[512,3584]{1,0:T(8,128)(2,1)S(1)}, bf16[512,3584]{1,0:T(8,128)(2,1)S(1)}, bf16[512,3584]{1,0:T(8,128)(2,1)...) custom-call(s32[6]{0:T(128)S(1)} %pad_add_fusion.order, ...), custom_call_target="tpu_custom_call" | custom-call | flops 7516192768 | bytes 14680064 | tf_op jit(solution)/shard_map/gram/pallas_call | solution.py:124
  19.6 2.0 %collective-permute-start.4 = (bf16[528,256]{1,0:T(8,128)(2,1)S(1)}, bf16[528,256]{1,0:T(8,128)(2,1)S(1)}, u32[]{:S(2)}, u32[]{:S(2)}) collective-permute-start(bf16[528,256]{1,0:T(8,128)(2,1)S(1)} %get-tuple-element.44), channel_id=1, source_target_pairs={{0,1},{1,0},{2,3},{3,2},{4,5},{5,4},{6,7},{7,6},{8,9},{9,8},{10,11... | collective-permute-start | bytes 811016 | tf_op jit(solution)/shard_map/ppermute | solution.py:340
  21.5 0.0 collective-permute-done.1
  21.5 0.0 collective-permute-done.2
  21.6 0.1 add_convert_fusion.1.mine
  21.7 2.7 %collective-permute-start.3 = (bf16[528,256]{1,0:T(8,128)(2,1)S(1)}, bf16[528,256]{1,0:T(8,128)(2,1)S(1)}, u32[]{:S(2)}, u32[]{:S(2)}) collective-permute-start(bf16[528,256]{1,0:T(8,128)(2,1)S(1)} %add_convert_fusion.1.mine), channel_id=1, source_target_pairs={{0,4},{1,5},{2,6},{3,7},{4,0},{5,1},{6,2},{7,3},{8,12},{9,13},{10,... | collective-permute-start | bytes 811016 | tf_op jit(solution)/shard_map/ppermute | solution.py:340
  24.4 2.9 %collective-permute-done.4 = bf16[528,256]{1,0:T(8,128)(2,1)S(1)} collective-permute-done((bf16[528,256]{1,0:T(8,128)(2,1)S(1)}, bf16[528,256]{1,0:T(8,128)(2,1)S(1)}, u32[]{:S(2)}, u32[]{:S(2)}) %collective-permute-start.4) | collective-permute-done | bytes 270368 | tf_op jit(solution)/shard_map/ppermute | solution.py:340
  27.3 0.1 add_convert_fusion
  27.4 1.7 %collective-permute-start.6 = (bf16[528,256]{1,0:T(8,128)(2,1)S(1)}, bf16[528,256]{1,0:T(8,128)(2,1)S(1)}, u32[]{:S(2)}, u32[]{:S(2)}) collective-permute-start(bf16[528,256]{1,0:T(8,128)(2,1)S(1)} %add_convert_fusion), channel_id=1, source_target_pairs={{0,2},{1,3},{2,0},{3,1},{4,6},{5,7},{6,4},{7,5},{8,10},{9,11},{10,... | collective-permute-start | bytes 811016 | tf_op jit(solution)/shard_map/ppermute | solution.py:340
  29.1 1.5 %collective-permute-start.5 = (bf16[528,256]{1,0:T(8,128)(2,1)S(1)}, bf16[528,256]{1,0:T(8,128)(2,1)S(1)}, u32[]{:S(2)}, u32[]{:S(2)}) collective-permute-start(bf16[528,256]{1,0:T(8,128)(2,1)S(1)} %get-tuple-element.46), channel_id=1, source_target_pairs={{0,1},{1,0},{2,3},{3,2},{4,5},{5,4},{6,7},{7,6},{8,9},{9,8},{10,11... | collective-permute-start | bytes 811016 | tf_op jit(solution)/shard_map/ppermute | solution.py:340
  30.6 5.0 %collective-permute-done.3.other = bf16[528,256]{1,0:T(8,128)(2,1)S(1)} collective-permute-done((bf16[528,256]{1,0:T(8,128)(2,1)S(1)}, bf16[528,256]{1,0:T(8,128)(2,1)S(1)}, u32[]{:S(2)}, u32[]{:S(2)}) %collective-permute-start.3) | collective-permute-done | bytes 270368 | tf_op jit(solution)/shard_map/ppermute | solution.py:340
  35.7 3.2 %newton.1.folded.after = bf16[528,256]{1,0:T(8,128)(2,1)S(1)} custom-call(f32[1,256]{1,0:T(1,128)S(1)} %get-tuple-element.39.after.squares, bf16[528,256]{1,0:T(8,128)(2,1)S(1)} %add_convert_fusion.1.mine, bf16[528,256]{1,0:T(8,128)(2,1)S(1)} %collective-permute-done.3.other), custom_call_target="tpu_custom_call" | custom-call | flops 2147483648 | bytes 2097152 | tf_op jit(solution)/shard_map/newton/pallas_call | solution.py:183
  38.9 0.6 collective-permute-start.10
  39.5 0.6 collective-permute-start.9
  40.1 0.6 norm.1
  40.7 1.6 %collective-permute-start.7 = (f32[8,128]{1,0:T(8,128)S(1)}, f32[8,128]{1,0:T(8,128)S(1)}, u32[]{:S(2)}, u32[]{:S(2)}) collective-permute-start(f32[8,128]{1,0:T(8,128)S(1)} %norm.1), channel_id=1, source_target_pairs={{0,16},{1,17},{2,18},{3,19},{4,20},{5,21},{6,22},{7,23},{8,24},{9,... | collective-permute-start | bytes 12296 | tf_op jit(solution)/shard_map/ppermute | solution.py:340
  42.2 2.1 %collective-permute-done.7 = f32[8,128]{1,0:T(8,128)S(1)} collective-permute-done((f32[8,128]{1,0:T(8,128)S(1)}, f32[8,128]{1,0:T(8,128)S(1)}, u32[]{:S(2)}, u32[]{:S(2)}) %collective-permute-start.7) | collective-permute-done | bytes 4128 | tf_op jit(solution)/shard_map/ppermute | solution.py:340
  44.3 1.2 %collective-permute-done.8 = f32[8,128]{1,0:T(8,128)S(1)} collective-permute-done((f32[8,128]{1,0:T(8,128)S(1)}, f32[8,128]{1,0:T(8,128)S(1)}, u32[]{:S(2)}, u32[]{:S(2)}) %collective-permute-start.8) | collective-permute-done | bytes 4128 | tf_op jit(solution)/shard_map/ppermute | solution.py:340
  45.5 1.4 %collective-permute-start.11 = (f32[8,128]{1,0:T(8,128)S(1)}, f32[8,128]{1,0:T(8,128)S(1)}, u32[]{:S(2)}, u32[]{:S(2)}) collective-permute-start(f32[8,128]{1,0:T(8,128)S(1)} %add.37), channel_id=1, source_target_pairs={{0,2},{1,3},{2,0},{3,1},{4,6},{5,7},{6,4},{7,5},{8,10},{9,11},{10,... | collective-permute-start | bytes 12296 | tf_op jit(solution)/shard_map/ppermute | solution.py:340
  46.9 2.3 %multiply.3 = (bf16[512,3584]{1,0:T(8,128)(2,1)S(1)}, bf16[512,512]{1,0:T(8,128)(2,1)S(1)}) custom-call(bf16[528,256]{1,0:T(8,128)(2,1)S(1)} %newton.1.folded.after, bf16[528,256]{1,0:T(8,128)(2,1)S(1)} %newton.1.folded.after, bf16[512,3584]{1,0:T(8,128)(2,1)S(1)} %get-tuple-element.49.held_ref), custom_call_target="tpu_custom_call", output_to_operand_aliasing={{0}: (2, {})} | custom-call | flops 1880000000 | bytes 1 | tf_op jit(solution)/shard_map/multiply/pallas_call | solution.py:242
  49.3 1.6 %collective-permute-start.12 = (f32[8,128]{1,0:T(8,128)S(1)}, f32[8,128]{1,0:T(8,128)S(1)}, u32[]{:S(2)}, u32[]{:S(2)}) collective-permute-start(f32[8,128]{1,0:T(8,128)S(1)} %add.38), channel_id=1, source_target_pairs={{0,1},{1,0},{2,3},{3,2},{4,5},{5,4},{6,7},{7,6},{8,9},{9,8},{10,11... | collective-permute-start | bytes 12296 | tf_op jit(solution)/shard_map/ppermute | solution.py:340
  50.9 0.5 collective-permute-start.13
  51.4 2.5 %multiply.4 = (bf16[512,3584]{1,0:T(8,128)(2,1)S(1)}, bf16[512,512]{1,0:T(8,128)(2,1)S(1)}) custom-call(bf16[528,256]{1,0:T(8,128)(2,1)S(1)} %collective-permute-done.10.after.folded, bf16[528,256]{1,0:T(8,128)(2,1)S(1)} %collective-permute-done.10.after.folded, bf16[512,3584]{1,0:T(8,128)(2,1)S(1)} %get-tuple-element.55.held_ref), custom_call_target="tpu_custom_call", output_to_operand_aliasing={{0}: (2, {})} | custom-call | flops 1880000000 | bytes 1 | tf_op jit(solution)/shard_map/multiply/pallas_call | solution.py:242
  53.9 0.0 copy-start.1
  53.9 3.3 %collective-permute-start.14 = (f32[8,128]{1,0:T(8,128)S(1)}, f32[8,128]{1,0:T(8,128)S(1)}, u32[]{:S(2)}, u32[]{:S(2)}) collective-permute-start(f32[8,128]{1,0:T(8,128)S(1)} %add.39), channel_id=1, source_target_pairs={{0,4},{1,5},{2,6},{3,7},{4,0},{5,1},{6,2},{7,3},{8,12},{9,13},{10,... | collective-permute-start | bytes 12296 | tf_op jit(solution)/shard_map/ppermute | solution.py:340
  57.3 2.3 %multiply.5 = (bf16[512,3584]{1,0:T(8,128)(2,1)S(1)}, bf16[512,512]{1,0:T(8,128)(2,1)S(1)}) custom-call(bf16[528,256]{1,0:T(8,128)(2,1)S(1)} %collective-permute-done.9.after.folded, bf16[528,256]{1,0:T(8,128)(2,1)S(1)} %collective-permute-done.9.after.folded, bf16[512,3584]{1,0:T(8,128)(2,1)S(1)} %get-tuple-element.60.held_ref), custom_call_target="tpu_custom_call", output_to_operand_aliasing={{0}: (2, {})} | custom-call | flops 1880000000 | bytes 1 | tf_op jit(solution)/shard_map/multiply/pallas_call | solution.py:242
  59.6 7.7 %finish.1 = (bf16[2048,3584]{1,0:T(8,128)(2,1)}, bf16[2,512,512]{2,1,0:T(8,128)(2,1)}, bf16[512,3584]{1,0:T(8,128)(2,1)S(1)}, bf16[512,3584]{1,0:T(8,128)(2,1)S(...) custom-call(s32[6]{0:T(128)S(1)} %pad_add_fusion.order, ...), custom_call_target="tpu_custom_call", output_to_operand_aliasing={{2}: (7, {}), {3}: (8, {}), {4}: (9, {}), {5}: (10, {})} | custom-call | tf_op jit(solution)/shard_map/finish/pallas_call | solution.py:316
  (19 shorter events, 0.1 us)
Async XLA Ops:
  0.7 1.6 %copy-start = (bf16[512,2048]{1,0:T(8,128)(2,1)S(1)}, bf16[512,2048]{1,0:T(8,128)(2,1)}, u32[]{:S(2)}) copy-start(bf16[512,2048]{1,0:T(8,128)(2,1)} %x_ref.1) | copy-start | bytes 6291460
  3.9 17.6 %collective-permute-start = (bf16[528,256]{1,0:T(8,128)(2,1)S(1)}, bf16[528,256]{1,0:T(8,128)(2,1)S(1)}, u32[]{:S(2)}, u32[]{:S(2)}) collective-permute-start(bf16[528,256]{1,0:T(8,128)(2,1)S(1)} %get-tuple-element.40), channel_id=1, source_target_pairs={{0,1},{1,0},{2,3},{3,2},{4,5},{5,4},{6,7},{7,6},{8,9},{9,8},{10,11... | collective-permute-start | bytes 811016 | tf_op jit(solution)/shard_map/ppermute | solution.py:340
  6.9 14.6 %collective-permute-start.1 = (bf16[528,256]{1,0:T(8,128)(2,1)S(1)}, bf16[528,256]{1,0:T(8,128)(2,1)S(1)}, u32[]{:S(2)}, u32[]{:S(2)}) collective-permute-start(bf16[528,256]{1,0:T(8,128)(2,1)S(1)} %get-tuple-element.41), channel_id=1, source_target_pairs={{0,2},{1,3},{2,0},{3,1},{4,6},{5,7},{6,4},{7,5},{8,10},{9,11},{10,... | collective-permute-start | bytes 811016 | tf_op jit(solution)/shard_map/ppermute | solution.py:340
  8.5 13.0 %collective-permute-start.2 = (bf16[528,256]{1,0:T(8,128)(2,1)S(1)}, bf16[528,256]{1,0:T(8,128)(2,1)S(1)}, u32[]{:S(2)}, u32[]{:S(2)}) collective-permute-start(bf16[528,256]{1,0:T(8,128)(2,1)S(1)} %get-tuple-element.42), channel_id=1, source_target_pairs={{0,3},{1,2},{2,1},{3,0},{4,7},{5,6},{6,5},{7,4},{8,11},{9,10},{10,... | collective-permute-start | bytes 811016 | tf_op jit(solution)/shard_map/ppermute | solution.py:340
  19.6 7.7 %collective-permute-start.4 = (bf16[528,256]{1,0:T(8,128)(2,1)S(1)}, bf16[528,256]{1,0:T(8,128)(2,1)S(1)}, u32[]{:S(2)}, u32[]{:S(2)}) collective-permute-start(bf16[528,256]{1,0:T(8,128)(2,1)S(1)} %get-tuple-element.44), channel_id=1, source_target_pairs={{0,1},{1,0},{2,3},{3,2},{4,5},{5,4},{6,7},{7,6},{8,9},{9,8},{10,11... | collective-permute-start | bytes 811016 | tf_op jit(solution)/shard_map/ppermute | solution.py:340
  21.7 14.0 %collective-permute-start.3 = (bf16[528,256]{1,0:T(8,128)(2,1)S(1)}, bf16[528,256]{1,0:T(8,128)(2,1)S(1)}, u32[]{:S(2)}, u32[]{:S(2)}) collective-permute-start(bf16[528,256]{1,0:T(8,128)(2,1)S(1)} %add_convert_fusion.1.mine), channel_id=1, source_target_pairs={{0,4},{1,5},{2,6},{3,7},{4,0},{5,1},{6,2},{7,3},{8,12},{9,13},{10,... | collective-permute-start | bytes 811016 | tf_op jit(solution)/shard_map/ppermute | solution.py:340
  27.4 12.7 %collective-permute-start.6 = (bf16[528,256]{1,0:T(8,128)(2,1)S(1)}, bf16[528,256]{1,0:T(8,128)(2,1)S(1)}, u32[]{:S(2)}, u32[]{:S(2)}) collective-permute-start(bf16[528,256]{1,0:T(8,128)(2,1)S(1)} %add_convert_fusion), channel_id=1, source_target_pairs={{0,2},{1,3},{2,0},{3,1},{4,6},{5,7},{6,4},{7,5},{8,10},{9,11},{10,... | collective-permute-start | bytes 811016 | tf_op jit(solution)/shard_map/ppermute | solution.py:340
  29.1 11.0 %collective-permute-start.5 = (bf16[528,256]{1,0:T(8,128)(2,1)S(1)}, bf16[528,256]{1,0:T(8,128)(2,1)S(1)}, u32[]{:S(2)}, u32[]{:S(2)}) collective-permute-start(bf16[528,256]{1,0:T(8,128)(2,1)S(1)} %get-tuple-element.46), channel_id=1, source_target_pairs={{0,1},{1,0},{2,3},{3,2},{4,5},{5,4},{6,7},{7,6},{8,9},{9,8},{10,11... | collective-permute-start | bytes 811016 | tf_op jit(solution)/shard_map/ppermute | solution.py:340
  38.9 10.4 %collective-permute-start.10 = (bf16[528,256]{1,0:T(8,128)(2,1)S(1)}, bf16[528,256]{1,0:T(8,128)(2,1)S(1)}, u32[]{:S(2)}, u32[]{:S(2)}) collective-permute-start(bf16[528,256]{1,0:T(8,128)(2,1)S(1)} %newton.1.folded.after), channel_id=1, source_target_pairs={{0,1},{1,0},{2,3},{3,2},{4,5},{5,4},{6,7},{7,6},{8,9},{9,8},{10,11... | collective-permute-start | bytes 811016 | tf_op jit(solution)/shard_map/ppermute | solution.py:340
  39.5 9.8 %collective-permute-start.9 = (bf16[528,256]{1,0:T(8,128)(2,1)S(1)}, bf16[528,256]{1,0:T(8,128)(2,1)S(1)}, u32[]{:S(2)}, u32[]{:S(2)}) collective-permute-start(bf16[528,256]{1,0:T(8,128)(2,1)S(1)} %newton.1.folded.after), channel_id=1, source_target_pairs={{0,2},{1,3},{2,0},{3,1},{4,6},{5,7},{6,4},{7,5},{8,10},{9,11},{10,... | collective-permute-start | bytes 811016 | tf_op jit(solution)/shard_map/ppermute | solution.py:340
  40.7 3.7 %collective-permute-start.7 = (f32[8,128]{1,0:T(8,128)S(1)}, f32[8,128]{1,0:T(8,128)S(1)}, u32[]{:S(2)}, u32[]{:S(2)}) collective-permute-start(f32[8,128]{1,0:T(8,128)S(1)} %norm.1), channel_id=1, source_target_pairs={{0,16},{1,17},{2,18},{3,19},{4,20},{5,21},{6,22},{7,23},{8,24},{9,... | collective-permute-start | bytes 12296 | tf_op jit(solution)/shard_map/ppermute | solution.py:340
  44.3 1.2 %collective-permute-start.8 = (f32[8,128]{1,0:T(8,128)S(1)}, f32[8,128]{1,0:T(8,128)S(1)}, u32[]{:S(2)}, u32[]{:S(2)}) collective-permute-start(f32[8,128]{1,0:T(8,128)S(1)} %add.36), channel_id=1, source_target_pairs={{0,8},{1,9},{2,10},{3,11},{4,12},{5,13},{6,14},{7,15},{8,0},{9,1},... | collective-permute-start | bytes 12296 | tf_op jit(solution)/shard_map/ppermute | solution.py:340
  45.5 3.7 %collective-permute-start.11 = (f32[8,128]{1,0:T(8,128)S(1)}, f32[8,128]{1,0:T(8,128)S(1)}, u32[]{:S(2)}, u32[]{:S(2)}) collective-permute-start(f32[8,128]{1,0:T(8,128)S(1)} %add.37), channel_id=1, source_target_pairs={{0,2},{1,3},{2,0},{3,1},{4,6},{5,7},{6,4},{7,5},{8,10},{9,11},{10,... | collective-permute-start | bytes 12296 | tf_op jit(solution)/shard_map/ppermute | solution.py:340
  49.3 4.6 %collective-permute-start.12 = (f32[8,128]{1,0:T(8,128)S(1)}, f32[8,128]{1,0:T(8,128)S(1)}, u32[]{:S(2)}, u32[]{:S(2)}) collective-permute-start(f32[8,128]{1,0:T(8,128)S(1)} %add.38), channel_id=1, source_target_pairs={{0,1},{1,0},{2,3},{3,2},{4,5},{5,4},{6,7},{7,6},{8,9},{9,8},{10,11... | collective-permute-start | bytes 12296 | tf_op jit(solution)/shard_map/ppermute | solution.py:340
  50.9 8.8 %collective-permute-start.13 = (bf16[528,256]{1,0:T(8,128)(2,1)S(1)}, bf16[528,256]{1,0:T(8,128)(2,1)S(1)}, u32[]{:S(2)}, u32[]{:S(2)}) collective-permute-start(bf16[528,256]{1,0:T(8,128)(2,1)S(1)} %collective-permute-done.9.after.folded), channel_id=1, source_target_pairs={{0,1},{1,0},{2,3},{3,2},{4,5},{5,4},{6,7},{7,6},{8,9},{9,8},{10,11... | collective-permute-start | bytes 811016 | tf_op jit(solution)/shard_map/ppermute | solution.py:340
  53.9 5.7 %copy-start.1 = (s32[4,4]{1,0:T(4,128)S(1)}, s32[4,4]{1,0:T(4,128)}, u32[]{:S(2)}) copy-start(s32[4,4]{1,0:T(4,128)} %owner_slot.1) | copy-start | bytes 196
  53.9 5.7 %collective-permute-start.14 = (f32[8,128]{1,0:T(8,128)S(1)}, f32[8,128]{1,0:T(8,128)S(1)}, u32[]{:S(2)}, u32[]{:S(2)}) collective-permute-start(f32[8,128]{1,0:T(8,128)S(1)} %add.39), channel_id=1, source_target_pairs={{0,4},{1,5},{2,6},{3,7},{4,0},{5,1},{6,2},{7,3},{8,12},{9,13},{10,... | collective-permute-start | bytes 12296 | tf_op jit(solution)/shard_map/ppermute | solution.py:340

commit v16 on v15

--- a/solution.py
+++ b/solution.py
@@ -343,7 +343,8 @@
 def rounds():
     peer_bits = lax.axis_size("dp").bit_length() - 1
     bits = [1 << i for i in range(peer_bits + lax.axis_size("pool").bit_length() - 1)]
-    return bits[peer_bits:][::-1] + [bits[1], bits[0]] + bits[2:peer_bits]
+    first = [bits[2], bits[-1], bits[2] + bits[-1]] if peer_bits > 2 else [bits[-1]]
+    return [first] + [[bit] for bit in (bits[0], *bits[peer_bits:-1], bits[1], *bits[3:peer_bits])]
 
 
 def add(*values):
@@ -383,18 +384,18 @@
         roots.append(root)
 
     sums = norm(root, grams[0], from_y, from_z, squares)
-    early, arrivals = {2:[0],3:[1],4:[2]}, {2:[1,2],4:[3]}
-    for step, flip in enumerate(rounds()):
-        received = swap(sums, flip)
-        if step == 3:
+    early, arrivals = {0:[0],1:[1],3:[2]}, {0:[1,2],3:[3]}
+    for step, flips in enumerate(rounds()):
+        received = [swap(sums, flip) for flip in flips]
+        if step == 1:
             folded[2], _ = lax.optimization_barrier((folded[2], sums))
             folded.append(swap(folded[2], 1))
         for place in early.get(step, ()):
             precondition(place)
-            blocks[place], received = lax.optimization_barrier((blocks[place], received))
+            blocks[place], *received = lax.optimization_barrier((blocks[place], *received))
         for place in arrivals.get(step, ()):
-            folded[place], received = lax.optimization_barrier((folded[place], received))
-        sums = sums + received
+            folded[place], *received = lax.optimization_barrier((folded[place], *received))
+        sums = sums + sum(received)
     update, owned = finish(order, owner_slot, sums, roots, folded[EARLY:], blocks)
     return (update, owned[None])
 

time: 67.7 us -> 67.7 us (level)
    ppermute x15 -> x16, waiting for transfers between devices: 11.3 us -> 11.7 us  [swap(): return lax.ppermute(value, axes, [(i, i ^ flip) for i in range(count)])]
    ppermute x15 -> x16, starting transfers between devices: 22.1 us -> 21.8 us  [swap(): return lax.ppermute(value, axes, [(i, i ^ flip) for i in range(count)])]
  transfers between devices with their start and end apart: 15 -> 16, of which waited for: 4 -> 6; matrix products, arithmetic and copies ran while one was open for 0% -> 0% of each run, Pallas kernels for 32% -> 32%
where the time goes in v16:
time: 67.7 us; the launch traced here: 67.5 us
  Pallas kernels  31.2 us (46%)
  starting transfers between devices  21.8 us (32%)
  waiting for transfers between devices  11.7 us (17%)
  local copies, waits for them, and re-layouts  1.6 us (2%)
  between operations  0.92 us (1%)
    ppermute x16, starting transfers between devices, swap(): return lax.ppermute(value, axes, [(i, i ^ flip) for i in range(count)])  21.8 us
    ppermute x16, waiting for transfers between devices, swap(): return lax.ppermute(value, axes, [(i, i ^ flip) for i in range(count)])  11.7 us
    pallas_call x1, Pallas kernels, gram(): pl.pallas_call(gram_kernel, out_shape=[pltpu.VMEM((BLK, columns), BF16)]...  11 us
    pallas_call x1, Pallas kernels, finish(): pl.pallas_call(finish_kernel, out_shape=[jax.ShapeDtypeStruct((QUAD * BLK...  7.72 us
    pallas_call x3, Pallas kernels, multiply(): pl.pallas_call(multiply_kernel, out_shape=[pltpu.VMEM(held.shape, BF16),...  7.11 us
    pallas_call x1, Pallas kernels, newton(): pl.pallas_call(functools.partial(newton_kernel, tokens), out_shape=jax.Sh...  3.2 us
    unnamed x4, local copies, waits for them, and re-layouts  1.6 us
    pallas_call x1, Pallas kernels, statistics(): pl.pallas_call(stat_kernel, out_shape=[jax.ShapeDtypeStruct((FOLD, HALF),...  1.59 us
  transfers between devices with their start and end apart: 16, of which 6 were waited for; matrix products, arithmetic and copies ran while one was open for 0% of the time, Pallas kernels for 32%

profile of v16, /device:TPU:0, one launch (start us, length us, event | category | flops | bytes accessed | tf_op | source)
XLA Modules:
  0.0 67.5 jit_solution(1047440666942746020)
XLA Ops:
  0.7 0.1 pad_add_fusion.order
  0.7 1.6 %copy-done = bf16[512,2048]{1,0:T(8,128)(2,1)S(1)} copy-done((bf16[512,2048]{1,0:T(8,128)(2,1)S(1)}, bf16[512,2048]{1,0:T(8,128)(2,1)}, u32[]{:S(2)}) %copy-start) | copy-done | bytes 2097176
  2.3 1.6 %statistics.1 = (bf16[528,256]{1,0:T(8,128)(2,1)S(1)}, bf16[528,256]{1,0:T(8,128)(2,1)S(1)}, bf16[528,256]{1,0:T(8,128)(2,1)S(1)}, bf16[528,256]{1,0:T(8,128)(2,1)S(1)}) custom-call(s32[6]{0:T(128)S(1)} %pad_add_fusion.order, bf16[512,2048]{1,0:T(8,128)(2,1)S(1)} %copy-done), custom_call_target="tpu_custom_call" | custom-call | tf_op jit(solution)/shard_map/statistics/pallas_call | solution.py:72
  3.9 3.0 %collective-permute-start = (bf16[528,256]{1,0:T(8,128)(2,1)S(1)}, bf16[528,256]{1,0:T(8,128)(2,1)S(1)}, u32[]{:S(2)}, u32[]{:S(2)}) collective-permute-start(bf16[528,256]{1,0:T(8,128)(2,1)S(1)} %get-tuple-element.46), channel_id=1, source_target_pairs={{0,1},{1,0},{2,3},{3,2},{4,5},{5,4},{6,7},{7,6},{8,9},{9,8},{10,11... | collective-permute-start | bytes 811016 | tf_op jit(solution)/shard_map/ppermute | solution.py:340
  6.9 1.6 %collective-permute-start.1 = (bf16[528,256]{1,0:T(8,128)(2,1)S(1)}, bf16[528,256]{1,0:T(8,128)(2,1)S(1)}, u32[]{:S(2)}, u32[]{:S(2)}) collective-permute-start(bf16[528,256]{1,0:T(8,128)(2,1)S(1)} %get-tuple-element.47), channel_id=1, source_target_pairs={{0,2},{1,3},{2,0},{3,1},{4,6},{5,7},{6,4},{7,5},{8,10},{9,11},{10,... | collective-permute-start | bytes 811016 | tf_op jit(solution)/shard_map/ppermute | solution.py:340
  8.5 11.0 %gram.1 = (bf16[512,3584]{1,0:T(8,128)(2,1)S(1)}, bf16[512,3584]{1,0:T(8,128)(2,1)S(1)}, bf16[512,3584]{1,0:T(8,128)(2,1)S(1)}, bf16[512,3584]{1,0:T(8,128)(2,1)...) custom-call(s32[6]{0:T(128)S(1)} %pad_add_fusion.order, ...), custom_call_target="tpu_custom_call" | custom-call | flops 7516192768 | bytes 14680064 | tf_op jit(solution)/shard_map/gram/pallas_call | solution.py:124
  19.6 2.0 %collective-permute-start.4 = (bf16[528,256]{1,0:T(8,128)(2,1)S(1)}, bf16[528,256]{1,0:T(8,128)(2,1)S(1)}, u32[]{:S(2)}, u32[]{:S(2)}) collective-permute-start(bf16[528,256]{1,0:T(8,128)(2,1)S(1)} %get-tuple-element.50), channel_id=1, source_target_pairs={{0,1},{1,0},{2,3},{3,2},{4,5},{5,4},{6,7},{7,6},{8,9},{9,8},{10,11... | collective-permute-start | bytes 811016 | tf_op jit(solution)/shard_map/ppermute | solution.py:340
  21.6 0.1 add_convert_fusion.1.mine
  21.7 2.7 %collective-permute-start.3 = (bf16[528,256]{1,0:T(8,128)(2,1)S(1)}, bf16[528,256]{1,0:T(8,128)(2,1)S(1)}, u32[]{:S(2)}, u32[]{:S(2)}) collective-permute-start(bf16[528,256]{1,0:T(8,128)(2,1)S(1)} %add_convert_fusion.1.mine), channel_id=1, source_target_pairs={{0,4},{1,5},{2,6},{3,7},{4,0},{5,1},{6,2},{7,3},{8,12},{9,13},{10,... | collective-permute-start | bytes 811016 | tf_op jit(solution)/shard_map/ppermute | solution.py:340
  24.4 2.9 %collective-permute-done.4 = bf16[528,256]{1,0:T(8,128)(2,1)S(1)} collective-permute-done((bf16[528,256]{1,0:T(8,128)(2,1)S(1)}, bf16[528,256]{1,0:T(8,128)(2,1)S(1)}, u32[]{:S(2)}, u32[]{:S(2)}) %collective-permute-start.4) | collective-permute-done | bytes 270368 | tf_op jit(solution)/shard_map/ppermute | solution.py:340
  27.4 1.7 %collective-permute-start.6 = (bf16[528,256]{1,0:T(8,128)(2,1)S(1)}, bf16[528,256]{1,0:T(8,128)(2,1)S(1)}, u32[]{:S(2)}, u32[]{:S(2)}) collective-permute-start(bf16[528,256]{1,0:T(8,128)(2,1)S(1)} %add_convert_fusion), channel_id=1, source_target_pairs={{0,2},{1,3},{2,0},{3,1},{4,6},{5,7},{6,4},{7,5},{8,10},{9,11},{10,... | collective-permute-start | bytes 811016 | tf_op jit(solution)/shard_map/ppermute | solution.py:340
  29.1 1.5 %collective-permute-start.5 = (bf16[528,256]{1,0:T(8,128)(2,1)S(1)}, bf16[528,256]{1,0:T(8,128)(2,1)S(1)}, u32[]{:S(2)}, u32[]{:S(2)}) collective-permute-start(bf16[528,256]{1,0:T(8,128)(2,1)S(1)} %get-tuple-element.52), channel_id=1, source_target_pairs={{0,1},{1,0},{2,3},{3,2},{4,5},{5,4},{6,7},{7,6},{8,9},{9,8},{10,11... | collective-permute-start | bytes 811016 | tf_op jit(solution)/shard_map/ppermute | solution.py:340
  30.6 5.0 %collective-permute-done.3.other = bf16[528,256]{1,0:T(8,128)(2,1)S(1)} collective-permute-done((bf16[528,256]{1,0:T(8,128)(2,1)S(1)}, bf16[528,256]{1,0:T(8,128)(2,1)S(1)}, u32[]{:S(2)}, u32[]{:S(2)}) %collective-permute-start.3) | collective-permute-done | bytes 270368 | tf_op jit(solution)/shard_map/ppermute | solution.py:340
  35.7 3.2 %newton.1.folded.after = bf16[528,256]{1,0:T(8,128)(2,1)S(1)} custom-call(f32[1,256]{1,0:T(1,128)S(1)} %get-tuple-element.45.after.squares, bf16[528,256]{1,0:T(8,128)(2,1)S(1)} %add_convert_fusion.1.mine, bf16[528,256]{1,0:T(8,128)(2,1)S(1)} %collective-permute-done.3.other), custom_call_target="tpu_custom_call" | custom-call | flops 2147483648 | bytes 2097152 | tf_op jit(solution)/shard_map/newton/pallas_call | solution.py:183
  38.9 0.6 collective-permute-start.8
  39.5 0.6 collective-permute-start.7
  40.1 0.6 norm.1
  40.7 4.4 %collective-permute-start.11 = (f32[8,128]{1,0:T(8,128)S(1)}, f32[8,128]{1,0:T(8,128)S(1)}, u32[]{:S(2)}, u32[]{:S(2)}) collective-permute-start(f32[8,128]{1,0:T(8,128)S(1)} %norm.1), channel_id=1, source_target_pairs={{0,20},{1,21},{2,22},{3,23},{4,16},{5,17},{6,18},{7,19},{8,28},{9,... | collective-permute-start | bytes 12296 | tf_op jit(solution)/shard_map/ppermute | solution.py:340
  45.1 0.5 collective-permute-start.10
  45.6 0.1 collective-permute-start.9
  45.7 2.3 %multiply.3 = (bf16[512,3584]{1,0:T(8,128)(2,1)S(1)}, bf16[512,512]{1,0:T(8,128)(2,1)S(1)}) custom-call(bf16[528,256]{1,0:T(8,128)(2,1)S(1)} %newton.1.folded.after, bf16[528,256]{1,0:T(8,128)(2,1)S(1)} %newton.1.folded.after, bf16[512,3584]{1,0:T(8,128)(2,1)S(1)} %get-tuple-element.55.held_ref), custom_call_target="tpu_custom_call", output_to_operand_aliasing={{0}: (2, {})} | custom-call | flops 1880000000 | bytes 1 | tf_op jit(solution)/shard_map/multiply/pallas_call | solution.py:242
  48.1 0.6 collective-permute-done.10
  48.7 1.4 %collective-permute-done.9 = f32[8,128]{1,0:T(8,128)S(1)} collective-permute-done((f32[8,128]{1,0:T(8,128)S(1)}, f32[8,128]{1,0:T(8,128)S(1)}, u32[]{:S(2)}, u32[]{:S(2)}) %collective-permute-start.9) | collective-permute-done | bytes 4128 | tf_op jit(solution)/shard_map/ppermute | solution.py:340
  50.1 1.6 %collective-permute-start.12 = (f32[8,128]{1,0:T(8,128)S(1)}, f32[8,128]{1,0:T(8,128)S(1)}, u32[]{:S(2)}, u32[]{:S(2)}) collective-permute-start(f32[8,128]{1,0:T(8,128)S(1)} %add_add_fusion), channel_id=1, source_target_pairs={{0,1},{1,0},{2,3},{3,2},{4,5},{5,4},{6,7},{7,6},{8,9},{9,8},{10,11... | collective-permute-start | bytes 12296 | tf_op jit(solution)/shard_map/ppermute | solution.py:340
  51.7 0.5 collective-permute-start.14
  52.2 2.5 %multiply.4 = (bf16[512,3584]{1,0:T(8,128)(2,1)S(1)}, bf16[512,512]{1,0:T(8,128)(2,1)S(1)}) custom-call(bf16[528,256]{1,0:T(8,128)(2,1)S(1)} %collective-permute-done.8.after.folded, bf16[528,256]{1,0:T(8,128)(2,1)S(1)} %collective-permute-done.8.after.folded, bf16[512,3584]{1,0:T(8,128)(2,1)S(1)} %get-tuple-element.67.held_ref), custom_call_target="tpu_custom_call", output_to_operand_aliasing={{0}: (2, {})} | custom-call | flops 1880000000 | bytes 1 | tf_op jit(solution)/shard_map/multiply/pallas_call | solution.py:242
  54.8 0.1 collective-permute-start.13
  54.8 1.2 %collective-permute-done.13 = f32[8,128]{1,0:T(8,128)S(1)} collective-permute-done((f32[8,128]{1,0:T(8,128)S(1)}, f32[8,128]{1,0:T(8,128)S(1)}, u32[]{:S(2)}, u32[]{:S(2)}) %collective-permute-start.13) | collective-permute-done | bytes 4128 | tf_op jit(solution)/shard_map/ppermute | solution.py:340
  56.0 0.8 %collective-permute-start.15 = (f32[8,128]{1,0:T(8,128)S(1)}, f32[8,128]{1,0:T(8,128)S(1)}, u32[]{:S(2)}, u32[]{:S(2)}) collective-permute-start(f32[8,128]{1,0:T(8,128)S(1)} %add.43), channel_id=1, source_target_pairs={{0,2},{1,3},{2,0},{3,1},{4,6},{5,7},{6,4},{7,5},{8,10},{9,11},{10,... | collective-permute-start | bytes 12296 | tf_op jit(solution)/shard_map/ppermute | solution.py:340
  56.8 2.3 %multiply.5 = (bf16[512,3584]{1,0:T(8,128)(2,1)S(1)}, bf16[512,512]{1,0:T(8,128)(2,1)S(1)}) custom-call(bf16[528,256]{1,0:T(8,128)(2,1)S(1)} %collective-permute-done.7.after.folded, bf16[528,256]{1,0:T(8,128)(2,1)S(1)} %collective-permute-done.7.after.folded, bf16[512,3584]{1,0:T(8,128)(2,1)S(1)} %get-tuple-element.72.held_ref), custom_call_target="tpu_custom_call", output_to_operand_aliasing={{0}: (2, {})} | custom-call | flops 1880000000 | bytes 1 | tf_op jit(solution)/shard_map/multiply/pallas_call | solution.py:242
  59.1 0.5 collective-permute-done.15
  59.6 7.7 %finish.1 = (bf16[2048,3584]{1,0:T(8,128)(2,1)}, bf16[2,512,512]{2,1,0:T(8,128)(2,1)}, bf16[512,3584]{1,0:T(8,128)(2,1)S(1)}, bf16[512,3584]{1,0:T(8,128)(2,1)S(...) custom-call(s32[6]{0:T(128)S(1)} %pad_add_fusion.order, ...), custom_call_target="tpu_custom_call", output_to_operand_aliasing={{2}: (7, {}), {3}: (8, {}), {4}: (9, {}), {5}: (10, {})} | custom-call | tf_op jit(solution)/shard_map/finish/pallas_call | solution.py:316
  (20 shorter events, 0.1 us)
Async XLA Ops:
  0.7 1.6 %copy-start = (bf16[512,2048]{1,0:T(8,128)(2,1)S(1)}, bf16[512,2048]{1,0:T(8,128)(2,1)}, u32[]{:S(2)}) copy-start(bf16[512,2048]{1,0:T(8,128)(2,1)} %x_ref.1) | copy-start | bytes 6291460
  3.9 17.6 %collective-permute-start = (bf16[528,256]{1,0:T(8,128)(2,1)S(1)}, bf16[528,256]{1,0:T(8,128)(2,1)S(1)}, u32[]{:S(2)}, u32[]{:S(2)}) collective-permute-start(bf16[528,256]{1,0:T(8,128)(2,1)S(1)} %get-tuple-element.46), channel_id=1, source_target_pairs={{0,1},{1,0},{2,3},{3,2},{4,5},{5,4},{6,7},{7,6},{8,9},{9,8},{10,11... | collective-permute-start | bytes 811016 | tf_op jit(solution)/shard_map/ppermute | solution.py:340
  6.9 14.6 %collective-permute-start.1 = (bf16[528,256]{1,0:T(8,128)(2,1)S(1)}, bf16[528,256]{1,0:T(8,128)(2,1)S(1)}, u32[]{:S(2)}, u32[]{:S(2)}) collective-permute-start(bf16[528,256]{1,0:T(8,128)(2,1)S(1)} %get-tuple-element.47), channel_id=1, source_target_pairs={{0,2},{1,3},{2,0},{3,1},{4,6},{5,7},{6,4},{7,5},{8,10},{9,11},{10,... | collective-permute-start | bytes 811016 | tf_op jit(solution)/shard_map/ppermute | solution.py:340
  8.5 13.0 %collective-permute-start.2 = (bf16[528,256]{1,0:T(8,128)(2,1)S(1)}, bf16[528,256]{1,0:T(8,128)(2,1)S(1)}, u32[]{:S(2)}, u32[]{:S(2)}) collective-permute-start(bf16[528,256]{1,0:T(8,128)(2,1)S(1)} %get-tuple-element.48), channel_id=1, source_target_pairs={{0,3},{1,2},{2,1},{3,0},{4,7},{5,6},{6,5},{7,4},{8,11},{9,10},{10,... | collective-permute-start | bytes 811016 | tf_op jit(solution)/shard_map/ppermute | solution.py:340
  19.6 7.7 %collective-permute-start.4 = (bf16[528,256]{1,0:T(8,128)(2,1)S(1)}, bf16[528,256]{1,0:T(8,128)(2,1)S(1)}, u32[]{:S(2)}, u32[]{:S(2)}) collective-permute-start(bf16[528,256]{1,0:T(8,128)(2,1)S(1)} %get-tuple-element.50), channel_id=1, source_target_pairs={{0,1},{1,0},{2,3},{3,2},{4,5},{5,4},{6,7},{7,6},{8,9},{9,8},{10,11... | collective-permute-start | bytes 811016 | tf_op jit(solution)/shard_map/ppermute | solution.py:340
  21.7 14.0 %collective-permute-start.3 = (bf16[528,256]{1,0:T(8,128)(2,1)S(1)}, bf16[528,256]{1,0:T(8,128)(2,1)S(1)}, u32[]{:S(2)}, u32[]{:S(2)}) collective-permute-start(bf16[528,256]{1,0:T(8,128)(2,1)S(1)} %add_convert_fusion.1.mine), channel_id=1, source_target_pairs={{0,4},{1,5},{2,6},{3,7},{4,0},{5,1},{6,2},{7,3},{8,12},{9,13},{10,... | collective-permute-start | bytes 811016 | tf_op jit(solution)/shard_map/ppermute | solution.py:340
  27.4 12.7 %collective-permute-start.6 = (bf16[528,256]{1,0:T(8,128)(2,1)S(1)}, bf16[528,256]{1,0:T(8,128)(2,1)S(1)}, u32[]{:S(2)}, u32[]{:S(2)}) collective-permute-start(bf16[528,256]{1,0:T(8,128)(2,1)S(1)} %add_convert_fusion), channel_id=1, source_target_pairs={{0,2},{1,3},{2,0},{3,1},{4,6},{5,7},{6,4},{7,5},{8,10},{9,11},{10,... | collective-permute-start | bytes 811016 | tf_op jit(solution)/shard_map/ppermute | solution.py:340
  29.1 11.0 %collective-permute-start.5 = (bf16[528,256]{1,0:T(8,128)(2,1)S(1)}, bf16[528,256]{1,0:T(8,128)(2,1)S(1)}, u32[]{:S(2)}, u32[]{:S(2)}) collective-permute-start(bf16[528,256]{1,0:T(8,128)(2,1)S(1)} %get-tuple-element.52), channel_id=1, source_target_pairs={{0,1},{1,0},{2,3},{3,2},{4,5},{5,4},{6,7},{7,6},{8,9},{9,8},{10,11... | collective-permute-start | bytes 811016 | tf_op jit(solution)/shard_map/ppermute | solution.py:340
  38.9 11.3 %collective-permute-start.8 = (bf16[528,256]{1,0:T(8,128)(2,1)S(1)}, bf16[528,256]{1,0:T(8,128)(2,1)S(1)}, u32[]{:S(2)}, u32[]{:S(2)}) collective-permute-start(bf16[528,256]{1,0:T(8,128)(2,1)S(1)} %newton.1.folded.after), channel_id=1, source_target_pairs={{0,1},{1,0},{2,3},{3,2},{4,5},{5,4},{6,7},{7,6},{8,9},{9,8},{10,11... | collective-permute-start | bytes 811016 | tf_op jit(solution)/shard_map/ppermute | solution.py:340
  39.5 10.7 %collective-permute-start.7 = (bf16[528,256]{1,0:T(8,128)(2,1)S(1)}, bf16[528,256]{1,0:T(8,128)(2,1)S(1)}, u32[]{:S(2)}, u32[]{:S(2)}) collective-permute-start(bf16[528,256]{1,0:T(8,128)(2,1)S(1)} %newton.1.folded.after), channel_id=1, source_target_pairs={{0,2},{1,3},{2,0},{3,1},{4,6},{5,7},{6,4},{7,5},{8,10},{9,11},{10,... | collective-permute-start | bytes 811016 | tf_op jit(solution)/shard_map/ppermute | solution.py:340
  40.7 7.4 %collective-permute-start.11 = (f32[8,128]{1,0:T(8,128)S(1)}, f32[8,128]{1,0:T(8,128)S(1)}, u32[]{:S(2)}, u32[]{:S(2)}) collective-permute-start(f32[8,128]{1,0:T(8,128)S(1)} %norm.1), channel_id=1, source_target_pairs={{0,20},{1,21},{2,22},{3,23},{4,16},{5,17},{6,18},{7,19},{8,28},{9,... | collective-permute-start | bytes 12296 | tf_op jit(solution)/shard_map/ppermute | solution.py:340
  45.1 3.6 %collective-permute-start.10 = (f32[8,128]{1,0:T(8,128)S(1)}, f32[8,128]{1,0:T(8,128)S(1)}, u32[]{:S(2)}, u32[]{:S(2)}) collective-permute-start(f32[8,128]{1,0:T(8,128)S(1)} %norm.1), channel_id=1, source_target_pairs={{0,16},{1,17},{2,18},{3,19},{4,20},{5,21},{6,22},{7,23},{8,24},{9,... | collective-permute-start | bytes 12296 | tf_op jit(solution)/shard_map/ppermute | solution.py:340
  45.6 4.5 %collective-permute-start.9 = (f32[8,128]{1,0:T(8,128)S(1)}, f32[8,128]{1,0:T(8,128)S(1)}, u32[]{:S(2)}, u32[]{:S(2)}) collective-permute-start(f32[8,128]{1,0:T(8,128)S(1)} %norm.1), channel_id=1, source_target_pairs={{0,4},{1,5},{2,6},{3,7},{4,0},{5,1},{6,2},{7,3},{8,12},{9,13},{10,... | collective-permute-start | bytes 12296 | tf_op jit(solution)/shard_map/ppermute | solution.py:340
  50.1 4.6 %collective-permute-start.12 = (f32[8,128]{1,0:T(8,128)S(1)}, f32[8,128]{1,0:T(8,128)S(1)}, u32[]{:S(2)}, u32[]{:S(2)}) collective-permute-start(f32[8,128]{1,0:T(8,128)S(1)} %add_add_fusion), channel_id=1, source_target_pairs={{0,1},{1,0},{2,3},{3,2},{4,5},{5,4},{6,7},{7,6},{8,9},{9,8},{10,11... | collective-permute-start | bytes 12296 | tf_op jit(solution)/shard_map/ppermute | solution.py:340
  51.7 7.9 %collective-permute-start.14 = (bf16[528,256]{1,0:T(8,128)(2,1)S(1)}, bf16[528,256]{1,0:T(8,128)(2,1)S(1)}, u32[]{:S(2)}, u32[]{:S(2)}) collective-permute-start(bf16[528,256]{1,0:T(8,128)(2,1)S(1)} %collective-permute-done.7.after.folded), channel_id=1, source_target_pairs={{0,1},{1,0},{2,3},{3,2},{4,5},{5,4},{6,7},{7,6},{8,9},{9,8},{10,11... | collective-permute-start | bytes 811016 | tf_op jit(solution)/shard_map/ppermute | solution.py:340
  54.7 4.9 %copy-start.1 = (s32[4,4]{1,0:T(4,128)S(1)}, s32[4,4]{1,0:T(4,128)}, u32[]{:S(2)}) copy-start(s32[4,4]{1,0:T(4,128)} %owner_slot.1) | copy-start | bytes 196
  54.8 1.2 %collective-permute-start.13 = (f32[8,128]{1,0:T(8,128)S(1)}, f32[8,128]{1,0:T(8,128)S(1)}, u32[]{:S(2)}, u32[]{:S(2)}) collective-permute-start(f32[8,128]{1,0:T(8,128)S(1)} %add.42), channel_id=1, source_target_pairs={{0,8},{1,9},{2,10},{3,11},{4,12},{5,13},{6,14},{7,15},{8,0},{9,1},... | collective-permute-start | bytes 12296 | tf_op jit(solution)/shard_map/ppermute | solution.py:340
  56.0 3.6 %collective-permute-start.15 = (f32[8,128]{1,0:T(8,128)S(1)}, f32[8,128]{1,0:T(8,128)S(1)}, u32[]{:S(2)}, u32[]{:S(2)}) collective-permute-start(f32[8,128]{1,0:T(8,128)S(1)} %add.43), channel_id=1, source_target_pairs={{0,2},{1,3},{2,0},{3,1},{4,6},{5,7},{6,4},{7,5},{8,10},{9,11},{10,... | collective-permute-start | bytes 12296 | tf_op jit(solution)/shard_map/ppermute | solution.py:340

commit v17 on v16

--- a/solution.py
+++ b/solution.py
@@ -87,23 +87,24 @@
     yield pl.ds(start, width - start)
 
 
-def gram_kernel(order, after, g_ref, *refs):
-    held, folded = refs[:QUAD], refs[QUAD : 2 * QUAD]
-    norm_ref, left, last, arrived = refs[2 * QUAD :]
+def gram_kernel(places_held, order, after, g_ref, *refs):
+    count = len(places_held)
+    held, folded = refs[:count], refs[count : 2 * count]
+    norm_ref, left, last, arrived = refs[2 * count :]
     parts = list(chunks(g_ref.shape[1], 1792))
 
     def copy(place, index):
-        rows = pl.ds(pl.multiple_of(order[place] * BLK, BLK), BLK)
+        rows = pl.ds(pl.multiple_of(order[places_held[place]] * BLK, BLK), BLK)
         return pltpu.make_async_copy(
             g_ref.at[rows, parts[index]], held[place].at[:, parts[index]], arrived.at[place, index]
         )
 
-    for place in range(QUAD):
+    for place in range(count):
         for index in range(len(parts)):
             copy(place, index).start()
     norm_ref[...] = jnp.zeros_like(norm_ref)
     row, col = places()
-    for place in range(QUAD):
+    for place in range(count):
         for index in range(len(parts)):
             copy(place, index).wait()
         whole = held[place][...]
@@ -118,20 +119,21 @@
         folded[place][BLK:] = diagonal.astype(BF16)
 
 
-def gram(order, gradient, after):
-    rows, columns = gradient.shape
+def gram(places_held, order, gradient, after):
+    count, columns = len(places_held), gradient.shape[1]
+    rows = count * BLK
     parts = len(list(chunks(columns, 1792)))
     results = pl.pallas_call(
-        gram_kernel,
-        out_shape=[pltpu.VMEM((BLK, columns), BF16)] * QUAD
-        + [jax.ShapeDtypeStruct((FOLD, HALF), BF16)] * QUAD
+        functools.partial(gram_kernel, places_held),
+        out_shape=[pltpu.VMEM((BLK, columns), BF16)] * count
+        + [jax.ShapeDtypeStruct((FOLD, HALF), BF16)] * count
         + [jax.ShapeDtypeStruct((1, HALF), F32)],
         in_specs=[SMEM, ANY, ANY],
-        out_specs=[VMEM] * (2 * QUAD + 1),
+        out_specs=[VMEM] * (2 * count + 1),
         scratch_shapes=[
             pltpu.VMEM((BLK, HALF), F32),
             pltpu.VMEM((HALF, HALF), F32),
-            pltpu.SemaphoreType.DMA((QUAD, parts)),
+            pltpu.SemaphoreType.DMA((count, parts)),
         ],
         compiler_params=params(12),
         cost_estimate=pl.CostEstimate(
@@ -139,7 +141,7 @@
         ),
         name="gram",
     )(order, after, pltpu.with_memory_space_constraint(gradient, pltpu.HBM))
-    return results[:QUAD], results[QUAD : 2 * QUAD], results[-1]
+    return list(results[:count]), list(results[count : 2 * count]), results[-1]
 
 
 def product(left, right):
@@ -361,11 +363,12 @@
 
     a, b, c, d = statistics(order, activations)
     b, c, d = swap(b, 1), swap(c, 2), swap(d, 3)
-    blocks, grams, squares = gram(order, gradient, a)
+    blocks, grams, squares = gram((1, 2, 3), order, gradient, a)
     mine = add(a, b, c, d)
+    own, own_gram, own_squares = gram((0,), order, gradient, mine)
+    blocks, grams = own + blocks, own_gram + grams
     flip = QUAD
     other = swap(mine, flip)
-    grams = list(grams)
     while 2 * flip < peer_count:
         mine = add(mine, other)
         flip *= 2
@@ -375,7 +378,7 @@
     across, grams[1] = lax.optimization_barrier((across, grams[1]))
     from_y = swap(grams[1], 1)
     from_z = swap(add(grams[2], across), 2)
-    root = newton(tokens_all, squares, mine, other)
+    root = newton(tokens_all, own_squares, mine, other)
     folded = [root, swap(root, 1), swap(root, 2)]
     blocks, roots = list(blocks), []
 
@@ -383,7 +386,7 @@
         blocks[place], root = multiply(folded[place], blocks[place], folded[place])
         roots.append(root)
 
-    sums = norm(root, grams[0], from_y, from_z, squares)
+    sums = norm(root, grams[0], from_y, from_z, squares + own_squares)
     early, arrivals = {0:[0],1:[1],3:[2]}, {0:[1,2],3:[3]}
     for step, flips in enumerate(rounds()):
         received = [swap(sums, flip) for flip in flips]

time: 67.7 us -> 67.7 us (level)
  waiting for transfers between devices: 11.7 us -> 8.88 us
  Pallas kernels: 31.2 us -> 32.9 us
  starting transfers between devices: 21.8 us -> 22.8 us
    ppermute x16, waiting for transfers between devices: 11.7 us -> 8.88 us  [swap(): return lax.ppermute(value, axes, [(i, i ^ flip) for i in range(count)])]
    pallas_call x1 -> x2, Pallas kernels: 11 us -> 12.7 us  [gram(): pl.pallas_call(functools.partial(gram_kernel, places_held), out_shape=[pl...]
    ppermute x16, starting transfers between devices: 21.8 us -> 22.8 us  [swap(): return lax.ppermute(value, axes, [(i, i ^ flip) for i in range(count)])]
  transfers between devices with their start and end apart: 16 -> 16, of which waited for: 6 -> 7; matrix products, arithmetic and copies ran while one was open for 0% -> 0% of each run, Pallas kernels for 32% -> 35%
where the time goes in v17:
time: 67.7 us; the launch traced here: 67.5 us
  Pallas kernels  32.9 us (49%)
  starting transfers between devices  22.8 us (34%)
  waiting for transfers between devices  8.88 us (13%)
  local copies, waits for them, and re-layouts  1.6 us (2%)
  between operations  0.93 us (1%)
    ppermute x16, starting transfers between devices, swap(): return lax.ppermute(value, axes, [(i, i ^ flip) for i in range(count)])  22.8 us
    pallas_call x2, Pallas kernels, gram(): pl.pallas_call(functools.partial(gram_kernel, places_held), out_shape=[pl...  12.7 us
    ppermute x16, waiting for transfers between devices, swap(): return lax.ppermute(value, axes, [(i, i ^ flip) for i in range(count)])  8.88 us
    pallas_call x1, Pallas kernels, finish(): pl.pallas_call(finish_kernel, out_shape=[jax.ShapeDtypeStruct((QUAD * BLK...  7.69 us
    pallas_call x3, Pallas kernels, multiply(): pl.pallas_call(multiply_kernel, out_shape=[pltpu.VMEM(held.shape, BF16),...  7.13 us
    pallas_call x1, Pallas kernels, newton(): pl.pallas_call(functools.partial(newton_kernel, tokens), out_shape=jax.Sh...  3.2 us
    unnamed x4, local copies, waits for them, and re-layouts  1.6 us
    pallas_call x1, Pallas kernels, statistics(): pl.pallas_call(stat_kernel, out_shape=[jax.ShapeDtypeStruct((FOLD, HALF),...  1.59 us
  transfers between devices with their start and end apart: 16, of which 7 were waited for; matrix products, arithmetic and copies ran while one was open for 0% of the time, Pallas kernels for 35%

profile of v17, /device:TPU:0, one launch (start us, length us, event | category | flops | bytes accessed | tf_op | source)
XLA Modules:
  0.0 67.5 jit_solution(8309449938879569444)
XLA Ops:
  0.7 1.6 %copy-done = bf16[512,2048]{1,0:T(8,128)(2,1)S(1)} copy-done((bf16[512,2048]{1,0:T(8,128)(2,1)S(1)}, bf16[512,2048]{1,0:T(8,128)(2,1)}, u32[]{:S(2)}) %copy-start) | copy-done | bytes 2097176
  2.3 1.6 %statistics.1 = (bf16[528,256]{1,0:T(8,128)(2,1)S(1)}, bf16[528,256]{1,0:T(8,128)(2,1)S(1)}, bf16[528,256]{1,0:T(8,128)(2,1)S(1)}, bf16[528,256]{1,0:T(8,128)(2,1)S(1)}) custom-call(s32[6]{0:T(128)S(1)} %pad_add_fusion.order, bf16[512,2048]{1,0:T(8,128)(2,1)S(1)} %copy-done), custom_call_target="tpu_custom_call" | custom-call | tf_op jit(solution)/shard_map/statistics/pallas_call | solution.py:72
  3.9 3.0 %collective-permute-start = (bf16[528,256]{1,0:T(8,128)(2,1)S(1)}, bf16[528,256]{1,0:T(8,128)(2,1)S(1)}, u32[]{:S(2)}, u32[]{:S(2)}) collective-permute-start(bf16[528,256]{1,0:T(8,128)(2,1)S(1)} %get-tuple-element.46), channel_id=1, source_target_pairs={{0,1},{1,0},{2,3},{3,2},{4,5},{5,4},{6,7},{7,6},{8,9},{9,8},{10,11... | collective-permute-start | bytes 811016 | tf_op jit(solution)/shard_map/ppermute | solution.py:342
  6.9 1.6 %collective-permute-start.1 = (bf16[528,256]{1,0:T(8,128)(2,1)S(1)}, bf16[528,256]{1,0:T(8,128)(2,1)S(1)}, u32[]{:S(2)}, u32[]{:S(2)}) collective-permute-start(bf16[528,256]{1,0:T(8,128)(2,1)S(1)} %get-tuple-element.47), channel_id=1, source_target_pairs={{0,2},{1,3},{2,0},{3,1},{4,6},{5,7},{6,4},{7,5},{8,10},{9,11},{10,... | collective-permute-start | bytes 811016 | tf_op jit(solution)/shard_map/ppermute | solution.py:342
  8.5 8.5 %gram.3 = (bf16[512,3584]{1,0:T(8,128)(2,1)S(1)}, bf16[512,3584]{1,0:T(8,128)(2,1)S(1)}, bf16[512,3584]{1,0:T(8,128)(2,1)S(1)}, bf16[528,256]{1,0:T(8,128)(2,1)S...) custom-call(s32[6]{0:T(128)S(1)} %pad_add_fusion.order, ...), custom_call_target="tpu_custom_call" | custom-call | flops 5637144576 | bytes 11010048 | tf_op jit(solution)/shard_map/gram/pallas_call | solution.py:126
  17.0 2.0 %collective-permute-start.4 = (bf16[528,256]{1,0:T(8,128)(2,1)S(1)}, bf16[528,256]{1,0:T(8,128)(2,1)S(1)}, u32[]{:S(2)}, u32[]{:S(2)}) collective-permute-start(bf16[528,256]{1,0:T(8,128)(2,1)S(1)} %get-tuple-element.51), channel_id=1, source_target_pairs={{0,1},{1,0},{2,3},{3,2},{4,5},{5,4},{6,7},{7,6},{8,9},{9,8},{10,11... | collective-permute-start | bytes 811016 | tf_op jit(solution)/shard_map/ppermute | solution.py:342
  19.0 1.6 %collective-permute-done.2 = bf16[528,256]{1,0:T(8,128)(2,1)S(1)} collective-permute-done((bf16[528,256]{1,0:T(8,128)(2,1)S(1)}, bf16[528,256]{1,0:T(8,128)(2,1)S(1)}, u32[]{:S(2)}, u32[]{:S(2)}) %collective-permute-start.2) | collective-permute-done | bytes 270368 | tf_op jit(solution)/shard_map/ppermute | solution.py:342
  20.6 0.1 add_convert_fusion.1.after.mine
  20.7 2.8 %collective-permute-start.3 = (bf16[528,256]{1,0:T(8,128)(2,1)S(1)}, bf16[528,256]{1,0:T(8,128)(2,1)S(1)}, u32[]{:S(2)}, u32[]{:S(2)}) collective-permute-start(bf16[528,256]{1,0:T(8,128)(2,1)S(1)} %add_convert_fusion.1.after.mine), channel_id=1, source_target_pairs={{0,4},{1,5},{2,6},{3,7},{4,0},{5,1},{6,2},{7,3},{8,12},{9,13},{10,... | collective-permute-start | bytes 811016 | tf_op jit(solution)/shard_map/ppermute | solution.py:342
  23.5 2.7 %collective-permute-done.4 = bf16[528,256]{1,0:T(8,128)(2,1)S(1)} collective-permute-done((bf16[528,256]{1,0:T(8,128)(2,1)S(1)}, bf16[528,256]{1,0:T(8,128)(2,1)S(1)}, u32[]{:S(2)}, u32[]{:S(2)}) %collective-permute-start.4) | collective-permute-done | bytes 270368 | tf_op jit(solution)/shard_map/ppermute | solution.py:342
  26.4 1.8 %collective-permute-start.6 = (bf16[528,256]{1,0:T(8,128)(2,1)S(1)}, bf16[528,256]{1,0:T(8,128)(2,1)S(1)}, u32[]{:S(2)}, u32[]{:S(2)}) collective-permute-start(bf16[528,256]{1,0:T(8,128)(2,1)S(1)} %add_convert_fusion), channel_id=1, source_target_pairs={{0,2},{1,3},{2,0},{3,1},{4,6},{5,7},{6,4},{7,5},{8,10},{9,11},{10,... | collective-permute-start | bytes 811016 | tf_op jit(solution)/shard_map/ppermute | solution.py:342
  28.1 1.5 %collective-permute-start.5 = (bf16[528,256]{1,0:T(8,128)(2,1)S(1)}, bf16[528,256]{1,0:T(8,128)(2,1)S(1)}, u32[]{:S(2)}, u32[]{:S(2)}) collective-permute-start(bf16[528,256]{1,0:T(8,128)(2,1)S(1)} %get-tuple-element.53), channel_id=1, source_target_pairs={{0,1},{1,0},{2,3},{3,2},{4,5},{5,4},{6,7},{7,6},{8,9},{9,8},{10,11... | collective-permute-start | bytes 811016 | tf_op jit(solution)/shard_map/ppermute | solution.py:342
  29.7 4.3 %gram.2 = (bf16[512,3584]{1,0:T(8,128)(2,1)S(1)}, bf16[528,256]{1,0:T(8,128)(2,1)S(1)}, f32[1,256]{1,0:T(1,128)S(1)}) custom-call(s32[6]{0:T(128)S(1)} %pad_add_fusion.order, bf16[528,256]{1,0:T(8,128)(2,1)S(1)} %add_convert_fusion.1.after.mine, bf16[2048,3584]{1,0:T(8,128)(2,1)} %g_ref.3), custom_call_target="tpu_custom_call" | custom-call | flops 1879048192 | bytes 3670016 | tf_op jit(solution)/shard_map/gram/pallas_call | solution.py:126
  33.9 0.9 %collective-permute-done.3.other = bf16[528,256]{1,0:T(8,128)(2,1)S(1)} collective-permute-done((bf16[528,256]{1,0:T(8,128)(2,1)S(1)}, bf16[528,256]{1,0:T(8,128)(2,1)S(1)}, u32[]{:S(2)}, u32[]{:S(2)}) %collective-permute-start.3) | collective-permute-done | bytes 270368 | tf_op jit(solution)/shard_map/ppermute | solution.py:342
  34.9 3.2 %newton.1.folded.after = bf16[528,256]{1,0:T(8,128)(2,1)S(1)} custom-call(f32[1,256]{1,0:T(1,128)S(1)} %get-tuple-element.49.after, bf16[528,256]{1,0:T(8,128)(2,1)S(1)} %add_convert_fusion.1.after.mine, bf16[528,256]{1,0:T(8,128)(2,1)S(1)} %collective-permute-done.3.other), custom_call_target="tpu_custom_call" | custom-call | flops 2147483648 | bytes 2097152 | tf_op jit(solution)/shard_map/newton/pallas_call | solution.py:185
  38.1 1.4 %collective-permute-start.8 = (bf16[528,256]{1,0:T(8,128)(2,1)S(1)}, bf16[528,256]{1,0:T(8,128)(2,1)S(1)}, u32[]{:S(2)}, u32[]{:S(2)}) collective-permute-start(bf16[528,256]{1,0:T(8,128)(2,1)S(1)} %newton.1.folded.after), channel_id=1, source_target_pairs={{0,1},{1,0},{2,3},{3,2},{4,5},{5,4},{6,7},{7,6},{8,9},{9,8},{10,11... | collective-permute-start | bytes 811016 | tf_op jit(solution)/shard_map/ppermute | solution.py:342
  39.5 0.6 collective-permute-start.7
  40.1 0.6 norm.1
  40.7 4.5 %collective-permute-start.11 = (f32[8,128]{1,0:T(8,128)S(1)}, f32[8,128]{1,0:T(8,128)S(1)}, u32[]{:S(2)}, u32[]{:S(2)}) collective-permute-start(f32[8,128]{1,0:T(8,128)S(1)} %norm.1), channel_id=1, source_target_pairs={{0,20},{1,21},{2,22},{3,23},{4,16},{5,17},{6,18},{7,19},{8,28},{9,... | collective-permute-start | bytes 12296 | tf_op jit(solution)/shard_map/ppermute | solution.py:342
  45.1 0.5 collective-permute-start.10
  45.6 0.1 collective-permute-start.9
  45.7 2.3 %multiply.3 = (bf16[512,3584]{1,0:T(8,128)(2,1)S(1)}, bf16[512,512]{1,0:T(8,128)(2,1)S(1)}) custom-call(bf16[528,256]{1,0:T(8,128)(2,1)S(1)} %newton.1.folded.after, bf16[528,256]{1,0:T(8,128)(2,1)S(1)} %newton.1.folded.after, bf16[512,3584]{1,0:T(8,128)(2,1)S(1)} %get-tuple-element.57.held_ref), custom_call_target="tpu_custom_call", output_to_operand_aliasing={{0}: (2, {})} | custom-call | flops 1880000000 | bytes 1 | tf_op jit(solution)/shard_map/multiply/pallas_call | solution.py:244
  48.1 0.6 collective-permute-done.10
  48.7 1.4 %collective-permute-done.9 = f32[8,128]{1,0:T(8,128)S(1)} collective-permute-done((f32[8,128]{1,0:T(8,128)S(1)}, f32[8,128]{1,0:T(8,128)S(1)}, u32[]{:S(2)}, u32[]{:S(2)}) %collective-permute-start.9) | collective-permute-done | bytes 4128 | tf_op jit(solution)/shard_map/ppermute | solution.py:342
  50.1 0.6 collective-permute-start.12
  50.7 1.5 %collective-permute-start.14 = (bf16[528,256]{1,0:T(8,128)(2,1)S(1)}, bf16[528,256]{1,0:T(8,128)(2,1)S(1)}, u32[]{:S(2)}, u32[]{:S(2)}) collective-permute-start(bf16[528,256]{1,0:T(8,128)(2,1)S(1)} %collective-permute-done.7.after.folded), channel_id=1, source_target_pairs={{0,1},{1,0},{2,3},{3,2},{4,5},{5,4},{6,7},{7,6},{8,9},{9,8},{10,11... | collective-permute-start | bytes 811016 | tf_op jit(solution)/shard_map/ppermute | solution.py:342
  52.2 2.5 %multiply.4 = (bf16[512,3584]{1,0:T(8,128)(2,1)S(1)}, bf16[512,512]{1,0:T(8,128)(2,1)S(1)}) custom-call(bf16[528,256]{1,0:T(8,128)(2,1)S(1)} %collective-permute-done.8.after.folded, bf16[528,256]{1,0:T(8,128)(2,1)S(1)} %collective-permute-done.8.after.folded, bf16[512,3584]{1,0:T(8,128)(2,1)S(1)} %get-tuple-element.69.held_ref), custom_call_target="tpu_custom_call", output_to_operand_aliasing={{0}: (2, {})} | custom-call | flops 1880000000 | bytes 1 | tf_op jit(solution)/shard_map/multiply/pallas_call | solution.py:244
  54.9 1.2 %collective-permute-done.13 = f32[8,128]{1,0:T(8,128)S(1)} collective-permute-done((f32[8,128]{1,0:T(8,128)S(1)}, f32[8,128]{1,0:T(8,128)S(1)}, u32[]{:S(2)}, u32[]{:S(2)}) %collective-permute-start.13) | collective-permute-done | bytes 4128 | tf_op jit(solution)/shard_map/ppermute | solution.py:342
  56.0 0.9 %collective-permute-start.15 = (f32[8,128]{1,0:T(8,128)S(1)}, f32[8,128]{1,0:T(8,128)S(1)}, u32[]{:S(2)}, u32[]{:S(2)}) collective-permute-start(f32[8,128]{1,0:T(8,128)S(1)} %add.47), channel_id=1, source_target_pairs={{0,2},{1,3},{2,0},{3,1},{4,6},{5,7},{6,4},{7,5},{8,10},{9,11},{10,... | collective-permute-start | bytes 12296 | tf_op jit(solution)/shard_map/ppermute | solution.py:342
  56.9 2.3 %multiply.5 = (bf16[512,3584]{1,0:T(8,128)(2,1)S(1)}, bf16[512,512]{1,0:T(8,128)(2,1)S(1)}) custom-call(bf16[528,256]{1,0:T(8,128)(2,1)S(1)} %collective-permute-done.7.after.folded, bf16[528,256]{1,0:T(8,128)(2,1)S(1)} %collective-permute-done.7.after.folded, bf16[512,3584]{1,0:T(8,128)(2,1)S(1)} %get-tuple-element.74.held_ref), custom_call_target="tpu_custom_call", output_to_operand_aliasing={{0}: (2, {})} | custom-call | flops 1880000000 | bytes 1 | tf_op jit(solution)/shard_map/multiply/pallas_call | solution.py:244
  59.2 0.4 collective-permute-done.15
  59.6 7.7 %finish.1 = (bf16[2048,3584]{1,0:T(8,128)(2,1)}, bf16[2,512,512]{2,1,0:T(8,128)(2,1)}, bf16[512,3584]{1,0:T(8,128)(2,1)S(1)}, bf16[512,3584]{1,0:T(8,128)(2,1)S(...) custom-call(s32[6]{0:T(128)S(1)} %pad_add_fusion.order, ...), custom_call_target="tpu_custom_call", output_to_operand_aliasing={{2}: (7, {}), {3}: (8, {}), {4}: (9, {}), {5}: (10, {})} | custom-call | tf_op jit(solution)/shard_map/finish/pallas_call | solution.py:318
  (22 shorter events, 0.3 us)
Async XLA Ops:
  0.7 1.6 %copy-start = (bf16[512,2048]{1,0:T(8,128)(2,1)S(1)}, bf16[512,2048]{1,0:T(8,128)(2,1)}, u32[]{:S(2)}) copy-start(bf16[512,2048]{1,0:T(8,128)(2,1)} %x_ref.1) | copy-start | bytes 6291460
  3.9 15.1 %collective-permute-start = (bf16[528,256]{1,0:T(8,128)(2,1)S(1)}, bf16[528,256]{1,0:T(8,128)(2,1)S(1)}, u32[]{:S(2)}, u32[]{:S(2)}) collective-permute-start(bf16[528,256]{1,0:T(8,128)(2,1)S(1)} %get-tuple-element.46), channel_id=1, source_target_pairs={{0,1},{1,0},{2,3},{3,2},{4,5},{5,4},{6,7},{7,6},{8,9},{9,8},{10,11... | collective-permute-start | bytes 811016 | tf_op jit(solution)/shard_map/ppermute | solution.py:342
  6.9 12.1 %collective-permute-start.1 = (bf16[528,256]{1,0:T(8,128)(2,1)S(1)}, bf16[528,256]{1,0:T(8,128)(2,1)S(1)}, u32[]{:S(2)}, u32[]{:S(2)}) collective-permute-start(bf16[528,256]{1,0:T(8,128)(2,1)S(1)} %get-tuple-element.47), channel_id=1, source_target_pairs={{0,2},{1,3},{2,0},{3,1},{4,6},{5,7},{6,4},{7,5},{8,10},{9,11},{10,... | collective-permute-start | bytes 811016 | tf_op jit(solution)/shard_map/ppermute | solution.py:342
  8.5 12.1 %collective-permute-start.2 = (bf16[528,256]{1,0:T(8,128)(2,1)S(1)}, bf16[528,256]{1,0:T(8,128)(2,1)S(1)}, u32[]{:S(2)}, u32[]{:S(2)}) collective-permute-start(bf16[528,256]{1,0:T(8,128)(2,1)S(1)} %get-tuple-element.48), channel_id=1, source_target_pairs={{0,3},{1,2},{2,1},{3,0},{4,7},{5,6},{6,5},{7,4},{8,11},{9,10},{10,... | collective-permute-start | bytes 811016 | tf_op jit(solution)/shard_map/ppermute | solution.py:342
  17.0 9.3 %collective-permute-start.4 = (bf16[528,256]{1,0:T(8,128)(2,1)S(1)}, bf16[528,256]{1,0:T(8,128)(2,1)S(1)}, u32[]{:S(2)}, u32[]{:S(2)}) collective-permute-start(bf16[528,256]{1,0:T(8,128)(2,1)S(1)} %get-tuple-element.51), channel_id=1, source_target_pairs={{0,1},{1,0},{2,3},{3,2},{4,5},{5,4},{6,7},{7,6},{8,9},{9,8},{10,11... | collective-permute-start | bytes 811016 | tf_op jit(solution)/shard_map/ppermute | solution.py:342
  20.7 14.1 %collective-permute-start.3 = (bf16[528,256]{1,0:T(8,128)(2,1)S(1)}, bf16[528,256]{1,0:T(8,128)(2,1)S(1)}, u32[]{:S(2)}, u32[]{:S(2)}) collective-permute-start(bf16[528,256]{1,0:T(8,128)(2,1)S(1)} %add_convert_fusion.1.after.mine), channel_id=1, source_target_pairs={{0,4},{1,5},{2,6},{3,7},{4,0},{5,1},{6,2},{7,3},{8,12},{9,13},{10,... | collective-permute-start | bytes 811016 | tf_op jit(solution)/shard_map/ppermute | solution.py:342
  26.4 13.7 %collective-permute-start.6 = (bf16[528,256]{1,0:T(8,128)(2,1)S(1)}, bf16[528,256]{1,0:T(8,128)(2,1)S(1)}, u32[]{:S(2)}, u32[]{:S(2)}) collective-permute-start(bf16[528,256]{1,0:T(8,128)(2,1)S(1)} %add_convert_fusion), channel_id=1, source_target_pairs={{0,2},{1,3},{2,0},{3,1},{4,6},{5,7},{6,4},{7,5},{8,10},{9,11},{10,... | collective-permute-start | bytes 811016 | tf_op jit(solution)/shard_map/ppermute | solution.py:342
  28.1 11.9 %collective-permute-start.5 = (bf16[528,256]{1,0:T(8,128)(2,1)S(1)}, bf16[528,256]{1,0:T(8,128)(2,1)S(1)}, u32[]{:S(2)}, u32[]{:S(2)}) collective-permute-start(bf16[528,256]{1,0:T(8,128)(2,1)S(1)} %get-tuple-element.53), channel_id=1, source_target_pairs={{0,1},{1,0},{2,3},{3,2},{4,5},{5,4},{6,7},{7,6},{8,9},{9,8},{10,11... | collective-permute-start | bytes 811016 | tf_op jit(solution)/shard_map/ppermute | solution.py:342
  38.1 12.1 %collective-permute-start.8 = (bf16[528,256]{1,0:T(8,128)(2,1)S(1)}, bf16[528,256]{1,0:T(8,128)(2,1)S(1)}, u32[]{:S(2)}, u32[]{:S(2)}) collective-permute-start(bf16[528,256]{1,0:T(8,128)(2,1)S(1)} %newton.1.folded.after), channel_id=1, source_target_pairs={{0,1},{1,0},{2,3},{3,2},{4,5},{5,4},{6,7},{7,6},{8,9},{9,8},{10,11... | collective-permute-start | bytes 811016 | tf_op jit(solution)/shard_map/ppermute | solution.py:342
  39.5 10.7 %collective-permute-start.7 = (bf16[528,256]{1,0:T(8,128)(2,1)S(1)}, bf16[528,256]{1,0:T(8,128)(2,1)S(1)}, u32[]{:S(2)}, u32[]{:S(2)}) collective-permute-start(bf16[528,256]{1,0:T(8,128)(2,1)S(1)} %newton.1.folded.after), channel_id=1, source_target_pairs={{0,2},{1,3},{2,0},{3,1},{4,6},{5,7},{6,4},{7,5},{8,10},{9,11},{10,... | collective-permute-start | bytes 811016 | tf_op jit(solution)/shard_map/ppermute | solution.py:342
  40.7 7.4 %collective-permute-start.11 = (f32[8,128]{1,0:T(8,128)S(1)}, f32[8,128]{1,0:T(8,128)S(1)}, u32[]{:S(2)}, u32[]{:S(2)}) collective-permute-start(f32[8,128]{1,0:T(8,128)S(1)} %norm.1), channel_id=1, source_target_pairs={{0,20},{1,21},{2,22},{3,23},{4,16},{5,17},{6,18},{7,19},{8,28},{9,... | collective-permute-start | bytes 12296 | tf_op jit(solution)/shard_map/ppermute | solution.py:342
  45.1 3.6 %collective-permute-start.10 = (f32[8,128]{1,0:T(8,128)S(1)}, f32[8,128]{1,0:T(8,128)S(1)}, u32[]{:S(2)}, u32[]{:S(2)}) collective-permute-start(f32[8,128]{1,0:T(8,128)S(1)} %norm.1), channel_id=1, source_target_pairs={{0,16},{1,17},{2,18},{3,19},{4,20},{5,21},{6,22},{7,23},{8,24},{9,... | collective-permute-start | bytes 12296 | tf_op jit(solution)/shard_map/ppermute | solution.py:342
  45.6 4.5 %collective-permute-start.9 = (f32[8,128]{1,0:T(8,128)S(1)}, f32[8,128]{1,0:T(8,128)S(1)}, u32[]{:S(2)}, u32[]{:S(2)}) collective-permute-start(f32[8,128]{1,0:T(8,128)S(1)} %norm.1), channel_id=1, source_target_pairs={{0,4},{1,5},{2,6},{3,7},{4,0},{5,1},{6,2},{7,3},{8,12},{9,13},{10,... | collective-permute-start | bytes 12296 | tf_op jit(solution)/shard_map/ppermute | solution.py:342
  50.1 4.6 %collective-permute-start.12 = (f32[8,128]{1,0:T(8,128)S(1)}, f32[8,128]{1,0:T(8,128)S(1)}, u32[]{:S(2)}, u32[]{:S(2)}) collective-permute-start(f32[8,128]{1,0:T(8,128)S(1)} %add_add_fusion), channel_id=1, source_target_pairs={{0,1},{1,0},{2,3},{3,2},{4,5},{5,4},{6,7},{7,6},{8,9},{9,8},{10,11... | collective-permute-start | bytes 12296 | tf_op jit(solution)/shard_map/ppermute | solution.py:342
  50.7 8.9 %collective-permute-start.14 = (bf16[528,256]{1,0:T(8,128)(2,1)S(1)}, bf16[528,256]{1,0:T(8,128)(2,1)S(1)}, u32[]{:S(2)}, u32[]{:S(2)}) collective-permute-start(bf16[528,256]{1,0:T(8,128)(2,1)S(1)} %collective-permute-done.7.after.folded), channel_id=1, source_target_pairs={{0,1},{1,0},{2,3},{3,2},{4,5},{5,4},{6,7},{7,6},{8,9},{9,8},{10,11... | collective-permute-start | bytes 811016 | tf_op jit(solution)/shard_map/ppermute | solution.py:342
  54.8 4.9 %copy-start.1 = (s32[4,4]{1,0:T(4,128)S(1)}, s32[4,4]{1,0:T(4,128)}, u32[]{:S(2)}) copy-start(s32[4,4]{1,0:T(4,128)} %owner_slot.1) | copy-start | bytes 196
  54.8 1.2 %collective-permute-start.13 = (f32[8,128]{1,0:T(8,128)S(1)}, f32[8,128]{1,0:T(8,128)S(1)}, u32[]{:S(2)}, u32[]{:S(2)}) collective-permute-start(f32[8,128]{1,0:T(8,128)S(1)} %add.46), channel_id=1, source_target_pairs={{0,8},{1,9},{2,10},{3,11},{4,12},{5,13},{6,14},{7,15},{8,0},{9,1},... | collective-permute-start | bytes 12296 | tf_op jit(solution)/shard_map/ppermute | solution.py:342
  56.0 3.6 %collective-permute-start.15 = (f32[8,128]{1,0:T(8,128)S(1)}, f32[8,128]{1,0:T(8,128)S(1)}, u32[]{:S(2)}, u32[]{:S(2)}) collective-permute-start(f32[8,128]{1,0:T(8,128)S(1)} %add.47), channel_id=1, source_target_pairs={{0,2},{1,3},{2,0},{3,1},{4,6},{5,7},{6,4},{7,5},{8,10},{9,11},{10,... | collective-permute-start | bytes 12296 | tf_op jit(solution)/shard_map/ppermute | solution.py:342
